TPU v7x, 32 devices: a whole 2x2x4 slice. The times are simulated.
32 devices in a mesh: dp: 4 (over y, x), tensor: 4 (over z), chip: 2 (over core).
Axes of the slice: x: 2, y: 2, z: 4, core: 2. Of those that a mesh axis runs over, the one named last changes fastest.
Arguments:
- residual: bfloat16 [8, 1024, 2048], P(('dp', 'chip'), 'tensor'), may hold values from -6 to 6
- cotangent: bfloat16 [8, 1024, 2048], P(('dp', 'chip'), 'tensor'), may hold values from -6 to 6
- lengths: int32 [8, 5], P(('dp', 'chip')), may hold values from 1 to 512, 1024 in all within a row
- owners: int32 [8], replicated, may hold values from 0 to 7, as said below
- step_count: int32 [1], replicated, may hold values from 1 to 20
- rates: float32 [8], replicated, as said below
- weight_decay: float32 [1], replicated, may hold values from 0.1 to 1
- ema_decay: float32 [1], replicated, may hold values from 0.5 to 0.95
- master: float32 [4, 8, 1574912], P('tensor', ('dp', 'chip')), as said below
- moment_one: float32 [4, 8, 1574912], P('tensor', ('dp', 'chip')), as said below
- moment_two: float32 [4, 8, 1574912], P('tensor', ('dp', 'chip')), as said below
- average: float32 [4, 8, 1574912], P('tensor', ('dp', 'chip')), as said below
Outputs:
- output: float32 [8, 1024, 2048], P(('dp', 'chip'), 'tensor')
- input_grad: float32 [8, 1024, 2048], P(('dp', 'chip'), 'tensor')
- new_master: float32 [4, 8, 1574912], P('tensor', ('dp', 'chip'))
- new_moment_one: float32 [4, 8, 1574912], P('tensor', ('dp', 'chip'))
- new_moment_two: float32 [4, 8, 1574912], P('tensor', ('dp', 'chip'))
- new_average: float32 [4, 8, 1574912], P('tensor', ('dp', 'chip'))
- reduced_grad: float32 [4, 8, 1574912], P('tensor', ('dp', 'chip'))
Inputs may be any that keep to these rules, and one draw needn't show every extreme that they name: Row g lists the lengths of group g's sequences in order; they sum to 1024 and the longest is 512. `owners`: a permutation of 0 to 7. `master`: the entries of S are equal for every tensor index. `moment_one`: the entries of S are equal for every tensor index. `moment_two`: every entry is positive; the entries of S are equal for every tensor index. `average`: the entries of S are equal for every tensor index. `rates`: every rate is positive.
All inputs are finite; a program needn't handle non-finite values.
Results may differ from a plain program's by a relative error of at most 0.003.
The roundings to bfloat16 on the way count: a program that leaves them out, or rounds other values in their place, can miss the bound.
Values may be sent and summed in bfloat16 or wider, within the bound.
No kernel may reach another device: no remote copies, remote signals or barrier semaphores. Data moves between devices by JAX's collectives and lax.ppermute only.
A program may use at most 384 MiB of HBM per device.

v0:
```python
import math

import jax
import jax.numpy as jnp
from jax import lax
from jax.sharding import PartitionSpec as P

D = 2048
H = 16
HD = 128
FF = 8192
ROT = 32


norm_epsilon = 1e-05
adam_epsilon = 1e-08
beta_one = 0.5
beta_two = 0.5
rope_base = 10000.0
masked_score = -1e30


def matmul(left, right):
    return jnp.dot(left, right, preferred_element_type=jnp.float32)


def product_rows(left, right):
    return lax.dot_general(
        left, right, (((0,), (0,)), ((), ())), preferred_element_type=jnp.float32
    )


def product_back(left, right):
    return lax.dot_general(
        left, right, (((1,), (1,)), ((), ())), preferred_element_type=jnp.float32
    )


def bound_list(local_width, local_ff):
    widths = [
        D * 3 * local_width,
        local_width * D,
        D * local_ff,
        local_ff * D,
        3 * local_width,
        local_ff,
        6 * D,
    ]
    bounds = [0]
    for part_width in widths:
        bounds.append(bounds[-1] + part_width)
    return bounds


def group_layout(seq_lengths, group_rows):
    seq_ends = jnp.cumsum(seq_lengths)
    starts = seq_ends - seq_lengths
    token_index = jnp.arange(group_rows, dtype=jnp.int32)
    segment = jnp.sum((token_index[:, None] >= seq_ends[None, :]).astype(jnp.int32), axis=1)
    chosen = (
        segment[:, None] == jnp.arange(seq_lengths.shape[0], dtype=jnp.int32)[None, :]
    ).astype(jnp.int32)
    places = token_index - jnp.sum(chosen * starts[None, :], axis=1)
    return (segment, places.astype(jnp.float32))


def rotary_tables(places):
    half_rot = ROT // 2
    frequency = rope_base ** (-2.0 * jnp.arange(half_rot, dtype=jnp.float32) / ROT)
    angles = places[:, None] * frequency[None, :]
    return (jnp.cos(angles)[:, None, :], jnp.sin(angles)[:, None, :])


def rotate(values, cosine, sines):
    half_rot = ROT // 2
    first = values[..., :half_rot]
    second = values[..., half_rot:ROT]
    return jnp.concatenate(
        [first * cosine - second * sines, second * cosine + first * sines, values[..., ROT:]],
        axis=-1,
    )


def norm_stats(inputs):
    center = inputs - jnp.mean(inputs, axis=-1, keepdims=True)
    scale = lax.rsqrt(jnp.mean(center * center, axis=-1, keepdims=True) + norm_epsilon)
    return (center * scale, scale)


def norm_back(grad_norm, gain, unit_rows, scale):
    scaled = grad_norm * gain
    return scale * (
        scaled
        - jnp.mean(scaled, axis=-1, keepdims=True)
        - unit_rows * jnp.mean(scaled * unit_rows, axis=-1, keepdims=True)
    )


def adam_update(
    weights, first, second, moving, gradient, step_rate, step_value, decay_rate, ema_keep
):
    bias_one = 1.0 - jnp.power(beta_one, step_value)
    bias_two = 1.0 - jnp.power(beta_two, step_value)
    new_first = beta_one * first + (1.0 - beta_one) * gradient
    new_second = beta_two * second + (1.0 - beta_two) * gradient * gradient
    ratio = new_first / bias_one / (jnp.sqrt(new_second / bias_two) + adam_epsilon)
    new_weights = weights - step_rate * (ratio + decay_rate * weights)
    new_moving = ema_keep * moving + (1.0 - ema_keep) * new_weights
    return (new_weights, new_first, new_second, new_moving)


def on_device(
    residual,
    cotangent,
    lengths,
    owners,
    step_count,
    rates,
    weight_decay,
    ema_decay,
    master,
    moment_one,
    moment_two,
    average,
):
    tensor_count = lax.axis_size("tensor")
    group_count = lax.axis_size(("dp", "chip"))
    local_heads = H // tensor_count
    local_width = local_heads * HD
    local_ff = FF // tensor_count
    rows_here = residual.shape[1]
    group_rows = rows_here * tensor_count
    bucket_size = master.shape[2]
    bounds = bound_list(local_width, local_ff)
    slots = jnp.arange(group_count, dtype=jnp.int32)
    inverse = jnp.sum(
        slots[None, :] * (owners[None, :] == slots[:, None]).astype(jnp.int32), axis=1
    )
    gathered = lax.all_gather(master.astype(jnp.bfloat16), ("dp", "chip"), axis=1, tiled=True)
    flat_params = jnp.take(gathered[0], owners, axis=0).reshape(-1)
    mixer_in = flat_params[bounds[0] : bounds[1]].reshape(D, 3 * local_width)
    mixer_out = flat_params[bounds[1] : bounds[2]].reshape(local_width, D)
    expand_weight = flat_params[bounds[2] : bounds[3]].reshape(D, local_ff)
    shrink_weight = flat_params[bounds[3] : bounds[4]].reshape(local_ff, D)
    mixer_bias = flat_params[bounds[4] : bounds[5]].astype(jnp.float32)
    expand_bias = flat_params[bounds[5] : bounds[6]].astype(jnp.float32)
    small_params = flat_params[bounds[6] : bounds[7]].reshape(6, D).astype(jnp.float32)
    own_rows = residual[0].astype(jnp.float32)
    segment, places = group_layout(lengths[0], group_rows)
    cosine, sines = rotary_tables(places)
    own_unit, own_scale = norm_stats(own_rows)
    normed_one = (own_unit * small_params[0] + small_params[1]).astype(jnp.bfloat16)
    normed_two = (own_unit * small_params[2] + small_params[3]).astype(jnp.bfloat16)
    full_one, full_two = (
        lax.all_gather(normed_one, "tensor", axis=0, tiled=True),
        lax.all_gather(normed_two, "tensor", axis=0, tiled=True),
    )
    projected = matmul(full_one, mixer_in) + mixer_bias
    head_shape = (group_rows, local_heads, HD)
    queries = rotate(projected[:, :local_width].reshape(head_shape), cosine, sines).astype(
        jnp.bfloat16
    )
    keys = rotate(
        projected[:, local_width : 2 * local_width].reshape(head_shape), cosine, sines
    ).astype(jnp.bfloat16)
    values = projected[:, 2 * local_width :].reshape(head_shape).astype(jnp.bfloat16)
    block_rows = min(512, group_rows)
    block_count = group_rows // block_rows
    score_scale = 1.0 / math.sqrt(HD)
    key_index = jnp.arange(group_rows, dtype=jnp.int32)

    def block_scores(start):
        query_block = lax.dynamic_slice_in_dim(queries, start, block_rows, 0)
        scores = (
            jnp.einsum("qhd,khd->hqk", query_block, keys, preferred_element_type=jnp.float32)
            * score_scale
        )
        row_index = start + jnp.arange(block_rows, dtype=jnp.int32)
        row_segment = lax.dynamic_slice_in_dim(segment, start, block_rows, 0)
        allowed = (row_segment[:, None] == segment[None, :]) & (
            key_index[None, :] <= row_index[:, None]
        )
        return (query_block, jnp.where(allowed[None], scores, masked_score))

    def attend_block(index):
        query_block, scores = block_scores(index * block_rows)
        row_top = jnp.max(scores, axis=-1, keepdims=True)
        raised = jnp.exp(scores - row_top)
        totals = jnp.sum(raised, axis=-1, keepdims=True)
        soft_weights = (raised / totals).astype(jnp.bfloat16)
        mixed = jnp.einsum("hqk,khd->qhd", soft_weights, values, preferred_element_type=jnp.float32)
        return (mixed.reshape(block_rows, local_width), (row_top + jnp.log(totals))[..., 0])

    context_blocks, log_blocks = lax.map(attend_block, jnp.arange(block_count, dtype=jnp.int32))
    context = context_blocks.reshape(group_rows, local_width).astype(jnp.bfloat16)
    before = matmul(full_two, expand_weight) + expand_bias
    hidden = jax.nn.gelu(before, approximate=False).astype(jnp.bfloat16)
    branches = lax.psum_scatter(
        matmul(context, mixer_out) + matmul(hidden, shrink_weight),
        "tensor",
        scatter_dimension=0,
        tiled=True,
    )
    output = own_rows + branches + small_params[4] + small_params[5]
    grad_own = cotangent[0].astype(jnp.float32)
    grad_rows = lax.all_gather(cotangent[0], "tensor", axis=0, tiled=True)
    grad_mixer_out = product_rows(context, grad_rows)
    grad_shrink = product_rows(hidden, grad_rows)
    grad_context = product_back(grad_rows, mixer_out).astype(jnp.bfloat16)
    grad_hidden = product_back(grad_rows, shrink_weight)
    gelu_pull = jax.vjp(lambda inner: jax.nn.gelu(inner, approximate=False), before)[1]
    grad_before = gelu_pull(grad_hidden)[0].astype(jnp.bfloat16)
    grad_expand = product_rows(full_two, grad_before)
    grad_expand_bias = jnp.sum(grad_before.astype(jnp.float32), axis=0)
    partial_two = product_back(grad_before, expand_weight)

    def attention_back(carry, index):
        grad_keys, grad_values = carry
        start = index * block_rows
        query_block, scores = block_scores(start)
        log_rows = lax.dynamic_index_in_dim(log_blocks, index, 0, keepdims=False)
        soft_weights = jnp.exp(scores - log_rows[..., None])
        grad_block = lax.dynamic_slice_in_dim(grad_context, start, block_rows, 0).reshape(
            block_rows, local_heads, HD
        )
        grad_weights = jnp.einsum(
            "qhd,khd->hqk", grad_block, values, preferred_element_type=jnp.float32
        )
        delta = jnp.sum(soft_weights * grad_weights, axis=-1, keepdims=True)
        grad_scores = (soft_weights * (grad_weights - delta)).astype(jnp.bfloat16)
        grad_query = (
            jnp.einsum("hqk,khd->qhd", grad_scores, keys, preferred_element_type=jnp.float32)
            * score_scale
        )
        grad_keys = (
            grad_keys
            + jnp.einsum(
                "hqk,qhd->khd", grad_scores, query_block, preferred_element_type=jnp.float32
            )
            * score_scale
        )
        grad_values = grad_values + jnp.einsum(
            "hqk,qhd->khd",
            soft_weights.astype(jnp.bfloat16),
            grad_block,
            preferred_element_type=jnp.float32,
        )
        return ((grad_keys, grad_values), grad_query)

    zero_heads = jnp.zeros(head_shape, jnp.float32)
    (grad_keys, grad_values), grad_query = lax.scan(
        attention_back, (zero_heads, zero_heads), jnp.arange(block_count, dtype=jnp.int32)
    )
    grad_query = grad_query.reshape(head_shape)
    grad_projected = jnp.concatenate(
        [
            rotate(grad_query, cosine, -sines).reshape(group_rows, local_width),
            rotate(grad_keys, cosine, -sines).reshape(group_rows, local_width),
            grad_values.reshape(group_rows, local_width),
        ],
        axis=1,
    ).astype(jnp.bfloat16)
    grad_mixer_in = product_rows(full_one, grad_projected)
    grad_mixer_bias = jnp.sum(grad_projected.astype(jnp.float32), axis=0)
    partial_one = product_back(grad_projected, mixer_in)
    bias_grad = jnp.sum(grad_own, axis=0)
    grad_one, grad_two = (
        lax.psum_scatter(partial_one, "tensor", scatter_dimension=0, tiled=True),
        lax.psum_scatter(partial_two, "tensor", scatter_dimension=0, tiled=True),
    )
    norm_grads = [
        jnp.sum(grad_one * own_unit, axis=0),
        jnp.sum(grad_one, axis=0),
        jnp.sum(grad_two * own_unit, axis=0),
        jnp.sum(grad_two, axis=0),
    ]
    input_grad = (
        grad_own
        + norm_back(grad_one, small_params[0], own_unit, own_scale)
        + norm_back(grad_two, small_params[2], own_unit, own_scale)
    )
    small_grad = jnp.stack(norm_grads + [bias_grad, bias_grad])
    small_grad = lax.psum(small_grad, "tensor")
    flat_grad = jnp.concatenate(
        [
            grad_mixer_in.reshape(-1),
            grad_mixer_out.reshape(-1),
            grad_expand.reshape(-1),
            grad_shrink.reshape(-1),
            grad_mixer_bias,
            grad_expand_bias,
            small_grad.reshape(-1),
            jnp.zeros((group_count * bucket_size - bounds[7],), jnp.float32),
        ]
    )
    stored_grad = jnp.take(flat_grad.reshape(group_count, bucket_size), inverse, axis=0)
    reduced = lax.psum_scatter(stored_grad, ("dp", "chip"), scatter_dimension=0, tiled=True)[0]
    my_bucket = inverse[lax.axis_index(("dp", "chip"))]
    position = my_bucket * bucket_size + jnp.arange(bucket_size, dtype=jnp.int32)
    step_rate = jnp.zeros((bucket_size,), jnp.float32) + rates[0]
    for kind_index in range(1, 8):
        step_rate = jnp.where(position >= bounds[kind_index], rates[kind_index], step_rate)
    step_value = step_count[0].astype(jnp.float32)
    new_weights, new_first, new_second, new_moving = adam_update(
        master[0, 0],
        moment_one[0, 0],
        moment_two[0, 0],
        average[0, 0],
        reduced,
        step_rate,
        step_value,
        weight_decay[0],
        ema_decay[0],
    )
    return (
        output[None],
        input_grad[None],
        new_weights[None, None],
        new_first[None, None],
        new_second[None, None],
        new_moving[None, None],
        reduced[None, None],
    )


def solution(mesh):
    placed = (
        P(("dp", "chip"), "tensor", None),
        P(("dp", "chip"), "tensor", None),
        P(("dp", "chip"), None),
        P(),
        P(),
        P(),
        P(),
        P(),
        P("tensor", ("dp", "chip"), None),
        P("tensor", ("dp", "chip"), None),
        P("tensor", ("dp", "chip"), None),
        P("tensor", ("dp", "chip"), None),
    )
    return jax.shard_map(
        on_device,
        mesh=mesh,
        in_specs=placed,
        out_specs=(
            P(("dp", "chip"), "tensor", None),
            P(("dp", "chip"), "tensor", None),
            P("tensor", ("dp", "chip"), None),
            P("tensor", ("dp", "chip"), None),
            P("tensor", ("dp", "chip"), None),
            P("tensor", ("dp", "chip"), None),
            P("tensor", ("dp", "chip"), None),
        ),
        check_vma=False,
    )
```

profile of v0, /device:TPU:0, one launch (start us, length us, event | category | flops | bytes accessed | tf_op | source)
XLA Modules:
  0.0 1929.3 jit_solution(10903545629987534162)
XLA Ops:
  7.2 6.6 bitcast_convert_fusion
  16.6 232.6 %all-gather.6.cloned.1.call-done = bf16[1,8,1574912]{2,0,1:T(2,128)(2,1)} async-done(((bf16[1,1,1574912]{2,0,1:T(2,128)(2,1)}), bf16[1,8,1574912]{2,0,1:T(2,128)(2,1)}) %all-gather.6.cloned.1.call-update) | async-done | bytes 25198608 | tf_op jit(solution)/shard_map/all_gather | solution.py:139
  249.1 26.4 %copy.190 = bf16[1,8,1574912]{2,1,0:T(8,128)(2,1)} copy(bf16[1,8,1574912]{2,0,1:T(2,128)(2,1)} %all-gather.6.cloned.1.call-done) | data formatting | bytes 50397184
  278.5 16.9 fusion.123
  295.5 6.5 gather_fusion.11
  301.9 6.4 gather_fusion.12
  308.4 6.5 gather_fusion.10
  314.8 6.7 gather_fusion.9
  321.5 6.5 gather_fusion.8
  328.1 6.5 gather_fusion.7
  334.6 6.5 gather_fusion.6
  341.0 6.7 gather_fusion.5
  347.7 6.4 gather_fusion.4
  354.1 6.4 gather_fusion.3
  360.6 6.9 gather_fusion.2
  367.4 6.4 gather_fusion.1
  397.0 17.4 select_bitcast_fusion
  414.4 14.4 copy.171
  428.8 8.3 copy-done.2
  442.5 55.7 %gather.11 = bf16[6152,2048]{1,0:T(8,128)(2,1)} reshape(bf16[8,1574912]{1,0:T(8,128)(2,1)} %constant_dynamic-update-slice_fusion.1) | data formatting | bytes 50397184 | tf_op jit(solution)/shard_map/jit(_take)/gather | solution.py:140
  498.1 6.4 slice.215
  504.6 12.3 reshape.479
  517.6 21.9 %broadcast_select_fusion.1 = bf16[6152,2048]{1,0:T(8,128)(2,1)} fusion(bf16[6152,2048]{1,0:T(8,128)(2,1)} %gather.11, pred[6152]{0:T(1024)(128)(4,1)S(1)} %broadcast_in_dim.147), kind=kLoop, calls=%fused_computation.73 | loop fusion | flops 12599296 | bytes 50403336 | tf_op jit(solution)/shard_map/jit(_take)/select_n | solution.py:140
  539.6 6.1 fusion.109
  545.7 10.8 convolution_add_fusion
  585.7 30.3 %while.28 = (s32[]{:T(128)}, bf16[2,512,512]{2,1,0:T(8,128)(2,1)}, f32[2,4,512]{2,1,0:T(4,128)S(1)}, s32[2]{0:T(128)S(1)}, s32[1024]{0:T(1024)S(1)}, /*index=5*/...) while((s32[]{:T(128)}, bf16[2,512,512]{2,1,0:T(8,128)(2,1)}, ...), condition=%wide.region_8.9_spmd.clone, body=%wide.region_5.8_spmd.clone.sunk | while | flops 1100478976 | bytes 36780264 | solution.py:194
  616.1 45.2 %while.29 = (s32[]{:T(128)}, f32[1024,4,128]{0,2,1:T(8,128)S(1)}, f32[1024,4,128]{0,2,1:T(8,128)}, f32[2,512,4,128]{3,1,0,2:T(8,128)}, s32[2]{0:T(128)S(1)}, /*i...) while((s32[]{:T(128)}, f32[1024,4,128]{0,2,1:T(8,128)S(1)}, ...), condition=%wide.region_12.13_spmd.clone, body=%wide.region_10.12_spmd.clone.sunk | while | flops 2720266752 | bytes 105978256 | solution.py:251
  645.5 5.3 bitcast_add_fusion.5
  679.0 11.1 fusion.118
  693.3 11.5 fusion.117
  704.8 13.4 reshape.487
  718.2 31.6 %multiply_convert_fusion.1 = (bf16[1024,2048]{1,0:T(8,128)(2,1)}, f32[1024,2048]{1,0:T(8,128)}, f32[1024,2048]{1,0:T(8,128)}) fusion(f32[2048]{0:T(1024)S(1)} %slice_convert_fusion.4, bf16[1024,2048]{1,0:T(8,128)(2,1)} %all-gather.10.cloned.1.call-done, bf16[6152,2048]{1,0:T(8,128)(2,1)} %broadcast_select_fusion.1), kind=kOutput, calls=%fused_computation.95 | convolution fusion | flops 8728346624 | bytes 33562624 | tf_op jit(solution)/shard_map/dot_general | solution.py:24
  749.8 17.9 convert_reduce_fusion
  769.7 13.3 fusion.49
  783.1 11.6 constant_dynamic-update-slice_fusion.14
  800.2 9.0 convolution_bitcast_fusion
  809.2 7.8 copy.174
  817.1 11.1 convolution_bitcast_fusion.1
  828.2 7.6 copy.173
  840.3 13.8 fusion.58
  858.8 13.2 constant_dynamic-update-slice_fusion.33
  874.2 6.1 constant_dynamic-update-slice_fusion.32
  883.0 99.2 %reduce-scatter.8.cloned.1.call-done = f32[256,2048]{1,0:T(8,128)} async-done(((f32[1024,2048]{1,0:T(8,128)}), f32[256,2048]{1,0:T(8,128)}) %reduce-scatter.8.cloned.1.call-update) | async-done | bytes 2097168 | tf_op jit(solution)/shard_map/reduce_scatter | solution.py:269
  982.3 4.6 fusion.95
  987.0 20.2 %psum.7 = f32[12288]{0:T(1024)S(1)} all-reduce(f32[12288]{0:T(1024)S(1)} %reshape.491), channel_id=1, replica_groups=mesh['dp'=4,'tensor'=4,'chip'=2] {'tensor'}, use_global_device_ids=true, to_apply=%region_27.28 | all-reduce | flops 12288 | bytes 98304 | tf_op jit(solution)/shard_map/psum | solution.py:283
  1009.9 42.9 %reshape.492 = f32[8,1574912]{1,0:T(8,128)} reshape(f32[12599296]{0:T(1024)} %constant_dynamic-update-slice_fusion.28) | data formatting | bytes 100794368 | tf_op jit(solution)/shard_map/reshape | solution.py:296
  1057.1 32.3 %fusion.122 = (f32[8,121216]{1,0:T(8,128)}, f32[8,121216]{1,0:T(8,128)}, f32[8,121216]{1,0:T(8,128)}, f32[8,121216]{1,0:T(8,128)}, f32[8,121216]{1,0:T(8,128)}, ...) fusion(f32[8,1574912]{1,0:T(8,128)} %reshape.492), kind=kLoop, calls=%fused_computation.262 | loop fusion | bytes 93093888 | tf_op jit(solution)/shard_map/jit(_take)/gather | solution.py:296
  1089.4 7.3 gather_fusion.24
  1096.6 7.3 gather_fusion.25
  1103.9 7.3 gather_fusion.23
  1111.2 7.2 gather_fusion.22
  1118.3 7.5 gather_fusion.21
  1125.9 7.2 gather_fusion.20
  1133.0 7.2 gather_fusion.19
  1140.2 7.2 gather_fusion.18
  1147.4 7.6 gather_fusion.17
  1155.0 7.2 gather_fusion.16
  1162.2 7.2 gather_fusion.15
  1169.4 7.2 gather_fusion.14
  1176.6 7.4 gather_fusion.13
  1229.1 34.4 %broadcast_select_fusion = f32[8,1574912]{1,0:T(8,128)} fusion(f32[8,1574912]{1,0:T(8,128)} %constant_dynamic-update-slice_fusion.15, pred[8]{0:T(512)(128)(4,1)S(1)} %copy-done.73), kind=kLoop, calls=%fused_computation.71 | loop fusion | flops 12599296 | bytes 100794376 | tf_op jit(solution)/shard_map/jit(_take)/select_n | solution.py:296
  1268.5 5.3 fusion.91
  1273.8 568.0 %all-reduce.3.cloned.1.call-done = f32[8,1574912]{1,0:T(8,128)} async-done(((f32[8,1574912]{1,0:T(8,128)}), f32[8,1574912]{1,0:T(8,128)}) %all-reduce.3.cloned.1.call-update) | async-done | bytes 50397200
  1841.8 80.4 %multiply_add_fusion.1 = (f32[1,1,1574912]{2,1,0:T(1,128)}, f32[1,1,1574912]{2,1,0:T(1,128)}, f32[1,1,1574912]{2,1,0:T(1,128)}, f32[1,1,1574912]{2,1,0:T(1,128)}, f32[1,1,1574912]{2,1,0:T(1,128)}) fusion(f32[1,1,1574912]{2,1,0:T(1,128)} %param.27, f32[]{:T(128)S(6)} %sub.111, f32[]{:T(128)} %bitcast.257, f32[1,1,1574912]{2,1,0:T(1,128)} %param.24, ...), kind=kLoop, calls=%fused_computation.124 | loop fusion | flops 50397184 | bytes 62996536 | tf_op jit(solution)/shard_map/add | solution.py:108
  (356 shorter events, 223.5 us)
Async XLA Ops:
  7.2 242.0 %all-gather.6.cloned.1.call-start = ((), (), s32[]{:S(2)}) async-start(), calls=%async_computation.3 | async-start | bytes 56696832 | tf_op jit(solution)/shard_map/all_gather | solution.py:139
  13.8 525.8 %all-gather.12.cloned.1.call-start = ((), (), s32[]{:S(2)}) async-start(), calls=%async_computation.9 | async-start | bytes 5242880 | tf_op jit(solution)/shard_map/all_gather | solution.py:206
  14.6 531.2 %all-gather.8.cloned.1.call-start = ((), (), s32[]{:S(2)}) async-start(), calls=%async_computation.4 | async-start | bytes 5242880 | tf_op jit(solution)/shard_map/all_gather | solution.py:155
  15.5 422.2 %copy-start.63 = (f32[256]{0:T(256)}, f32[256]{0:T(256)S(1)}, u32[]{:S(2)}) copy-start(f32[256]{0:T(256)S(1)} %broadcast_multiply_fusion.4) | copy-start | bytes 3076
  16.0 421.8 %copy-start.66 = (f32[256]{0:T(256)}, f32[256]{0:T(256)S(1)}, u32[]{:S(2)}) copy-start(f32[256]{0:T(256)S(1)} %add_rsqrt_fusion) | copy-start | bytes 3076
  377.0 4.5 copy-start.40
  428.8 8.3 copy-start.2
  428.8 11.3 copy-start.76
  439.9 278.3 %all-gather.10.cloned.1.call-start = ((), (), s32[]{:S(2)}) async-start(), calls=%async_computation.5 | async-start | bytes 5242880 | tf_op jit(solution)/shard_map/all_gather | solution.py:156
  442.2 137.9 %copy-start.26 = (f32[1024,16]{1,0:T(8,128)}, f32[1024,16]{1,0:T(8,128)S(1)}, u32[]{:S(2)}) copy-start(f32[1024,16]{1,0:T(8,128)S(1)} %copy.125) | copy-start | bytes 196612
  539.5 343.5 %reduce-scatter.6.cloned.1.call-start = ((), (), s32[]{:S(2)}) async-start(), calls=%async_computation.7 | async-start | bytes 10485760 | tf_op jit(solution)/shard_map/reduce_scatter | solution.py:268
  574.7 5.4 copy-start.28
  585.7 30.4 %copy-start = (f32[1024,4,128]{0,2,1:T(8,128)S(1)}, f32[1024,4,128]{0,2,1:T(8,128)}, u32[]{:S(2)}) copy-start(f32[1024,4,128]{0,2,1:T(8,128)} %custom-call) | copy-start | bytes 6291460
  623.8 4.0 copy-start.3
  645.5 5.3 copy-start.3
  664.1 7.5 copy-start.21
  674.2 19.1 copy-start.46
  676.4 16.9 copy-start.44
  690.1 292.2 %reduce-scatter.8.cloned.1.call-start = ((), (), s32[]{:S(2)}) async-start(), calls=%async_computation.8 | async-start | bytes 10485760 | tf_op jit(solution)/shard_map/reduce_scatter | solution.py:269
  718.2 31.6 %copy-start.22 = (bf16[1,1024,2048]{2,1,0:T(8,128)(2,1)S(1)}, bf16[1,1024,2048]{2,1,0:T(8,128)(2,1)}, u32[]{:S(2)}) copy-start(bf16[1,1024,2048]{2,1,0:T(8,128)(2,1)} %all-gather.12.cloned.1.call-done) | copy-start | bytes 12582916
  783.1 11.6 copy-start.50
  783.1 485.4 %reduce-scatter.4.cloned.1.call-start = ((), (), s32[]{:S(2)}) async-start(), calls=%async_computation.6 | async-start | bytes 10485760 | tf_op jit(solution)/shard_map/reduce_scatter | solution.py:198
  783.1 11.6 copy-start.23
  809.2 7.8 copy-start.74
  828.2 7.6 copy-start.45
  828.2 7.6 copy-start.47
  828.2 7.6 copy-start.49
  854.2 987.6 %all-reduce.3.cloned.1.call-start = ((), (), s32[]{:S(2)}) async-start(), calls=%async_computation.10 | async-start | bytes 100794368
  854.2 17.8 slice-start
  858.8 13.2 slice-start.1
  858.8 14.0 slice-start.2
  858.8 15.4 slice-start.3
  874.2 108.0 %copy-start.5 = (bf16[1,256,2048]{2,1,0:T(8,128)(2,1)S(1)}, bf16[1,256,2048]{2,1,0:T(8,128)(2,1)}, u32[]{:S(2)}) copy-start(bf16[1,256,2048]{2,1,0:T(8,128)(2,1)} %param.16) | copy-start | bytes 3145732
  874.2 108.0 %copy-start.53 = (f32[2048]{0:T(1024)S(1)}, f32[2048]{0:T(1024)}, u32[]{:S(2)}) copy-start(f32[2048]{0:T(1024)} %copy-done.52) | copy-start | bytes 24580
  874.2 108.0 %copy-start.56 = (f32[2048]{0:T(1024)S(1)}, f32[2048]{0:T(1024)}, u32[]{:S(2)}) copy-start(f32[2048]{0:T(1024)} %copy-done.55) | copy-start | bytes 24580
  874.2 108.0 %copy-start.64 = (f32[256]{0:T(256)S(1)}, f32[256]{0:T(256)}, u32[]{:S(2)}) copy-start(f32[256]{0:T(256)} %copy-done.63) | copy-start | bytes 3076
  874.2 108.0 %copy-start.67 = (f32[256]{0:T(256)S(1)}, f32[256]{0:T(256)}, u32[]{:S(2)}) copy-start(f32[256]{0:T(256)} %copy-done.66) | copy-start | bytes 3076
  880.4 106.5 %copy-start.58 = (f32[2048]{0:T(1024)S(1)}, f32[2048]{0:T(1024)}, u32[]{:S(2)}) copy-start(f32[2048]{0:T(1024)} %convert_reduce_fusion.2) | copy-start | bytes 24580
  1057.1 32.3 %copy-start.62 = (s32[1024]{0:T(1024)S(1)}, s32[1024]{0:T(1024)}, u32[]{:S(2)}) copy-start(s32[1024]{0:T(1024)} %get-tuple-element.438) | copy-start | bytes 12292
  1184.0 4.5 copy-start.17
  1188.5 3.5 copy-start.16
  1192.0 3.5 copy-start.15
  1195.5 3.5 copy-start.14
  1199.0 3.5 copy-start.13
  1202.5 3.5 copy-start.12
  1206.0 3.5 copy-start.11
  1209.5 3.5 copy-start.10
  1213.0 3.5 copy-start.9
  1216.5 3.5 copy-start.8
  1220.0 3.5 copy-start.7
  1223.5 3.5 copy-start.18
  1263.4 4.2 copy-start.61
  1263.5 4.9 copy-start.72
  1263.5 4.9 copy-start.71
  1263.5 4.9 copy-start.70
  1263.5 4.9 copy-start.69
  1263.5 5.0 copy-start.6
  1263.5 5.0 copy-start.25
  1263.5 5.0 copy-start.54
  1263.5 5.0 copy-start.57
  1263.5 5.0 copy-start.59
  1263.6 5.0 copy-start.60
  1263.6 5.0 copy-start.65
  1263.6 5.0 copy-start.68
  (36 other events, 81.9 us)
Sparse Core Ops, SparseCore 0:
  13.9 235.1 all-gather.5
  250.7 80.7 all-gather.11
  440.0 80.8 all-gather.7
  539.6 80.8 all-gather.9
  690.2 144.5 reduce-scatter.5
  837.0 145.1 reduce-scatter.7
  984.6 146.3 reduce-scatter.3
  1263.7 578.0 all-reduce.2
where the time goes:
time: 1940 us; the launch traced here: 1930 us
  waiting for transfers between devices  901 us (46%)
  local copies, waits for them, and re-layouts  594 us (31%)
  other arithmetic  205 us (11%)
  matrix products  183 us (9%)
  blocking collectives  20.2 us (1%)
    unnamed x9, waiting for transfers between devices  569 us
    all_gather x1, waiting for transfers between devices, on_device(): lax.all_gather(master.astype(jnp.bfloat16), ('dp', 'chip'), axis=1, tiled...  233 us
    unnamed x207, local copies, waits for them, and re-layouts  186 us
    gather x16, local copies, waits for them, and re-layouts, on_device(): flat_params = jnp.take(gathered[0], owners, axis=0).reshape(-1)  157 us
    gather x15, local copies, waits for them, and re-layouts, on_device(): jnp.take(flat_grad.reshape(group_count, bucket_size), inverse, axis=0)  131 us
    reduce_scatter x1, waiting for transfers between devices, on_device(): lax.psum_scatter(partial_two, 'tensor', scatter_dimension=0, tiled=True)  99.2 us
    add x1, other arithmetic, adam_update(): new_moving = ema_keep * moving + (1.0 - ema_keep) * new_weights  80.4 us
    dot_general x4, matrix products, matmul(): return jnp.dot(left, right, preferred_element_type=jnp.float32)  60.1 us
  transfers between devices with their start and end apart: 8, of which 3 were waited for; matrix products, arithmetic and copies ran while one was open for 45% of the time, Pallas kernels for 0%

commit v1 on v0

--- a/solution.py
+++ b/solution.py
@@ -1,8 +1,11 @@
+import functools
 import math
 
 import jax
 import jax.numpy as jnp
 from jax import lax
+from jax.experimental import pallas as pl
+from jax.experimental.pallas import tpu as pltpu
 from jax.sharding import PartitionSpec as P
 
 D = 2048
@@ -53,7 +56,10 @@
 
 
 def group_layout(seq_lengths, group_rows):
-    seq_ends = jnp.cumsum(seq_lengths)
+    order = jnp.arange(seq_lengths.shape[0], dtype=jnp.int32)
+    seq_ends = jnp.sum(
+        jnp.where(order[None, :] <= order[:, None], seq_lengths[None, :], 0), axis=1
+    )
     starts = seq_ends - seq_lengths
     token_index = jnp.arange(group_rows, dtype=jnp.int32)
     segment = jnp.sum((token_index[:, None] >= seq_ends[None, :]).astype(jnp.int32), axis=1)
@@ -323,6 +329,891 @@
     )
 
 
+LANES = 128
+TROWS = 16
+
+
+def fits(mesh):
+    return mesh.shape["dp"] == 4 and mesh.shape["chip"] == 2 and mesh.shape["tensor"] == 4
+
+
+def device_program(mesh):
+    return on_device_fast if fits(mesh) else on_device
+
+
+CHUNKS = 4
+BROWS = 768
+QROWS = 1024
+FRONT = 128
+BACK = 256
+FLAT = 12304
+HBM = pl.ANY
+
+
+def params(limit_mb, **more):
+    return pltpu.CompilerParams(vmem_limit_bytes=limit_mb * 1024 * 1024, **more)
+
+
+def pack_kernel(bucket_ref, flat_ref, *refs):
+    outs, padded, sem = refs[:CHUNKS], refs[CHUNKS], refs[CHUNKS + 1]
+    bucket = bucket_ref[0]
+    load = pltpu.make_async_copy(flat_ref, padded.at[pl.ds(FRONT, FLAT)], sem)
+    load.start()
+    padded[pl.ds(0, FRONT)] = jnp.zeros((FRONT, LANES), jnp.float32)
+    padded[pl.ds(FRONT + FLAT, BACK)] = jnp.zeros((BACK, LANES), jnp.float32)
+    load.wait()
+    wide, narrow = 16 // CHUNKS, 12 // CHUNKS
+
+    def take(start, stride):
+        return padded[pl.ds(start, 16, stride=stride), :].astype(jnp.bfloat16)
+
+    @pl.when(bucket >= 2)
+    def _():
+        def step(tile, carry):
+            row = pl.multiple_of(tile * 16, 16)
+            for panel in range(16):
+                outs[panel // wide][pl.ds((panel % wide) * BROWS + row, 16), :] = take(
+                    (row - bucket) * 16 + panel + FRONT, 16
+                )
+            return carry
+
+        lax.fori_loop(0, BROWS // 16, step, 0)
+
+    @pl.when(bucket < 2)
+    def _():
+        def step(tile, carry):
+            row = pl.multiple_of(tile * 16, 16)
+            for panel in range(12):
+                outs[panel // narrow][pl.ds((panel % narrow) * QROWS + row, 16), :] = take(
+                    row * 12 + panel - 16 * bucket + FRONT, 12
+                )
+            return carry
+
+        lax.fori_loop(0, QROWS // 16, step, 0)
+
+    main = wide * BROWS
+
+    @pl.when(bucket >= 1)
+    def _():
+        for panel in range(16):
+            outs[panel // wide][pl.ds(main + (panel % wide) * TROWS, TROWS), :] = take(
+                (BROWS - bucket) * 16 + panel + FRONT, 16
+            )
+
+    @pl.when(bucket == 0)
+    def _():
+        for part in range(CHUNKS):
+            for panel in range(wide):
+                source = part * narrow + min(panel, narrow - 1)
+                outs[part][pl.ds(main + panel * TROWS, TROWS), :] = take(
+                    QROWS * 12 + source + FRONT, 12
+                )
+
+
+def chunk_rows():
+    return (16 // CHUNKS) * (BROWS + TROWS)
+
+
+def pack(bucket, flat):
+    return pl.pallas_call(
+        pack_kernel,
+        out_shape=[jax.ShapeDtypeStruct((chunk_rows(), LANES), jnp.bfloat16)] * CHUNKS,
+        in_specs=[pl.BlockSpec(memory_space=pltpu.SMEM), pl.BlockSpec(memory_space=HBM)],
+        out_specs=[pl.BlockSpec(memory_space=pltpu.VMEM)] * CHUNKS,
+        scratch_shapes=[
+            pltpu.VMEM((FRONT + FLAT + BACK, LANES), jnp.float32),
+            pltpu.SemaphoreType.DMA,
+        ],
+        compiler_params=params(24),
+        name="pack_params",
+    )(bucket, flat)
+
+
+PLACES = {
+    0: (("in", 0, 1024, 0),),
+    1: (("in", 1024, 1024, 0),),
+    2: (("out", 0, 512, 0), ("up", 0, 256, 512)),
+    3: (("up", 256, 768, 0),),
+    4: (("up", 1024, 768, 0),),
+    5: (("up", 1792, 256, 0), ("down", 0, 512, 256)),
+    6: (("down", 512, 768, 0),),
+    7: (("down", 1280, 768, 0),),
+}
+NAMES = ("in", "out", "up", "down", "bias")
+
+
+def panels_of(bucket):
+    return (12 if bucket < 2 else 16) // CHUNKS
+
+
+MATRICES = {
+    "in": (2048, 1536),
+    "out": (512, 2048),
+    "up": (2048, 2048),
+    "down": (2048, 2048),
+    "bias": (TROWS, 2048),
+}
+
+
+def head_of(bucket):
+    if bucket == 8:
+        return ("bias", 0)
+    name, first, _, _ = PLACES[bucket][0]
+    return (name, first)
+
+
+def columns(panel):
+    return pl.ds(panel * LANES, LANES)
+
+
+def unpack_kernel(part, bucket_ref, *refs):
+    sources = refs[:8]
+    staged, load_sems, store_sems = refs[-3:]
+    outs = dict(zip(NAMES, refs[-8:-3], strict=True))
+    main = (16 // CHUNKS) * BROWS
+    loads = [
+        pltpu.make_async_copy(sources[k], staged.at[bucket_ref[k]], load_sems.at[k])
+        for k in range(8)
+    ]
+    for load in loads:
+        load.start()
+    for load in loads:
+        load.wait()
+    stores = []
+
+    def store(bucket, row, name, first, rows, panel):
+        wide = panels_of(bucket)
+        stores.append(
+            pltpu.make_async_copy(
+                staged.at[bucket, pl.ds(row, rows)],
+                outs[name].at[pl.ds(first, rows), columns(part * wide + panel)],
+                store_sems.at[len(stores)],
+            )
+        )
+        stores[-1].start()
+
+    for bucket in range(8):
+        span = QROWS if bucket < 2 else BROWS
+        for panel in range(panels_of(bucket)):
+            if bucket:
+                head = pl.ds(panel * span, TROWS)
+                tail = pl.ds(main + panel * TROWS, TROWS)
+                staged[bucket, head, :] = staged[bucket, head, :] + staged[bucket - 1, tail, :]
+            for name, first, rows, offset in PLACES[bucket]:
+                store(bucket, panel * span + offset, name, first, rows, panel)
+    for panel in range(16 // CHUNKS):
+        store(7, main + panel * TROWS, "bias", 0, TROWS, panel)
+    for put in stores:
+        put.wait()
+
+
+def unpack(part, buckets, sources, before):
+    copies = sum(len(PLACES[b]) * panels_of(b) for b in range(8)) + 16 // CHUNKS
+    return pl.pallas_call(
+        functools.partial(unpack_kernel, part),
+        out_shape=[jax.ShapeDtypeStruct(MATRICES[name], jnp.bfloat16) for name in NAMES],
+        in_specs=[pl.BlockSpec(memory_space=pltpu.SMEM)]
+        + [pl.BlockSpec(memory_space=HBM)] * (8 + len(before)),
+        out_specs=[pl.BlockSpec(memory_space=HBM)] * 5,
+        input_output_aliases={9 + at: at for at in range(len(before))},
+        scratch_shapes=[
+            pltpu.VMEM((8, chunk_rows(), LANES), jnp.bfloat16),
+            pltpu.SemaphoreType.DMA((8,)),
+            pltpu.SemaphoreType.DMA((copies,)),
+        ],
+        compiler_params=params(16),
+        name="unpack_params",
+    )(buckets, *sources, *before)
+
+
+GRAD_ROWS = 256
+IN_STEPS, OUT_STEPS, UP_STEPS, DOWN_STEPS = 8, 2, 8, 8
+GRAD_STEPS = IN_STEPS + OUT_STEPS + UP_STEPS + DOWN_STEPS
+
+
+def weight_grad_kernel(table, *refs):
+    lefts, rights = refs[:8], refs[8:14]
+    sent, kept, wide32, wide16, tail32, tail16, sems, tail_sem = refs[14:]
+    step = pl.program_id(0)
+    main = (16 // CHUNKS) * BROWS
+
+    def bucket_of(at):
+        return jnp.where(at < IN_STEPS, at // 4, (at - 2) // 3)
+
+    def copies(at, act):
+        slot = lax.rem(at, 2)
+        bucket = bucket_of(at)
+        inner = at < IN_STEPS
+        goes, place = table[1 + bucket], table[9 + bucket]
+        for panels, span, mine in ((3, QROWS, inner), (4, BROWS, jnp.logical_not(inner))):
+            offset = pl.multiple_of(
+                (lax.rem(at, 4) if span == QROWS else lax.rem(at - 2, 3)) * GRAD_ROWS, GRAD_ROWS
+            )
+            for away, stage, target in ((1, wide16, sent), (0, wide32, kept)):
+
+                @pl.when(jnp.logical_and(mine, goes == away))
+                def _(panels=panels, span=span, offset=offset, stage=stage, target=target):
+                    for panel in range(panels):
+                        act(
+                            pltpu.make_async_copy(
+                                stage.at[slot, pl.ds(panel * GRAD_ROWS, GRAD_ROWS)],
+                                target.at[place, pl.ds(panel * span + offset, GRAD_ROWS)],
+                                sems.at[slot, panel],
+                            )
+                        )
+
+    @pl.when(step >= 2)
+    def _():
+        copies(step - 2, lambda copy: copy.wait())
+
+    @pl.when(step == 0)
+    def _():
+        tail32[...] = jnp.zeros_like(tail32)
+        tail16[...] = jnp.zeros_like(tail16)
+
+    def block(pair, right, panels, first):
+        left_own, left_other = lefts[2 * pair], lefts[2 * pair + 1]
+        right_own, right_other = rights[2 * right], rights[2 * right + 1]
+        value = product_rows(left_own[...], right_own[...]) + product_rows(
+            left_other[...], right_other[...]
+        )
+        slot = lax.rem(step, 2)
+        for panel in range(panels):
+            part = value[:, panel * LANES : (panel + 1) * LANES]
+            rows = pl.ds(panel * GRAD_ROWS, GRAD_ROWS)
+            wide32[slot, rows, :] = part
+            wide16[slot, rows, :] = part.astype(jnp.bfloat16)
+
+        @pl.when(first)
+        def _():
+            before = jnp.maximum(bucket_of(step) - 1, 0)
+            for panel in range(panels):
+                part = value[:TROWS, panel * LANES : (panel + 1) * LANES]
+                rows = pl.ds(panel * TROWS, TROWS)
+                tail32[before, rows, :] = part
+                tail16[before, rows, :] = part.astype(jnp.bfloat16)
+
+    third = lax.rem(step - 2, 3) == 0
+    edges = (0, IN_STEPS, IN_STEPS + OUT_STEPS, IN_STEPS + OUT_STEPS + UP_STEPS, GRAD_STEPS)
+    for pair, right in enumerate((0, 1, 2, 1)):
+
+        @pl.when(jnp.logical_and(step >= edges[pair], step < edges[pair + 1]))
+        def _(pair=pair, right=right):
+            block(pair, right, 3 if pair == 0 else 4, step == 4 if pair == 0 else third)
+
+    copies(step, lambda copy: copy.start())
+
+    @pl.when(step == GRAD_STEPS - 1)
+    def _():
+        def tails(act):
+            for bucket in range(8):
+                for away, stage, target in ((1, tail16, sent), (0, tail32, kept)):
+
+                    @pl.when(table[1 + bucket] == away)
+                    def _(bucket=bucket, stage=stage, target=target):
+                        act(
+                            pltpu.make_async_copy(
+                                stage.at[bucket],
+                                target.at[table[9 + bucket], pl.ds(main, stage.shape[1])],
+                                tail_sem.at[bucket],
+                            )
+                        )
+
+        tails(lambda copy: copy.start())
+        copies(step - 1, lambda copy: copy.wait())
+        copies(step, lambda copy: copy.wait())
+        tails(lambda copy: copy.wait())
+
+
+def weight_grads(part, table, lefts, rights):
+    tokens = lefts[0].shape[0]
+
+    def columns_at(first, count):
+        return pl.BlockSpec(
+            (tokens, GRAD_ROWS), lambda i, table: (0, jnp.clip(i - first, 0, count - 1))
+        )
+
+    firsts = (0, IN_STEPS, IN_STEPS + OUT_STEPS, IN_STEPS + OUT_STEPS + UP_STEPS)
+    left_specs = [
+        columns_at(first, count)
+        for first, count in zip(firsts, (IN_STEPS, OUT_STEPS, UP_STEPS, DOWN_STEPS), strict=True)
+        for _ in range(2)
+    ]
+    right_specs = []
+    for width in (384, 512, 512):
+        right_specs.append(
+            pl.BlockSpec((tokens, width), lambda i, table: (0, 2 * table[0] + part))
+        )
+        right_specs.append(pl.BlockSpec((tokens, width), lambda i, table: (0, part)))
+    rows = chunk_rows()
+    return pl.pallas_call(
+        weight_grad_kernel,
+        out_shape=[
+            jax.ShapeDtypeStruct((4, rows, LANES), jnp.bfloat16),
+            jax.ShapeDtypeStruct((4, rows, LANES), jnp.float32),
+        ],
+        grid_spec=pltpu.PrefetchScalarGridSpec(
+            num_scalar_prefetch=1,
+            grid=(GRAD_STEPS,),
+            in_specs=left_specs + right_specs,
+            out_specs=[pl.BlockSpec(memory_space=HBM)] * 2,
+            scratch_shapes=[
+                pltpu.VMEM((2, 4 * GRAD_ROWS, LANES), jnp.float32),
+                pltpu.VMEM((2, 4 * GRAD_ROWS, LANES), jnp.bfloat16),
+                pltpu.VMEM((8, 4 * TROWS, LANES), jnp.float32),
+                pltpu.VMEM((8, 4 * TROWS, LANES), jnp.bfloat16),
+                pltpu.SemaphoreType.DMA((2, 4)),
+                pltpu.SemaphoreType.DMA((8,)),
+            ],
+        ),
+        compiler_params=params(48),
+        name="weight_grads",
+    )(table, *lefts, *rights)
+
+
+def place_rows_kernel(index_ref, *refs):
+    pieces, out, sems = refs[:7], refs[7], refs[8]
+    rows = pieces[0].shape[0]
+    here = index_ref[0]
+
+    def each(act):
+        for at, piece in enumerate(pieces):
+            target = here + at - 3
+
+            @pl.when(jnp.logical_and(target >= 0, target <= 3))
+            def _(at=at, piece=piece, target=target):
+                spot = pl.ds(pl.multiple_of(jnp.clip(target, 0, 3) * rows, rows), rows)
+                act(pltpu.make_async_copy(piece, out.at[spot], sems.at[at]))
+
+    each(lambda copy: copy.start())
+    each(lambda copy: copy.wait())
+
+
+def place_rows(index, pieces):
+    rows, width = pieces[0].shape
+    return pl.pallas_call(
+        place_rows_kernel,
+        out_shape=jax.ShapeDtypeStruct((4 * rows, width), pieces[0].dtype),
+        in_specs=[pl.BlockSpec(memory_space=pltpu.SMEM)] + [pl.BlockSpec(memory_space=HBM)] * 7,
+        out_specs=pl.BlockSpec(memory_space=pltpu.VMEM),
+        scratch_shapes=[pltpu.SemaphoreType.DMA((7,))],
+        compiler_params=params(12),
+        name="place_rows",
+    )(index, *pieces)
+
+
+ADAM_ROWS = 1024
+
+
+def adam_kernel(table, scalar_ref, rate_ref, *refs):
+    pieces, small = refs[:4], refs[4]
+    weights, first, second, moving = refs[5:9]
+    new_weights, new_first, new_second, new_moving, reduced = refs[9:14]
+    held, flat, sems = refs[14:]
+    bucket, core = table[0], table[1]
+    wide, narrow = 16 // CHUNKS, 12 // CHUNKS
+    main = wide * BROWS
+
+    @pl.when(pl.program_id(0) == 0)
+    def _():
+        loads = []
+        for at, piece in enumerate(pieces):
+            half = core if at < 2 else 1 - core
+            loads.append(
+                pltpu.make_async_copy(piece, held.at[2 * half + at % 2], sems.at[at])
+            )
+            loads[-1].start()
+        for load in loads:
+            load.wait()
+
+        def put(part, row, start, stride):
+            flat[pl.ds(start, 16, stride=stride), :] = held[part, pl.ds(row, 16), :]
+
+        @pl.when(bucket >= 2)
+        def _():
+            def step(tile, carry):
+                row = pl.multiple_of(tile * 16, 16)
+                for panel in range(16):
+                    put(
+                        panel // wide,
+                        (panel % wide) * BROWS + row,
+                        (row - bucket) * 16 + panel + FRONT,
+                        16,
+                    )
+                return carry
+
+            lax.fori_loop(0, BROWS // 16, step, 0)
+
+        @pl.when(bucket < 2)
+        def _():
+            def step(tile, carry):
+                row = pl.multiple_of(tile * 16, 16)
+                for panel in range(12):
+                    put(
+                        panel // narrow,
+                        (panel % narrow) * QROWS + row,
+                        row * 12 + panel - 16 * bucket + FRONT,
+                        12,
+                    )
+                return carry
+
+            lax.fori_loop(0, QROWS // 16, step, 0)
+
+        @pl.when(bucket >= 1)
+        def _():
+            for panel in range(16):
+                put(
+                    panel // wide,
+                    main + (panel % wide) * TROWS,
+                    (BROWS - bucket) * 16 + panel + FRONT,
+                    16,
+                )
+
+        @pl.when(bucket == 0)
+        def _():
+            for panel in range(12):
+                put(
+                    panel // narrow,
+                    main + (panel % narrow) * TROWS,
+                    QROWS * 12 + panel + FRONT,
+                    12,
+                )
+
+        @pl.when(bucket == 7)
+        def _():
+            flat[pl.ds(FRONT + FLAT - LANES, LANES), :] = small[...]
+
+    start = pl.program_id(0) * ADAM_ROWS
+    gradient = flat[pl.ds(pl.multiple_of(FRONT + start, 8), ADAM_ROWS), :]
+    row = bucket * FLAT + start + lax.broadcasted_iota(jnp.int32, (ADAM_ROWS, LANES), 0)
+    rate = jnp.full((ADAM_ROWS, LANES), rate_ref[0], jnp.float32)
+    for kind, bound in enumerate(bound_list(512, 2048)[1:]):
+        rate = jnp.where(row >= bound // LANES, rate_ref[kind + 1], rate)
+    reduced[...] = gradient
+    bias_one, bias_two, decay, keep = (scalar_ref[at] for at in range(4))
+    one = beta_one * first[...] + (1.0 - beta_one) * gradient
+    two = beta_two * second[...] + (1.0 - beta_two) * gradient * gradient
+    old = weights[...]
+    ratio = one / bias_one / (jnp.sqrt(two / bias_two) + adam_epsilon)
+    fresh = old - rate * (ratio + decay * old)
+    new_weights[...] = fresh
+    new_first[...] = one
+    new_second[...] = two
+    new_moving[...] = keep * moving[...] + (1.0 - keep) * fresh
+
+
+def adam(table, scalars, rates, pieces, small, state):
+    steps = -(-FLAT // ADAM_ROWS)
+    block = pl.BlockSpec((ADAM_ROWS, LANES), lambda i: (i, 0))
+    return pl.pallas_call(
+        adam_kernel,
+        grid=(steps,),
+        out_shape=[jax.ShapeDtypeStruct((FLAT, LANES), jnp.float32)] * 5,
+        in_specs=[pl.BlockSpec(memory_space=pltpu.SMEM)] * 3
+        + [pl.BlockSpec(memory_space=HBM)] * 4
+        + [pl.BlockSpec(memory_space=pltpu.VMEM)]
+        + [block] * 4,
+        out_specs=[block] * 5,
+        scratch_shapes=[
+            pltpu.VMEM((4, chunk_rows(), LANES), jnp.float32),
+            pltpu.VMEM((FRONT + steps * ADAM_ROWS, LANES), jnp.float32),
+            pltpu.SemaphoreType.DMA((4,)),
+        ],
+        compiler_params=params(40),
+        name="adam",
+    )(table, scalars, rates, *pieces, small, *state)
+
+
+FF_BLOCK = 256
+
+
+def hidden_kernel(normed, up, up_bias, hidden, slope):
+    before = matmul(normed[...], up[...]) + up_bias[...]
+    half = 0.5 + 0.5 * lax.erf(before * math.sqrt(0.5))
+    hidden[...] = (before * half).astype(jnp.bfloat16)
+    slope[...] = half + before * jnp.exp(-0.5 * before * before) * (1.0 / math.sqrt(2.0 * math.pi))
+
+
+def hidden_layer(normed, up, up_bias):
+    rows, units = normed.shape[0], up.shape[1]
+    block = pl.BlockSpec((rows, FF_BLOCK), lambda i: (0, i))
+    return pl.pallas_call(
+        hidden_kernel,
+        grid=(units // FF_BLOCK,),
+        out_shape=[
+            jax.ShapeDtypeStruct((rows, units), jnp.bfloat16),
+            jax.ShapeDtypeStruct((rows, units), jnp.float32),
+        ],
+        in_specs=[
+            pl.BlockSpec(memory_space=pltpu.VMEM),
+            pl.BlockSpec((D, FF_BLOCK), lambda i: (0, i)),
+            pl.BlockSpec((1, FF_BLOCK), lambda i: (0, i)),
+        ],
+        out_specs=[block, block],
+        compiler_params=params(40),
+        name="hidden_layer",
+    )(normed, up, up_bias)
+
+
+def hidden_back_kernel(grads, down, slope, grad_before, grad_bias):
+    rounded = (slope[...] * product_back(grads[...], down[...])).astype(jnp.bfloat16)
+    grad_before[...] = rounded
+    grad_bias[...] = jnp.sum(rounded.astype(jnp.float32), axis=0, keepdims=True)
+
+
+def hidden_back(grads, down, slope):
+    rows, units = slope.shape
+    block = pl.BlockSpec((rows, FF_BLOCK), lambda i: (0, i))
+    return pl.pallas_call(
+        hidden_back_kernel,
+        grid=(units // FF_BLOCK,),
+        out_shape=[
+            jax.ShapeDtypeStruct((rows, units), jnp.bfloat16),
+            jax.ShapeDtypeStruct((1, units), jnp.float32),
+        ],
+        in_specs=[
+            pl.BlockSpec(memory_space=pltpu.VMEM),
+            pl.BlockSpec((FF_BLOCK, D), lambda i: (i, 0)),
+            block,
+        ],
+        out_specs=[block, pl.BlockSpec((1, FF_BLOCK), lambda i: (0, i))],
+        compiler_params=params(40),
+        name="hidden_back",
+    )(grads, down, slope)
+
+
+QUERY_BLOCK = 256
+
+
+def turn(values, tables, sign):
+    plain, lower, upper = tables
+    half_rot = ROT // 2
+    return (
+        values * plain
+        + pltpu.roll(values, HD - half_rot, 1) * (sign * lower)
+        + pltpu.roll(values, half_rot, 1) * (sign * upper)
+    )
+
+
+def block_scores(query, keys, begins, first):
+    scores = product_back(query, keys) * (1.0 / math.sqrt(HD))
+    row_index = first + lax.broadcasted_iota(jnp.int32, scores.shape, 0)
+    key_index = lax.broadcasted_iota(jnp.int32, scores.shape, 1)
+    allowed = (key_index <= row_index) & (key_index >= begins)
+    return jnp.where(allowed, scores, masked_score)
+
+
+def head_columns(width, head):
+    return [pl.ds(pl.multiple_of(part * width + head * HD, HD), HD) for part in range(3)]
+
+
+def attend_kernel(projected, bias, plain, lower, upper, begins, context, turned, logs):
+    rows, width = context.shape
+
+    def one_head(head, carry):
+        cols = head_columns(width, head)
+        tables = (plain[...], lower[...], upper[...])
+        raw = [projected[:, col] + bias[:, col] for col in cols]
+        queries = turn(raw[0], tables, 1.0).astype(jnp.bfloat16)
+        keys = turn(raw[1], tables, 1.0).astype(jnp.bfloat16)
+        values = raw[2].astype(jnp.bfloat16)
+        for col, value in zip(cols, (queries, keys, values), strict=True):
+            turned[:, col] = value
+        for first in range(0, rows, QUERY_BLOCK):
+            last = first + QUERY_BLOCK
+            mine = slice(first, last)
+            scores = block_scores(queries[mine], keys[:last], begins[mine, :], first)
+            top = jnp.max(scores, axis=-1, keepdims=True)
+            raised = jnp.exp(scores - top)
+            total = jnp.sum(raised, axis=-1, keepdims=True)
+            rounded = (raised / total).astype(jnp.bfloat16)
+            context[mine, cols[0]] = matmul(rounded, values[:last]).astype(jnp.bfloat16)
+            logs[head, mine, :] = top + jnp.log(total)
+        return carry
+
+    lax.fori_loop(0, width // HD, one_head, 0)
+
+
+def attend(projected, bias, tables, begins):
+    rows, width = projected.shape[0], projected.shape[1] // 3
+    whole = pl.BlockSpec(memory_space=pltpu.VMEM)
+    return pl.pallas_call(
+        attend_kernel,
+        out_shape=[
+            jax.ShapeDtypeStruct((rows, width), jnp.bfloat16),
+            jax.ShapeDtypeStruct((rows, 3 * width), jnp.bfloat16),
+            jax.ShapeDtypeStruct((width // HD, rows, 1), jnp.float32),
+        ],
+        in_specs=[whole] * 6,
+        out_specs=[whole] * 3,
+        compiler_params=params(48),
+        name="attend",
+    )(projected, bias, *tables, begins)
+
+
+def attend_back_kernel(
+    turned, logs, plain, lower, upper, begins, grad_context, grad_projected, key_sum, value_sum
+):
+    rows, width = grad_context.shape
+    score_scale = 1.0 / math.sqrt(HD)
+
+    def one_head(head, carry):
+        cols = head_columns(width, head)
+        queries, keys, values = (turned[:, col] for col in cols)
+        key_sum[...] = jnp.zeros_like(key_sum)
+        value_sum[...] = jnp.zeros_like(value_sum)
+        for first in range(0, rows, QUERY_BLOCK):
+            last = first + QUERY_BLOCK
+            mine = slice(first, last)
+            query = queries[mine]
+            scores = block_scores(query, keys[:last], begins[mine, :], first)
+            soft = jnp.exp(scores - logs[head, mine, :])
+            grad_mine = grad_context[mine, cols[0]]
+            grad_soft = product_back(grad_mine, values[:last])
+            delta = jnp.sum(soft * grad_soft, axis=-1, keepdims=True)
+            grad_scores = (soft * (grad_soft - delta)).astype(jnp.bfloat16)
+            grad_query = matmul(grad_scores, keys[:last]) * score_scale
+            tables = (plain[mine, :], lower[mine, :], upper[mine, :])
+            grad_projected[mine, cols[0]] = turn(grad_query, tables, -1.0).astype(jnp.bfloat16)
+            key_sum[:last, :] += product_rows(grad_scores, query)
+            value_sum[:last, :] += product_rows(soft.astype(jnp.bfloat16), grad_mine)
+        tables = (plain[...], lower[...], upper[...])
+        grad_projected[:, cols[1]] = turn(key_sum[...] * score_scale, tables, -1.0).astype(
+            jnp.bfloat16
+        )
+        grad_projected[:, cols[2]] = value_sum[...].astype(jnp.bfloat16)
+        return carry
+
+    lax.fori_loop(0, width // HD, one_head, 0)
+
+
+def attend_back(turned, logs, tables, begins, grad_context):
+    rows, width = grad_context.shape
+    whole = pl.BlockSpec(memory_space=pltpu.VMEM)
+    return pl.pallas_call(
+        attend_back_kernel,
+        out_shape=jax.ShapeDtypeStruct((rows, 3 * width), jnp.bfloat16),
+        in_specs=[whole] * 7,
+        out_specs=whole,
+        scratch_shapes=[pltpu.VMEM((rows, HD), jnp.float32)] * 2,
+        compiler_params=params(48),
+        name="attend_back",
+    )(turned, logs, *tables, begins, grad_context)
+
+
+def rope_tables(places):
+    half_rot = ROT // 2
+    frequency = rope_base ** (-2.0 * jnp.arange(half_rot, dtype=jnp.float32) / ROT)
+    angles = places[:, None] * frequency[None, :]
+    cosine, sines = jnp.cos(angles), jnp.sin(angles)
+    rest = jnp.zeros((places.shape[0], HD - ROT), jnp.float32)
+    none = jnp.zeros_like(sines)
+    return (
+        jnp.concatenate([cosine, cosine, rest + 1.0], axis=1),
+        jnp.concatenate([-sines, none, rest], axis=1),
+        jnp.concatenate([none, sines, rest], axis=1),
+    )
+
+
+def along_x(value):
+    return lax.ppermute(value, "dp", [(i, i ^ 1) for i in range(4)])
+
+
+def along_y(value):
+    return lax.ppermute(value, "dp", [(i, i ^ 2) for i in range(4)])
+
+
+def across(value):
+    return lax.ppermute(value, "chip", [(0, 1), (1, 0)])
+
+
+def spread_rows(value):
+    ups, downs = [value], [value]
+    for hop in range(3):
+        ups.append(lax.ppermute(ups[-1], "tensor", [(i, i + 1) for i in range(hop, 3)]))
+        downs.append(lax.ppermute(downs[-1], "tensor", [(i + 1, i) for i in range(3 - hop)]))
+    return [ups[3], ups[2], ups[1], value, downs[1], downs[2], downs[3]]
+
+
+def sum_rows(partial, here):
+    rows = partial.shape[0] // 4
+
+    def block(index):
+        return lax.dynamic_slice_in_dim(partial, jnp.clip(index, 0, 3) * rows, rows, 0)
+
+    up = down = None
+    for hop in range(1, 4):
+        up_value, down_value = block(here + 4 - hop), block(here - 4 + hop)
+        if up is not None:
+            up_value = up_value + up.astype(jnp.float32)
+            down_value = down_value + down.astype(jnp.float32)
+        up = lax.ppermute(
+            up_value.astype(jnp.bfloat16), "tensor", [(i, i + 1) for i in range(hop)]
+        )
+        down = lax.ppermute(
+            down_value.astype(jnp.bfloat16), "tensor", [(i, i - 1) for i in range(4 - hop, 4)]
+        )
+    return block(here) + (up.astype(jnp.float32) + down.astype(jnp.float32))
+
+
+def on_device_fast(
+    residual,
+    cotangent,
+    lengths,
+    owners,
+    step_count,
+    rates,
+    weight_decay,
+    ema_decay,
+    master,
+    moment_one,
+    moment_two,
+    average,
+):
+    local_width = HD * H // lax.axis_size("tensor")
+    group_rows = residual.shape[1] * lax.axis_size("tensor")
+    slots = jnp.arange(8, dtype=jnp.int32)
+    inverse = jnp.sum(
+        slots[None, :] * (owners[None, :] == slots[:, None]).astype(jnp.int32), axis=1
+    )
+    data_index, core, here = lax.axis_index("dp"), lax.axis_index("chip"), lax.axis_index("tensor")
+    partners = jnp.stack([(data_index ^ j) * 2 + (core ^ c) for c in range(2) for j in range(4)])
+    buckets = jnp.sum(
+        jnp.where(partners[:, None] == slots[None, :], inverse[None, :], 0), axis=1
+    ).astype(jnp.int32)
+    partner_of = jnp.sum(
+        jnp.where(buckets[None, :] == slots[:, None], slots[None, :], 0), axis=1
+    )
+    hop, other = partner_of % 4, partner_of // 4
+    grad_tables = [
+        jnp.concatenate([core[None], hop % 2, (hop // 2) * 2 + other]).astype(jnp.int32),
+        jnp.concatenate([core[None], hop // 2, (hop % 2) * 2 + other]).astype(jnp.int32),
+    ]
+
+    row_pieces = spread_rows(residual[0])
+    grad_pieces = spread_rows(cotangent[0])
+    packed = pack(buckets[:1], master.reshape(FLAT, LANES))
+    weights = []
+    for part, own in enumerate(packed):
+        from_x, from_y = along_x(own), along_y(own)
+        diagonal = along_x(from_y) if part % 2 == 0 else along_y(from_x)
+        mine = [own, from_x, from_y, diagonal]
+        weights = unpack(part, buckets, mine + [across(value) for value in mine], weights)
+    mixer_in, mixer_out, expand_weight, shrink_weight, biases = weights
+    flat_bias = biases[:8].reshape(-1).astype(jnp.float32)
+    mixer_bias = flat_bias[: 3 * local_width]
+    expand_bias = flat_bias[3 * local_width : 3 * local_width + D]
+    small_params = flat_bias[3 * local_width + D : 3 * local_width + 7 * D].reshape(6, D)
+
+    index = here[None].astype(jnp.int32)
+    full_rows = place_rows(index, row_pieces)
+    other_rows = across(full_rows)
+    grad_rows = place_rows(index, grad_pieces)
+    half_width = D // 2
+    other_grads = across(lax.dynamic_slice_in_dim(grad_rows, (1 - core) * half_width, half_width, 1))
+
+    own_rows = residual[0].astype(jnp.float32)
+    own_unit, own_scale = norm_stats(own_rows)
+
+    def norms(rows):
+        unit, _ = norm_stats(rows.astype(jnp.float32))
+        return (
+            (unit * small_params[0] + small_params[1]).astype(jnp.bfloat16),
+            (unit * small_params[2] + small_params[3]).astype(jnp.bfloat16),
+        )
+
+    full_one, full_two = norms(full_rows)
+    other_one, other_two = norms(other_rows)
+
+    order = jnp.arange(lengths.shape[1], dtype=jnp.int32)
+    seq_ends = jnp.sum(jnp.where(order[None, :] <= order[:, None], lengths[0][None, :], 0), axis=1)
+    token_index = jnp.arange(group_rows, dtype=jnp.int32)
+    passed = (token_index[:, None] >= seq_ends[None, :]).astype(jnp.int32)
+    begins = jnp.sum(passed * lengths[0][None, :], axis=1)
+    tables = rope_tables((token_index - begins).astype(jnp.float32))
+    begins = begins[:, None]
+
+    projected = matmul(full_one, mixer_in)
+    context, turned, logs = attend(projected, mixer_bias[None], tables, begins)
+    hidden, slope = hidden_layer(full_two, expand_weight, expand_bias[None])
+    other_context, other_hidden = across(context), across(hidden)
+    branches = sum_rows(matmul(context, mixer_out) + matmul(hidden, shrink_weight), here)
+    output = own_rows + branches + small_params[4] + small_params[5]
+
+    grad_before, grad_expand_bias = hidden_back(grad_rows, shrink_weight, slope)
+    other_before = across(
+        lax.dynamic_slice_in_dim(grad_before, (1 - core) * half_width, half_width, 1)
+    )
+    grad_context = product_back(grad_rows, mixer_out).astype(jnp.bfloat16)
+    grad_projected = attend_back(turned, logs, tables, begins, grad_context)
+    half_in = 3 * local_width // 2
+    other_projected = across(
+        lax.dynamic_slice_in_dim(grad_projected, (1 - core) * half_in, half_in, 1)
+    )
+
+    lefts = [
+        full_one, other_one, context, other_context, full_two, other_two, hidden, other_hidden
+    ]
+    rights = [grad_projected, other_projected, grad_rows, other_grads, grad_before, other_before]
+    pieces = []
+    for part, (first, second) in enumerate(((along_x, along_y), (along_y, along_x))):
+        sent, kept = weight_grads(part, grad_tables[part], lefts, rights)
+        came = first(sent)
+        passed_on = second((kept[2:] + came[2:].astype(jnp.float32)).astype(jnp.bfloat16))
+        total = kept[:2] + came[:2].astype(jnp.float32) + passed_on.astype(jnp.float32)
+        pieces.append((total[0], across(total[1])))
+    pieces = [pieces[0][0], pieces[1][0], pieces[0][1], pieces[1][1]]
+
+    partial_one = product_back(grad_projected, mixer_in)
+    partial_two = product_back(grad_before, expand_weight)
+    unit_rows, _ = norm_stats(full_rows.astype(jnp.float32))
+    norm_grads = jnp.stack(
+        [
+            jnp.sum(partial_one * unit_rows, axis=0),
+            jnp.sum(partial_one, axis=0),
+            jnp.sum(partial_two * unit_rows, axis=0),
+            jnp.sum(partial_two, axis=0),
+        ]
+    )
+    scaled = sum_rows(partial_one * small_params[0] + partial_two * small_params[2], here)
+    grad_own = cotangent[0].astype(jnp.float32)
+    input_grad = grad_own + own_scale * (
+        scaled
+        - jnp.mean(scaled, axis=-1, keepdims=True)
+        - own_unit * jnp.mean(scaled * own_unit, axis=-1, keepdims=True)
+    )
+    seen = jnp.stack(spread_rows(norm_grads))
+    ordered = lax.dynamic_slice_in_dim(seen, 3 - here, 4, 0)
+    norm_grads = ((ordered[0] + ordered[1]) + ordered[2]) + ordered[3]
+    bias_grad = jnp.sum(grad_rows.astype(jnp.float32), axis=0)
+    small = jnp.concatenate(
+        [
+            jnp.sum(grad_projected.astype(jnp.float32), axis=0),
+            grad_expand_bias[0],
+            norm_grads.reshape(-1),
+            bias_grad,
+            bias_grad,
+            jnp.zeros((8 * D - 3 * local_width - 7 * D,), jnp.float32),
+        ]
+    ).reshape(LANES, LANES)
+    for move in (across, along_x, along_y):
+        small = small + move(small)
+
+    step_value = step_count[0].astype(jnp.float32)
+    scalars = jnp.stack(
+        [
+            1.0 - jnp.power(beta_one, step_value),
+            1.0 - jnp.power(beta_two, step_value),
+            weight_decay[0],
+            ema_decay[0],
+        ]
+    )
+    state = [v.reshape(FLAT, LANES) for v in (master, moment_one, moment_two, average)]
+    table = jnp.stack([buckets[0], core.astype(jnp.int32)])
+    results = adam(table, scalars, rates, pieces, small, state)
+    return (output[None], input_grad[None], *[v.reshape(master.shape) for v in results])
+
+
 def solution(mesh):
     placed = (
         P(("dp", "chip"), "tensor", None),
@@ -339,7 +1230,7 @@
         P("tensor", ("dp", "chip"), None),
     )
     return jax.shard_map(
-        on_device,
+        device_program(mesh),
         mesh=mesh,
         in_specs=placed,
         out_specs=(

time: 1940 us -> 720 us (0.37)
  waiting for transfers between devices: 901 us -> 290 us
  local copies, waits for them, and re-layouts: 594 us -> 45.4 us
  Pallas kernels: 0 us -> 175 us
  other arithmetic: 205 us -> 61.3 us
  matrix products: 183 us -> 50.6 us
  starting transfers between devices: 0.5 us -> 84.6 us
  blocking collectives: 20.2 us -> 0 us
    unnamed x9 -> x0, waiting for transfers between devices: 569 us -> none
    ppermute x0 -> x73, waiting for transfers between devices: none -> 290 us  [the longest x9 88.3 us: along_x(): return lax.ppermute(value, 'dp', [(i, i ^ 1) for i in range(4)])]
    gather x31 -> x0, local copies, waits for them, and re-layouts: 288 us -> none  [the longest x16 157 us: on_device(): flat_params = jnp.take(gathered[0], owners, axis=0).reshape(-1)]
    all_gather x4 -> x0, waiting for transfers between devices: 233 us -> none  [the longest x1 233 us: on_device(): lax.all_gather(master.astype(jnp.bfloat16), ('dp', 'chip'), axis=1, tiled...]
    pallas_call x0 -> x14, Pallas kernels: none -> 175 us  [the longest x2 65.5 us: weight_grads(): pl.pallas_call(weight_grad_kernel, out_shape=[jax.ShapeDtypeStruct((4, ro...]
    unnamed x207 -> x210, local copies, waits for them, and re-layouts: 186 us -> 34.6 us
    reduce_scatter x3 -> x0, waiting for transfers between devices: 99.3 us -> none  [the longest x1 99.2 us: on_device(): lax.psum_scatter(partial_two, 'tensor', scatter_dimension=0, tiled=True)]
    ppermute x0 -> x73, starting transfers between devices: none -> 84.6 us  [the longest x6 24.9 us: sum_rows(): lax.ppermute(up_value.astype(jnp.bfloat16), 'tensor', [(i, i + 1) for i i...]
  transfers between devices with their start and end apart: 8 -> 73, of which waited for: 3 -> 21; matrix products, arithmetic and copies ran while one was open for 45% -> 17% of each run, Pallas kernels for 0% -> 21%
where the time goes in v1:
time: 720 us; the launch traced here: 712 us
  waiting for transfers between devices  290 us (40%)
  Pallas kernels  175 us (24%)
  starting transfers between devices  84.6 us (12%)
  other arithmetic  61.3 us (9%)
  matrix products  50.6 us (7%)
  local copies, waits for them, and re-layouts  45.4 us (6%)
    ppermute x9, waiting for transfers between devices, along_x(): return lax.ppermute(value, 'dp', [(i, i ^ 1) for i in range(4)])  88.3 us
    ppermute x9, waiting for transfers between devices, along_y(): return lax.ppermute(value, 'dp', [(i, i ^ 2) for i in range(4)])  65.9 us
    pallas_call x2, Pallas kernels, weight_grads(): pl.pallas_call(weight_grad_kernel, out_shape=[jax.ShapeDtypeStruct((4, ro...  65.5 us
    ppermute x9, waiting for transfers between devices, spread_rows(): lax.ppermute(downs[-1], 'tensor', [(i + 1, i) for i in range(3 - hop)])  65 us
    unnamed x210, local copies, waits for them, and re-layouts  34.6 us
    ppermute x6, waiting for transfers between devices, sum_rows(): lax.ppermute(up_value.astype(jnp.bfloat16), 'tensor', [(i, i + 1) for i i...  33.4 us
    dot_general x3, matrix products, product_back(): lax.dot_general(left, right, (((1,), (1,)), ((), ())), preferred_element_...  30.7 us
    ppermute x6, starting transfers between devices, sum_rows(): lax.ppermute(up_value.astype(jnp.bfloat16), 'tensor', [(i, i + 1) for i i...  24.9 us
  transfers between devices with their start and end apart: 73, of which 21 were waited for; matrix products, arithmetic and copies ran while one was open for 17% of the time, Pallas kernels for 21%

profile of v1, /device:TPU:0, one launch (start us, length us, event | category | flops | bytes accessed | tf_op | source)
XLA Modules:
  0.0 711.8 jit_solution(9820409395802406092)
XLA Ops:
  1.8 2.8 copy-done.11
  6.4 3.8 collective-permute-start.28
  13.2 15.7 %collective-permute-done.28.refs_2_ = bf16[3136,128]{1,0:T(8,128)(2,1)S(1)} collective-permute-done((bf16[3136,128]{1,0:T(8,128)(2,1)S(1)}, bf16[3136,128]{1,0:T(8,128)(2,1)S(1)}, u32[]{:S(2)}, u32[]{:S(2)}) %collective-permute-start.28) | collective-permute-done | bytes 802848 | tf_op jit(solution)/shard_map/ppermute | solution.py:1023
  34.3 13.9 %collective-permute-done.20.refs_1_ = bf16[3136,128]{1,0:T(8,128)(2,1)S(1)} collective-permute-done((bf16[3136,128]{1,0:T(8,128)(2,1)S(1)}, bf16[3136,128]{1,0:T(8,128)(2,1)S(1)}, u32[]{:S(2)}, u32[]{:S(2)}) %collective-permute-start.20) | collective-permute-done | bytes 802848 | tf_op jit(solution)/shard_map/ppermute | solution.py:1019
  52.1 11.3 %collective-permute-done.14.refs_2_ = bf16[3136,128]{1,0:T(8,128)(2,1)S(1)} collective-permute-done((bf16[3136,128]{1,0:T(8,128)(2,1)S(1)}, bf16[3136,128]{1,0:T(8,128)(2,1)S(1)}, u32[]{:S(2)}, u32[]{:S(2)}) %collective-permute-start.14) | collective-permute-done | bytes 802848 | tf_op jit(solution)/shard_map/ppermute | solution.py:1023
  63.4 3.5 collective-permute-start
  70.0 11.3 %collective-permute-done.6.refs_1_ = bf16[3136,128]{1,0:T(8,128)(2,1)} collective-permute-done((bf16[3136,128]{1,0:T(8,128)(2,1)S(1)}, bf16[3136,128]{1,0:T(8,128)(2,1)}, u32[]{:S(2)}, u32[]{:S(2)}) %collective-permute-start.6) | collective-permute-done | bytes 802848 | tf_op jit(solution)/shard_map/ppermute | solution.py:1019
  81.3 3.5 collective-permute-start.40
  91.3 3.6 collective-permute-done.3.refs_4_
  95.8 15.0 %collective-permute-done.40.refs_2_ = bf16[256,2048]{1,0:T(8,128)(2,1)S(1)} collective-permute-done((bf16[256,2048]{1,0:T(8,128)(2,1)S(1)}, bf16[256,2048]{1,0:T(8,128)(2,1)S(1)}, u32[]{:S(2)}, u32[]{:S(2)}) %collective-permute-start.40) | collective-permute-done | bytes 1048608 | tf_op jit(solution)/shard_map/ppermute | solution.py:1033
  111.7 3.3 collective-permute-done.43.refs_4_
  124.1 4.5 collective-permute-done.22.refs_3_
  134.5 16.9 %collective-permute-done.4.refs_5_ = bf16[256,2048]{1,0:T(8,128)(2,1)} collective-permute-done((bf16[256,2048]{1,0:T(8,128)(2,1)S(1)}, bf16[256,2048]{1,0:T(8,128)(2,1)}, u32[]{:S(2)}, u32[]{:S(2)}) %collective-permute-start.4) | collective-permute-done | bytes 1048608 | tf_op jit(solution)/shard_map/ppermute | solution.py:1034
  160.2 19.6 %collective-permute-done.5.refs_6_ = bf16[256,2048]{1,0:T(8,128)(2,1)} collective-permute-done((bf16[256,2048]{1,0:T(8,128)(2,1)}, bf16[256,2048]{1,0:T(8,128)(2,1)}, u32[]{:S(2)}, u32[]{:S(2)}) %collective-permute-start.5) | collective-permute-done | bytes 1048608 | tf_op jit(solution)/shard_map/ppermute | solution.py:1034
  182.3 3.9 place_rows.2
  187.4 1.9 multiply_sine_fusion
  189.3 11.3 %collective-permute-done.44.refs_5_ = bf16[256,2048]{1,0:T(8,128)(2,1)S(1)} collective-permute-done((bf16[256,2048]{1,0:T(8,128)(2,1)}, bf16[256,2048]{1,0:T(8,128)(2,1)S(1)}, u32[]{:S(2)}, u32[]{:S(2)}) %collective-permute-start.44) | collective-permute-done | bytes 1048608 | tf_op jit(solution)/shard_map/ppermute | solution.py:1034
  204.9 4.1 unpack_params.4
  209.2 3.4 unpack_params.5
  212.6 3.4 unpack_params.6
  216.1 4.5 unpack_params.7
  220.6 3.4 copy-done.1
  224.7 4.2 collective-permute-done.45.refs_6_
  232.3 3.1 convert_reduce_fusion.1
  235.5 3.4 fusion.21
  239.5 3.3 convolution_convert_fusion.grad_context
  242.9 2.8 convert_reduce_fusion
  245.7 3.4 fusion.14
  249.1 11.6 %fusion.16 = (bf16[1024,2048]{1,0:T(8,128)(2,1)}, bf16[1024,2048]{1,0:T(8,128)(2,1)S(1)}, bf16[1024,2048]{1,0:T(8,128)(2,1)}, bf16[1024,2048]{1,0:T(8,128)(2,1)}) fusion(bf16[1024,2048]{1,0:T(8,128)(2,1)} %place_rows.2, f32[2048]{0:T(1024)S(1)} %get-tuple-element.129, f32[2048]{0:T(1024)S(1)} %get-tuple-element.130, f32[1024]{0:T(1024)S(1)} %add_rsqrt_fusion.1, ...), kind=kLoop, calls=%fused_computation.20 | loop fusion | flops 37748736 | bytes 25214976 | tf_op jit(solution)/shard_map/convert_element_type | solution.py:1121
  260.7 15.9 %hidden_layer.1 = (bf16[1024,2048]{1,0:T(8,128)(2,1)S(1)}, f32[1024,2048]{1,0:T(8,128)}) custom-call(bf16[1024,2048]{1,0:T(8,128)(2,1)S(1)} %get-tuple-element.115.normed.refs_4_, bf16[2048,2048]{1,0:T(8,128)(2,1)} %copy-done, f32[1,2048]{1,0:T(1,128)S(1)} %bitcast.98), custom_call_target="tpu_custom_call" | custom-call | tf_op jit(solution)/shard_map/hidden_layer/pallas_call | solution.py:840
  276.6 2.1 copy-done.12
  278.7 13.2 %hidden_back.1 = (bf16[1024,2048]{1,0:T(8,128)(2,1)S(1)}, f32[1,2048]{1,0:T(1,128)S(1)}) custom-call(bf16[1024,2048]{1,0:T(8,128)(2,1)S(1)} %place_rows.3.grads.refs_10_, bf16[2048,2048]{1,0:T(8,128)(2,1)} %copy-done.1, f32[1024,2048]{1,0:T(8,128)} %get-tuple-element.75.slope), custom_call_target="tpu_custom_call" | custom-call | tf_op jit(solution)/shard_map/hidden_back/pallas_call | solution.py:867
  291.9 11.0 %fusion.41 = f32[1024,2048]{1,0:T(8,128)} fusion(bf16[1024,2048]{1,0:T(8,128)(2,1)S(1)} %get-tuple-element.76.refs_12_, bf16[2048,2048]{1,0:T(8,128)(2,1)S(1)} %bitcast.85), kind=kOutput, calls=%fused_computation.137 | convolution fusion | flops 8589934592 | bytes 20971520 | tf_op jit(solution)/shard_map/dot_general | solution.py:37
  303.0 8.5 %fusion.39.projected = f32[1024,1536]{1,0:T(8,128)} fusion(bf16[1024,2048]{1,0:T(8,128)(2,1)S(1)} %copy-done.78, bf16[2048,1536]{1,0:T(8,128)(2,1)S(1)} %get-tuple-element.67), kind=kOutput, calls=%fused_computation.135 | convolution fusion | flops 6442450944 | bytes 16777216 | tf_op jit(solution)/shard_map/dot_general | solution.py:27
  311.5 16.7 %attend.1 = (bf16[1024,512]{1,0:T(8,128)(2,1)S(1)}, bf16[1024,1536]{1,0:T(8,128)(2,1)}, f32[4,1024,1]{2,1,0:T(8,128)S(1)}) custom-call(f32[1024,1536]{1,0:T(8,128)} %fusion.39.projected, f32[1,1536]{1,0:T(1,128)S(1)} %broadcast_in_dim.46.bias, f32[1024,128]{1,0:T(8,128)S(1)} %maximum_maximum_fusion.plain, f32[1024,128]{1,0:T(8,128)S(1)} %copy-done.16, ...), custom_call_target="tpu_custom_call" | custom-call | tf_op jit(solution)/shard_map/attend/pallas_call | solution.py:940
  329.1 17.1 %attend_back.1.refs_8_ = bf16[1024,1536]{1,0:T(8,128)(2,1)} custom-call(bf16[1024,1536]{1,0:T(8,128)(2,1)} %get-tuple-element.73.turned, f32[4,1024,1]{2,1,0:T(8,128)S(1)} %get-tuple-element.74.logs, f32[1024,128]{1,0:T(8,128)S(1)} %maximum_maximum_fusion.plain, f32[1024,128]{1,0:T(8,128)S(1)} %copy-done.16, f32[1024,128]{1,0:T(8,128)S(1)} %get-tuple-element.122.upper, ...), custom_call_target="tpu_custom_call" | custom-call | tf_op jit(solution)/shard_map/attend_back/pallas_call | solution.py:993
  346.3 16.3 %fusion.19 = (f32[2048]{0:T(1024)S(1)}, f32[2048]{0:T(1024)S(1)}, f32[2048]{0:T(1024)S(1)}, f32[2048]{0:T(1024)S(1)}, f32[1024,2048]{1,0:T(8,128)}) fusion(bf16[1024,2048]{1,0:T(8,128)(2,1)} %place_rows.2, f32[1024]{0:T(1024)S(1)} %add_rsqrt_fusion.1, f32[1024]{0:T(1024)S(1)} %broadcast_multiply_fusion.1, f32[1024,2048]{1,0:T(8,128)} %fusion.41, ...), kind=kOutput, calls=%fused_computation.23 | convolution fusion | flops 6467608576 | bytes 30466048 | tf_op jit(solution)/shard_map/dot_general | solution.py:37
  362.7 3.9 collective-permute-start.64
  368.4 8.8 %fusion.40 = f32[1024,2048]{1,0:T(8,128)S(1)} fusion(bf16[1024,2048]{1,0:T(8,128)(2,1)S(1)} %copy-done.13, bf16[2048,2048]{1,0:T(8,128)(2,1)S(1)} %bitcast.87), kind=kOutput, calls=%fused_computation.136 | convolution fusion | flops 8589934592 | bytes 20971520 | tf_op jit(solution)/shard_map/dot_general | solution.py:27
  379.1 2.5 convolution_add_fusion
  383.2 5.6 dynamic-slice_convert_fusion.1
  392.6 7.6 %collective-permute-start.34 = (bf16[256,2048]{1,0:T(8,128)(2,1)S(1)}, bf16[256,2048]{1,0:T(8,128)(2,1)S(1)}, u32[]{:S(2)}, u32[]{:S(2)}) collective-permute-start(bf16[256,2048]{1,0:T(8,128)(2,1)S(1)} %get-tuple-element.110), channel_id=1, source_target_pairs={{0,2},{1,3},{8,10},{9,11},{16,18},{17,19},{24,26},{25,27}} | collective-permute-start | bytes 3145736 | tf_op jit(solution)/shard_map/ppermute | solution.py:1050
  401.5 6.1 collective-permute-done.69
  407.8 15.4 %collective-permute-done.34 = bf16[256,2048]{1,0:T(8,128)(2,1)S(1)} collective-permute-done((bf16[256,2048]{1,0:T(8,128)(2,1)S(1)}, bf16[256,2048]{1,0:T(8,128)(2,1)S(1)}, u32[]{:S(2)}, u32[]{:S(2)}) %collective-permute-start.34) | collective-permute-done | bytes 1048608 | tf_op jit(solution)/shard_map/ppermute | solution.py:1050
  423.2 5.4 collective-permute-start.46
  431.5 2.5 collective-permute-start.35
  435.4 32.6 %weight_grads.3 = (bf16[4,3136,128]{2,1,0:T(8,128)(2,1)}, f32[4,3136,128]{2,1,0:T(8,128)}) custom-call(s32[17]{0:T(128)S(1)} %get-tuple-element.137.table, bf16[1024,2048]{1,0:T(8,128)(2,1)} %get-tuple-element.114.refs_0_, bf16[1024,2048]{1,0:T(8,128)(2,1)} %get-tuple-element.131.refs_1_, bf16[1024,512]{1,0:T(8,128)(2,1)S(1)} %copy-done.15, ...), custom_call_target="tpu_custom_call" | custom-call | tf_op jit(solution)/shard_map/weight_grads/pallas_call | solution.py:649
  473.5 3.3 add_convert_fusion.5
  476.8 32.9 %weight_grads.2 = (bf16[4,3136,128]{2,1,0:T(8,128)(2,1)}, f32[4,3136,128]{2,1,0:T(8,128)}) custom-call(s32[17]{0:T(128)S(1)} %get-tuple-element.136.table, bf16[1024,2048]{1,0:T(8,128)(2,1)} %get-tuple-element.114.refs_0_, bf16[1024,2048]{1,0:T(8,128)(2,1)} %get-tuple-element.131.refs_1_, bf16[1024,512]{1,0:T(8,128)(2,1)S(1)} %copy-done.15, ...), custom_call_target="tpu_custom_call" | custom-call | tf_op jit(solution)/shard_map/weight_grads/pallas_call | solution.py:649
  511.5 2.3 add_convert_fusion.8
  516.4 18.0 %collective-permute-done.47 = bf16[256,2048]{1,0:T(8,128)(2,1)S(1)} collective-permute-done((bf16[256,2048]{1,0:T(8,128)(2,1)}, bf16[256,2048]{1,0:T(8,128)(2,1)S(1)}, u32[]{:S(2)}, u32[]{:S(2)}) %collective-permute-start.47) | collective-permute-done | bytes 1048608 | tf_op jit(solution)/shard_map/ppermute | solution.py:1050
  534.4 5.4 collective-permute-start.36
  539.8 4.4 add_convert_fusion.4
  546.4 2.6 collective-permute-start.48
  549.0 2.0 add_convert_fusion
  552.7 31.0 %collective-permute-done.58 = bf16[4,3136,128]{2,1,0:T(8,128)(2,1)S(1)} collective-permute-done((bf16[4,3136,128]{2,1,0:T(8,128)(2,1)}, bf16[4,3136,128]{2,1,0:T(8,128)(2,1)S(1)}, u32[]{:S(2)}, u32[]{:S(2)}) %collective-permute-start.58) | collective-permute-done | bytes 3211296 | tf_op jit(solution)/shard_map/ppermute | solution.py:1019
  586.6 30.8 %collective-permute-done.61 = bf16[2,3136,128]{2,1,0:T(8,128)(2,1)S(1)} collective-permute-done((bf16[2,3136,128]{2,1,0:T(8,128)(2,1)S(1)}, bf16[2,3136,128]{2,1,0:T(8,128)(2,1)S(1)}, u32[]{:S(2)}, u32[]{:S(2)}) %collective-permute-start.61) | collective-permute-done | bytes 1605664 | tf_op jit(solution)/shard_map/ppermute | solution.py:1019
  617.5 1.9 convert_add_fusion
  619.6 34.4 %collective-permute-done.59 = bf16[2,3136,128]{2,1,0:T(8,128)(2,1)S(1)} collective-permute-done((bf16[2,3136,128]{2,1,0:T(8,128)(2,1)}, bf16[2,3136,128]{2,1,0:T(8,128)(2,1)S(1)}, u32[]{:S(2)}, u32[]{:S(2)}) %collective-permute-start.59) | collective-permute-done | bytes 1605664 | tf_op jit(solution)/shard_map/ppermute | solution.py:1023
  655.6 2.4 convert_add_fusion.1
  658.9 20.7 %collective-permute-done.51 = bf16[256,2048]{1,0:T(8,128)(2,1)S(1)} collective-permute-done((bf16[256,2048]{1,0:T(8,128)(2,1)}, bf16[256,2048]{1,0:T(8,128)(2,1)S(1)}, u32[]{:S(2)}, u32[]{:S(2)}) %collective-permute-start.51) | collective-permute-done | bytes 1048608 | tf_op jit(solution)/shard_map/ppermute | solution.py:1053
  679.6 2.0 fusion.37
  681.7 5.8 fusion.30
  687.5 23.8 %adam.1 = (f32[12304,128]{1,0:T(8,128)}, f32[12304,128]{1,0:T(8,128)}, f32[12304,128]{1,0:T(8,128)}, f32[12304,128]{1,0:T(8,128)}, f32[12304,128]{1,0:T(8,128)}) custom-call(s32[2]{0:T(128)S(1)} %pad_add_fusion.table, f32[4]{0:T(128)S(1)} %pad_maximum_fusion.1.scalar_ref, f32[8]{0:T(128)S(1)} %copy-done.75, f32[3136,128]{1,0:T(8,128)S(1)} %get-tuple-element.119.refs_0_, ...), custom_call_target="tpu_custom_call" | custom-call | tf_op jit(solution)/shard_map/adam/pallas_call | solution.py:808
  (389 shorter events, 95.6 us)
Async XLA Ops:
  6.4 22.5 %collective-permute-start.28 = (bf16[3136,128]{1,0:T(8,128)(2,1)S(1)}, bf16[3136,128]{1,0:T(8,128)(2,1)S(1)}, u32[]{:S(2)}, u32[]{:S(2)}) collective-permute-start(bf16[3136,128]{1,0:T(8,128)(2,1)S(1)} %get-tuple-element.50.refs_0_), channel_id=1, source_target_pairs={{0,16},{8,24},{16,0},{24,8},{1,17},{9,25},{17,1},{25,9},{2,18},{10... | collective-permute-start | bytes 2408456 | tf_op jit(solution)/shard_map/ppermute | solution.py:1023
  10.2 20.8 %collective-permute-start.27 = (bf16[3136,128]{1,0:T(8,128)(2,1)S(1)}, bf16[3136,128]{1,0:T(8,128)(2,1)S(1)}, u32[]{:S(2)}, u32[]{:S(2)}) collective-permute-start(bf16[3136,128]{1,0:T(8,128)(2,1)S(1)} %get-tuple-element.50.refs_0_), channel_id=1, source_target_pairs={{0,8},{8,0},{16,24},{24,16},{1,9},{9,1},{17,25},{25,17},{2,10},{10... | collective-permute-start | bytes 2408456 | tf_op jit(solution)/shard_map/ppermute | solution.py:1019
  11.7 20.2 %collective-permute-start.30 = (bf16[3136,128]{1,0:T(8,128)(2,1)S(1)}, bf16[3136,128]{1,0:T(8,128)(2,1)S(1)}, u32[]{:S(2)}, u32[]{:S(2)}) collective-permute-start(bf16[3136,128]{1,0:T(8,128)(2,1)S(1)} %get-tuple-element.50.refs_0_), channel_id=1, source_target_pairs={{0,1},{1,0},{2,3},{3,2},{4,5},{5,4},{6,7},{7,6},{8,9},{9,8},{10,11... | collective-permute-start | bytes 2408456 | tf_op jit(solution)/shard_map/ppermute | solution.py:1027
  12.6 35.6 %collective-permute-start.20 = (bf16[3136,128]{1,0:T(8,128)(2,1)S(1)}, bf16[3136,128]{1,0:T(8,128)(2,1)S(1)}, u32[]{:S(2)}, u32[]{:S(2)}) collective-permute-start(bf16[3136,128]{1,0:T(8,128)(2,1)S(1)} %get-tuple-element.49.refs_0_), channel_id=1, source_target_pairs={{0,8},{8,0},{16,24},{24,16},{1,9},{9,1},{17,25},{25,17},{2,10},{10... | collective-permute-start | bytes 2408456 | tf_op jit(solution)/shard_map/ppermute | solution.py:1019
  13.1 36.0 %collective-permute-start.21 = (bf16[3136,128]{1,0:T(8,128)(2,1)S(1)}, bf16[3136,128]{1,0:T(8,128)(2,1)S(1)}, u32[]{:S(2)}, u32[]{:S(2)}) collective-permute-start(bf16[3136,128]{1,0:T(8,128)(2,1)S(1)} %get-tuple-element.49.refs_0_), channel_id=1, source_target_pairs={{0,16},{8,24},{16,0},{24,8},{1,17},{9,25},{17,1},{25,9},{2,18},{10... | collective-permute-start | bytes 2408456 | tf_op jit(solution)/shard_map/ppermute | solution.py:1023
  28.9 21.7 %collective-permute-start.23 = (bf16[3136,128]{1,0:T(8,128)(2,1)S(1)}, bf16[3136,128]{1,0:T(8,128)(2,1)S(1)}, u32[]{:S(2)}, u32[]{:S(2)}) collective-permute-start(bf16[3136,128]{1,0:T(8,128)(2,1)S(1)} %get-tuple-element.49.refs_0_), channel_id=1, source_target_pairs={{0,1},{1,0},{2,3},{3,2},{4,5},{5,4},{6,7},{7,6},{8,9},{9,8},{10,11... | collective-permute-start | bytes 2408456 | tf_op jit(solution)/shard_map/ppermute | solution.py:1027
  31.0 32.3 %collective-permute-start.14 = (bf16[3136,128]{1,0:T(8,128)(2,1)S(1)}, bf16[3136,128]{1,0:T(8,128)(2,1)S(1)}, u32[]{:S(2)}, u32[]{:S(2)}) collective-permute-start(bf16[3136,128]{1,0:T(8,128)(2,1)S(1)} %get-tuple-element.48.refs_0_), channel_id=1, source_target_pairs={{0,16},{8,24},{16,0},{24,8},{1,17},{9,25},{17,1},{25,9},{2,18},{10... | collective-permute-start | bytes 2408456 | tf_op jit(solution)/shard_map/ppermute | solution.py:1023
  32.8 34.1 %collective-permute-start.13 = (bf16[3136,128]{1,0:T(8,128)(2,1)S(1)}, bf16[3136,128]{1,0:T(8,128)(2,1)S(1)}, u32[]{:S(2)}, u32[]{:S(2)}) collective-permute-start(bf16[3136,128]{1,0:T(8,128)(2,1)S(1)} %get-tuple-element.48.refs_0_), channel_id=1, source_target_pairs={{0,8},{8,0},{16,24},{24,16},{1,9},{9,1},{17,25},{25,17},{2,10},{10... | collective-permute-start | bytes 2408456 | tf_op jit(solution)/shard_map/ppermute | solution.py:1019
  48.2 19.9 %collective-permute-start.16 = (bf16[3136,128]{1,0:T(8,128)(2,1)S(1)}, bf16[3136,128]{1,0:T(8,128)(2,1)S(1)}, u32[]{:S(2)}, u32[]{:S(2)}) collective-permute-start(bf16[3136,128]{1,0:T(8,128)(2,1)S(1)} %get-tuple-element.48.refs_0_), channel_id=1, source_target_pairs={{0,1},{1,0},{2,3},{3,2},{4,5},{5,4},{6,7},{7,6},{8,9},{9,8},{10,11... | collective-permute-start | bytes 2408456 | tf_op jit(solution)/shard_map/ppermute | solution.py:1027
  49.1 32.1 %collective-permute-start.6 = (bf16[3136,128]{1,0:T(8,128)(2,1)S(1)}, bf16[3136,128]{1,0:T(8,128)(2,1)}, u32[]{:S(2)}, u32[]{:S(2)}) collective-permute-start(bf16[3136,128]{1,0:T(8,128)(2,1)S(1)} %get-tuple-element.47.refs_0_), channel_id=1, source_target_pairs={{0,8},{8,0},{16,24},{24,16},{1,9},{9,1},{17,25},{25,17},{2,10},{10... | collective-permute-start | bytes 2408456 | tf_op jit(solution)/shard_map/ppermute | solution.py:1019
  51.5 33.3 %collective-permute-start.7 = (bf16[3136,128]{1,0:T(8,128)(2,1)S(1)}, bf16[3136,128]{1,0:T(8,128)(2,1)S(1)}, u32[]{:S(2)}, u32[]{:S(2)}) collective-permute-start(bf16[3136,128]{1,0:T(8,128)(2,1)S(1)} %get-tuple-element.47.refs_0_), channel_id=1, source_target_pairs={{0,16},{8,24},{16,0},{24,8},{1,17},{9,25},{17,1},{25,9},{2,18},{10... | collective-permute-start | bytes 2408456 | tf_op jit(solution)/shard_map/ppermute | solution.py:1023
  63.4 27.0 %collective-permute-start = (bf16[256,2048]{1,0:T(8,128)(2,1)S(1)}, bf16[256,2048]{1,0:T(8,128)(2,1)S(1)}, u32[]{:S(2)}, u32[]{:S(2)}) collective-permute-start(bf16[256,2048]{1,0:T(8,128)(2,1)S(1)} %bitcast.88), channel_id=1, source_target_pairs={{0,2},{2,4},{4,6},{1,3},{3,5},{5,7},{8,10},{10,12},{12,14},{9,11},... | collective-permute-start | bytes 3145736 | tf_op jit(solution)/shard_map/ppermute | solution.py:1033
  66.9 28.0 %collective-permute-start.3 = (bf16[256,2048]{1,0:T(8,128)(2,1)S(1)}, bf16[256,2048]{1,0:T(8,128)(2,1)S(1)}, u32[]{:S(2)}, u32[]{:S(2)}) collective-permute-start(bf16[256,2048]{1,0:T(8,128)(2,1)S(1)} %bitcast.89), channel_id=1, source_target_pairs={{2,0},{4,2},{6,4},{3,1},{5,3},{7,5},{10,8},{12,10},{14,12},{11,9},... | collective-permute-start | bytes 3145736 | tf_op jit(solution)/shard_map/ppermute | solution.py:1034
  69.1 17.0 %collective-permute-start.9 = (bf16[3136,128]{1,0:T(8,128)(2,1)S(1)}, bf16[3136,128]{1,0:T(8,128)(2,1)S(1)}, u32[]{:S(2)}, u32[]{:S(2)}) collective-permute-start(bf16[3136,128]{1,0:T(8,128)(2,1)S(1)} %get-tuple-element.47.refs_0_), channel_id=1, source_target_pairs={{0,1},{1,0},{2,3},{3,2},{4,5},{5,4},{6,7},{7,6},{8,9},{9,8},{10,11... | collective-permute-start | bytes 2408456 | tf_op jit(solution)/shard_map/ppermute | solution.py:1027
  81.3 29.5 %collective-permute-start.40 = (bf16[256,2048]{1,0:T(8,128)(2,1)S(1)}, bf16[256,2048]{1,0:T(8,128)(2,1)S(1)}, u32[]{:S(2)}, u32[]{:S(2)}) collective-permute-start(bf16[256,2048]{1,0:T(8,128)(2,1)S(1)} %bitcast.95), channel_id=1, source_target_pairs={{0,2},{2,4},{4,6},{1,3},{3,5},{5,7},{8,10},{10,12},{12,14},{9,11},... | collective-permute-start | bytes 3145736 | tf_op jit(solution)/shard_map/ppermute | solution.py:1033
  84.9 30.2 %collective-permute-start.43 = (bf16[256,2048]{1,0:T(8,128)(2,1)S(1)}, bf16[256,2048]{1,0:T(8,128)(2,1)}, u32[]{:S(2)}, u32[]{:S(2)}) collective-permute-start(bf16[256,2048]{1,0:T(8,128)(2,1)S(1)} %bitcast.96), channel_id=1, source_target_pairs={{2,0},{4,2},{6,4},{3,1},{5,3},{7,5},{10,8},{12,10},{14,12},{11,9},... | collective-permute-start | bytes 3145736 | tf_op jit(solution)/shard_map/ppermute | solution.py:1034
  87.1 30.6 %collective-permute-start.29 = (bf16[3136,128]{1,0:T(8,128)(2,1)S(1)}, bf16[3136,128]{1,0:T(8,128)(2,1)}, u32[]{:S(2)}, u32[]{:S(2)}) collective-permute-start(bf16[3136,128]{1,0:T(8,128)(2,1)S(1)} %collective-permute-done.28.refs_2_), channel_id=1, source_target_pairs={{0,8},{8,0},{16,24},{24,16},{1,9},{9,1},{17,25},{25,17},{2,10},{10... | collective-permute-start | bytes 2408456 | tf_op jit(solution)/shard_map/ppermute | solution.py:1019
  90.4 28.2 %collective-permute-start.32 = (bf16[3136,128]{1,0:T(8,128)(2,1)S(1)}, bf16[3136,128]{1,0:T(8,128)(2,1)S(1)}, u32[]{:S(2)}, u32[]{:S(2)}) collective-permute-start(bf16[3136,128]{1,0:T(8,128)(2,1)S(1)} %collective-permute-done.28.refs_2_), channel_id=1, source_target_pairs={{0,1},{1,0},{2,3},{3,2},{4,5},{5,4},{6,7},{7,6},{8,9},{9,8},{10,11... | collective-permute-start | bytes 2408456 | tf_op jit(solution)/shard_map/ppermute | solution.py:1027
  94.9 26.1 %collective-permute-start.31 = (bf16[3136,128]{1,0:T(8,128)(2,1)S(1)}, bf16[3136,128]{1,0:T(8,128)(2,1)S(1)}, u32[]{:S(2)}, u32[]{:S(2)}) collective-permute-start(bf16[3136,128]{1,0:T(8,128)(2,1)S(1)} %collective-permute-done.27.refs_1_), channel_id=1, source_target_pairs={{0,1},{1,0},{2,3},{3,2},{4,5},{5,4},{6,7},{7,6},{8,9},{9,8},{10,11... | collective-permute-start | bytes 2408456 | tf_op jit(solution)/shard_map/ppermute | solution.py:1027
  110.8 17.8 %collective-permute-start.22 = (bf16[3136,128]{1,0:T(8,128)(2,1)S(1)}, bf16[3136,128]{1,0:T(8,128)(2,1)S(1)}, u32[]{:S(2)}, u32[]{:S(2)}) collective-permute-start(bf16[3136,128]{1,0:T(8,128)(2,1)S(1)} %collective-permute-done.20.refs_1_), channel_id=1, source_target_pairs={{0,16},{8,24},{16,0},{24,8},{1,17},{9,25},{17,1},{25,9},{2,18},{10... | collective-permute-start | bytes 2408456 | tf_op jit(solution)/shard_map/ppermute | solution.py:1023
  115.1 17.8 %collective-permute-start.1 = (bf16[256,2048]{1,0:T(8,128)(2,1)S(1)}, bf16[256,2048]{1,0:T(8,128)(2,1)}, u32[]{:S(2)}, u32[]{:S(2)}) collective-permute-start(bf16[256,2048]{1,0:T(8,128)(2,1)S(1)} %collective-permute-done.refs_2_), channel_id=1, source_target_pairs={{2,4},{4,6},{3,5},{5,7},{10,12},{12,14},{11,13},{13,15},{18,20},{2... | collective-permute-start | bytes 3145736 | tf_op jit(solution)/shard_map/ppermute | solution.py:1033
  121.8 29.7 %collective-permute-start.4 = (bf16[256,2048]{1,0:T(8,128)(2,1)S(1)}, bf16[256,2048]{1,0:T(8,128)(2,1)}, u32[]{:S(2)}, u32[]{:S(2)}) collective-permute-start(bf16[256,2048]{1,0:T(8,128)(2,1)S(1)} %collective-permute-done.3.refs_4_), channel_id=1, source_target_pairs={{2,0},{4,2},{3,1},{5,3},{10,8},{12,10},{11,9},{13,11},{18,16},{20,... | collective-permute-start | bytes 3145736 | tf_op jit(solution)/shard_map/ppermute | solution.py:1034
  128.6 24.1 %collective-permute-start.15 = (bf16[3136,128]{1,0:T(8,128)(2,1)S(1)}, bf16[3136,128]{1,0:T(8,128)(2,1)S(1)}, u32[]{:S(2)}, u32[]{:S(2)}) collective-permute-start(bf16[3136,128]{1,0:T(8,128)(2,1)S(1)} %collective-permute-done.14.refs_2_), channel_id=1, source_target_pairs={{0,8},{8,0},{16,24},{24,16},{1,9},{9,1},{17,25},{25,17},{2,10},{10... | collective-permute-start | bytes 2408456 | tf_op jit(solution)/shard_map/ppermute | solution.py:1019
  129.6 25.0 %collective-permute-start.18 = (bf16[3136,128]{1,0:T(8,128)(2,1)S(1)}, bf16[3136,128]{1,0:T(8,128)(2,1)S(1)}, u32[]{:S(2)}, u32[]{:S(2)}) collective-permute-start(bf16[3136,128]{1,0:T(8,128)(2,1)S(1)} %collective-permute-done.14.refs_2_), channel_id=1, source_target_pairs={{0,1},{1,0},{2,3},{3,2},{4,5},{5,4},{6,7},{7,6},{8,9},{9,8},{10,11... | collective-permute-start | bytes 2408456 | tf_op jit(solution)/shard_map/ppermute | solution.py:1027
  131.5 24.9 %collective-permute-start.17 = (bf16[3136,128]{1,0:T(8,128)(2,1)S(1)}, bf16[3136,128]{1,0:T(8,128)(2,1)S(1)}, u32[]{:S(2)}, u32[]{:S(2)}) collective-permute-start(bf16[3136,128]{1,0:T(8,128)(2,1)S(1)} %collective-permute-done.13.refs_1_), channel_id=1, source_target_pairs={{0,1},{1,0},{2,3},{3,2},{4,5},{5,4},{6,7},{7,6},{8,9},{9,8},{10,11... | collective-permute-start | bytes 2408456 | tf_op jit(solution)/shard_map/ppermute | solution.py:1027
  132.9 25.1 %collective-permute-start.2 = (bf16[256,2048]{1,0:T(8,128)(2,1)}, bf16[256,2048]{1,0:T(8,128)(2,1)}, u32[]{:S(2)}, u32[]{:S(2)}) collective-permute-start(bf16[256,2048]{1,0:T(8,128)(2,1)} %collective-permute-done.1.refs_1_), channel_id=1, source_target_pairs={{4,6},{5,7},{12,14},{13,15},{20,22},{21,23},{28,30},{29,31}} | collective-permute-start | bytes 3145736 | tf_op jit(solution)/shard_map/ppermute | solution.py:1033
  151.5 28.3 %collective-permute-start.5 = (bf16[256,2048]{1,0:T(8,128)(2,1)}, bf16[256,2048]{1,0:T(8,128)(2,1)}, u32[]{:S(2)}, u32[]{:S(2)}) collective-permute-start(bf16[256,2048]{1,0:T(8,128)(2,1)} %collective-permute-done.4.refs_5_), channel_id=1, source_target_pairs={{2,0},{3,1},{10,8},{11,9},{18,16},{19,17},{26,24},{27,25}} | collective-permute-start | bytes 3145736 | tf_op jit(solution)/shard_map/ppermute | solution.py:1034
  152.8 34.1 %collective-permute-start.41 = (bf16[256,2048]{1,0:T(8,128)(2,1)S(1)}, bf16[256,2048]{1,0:T(8,128)(2,1)}, u32[]{:S(2)}, u32[]{:S(2)}) collective-permute-start(bf16[256,2048]{1,0:T(8,128)(2,1)S(1)} %collective-permute-done.40.refs_2_), channel_id=1, source_target_pairs={{2,4},{4,6},{3,5},{5,7},{10,12},{12,14},{11,13},{13,15},{18,20},{2... | collective-permute-start | bytes 3145736 | tf_op jit(solution)/shard_map/ppermute | solution.py:1033
  155.4 30.8 %collective-permute-start.8 = (bf16[3136,128]{1,0:T(8,128)(2,1)}, bf16[3136,128]{1,0:T(8,128)(2,1)}, u32[]{:S(2)}, u32[]{:S(2)}) collective-permute-start(bf16[3136,128]{1,0:T(8,128)(2,1)} %collective-permute-done.6.refs_1_), channel_id=1, source_target_pairs={{0,16},{8,24},{16,0},{24,8},{1,17},{9,25},{17,1},{25,9},{2,18},{10... | collective-permute-start | bytes 2408456 | tf_op jit(solution)/shard_map/ppermute | solution.py:1023
  157.3 29.5 %collective-permute-start.10 = (bf16[3136,128]{1,0:T(8,128)(2,1)}, bf16[3136,128]{1,0:T(8,128)(2,1)}, u32[]{:S(2)}, u32[]{:S(2)}) collective-permute-start(bf16[3136,128]{1,0:T(8,128)(2,1)} %collective-permute-done.6.refs_1_), channel_id=1, source_target_pairs={{0,1},{1,0},{2,3},{3,2},{4,5},{5,4},{6,7},{7,6},{8,9},{9,8},{10,11... | collective-permute-start | bytes 2408456 | tf_op jit(solution)/shard_map/ppermute | solution.py:1027
  158.0 42.6 %collective-permute-start.44 = (bf16[256,2048]{1,0:T(8,128)(2,1)}, bf16[256,2048]{1,0:T(8,128)(2,1)S(1)}, u32[]{:S(2)}, u32[]{:S(2)}) collective-permute-start(bf16[256,2048]{1,0:T(8,128)(2,1)} %collective-permute-done.43.refs_4_), channel_id=1, source_target_pairs={{2,0},{4,2},{3,1},{5,3},{10,8},{12,10},{11,9},{13,11},{18,16},{20,... | collective-permute-start | bytes 3145736 | tf_op jit(solution)/shard_map/ppermute | solution.py:1034
  179.8 20.8 %collective-permute-start.33 = (bf16[3136,128]{1,0:T(8,128)(2,1)}, bf16[3136,128]{1,0:T(8,128)(2,1)S(1)}, u32[]{:S(2)}, u32[]{:S(2)}) collective-permute-start(bf16[3136,128]{1,0:T(8,128)(2,1)} %collective-permute-done.29.refs_3_), channel_id=1, source_target_pairs={{0,1},{1,0},{2,3},{3,2},{4,5},{5,4},{6,7},{7,6},{8,9},{9,8},{10,11... | collective-permute-start | bytes 2408456 | tf_op jit(solution)/shard_map/ppermute | solution.py:1027
  186.8 15.0 %collective-permute-start.19 = (bf16[3136,128]{1,0:T(8,128)(2,1)S(1)}, bf16[3136,128]{1,0:T(8,128)(2,1)S(1)}, u32[]{:S(2)}, u32[]{:S(2)}) collective-permute-start(bf16[3136,128]{1,0:T(8,128)(2,1)S(1)} %copy-done.68), channel_id=1, source_target_pairs={{0,1},{1,0},{2,3},{3,2},{4,5},{5,4},{6,7},{7,6},{8,9},{9,8},{10,11... | collective-permute-start | bytes 2408456 | tf_op jit(solution)/shard_map/ppermute | solution.py:1027
  186.9 55.9 %collective-permute-start.52 = (bf16[1024,2048]{1,0:T(8,128)(2,1)}, bf16[1024,2048]{1,0:T(8,128)(2,1)}, u32[]{:S(2)}, u32[]{:S(2)}) collective-permute-start(bf16[1024,2048]{1,0:T(8,128)(2,1)} %place_rows.2), channel_id=1, source_target_pairs={{0,1},{1,0},{2,3},{3,2},{4,5},{5,4},{6,7},{7,6},{8,9},{9,8},{10,11... | collective-permute-start | bytes 12582920 | tf_op jit(solution)/shard_map/ppermute | solution.py:1027
  200.6 15.4 %collective-permute-start.11 = (bf16[3136,128]{1,0:T(8,128)(2,1)S(1)}, bf16[3136,128]{1,0:T(8,128)(2,1)S(1)}, u32[]{:S(2)}, u32[]{:S(2)}) collective-permute-start(bf16[3136,128]{1,0:T(8,128)(2,1)S(1)} %copy-done.52), channel_id=1, source_target_pairs={{0,1},{1,0},{2,3},{3,2},{4,5},{5,4},{6,7},{7,6},{8,9},{9,8},{10,11... | collective-permute-start | bytes 2408456 | tf_op jit(solution)/shard_map/ppermute | solution.py:1027
  200.6 15.4 %collective-permute-start.12 = (bf16[3136,128]{1,0:T(8,128)(2,1)}, bf16[3136,128]{1,0:T(8,128)(2,1)S(1)}, u32[]{:S(2)}, u32[]{:S(2)}) collective-permute-start(bf16[3136,128]{1,0:T(8,128)(2,1)} %collective-permute-done.8.refs_3_), channel_id=1, source_target_pairs={{0,1},{1,0},{2,3},{3,2},{4,5},{5,4},{6,7},{7,6},{8,9},{9,8},{10,11... | collective-permute-start | bytes 2408456 | tf_op jit(solution)/shard_map/ppermute | solution.py:1027
  201.1 23.6 %collective-permute-start.42 = (bf16[256,2048]{1,0:T(8,128)(2,1)}, bf16[256,2048]{1,0:T(8,128)(2,1)S(1)}, u32[]{:S(2)}, u32[]{:S(2)}) collective-permute-start(bf16[256,2048]{1,0:T(8,128)(2,1)} %collective-permute-done.41.refs_1_), channel_id=1, source_target_pairs={{4,6},{5,7},{12,14},{13,15},{20,22},{21,23},{28,30},{29,31}} | collective-permute-start | bytes 3145736 | tf_op jit(solution)/shard_map/ppermute | solution.py:1033
  201.9 27.0 %collective-permute-start.45 = (bf16[256,2048]{1,0:T(8,128)(2,1)S(1)}, bf16[256,2048]{1,0:T(8,128)(2,1)S(1)}, u32[]{:S(2)}, u32[]{:S(2)}) collective-permute-start(bf16[256,2048]{1,0:T(8,128)(2,1)S(1)} %collective-permute-done.44.refs_5_), channel_id=1, source_target_pairs={{2,0},{3,1},{10,8},{11,9},{18,16},{19,17},{26,24},{27,25}} | collective-permute-start | bytes 3145736 | tf_op jit(solution)/shard_map/ppermute | solution.py:1034
  232.3 160.3 %collective-permute-start.56 = (bf16[1024,1024]{1,0:T(8,128)(2,1)}, bf16[1024,1024]{1,0:T(8,128)(2,1)}, u32[]{:S(2)}, u32[]{:S(2)}) collective-permute-start(bf16[1024,1024]{1,0:T(8,128)(2,1)} %constant_dynamic-slice_fusion.1), channel_id=1, source_target_pairs={{0,1},{1,0},{2,3},{3,2},{4,5},{5,4},{6,7},{7,6},{8,9},{9,8},{10,11... | collective-permute-start | bytes 6291464 | tf_op jit(solution)/shard_map/ppermute | solution.py:1027
  362.7 26.6 %collective-permute-start.64 = (f32[4,2048]{1,0:T(4,128)S(1)}, f32[4,2048]{1,0:T(4,128)S(1)}, u32[]{:S(2)}, u32[]{:S(2)}) collective-permute-start(f32[4,2048]{1,0:T(4,128)S(1)} %pad_maximum_fusion), channel_id=1, source_target_pairs={{0,2},{2,4},{4,6},{1,3},{3,5},{5,7},{8,10},{10,12},{12,14},{9,11},... | collective-permute-start | bytes 98312 | tf_op jit(solution)/shard_map/ppermute | solution.py:1033
  366.5 24.1 %collective-permute-start.67 = (f32[4,2048]{1,0:T(4,128)S(1)}, f32[4,2048]{1,0:T(4,128)S(1)}, u32[]{:S(2)}, u32[]{:S(2)}) collective-permute-start(f32[4,2048]{1,0:T(4,128)S(1)} %pad_maximum_fusion), channel_id=1, source_target_pairs={{2,0},{4,2},{6,4},{3,1},{5,3},{7,5},{10,8},{12,10},{14,12},{11,9},... | collective-permute-start | bytes 98312 | tf_op jit(solution)/shard_map/ppermute | solution.py:1034
  368.3 65.8 %collective-permute-start.54 = (bf16[1024,2048]{1,0:T(8,128)(2,1)S(1)}, bf16[1024,2048]{1,0:T(8,128)(2,1)}, u32[]{:S(2)}, u32[]{:S(2)}) collective-permute-start(bf16[1024,2048]{1,0:T(8,128)(2,1)S(1)} %copy-done.13), channel_id=1, source_target_pairs={{0,1},{1,0},{2,3},{3,2},{4,5},{5,4},{6,7},{7,6},{8,9},{9,8},{10,11... | collective-permute-start | bytes 12582920 | tf_op jit(solution)/shard_map/ppermute | solution.py:1027
  377.4 54.1 %collective-permute-start.55 = (bf16[1024,768]{1,0:T(8,128)(2,1)S(1)}, bf16[1024,768]{1,0:T(8,128)(2,1)S(1)}, u32[]{:S(2)}, u32[]{:S(2)}) collective-permute-start(bf16[1024,768]{1,0:T(8,128)(2,1)S(1)} %constant_dynamic-slice_fusion.2), channel_id=1, source_target_pairs={{0,1},{1,0},{2,3},{3,2},{4,5},{5,4},{6,7},{7,6},{8,9},{9,8},{10,11... | collective-permute-start | bytes 4718600 | tf_op jit(solution)/shard_map/ppermute | solution.py:1027
  390.7 43.4 %collective-permute-start.57 = (bf16[1024,1024]{1,0:T(8,128)(2,1)S(1)}, bf16[1024,1024]{1,0:T(8,128)(2,1)S(1)}, u32[]{:S(2)}, u32[]{:S(2)}) collective-permute-start(bf16[1024,1024]{1,0:T(8,128)(2,1)S(1)} %constant_dynamic-slice_fusion), channel_id=1, source_target_pairs={{0,1},{1,0},{2,3},{3,2},{4,5},{5,4},{6,7},{7,6},{8,9},{9,8},{10,11... | collective-permute-start | bytes 6291464 | tf_op jit(solution)/shard_map/ppermute | solution.py:1027
  392.6 30.6 %collective-permute-start.34 = (bf16[256,2048]{1,0:T(8,128)(2,1)S(1)}, bf16[256,2048]{1,0:T(8,128)(2,1)S(1)}, u32[]{:S(2)}, u32[]{:S(2)}) collective-permute-start(bf16[256,2048]{1,0:T(8,128)(2,1)S(1)} %get-tuple-element.110), channel_id=1, source_target_pairs={{0,2},{1,3},{8,10},{9,11},{16,18},{17,19},{24,26},{25,27}} | collective-permute-start | bytes 3145736 | tf_op jit(solution)/shard_map/ppermute | solution.py:1050
  407.7 22.2 %collective-permute-start.53 = (bf16[1024,512]{1,0:T(8,128)(2,1)S(1)}, bf16[1024,512]{1,0:T(8,128)(2,1)S(1)}, u32[]{:S(2)}, u32[]{:S(2)}) collective-permute-start(bf16[1024,512]{1,0:T(8,128)(2,1)S(1)} %copy-done.15), channel_id=1, source_target_pairs={{0,1},{1,0},{2,3},{3,2},{4,5},{5,4},{6,7},{7,6},{8,9},{9,8},{10,11... | collective-permute-start | bytes 3145736 | tf_op jit(solution)/shard_map/ppermute | solution.py:1027
  423.2 48.7 %collective-permute-start.46 = (bf16[256,2048]{1,0:T(8,128)(2,1)}, bf16[256,2048]{1,0:T(8,128)(2,1)}, u32[]{:S(2)}, u32[]{:S(2)}) collective-permute-start(bf16[256,2048]{1,0:T(8,128)(2,1)} %get-tuple-element.106), channel_id=1, source_target_pairs={{0,2},{1,3},{8,10},{9,11},{16,18},{17,19},{24,26},{25,27}} | collective-permute-start | bytes 3145736 | tf_op jit(solution)/shard_map/ppermute | solution.py:1050
  429.9 79.8 %collective-permute-start.37 = (bf16[256,2048]{1,0:T(8,128)(2,1)}, bf16[256,2048]{1,0:T(8,128)(2,1)}, u32[]{:S(2)}, u32[]{:S(2)}) collective-permute-start(bf16[256,2048]{1,0:T(8,128)(2,1)} %get-tuple-element.111), channel_id=1, source_target_pairs={{6,4},{7,5},{14,12},{15,13},{22,20},{23,21},{30,28},{31,29}} | collective-permute-start | bytes 3145736 | tf_op jit(solution)/shard_map/ppermute | solution.py:1053
  431.5 79.5 %collective-permute-start.35 = (bf16[256,2048]{1,0:T(8,128)(2,1)}, bf16[256,2048]{1,0:T(8,128)(2,1)}, u32[]{:S(2)}, u32[]{:S(2)}) collective-permute-start(bf16[256,2048]{1,0:T(8,128)(2,1)} %add_convert_fusion.9), channel_id=1, source_target_pairs={{0,2},{2,4},{1,3},{3,5},{8,10},{10,12},{9,11},{11,13},{16,18},{18,... | collective-permute-start | bytes 3145736 | tf_op jit(solution)/shard_map/ppermute | solution.py:1050
  468.0 78.3 %collective-permute-start.60 = (bf16[4,3136,128]{2,1,0:T(8,128)(2,1)}, bf16[4,3136,128]{2,1,0:T(8,128)(2,1)}, u32[]{:S(2)}, u32[]{:S(2)}) collective-permute-start(bf16[4,3136,128]{2,1,0:T(8,128)(2,1)} %get-tuple-element.80), channel_id=1, source_target_pairs={{0,16},{8,24},{16,0},{24,8},{1,17},{9,25},{17,1},{25,9},{2,18},{10... | collective-permute-start | bytes 9633800 | tf_op jit(solution)/shard_map/ppermute | solution.py:1023
  471.0 44.1 %collective-permute-start.49 = (bf16[256,2048]{1,0:T(8,128)(2,1)}, bf16[256,2048]{1,0:T(8,128)(2,1)S(1)}, u32[]{:S(2)}, u32[]{:S(2)}) collective-permute-start(bf16[256,2048]{1,0:T(8,128)(2,1)} %get-tuple-element.107), channel_id=1, source_target_pairs={{6,4},{7,5},{14,12},{15,13},{22,20},{23,21},{30,28},{31,29}} | collective-permute-start | bytes 3145736 | tf_op jit(solution)/shard_map/ppermute | solution.py:1053
  471.9 42.0 %collective-permute-start.71 = (f32[128,128]{1,0:T(8,128)S(1)}, f32[128,128]{1,0:T(8,128)S(1)}, u32[]{:S(2)}, u32[]{:S(2)}) collective-permute-start(f32[128,128]{1,0:T(8,128)S(1)} %bitcast_add_fusion), channel_id=1, source_target_pairs={{0,8},{8,0},{16,24},{24,16},{1,9},{9,1},{17,25},{25,17},{2,10},{10... | collective-permute-start | bytes 196616 | tf_op jit(solution)/shard_map/ppermute | solution.py:1019
  509.7 24.7 %collective-permute-start.47 = (bf16[256,2048]{1,0:T(8,128)(2,1)}, bf16[256,2048]{1,0:T(8,128)(2,1)S(1)}, u32[]{:S(2)}, u32[]{:S(2)}) collective-permute-start(bf16[256,2048]{1,0:T(8,128)(2,1)} %add_convert_fusion.5), channel_id=1, source_target_pairs={{0,2},{2,4},{1,3},{3,5},{8,10},{10,12},{9,11},{11,13},{16,18},{18,... | collective-permute-start | bytes 3145736 | tf_op jit(solution)/shard_map/ppermute | solution.py:1050
  511.1 72.6 %collective-permute-start.58 = (bf16[4,3136,128]{2,1,0:T(8,128)(2,1)}, bf16[4,3136,128]{2,1,0:T(8,128)(2,1)S(1)}, u32[]{:S(2)}, u32[]{:S(2)}) collective-permute-start(bf16[4,3136,128]{2,1,0:T(8,128)(2,1)} %get-tuple-element.78), channel_id=1, source_target_pairs={{0,8},{8,0},{16,24},{24,16},{1,9},{9,1},{17,25},{25,17},{2,10},{10... | collective-permute-start | bytes 9633800 | tf_op jit(solution)/shard_map/ppermute | solution.py:1019
  513.9 30.3 %collective-permute-start.38 = (bf16[256,2048]{1,0:T(8,128)(2,1)S(1)}, bf16[256,2048]{1,0:T(8,128)(2,1)S(1)}, u32[]{:S(2)}, u32[]{:S(2)}) collective-permute-start(bf16[256,2048]{1,0:T(8,128)(2,1)S(1)} %get-tuple-element.109), channel_id=1, source_target_pairs={{4,2},{6,4},{5,3},{7,5},{12,10},{14,12},{13,11},{15,13},{20,18},{2... | collective-permute-start | bytes 3145736 | tf_op jit(solution)/shard_map/ppermute | solution.py:1053
  515.2 143.1 %collective-permute-start.72 = (f32[128,128]{1,0:T(8,128)S(1)}, f32[128,128]{1,0:T(8,128)S(1)}, u32[]{:S(2)}, u32[]{:S(2)}) collective-permute-start(f32[128,128]{1,0:T(8,128)S(1)} %fusion.54), channel_id=1, source_target_pairs={{0,16},{8,24},{16,0},{24,8},{1,17},{9,25},{17,1},{25,9},{2,18},{10... | collective-permute-start | bytes 196616 | tf_op jit(solution)/shard_map/ppermute | solution.py:1023
  534.4 147.3 %collective-permute-start.36 = (bf16[256,2048]{1,0:T(8,128)(2,1)S(1)}, bf16[256,2048]{1,0:T(8,128)(2,1)}, u32[]{:S(2)}, u32[]{:S(2)}) collective-permute-start(bf16[256,2048]{1,0:T(8,128)(2,1)S(1)} %get-tuple-element.108), channel_id=1, source_target_pairs={{0,2},{2,4},{4,6},{1,3},{3,5},{5,7},{8,10},{10,12},{12,14},{9,11},... | collective-permute-start | bytes 3145736 | tf_op jit(solution)/shard_map/ppermute | solution.py:1050
  546.4 112.0 %collective-permute-start.48 = (bf16[256,2048]{1,0:T(8,128)(2,1)}, bf16[256,2048]{1,0:T(8,128)(2,1)}, u32[]{:S(2)}, u32[]{:S(2)}) collective-permute-start(bf16[256,2048]{1,0:T(8,128)(2,1)} %get-tuple-element.104), channel_id=1, source_target_pairs={{0,2},{2,4},{4,6},{1,3},{3,5},{5,7},{8,10},{10,12},{12,14},{9,11},... | collective-permute-start | bytes 3145736 | tf_op jit(solution)/shard_map/ppermute | solution.py:1050
  551.0 66.4 %collective-permute-start.61 = (bf16[2,3136,128]{2,1,0:T(8,128)(2,1)S(1)}, bf16[2,3136,128]{2,1,0:T(8,128)(2,1)S(1)}, u32[]{:S(2)}, u32[]{:S(2)}) collective-permute-start(bf16[2,3136,128]{2,1,0:T(8,128)(2,1)S(1)} %add_convert_fusion), channel_id=1, source_target_pairs={{0,8},{8,0},{16,24},{24,16},{1,9},{9,1},{17,25},{25,17},{2,10},{10... | collective-permute-start | bytes 4816904 | tf_op jit(solution)/shard_map/ppermute | solution.py:1019
  583.7 97.9 %collective-permute-start.39 = (bf16[256,2048]{1,0:T(8,128)(2,1)}, bf16[256,2048]{1,0:T(8,128)(2,1)}, u32[]{:S(2)}, u32[]{:S(2)}) collective-permute-start(bf16[256,2048]{1,0:T(8,128)(2,1)} %add_convert_fusion.6), channel_id=1, source_target_pairs={{2,0},{4,2},{6,4},{3,1},{5,3},{7,5},{10,8},{12,10},{14,12},{11,9},... | collective-permute-start | bytes 3145736 | tf_op jit(solution)/shard_map/ppermute | solution.py:1053
  617.4 36.6 %collective-permute-start.59 = (bf16[2,3136,128]{2,1,0:T(8,128)(2,1)}, bf16[2,3136,128]{2,1,0:T(8,128)(2,1)S(1)}, u32[]{:S(2)}, u32[]{:S(2)}) collective-permute-start(bf16[2,3136,128]{2,1,0:T(8,128)(2,1)} %add_convert_fusion.1), channel_id=1, source_target_pairs={{0,16},{8,24},{16,0},{24,8},{1,17},{9,25},{17,1},{25,9},{2,18},{10... | collective-permute-start | bytes 4816904 | tf_op jit(solution)/shard_map/ppermute | solution.py:1023
  654.0 25.6 %collective-permute-start.51 = (bf16[256,2048]{1,0:T(8,128)(2,1)}, bf16[256,2048]{1,0:T(8,128)(2,1)S(1)}, u32[]{:S(2)}, u32[]{:S(2)}) collective-permute-start(bf16[256,2048]{1,0:T(8,128)(2,1)} %add_convert_fusion.2), channel_id=1, source_target_pairs={{2,0},{4,2},{6,4},{3,1},{5,3},{7,5},{10,8},{12,10},{14,12},{11,9},... | collective-permute-start | bytes 3145736 | tf_op jit(solution)/shard_map/ppermute | solution.py:1053
  658.2 29.2 %collective-permute-start.63 = (f32[3136,128]{1,0:T(8,128)S(1)}, f32[3136,128]{1,0:T(8,128)S(1)}, u32[]{:S(2)}, u32[]{:S(2)}) collective-permute-start(f32[3136,128]{1,0:T(8,128)S(1)} %get-tuple-element.116), channel_id=1, source_target_pairs={{0,1},{1,0},{2,3},{3,2},{4,5},{5,4},{6,7},{7,6},{8,9},{9,8},{10,11... | collective-permute-start | bytes 4816904 | tf_op jit(solution)/shard_map/ppermute | solution.py:1027
  658.3 29.2 %collective-permute-start.62 = (f32[3136,128]{1,0:T(8,128)S(1)}, f32[3136,128]{1,0:T(8,128)S(1)}, u32[]{:S(2)}, u32[]{:S(2)}) collective-permute-start(f32[3136,128]{1,0:T(8,128)S(1)} %get-tuple-element.118), channel_id=1, source_target_pairs={{0,1},{1,0},{2,3},{3,2},{4,5},{5,4},{6,7},{7,6},{8,9},{9,8},{10,11... | collective-permute-start | bytes 4816904 | tf_op jit(solution)/shard_map/ppermute | solution.py:1027
  (108 other events, 1612.3 us)

commit v2 on v1

--- a/solution.py
+++ b/solution.py
@@ -347,7 +347,7 @@
 FRONT = 128
 BACK = 256
 FLAT = 12304
-HBM = pl.ANY
+HBM = pltpu.HBM
 
 
 def params(limit_mb, **more):
@@ -396,18 +396,16 @@
     @pl.when(bucket >= 1)
     def _():
         for panel in range(16):
-            outs[panel // wide][pl.ds(main + (panel % wide) * TROWS, TROWS), :] = take(
+            outs[0][pl.ds(main + panel * TROWS, TROWS), :] = take(
                 (BROWS - bucket) * 16 + panel + FRONT, 16
             )
 
     @pl.when(bucket == 0)
     def _():
-        for part in range(CHUNKS):
-            for panel in range(wide):
-                source = part * narrow + min(panel, narrow - 1)
-                outs[part][pl.ds(main + panel * TROWS, TROWS), :] = take(
-                    QROWS * 12 + source + FRONT, 12
-                )
+        for panel in range(16):
+            outs[0][pl.ds(main + panel * TROWS, TROWS), :] = take(
+                QROWS * 12 + min(panel, 11) + FRONT, 12
+            )
 
 
 def chunk_rows():
@@ -417,14 +415,19 @@
 def pack(bucket, flat):
     return pl.pallas_call(
         pack_kernel,
-        out_shape=[jax.ShapeDtypeStruct((chunk_rows(), LANES), jnp.bfloat16)] * CHUNKS,
+        out_shape=[
+            jax.ShapeDtypeStruct(
+                ((16 // CHUNKS) * BROWS + (0 if part else 16 * TROWS), LANES), jnp.bfloat16
+            )
+            for part in range(CHUNKS)
+        ],
         in_specs=[pl.BlockSpec(memory_space=pltpu.SMEM), pl.BlockSpec(memory_space=HBM)],
         out_specs=[pl.BlockSpec(memory_space=pltpu.VMEM)] * CHUNKS,
         scratch_shapes=[
             pltpu.VMEM((FRONT + FLAT + BACK, LANES), jnp.float32),
             pltpu.SemaphoreType.DMA,
         ],
-        compiler_params=params(24),
+        compiler_params=params(60),
         name="pack_params",
     )(bucket, flat)
 
@@ -468,99 +471,140 @@
 
 def unpack_kernel(part, bucket_ref, *refs):
     sources = refs[:8]
-    staged, load_sems, store_sems = refs[-3:]
-    outs = dict(zip(NAMES, refs[-8:-3], strict=True))
+    staged, tails, load_sems, tail_sem, store_sems = refs[-5:]
+    matrices = refs[-11:-5] if part == 0 else refs[-9:-5]
+    outs = dict(zip(NAMES[: len(matrices)], matrices, strict=False))
     main = (16 // CHUNKS) * BROWS
     loads = [
-        pltpu.make_async_copy(sources[k], staged.at[bucket_ref[k]], load_sems.at[k])
+        pltpu.make_async_copy(
+            sources[k].at[pl.ds(0, main)], staged.at[bucket_ref[k]], load_sems.at[k]
+        )
         for k in range(8)
     ]
+    if part == 0:
+        for k in range(8):
+            pltpu.make_async_copy(
+                sources[k].at[pl.ds(main, 16 * TROWS)], tails.at[bucket_ref[k]], tail_sem
+            ).start()
+        take_tails = pltpu.make_async_copy(tails, tails, tail_sem)
+    else:
+        take_tails = pltpu.make_async_copy(refs[8], tails, tail_sem)
+        take_tails.start()
     for load in loads:
         load.start()
+    take_tails.wait()
     for load in loads:
         load.wait()
     stores = []
 
-    def store(bucket, row, name, first, rows, panel):
-        wide = panels_of(bucket)
-        stores.append(
-            pltpu.make_async_copy(
-                staged.at[bucket, pl.ds(row, rows)],
-                outs[name].at[pl.ds(first, rows), columns(part * wide + panel)],
-                store_sems.at[len(stores)],
+    def store(source, target):
+        stores.append(pltpu.make_async_copy(source, target, store_sems.at[len(stores)]))
+        stores[-1].start()
+
+    if part == 0:
+        store(tails, matrices[5])
+        for panel in range(16):
+            store(
+                tails.at[7, pl.ds(panel * TROWS, TROWS)],
+                outs["bias"].at[pl.ds(0, TROWS), columns(panel)],
             )
-        )
-        stores[-1].start()
-
     for bucket in range(8):
         span = QROWS if bucket < 2 else BROWS
-        for panel in range(panels_of(bucket)):
+        wide = panels_of(bucket)
+        for panel in range(wide):
             if bucket:
                 head = pl.ds(panel * span, TROWS)
-                tail = pl.ds(main + panel * TROWS, TROWS)
-                staged[bucket, head, :] = staged[bucket, head, :] + staged[bucket - 1, tail, :]
+                tail = pl.ds((part * wide + panel) * TROWS, TROWS)
+                staged[bucket, head, :] = staged[bucket, head, :] + tails[bucket - 1, tail, :]
             for name, first, rows, offset in PLACES[bucket]:
-                store(bucket, panel * span + offset, name, first, rows, panel)
-    for panel in range(16 // CHUNKS):
-        store(7, main + panel * TROWS, "bias", 0, TROWS, panel)
+                store(
+                    staged.at[bucket, pl.ds(panel * span + offset, rows)],
+                    outs[name].at[pl.ds(first, rows), columns(part * wide + panel)],
+                )
     for put in stores:
         put.wait()
 
 
 def unpack(part, buckets, sources, before):
-    copies = sum(len(PLACES[b]) * panels_of(b) for b in range(8)) + 16 // CHUNKS
-    return pl.pallas_call(
+    copies = sum(len(PLACES[b]) * panels_of(b) for b in range(8)) + (0 if part else 17)
+    names = NAMES[:4] if part else NAMES
+    tails = jax.ShapeDtypeStruct((8, 16 * TROWS, LANES), jnp.bfloat16)
+    shapes = [jax.ShapeDtypeStruct(MATRICES[name], jnp.bfloat16) for name in names]
+    results = pl.pallas_call(
         functools.partial(unpack_kernel, part),
-        out_shape=[jax.ShapeDtypeStruct(MATRICES[name], jnp.bfloat16) for name in NAMES],
+        out_shape=shapes if part else [*shapes, tails],
         in_specs=[pl.BlockSpec(memory_space=pltpu.SMEM)]
-        + [pl.BlockSpec(memory_space=HBM)] * (8 + len(before)),
-        out_specs=[pl.BlockSpec(memory_space=HBM)] * 5,
-        input_output_aliases={9 + at: at for at in range(len(before))},
+        + [pl.BlockSpec(memory_space=HBM)] * (8 + (5 if part else 0)),
+        out_specs=[pl.BlockSpec(memory_space=HBM)] * (4 if part else 6),
+        input_output_aliases={10 + at: at for at in range(4)} if part else {},
         scratch_shapes=[
-            pltpu.VMEM((8, chunk_rows(), LANES), jnp.bfloat16),
+            pltpu.VMEM((8, (16 // CHUNKS) * BROWS, LANES), jnp.bfloat16),
+            pltpu.VMEM(tails.shape, tails.dtype),
             pltpu.SemaphoreType.DMA((8,)),
+            pltpu.SemaphoreType.DMA,
             pltpu.SemaphoreType.DMA((copies,)),
         ],
-        compiler_params=params(16),
+        compiler_params=params(60),
         name="unpack_params",
-    )(buckets, *sources, *before)
+    )(buckets, *sources, *((before[5], *before[:4]) if part else ()))
+    return [*results, *before[4:]] if part else results
 
 
 GRAD_ROWS = 256
-IN_STEPS, OUT_STEPS, UP_STEPS, DOWN_STEPS = 8, 2, 8, 8
-GRAD_STEPS = IN_STEPS + OUT_STEPS + UP_STEPS + DOWN_STEPS
+PAIR = 2 * GRAD_ROWS
+IN_STEPS, OUT_STEPS, UP_STEPS, DOWN_STEPS = 4, 1, 4, 4
+GRAD_EDGES = (0, 4, 5, 9, 13)
+GRAD_STEPS = 13
+KEPT, NEAR, FAR = 0, 1, 2
 
 
 def weight_grad_kernel(table, *refs):
-    lefts, rights = refs[:8], refs[8:14]
-    sent, kept, wide32, wide16, tail32, tail16, sems, tail_sem = refs[14:]
+    lefts, rights, outs = refs[:8], refs[8:14], refs[14:20]
+    wide32, wide16, tail32, tail16, sems, tail_sem = refs[20:]
     step = pl.program_id(0)
     main = (16 // CHUNKS) * BROWS
 
-    def bucket_of(at):
-        return jnp.where(at < IN_STEPS, at // 4, (at - 2) // 3)
+    def bucket_of(block):
+        return jnp.where(block < 2 * IN_STEPS, block // 4, (block - 2) // 3)
+
+    def target(part, bucket):
+        kind, place = table[1 + 16 * part + bucket], table[9 + 16 * part + bucket]
+        return [
+            (kind == KEPT, False, outs[3 * part + 2].at[place]),
+            (kind == NEAR, True, outs[3 * part].at[jnp.minimum(place, 1)]),
+            (kind == FAR, True, outs[3 * part + 1].at[jnp.minimum(place, 1)]),
+        ]
 
     def copies(at, act):
         slot = lax.rem(at, 2)
-        bucket = bucket_of(at)
-        inner = at < IN_STEPS
-        goes, place = table[1 + bucket], table[9 + bucket]
-        for panels, span, mine in ((3, QROWS, inner), (4, BROWS, jnp.logical_not(inner))):
-            offset = pl.multiple_of(
-                (lax.rem(at, 4) if span == QROWS else lax.rem(at - 2, 3)) * GRAD_ROWS, GRAD_ROWS
-            )
-            for away, stage, target in ((1, wide16, sent), (0, wide32, kept)):
-
-                @pl.when(jnp.logical_and(mine, goes == away))
-                def _(panels=panels, span=span, offset=offset, stage=stage, target=target):
-                    for panel in range(panels):
-                        act(
-                            pltpu.make_async_copy(
-                                stage.at[slot, pl.ds(panel * GRAD_ROWS, GRAD_ROWS)],
-                                target.at[place, pl.ds(panel * span + offset, GRAD_ROWS)],
-                                sems.at[slot, panel],
-                            )
-                        )
+        for half in range(2):
+            block = 2 * at + half
+            bucket = bucket_of(block)
+            inner = block < 2 * IN_STEPS
+            for panels, span, mine in ((3, QROWS, inner), (4, BROWS, jnp.logical_not(inner))):
+                offset = pl.multiple_of(
+                    (lax.rem(block, 4) if span == QROWS else lax.rem(block - 2, 3)) * GRAD_ROWS,
+                    GRAD_ROWS,
+                )
+                for part in range(2):
+                    for which, (is_it, short, place) in enumerate(target(part, bucket)):
+
+                        @pl.when(jnp.logical_and(mine, is_it))
+                        def _(
+                            panels=panels, span=span, offset=offset, part=part, short=short,
+                            place=place, half=half,
+                        ):
+                            stage = wide16 if short else wide32
+                            for panel in range(panels):
+                                act(
+                                    pltpu.make_async_copy(
+                                        stage.at[
+                                            slot, part, half, pl.ds(panel * GRAD_ROWS, GRAD_ROWS)
+                                        ],
+                                        place.at[pl.ds(panel * span + offset, GRAD_ROWS)],
+                                        sems.at[slot, part, half, panel],
+                                    )
+                                )
 
     @pl.when(step >= 2)
     def _():
@@ -571,53 +615,60 @@
         tail32[...] = jnp.zeros_like(tail32)
         tail16[...] = jnp.zeros_like(tail16)
 
-    def block(pair, right, panels, first):
-        left_own, left_other = lefts[2 * pair], lefts[2 * pair + 1]
-        right_own, right_other = rights[2 * right], rights[2 * right + 1]
-        value = product_rows(left_own[...], right_own[...]) + product_rows(
-            left_other[...], right_other[...]
+    def multiply(pair, right, panels):
+        value = product_rows(lefts[2 * pair][...], rights[2 * right][...]) + product_rows(
+            lefts[2 * pair + 1][...], rights[2 * right + 1][...]
         )
         slot = lax.rem(step, 2)
-        for panel in range(panels):
-            part = value[:, panel * LANES : (panel + 1) * LANES]
-            rows = pl.ds(panel * GRAD_ROWS, GRAD_ROWS)
-            wide32[slot, rows, :] = part
-            wide16[slot, rows, :] = part.astype(jnp.bfloat16)
-
-        @pl.when(first)
-        def _():
-            before = jnp.maximum(bucket_of(step) - 1, 0)
-            for panel in range(panels):
-                part = value[:TROWS, panel * LANES : (panel + 1) * LANES]
-                rows = pl.ds(panel * TROWS, TROWS)
-                tail32[before, rows, :] = part
-                tail16[before, rows, :] = part.astype(jnp.bfloat16)
-
-    third = lax.rem(step - 2, 3) == 0
-    edges = (0, IN_STEPS, IN_STEPS + OUT_STEPS, IN_STEPS + OUT_STEPS + UP_STEPS, GRAD_STEPS)
+        for half in range(2):
+            block = 2 * step + half
+            before = jnp.maximum(bucket_of(block) - 1, 0)
+            first = block == 4 if pair == 0 else lax.rem(block - 2, 3) == 0
+            for part in range(2):
+                for panel in range(panels):
+                    left = (part * panels + panel) * LANES
+                    tile = value[half * GRAD_ROWS : (half + 1) * GRAD_ROWS, left : left + LANES]
+                    rows = pl.ds(panel * GRAD_ROWS, GRAD_ROWS)
+                    wide32[slot, part, half, rows, :] = tile
+                    wide16[slot, part, half, rows, :] = tile.astype(jnp.bfloat16)
+
+            @pl.when(first)
+            def _(half=half, before=before):
+                for part in range(2):
+                    for panel in range(panels):
+                        left = (part * panels + panel) * LANES
+                        tile = value[
+                            half * GRAD_ROWS : half * GRAD_ROWS + TROWS, left : left + LANES
+                        ]
+                        rows = pl.ds(panel * TROWS, TROWS)
+                        tail32[part, before, rows, :] = tile
+                        tail16[part, before, rows, :] = tile.astype(jnp.bfloat16)
+
     for pair, right in enumerate((0, 1, 2, 1)):
 
-        @pl.when(jnp.logical_and(step >= edges[pair], step < edges[pair + 1]))
+        @pl.when(jnp.logical_and(step >= GRAD_EDGES[pair], step < GRAD_EDGES[pair + 1]))
         def _(pair=pair, right=right):
-            block(pair, right, 3 if pair == 0 else 4, step == 4 if pair == 0 else third)
+            multiply(pair, right, 3 if pair == 0 else 4)
 
     copies(step, lambda copy: copy.start())
 
     @pl.when(step == GRAD_STEPS - 1)
     def _():
         def tails(act):
-            for bucket in range(8):
-                for away, stage, target in ((1, tail16, sent), (0, tail32, kept)):
-
-                    @pl.when(table[1 + bucket] == away)
-                    def _(bucket=bucket, stage=stage, target=target):
-                        act(
-                            pltpu.make_async_copy(
-                                stage.at[bucket],
-                                target.at[table[9 + bucket], pl.ds(main, stage.shape[1])],
-                                tail_sem.at[bucket],
+            for part in range(2):
+                for bucket in range(8):
+                    for is_it, short, place in target(part, bucket):
+
+                        @pl.when(is_it)
+                        def _(part=part, bucket=bucket, short=short, place=place):
+                            stage = tail16 if short else tail32
+                            act(
+                                pltpu.make_async_copy(
+                                    stage.at[part, bucket],
+                                    place.at[pl.ds(main, stage.shape[2])],
+                                    tail_sem.at[part, bucket],
+                                )
                             )
-                        )
 
         tails(lambda copy: copy.start())
         copies(step - 1, lambda copy: copy.wait())
@@ -625,81 +676,99 @@
         tails(lambda copy: copy.wait())
 
 
-def weight_grads(part, table, lefts, rights):
+def weight_grads(table, lefts, rights):
     tokens = lefts[0].shape[0]
 
     def columns_at(first, count):
         return pl.BlockSpec(
-            (tokens, GRAD_ROWS), lambda i, table: (0, jnp.clip(i - first, 0, count - 1))
+            (tokens, PAIR), lambda i, table: (0, jnp.clip(i - first, 0, count - 1))
         )
 
-    firsts = (0, IN_STEPS, IN_STEPS + OUT_STEPS, IN_STEPS + OUT_STEPS + UP_STEPS)
     left_specs = [
-        columns_at(first, count)
-        for first, count in zip(firsts, (IN_STEPS, OUT_STEPS, UP_STEPS, DOWN_STEPS), strict=True)
+        columns_at(first, last - first)
+        for first, last in zip(GRAD_EDGES, GRAD_EDGES[1:], strict=False)
         for _ in range(2)
     ]
     right_specs = []
-    for width in (384, 512, 512):
-        right_specs.append(
-            pl.BlockSpec((tokens, width), lambda i, table: (0, 2 * table[0] + part))
-        )
-        right_specs.append(pl.BlockSpec((tokens, width), lambda i, table: (0, part)))
+    for own, other in zip(rights[::2], rights[1::2], strict=True):
+        if own.shape == other.shape:
+            right_specs.append(pl.BlockSpec(other.shape, lambda i, table: (0, 0)))
+        else:
+            right_specs.append(pl.BlockSpec(other.shape, lambda i, table: (0, table[0])))
+        right_specs.append(pl.BlockSpec(other.shape, lambda i, table: (0, 0)))
     rows = chunk_rows()
+    short = jax.ShapeDtypeStruct((2, rows, LANES), jnp.bfloat16)
     return pl.pallas_call(
         weight_grad_kernel,
-        out_shape=[
-            jax.ShapeDtypeStruct((4, rows, LANES), jnp.bfloat16),
-            jax.ShapeDtypeStruct((4, rows, LANES), jnp.float32),
-        ],
+        out_shape=[short, short, jax.ShapeDtypeStruct((4, rows, LANES), jnp.float32)] * 2,
         grid_spec=pltpu.PrefetchScalarGridSpec(
             num_scalar_prefetch=1,
             grid=(GRAD_STEPS,),
             in_specs=left_specs + right_specs,
-            out_specs=[pl.BlockSpec(memory_space=HBM)] * 2,
+            out_specs=[pl.BlockSpec(memory_space=HBM)] * 6,
             scratch_shapes=[
-                pltpu.VMEM((2, 4 * GRAD_ROWS, LANES), jnp.float32),
-                pltpu.VMEM((2, 4 * GRAD_ROWS, LANES), jnp.bfloat16),
-                pltpu.VMEM((8, 4 * TROWS, LANES), jnp.float32),
-                pltpu.VMEM((8, 4 * TROWS, LANES), jnp.bfloat16),
-                pltpu.SemaphoreType.DMA((2, 4)),
-                pltpu.SemaphoreType.DMA((8,)),
+                pltpu.VMEM((2, 2, 2, 4 * GRAD_ROWS, LANES), jnp.float32),
+                pltpu.VMEM((2, 2, 2, 4 * GRAD_ROWS, LANES), jnp.bfloat16),
+                pltpu.VMEM((2, 8, 4 * TROWS, LANES), jnp.float32),
+                pltpu.VMEM((2, 8, 4 * TROWS, LANES), jnp.bfloat16),
+                pltpu.SemaphoreType.DMA((2, 2, 2, 4)),
+                pltpu.SemaphoreType.DMA((2, 8)),
             ],
         ),
-        compiler_params=params(48),
+        compiler_params=params(60),
         name="weight_grads",
     )(table, *lefts, *rights)
 
 
-def place_rows_kernel(index_ref, *refs):
-    pieces, out, sems = refs[:7], refs[7], refs[8]
-    rows = pieces[0].shape[0]
-    here = index_ref[0]
-
-    def each(act):
-        for at, piece in enumerate(pieces):
-            target = here + at - 3
-
-            @pl.when(jnp.logical_and(target >= 0, target <= 3))
-            def _(at=at, piece=piece, target=target):
-                spot = pl.ds(pl.multiple_of(jnp.clip(target, 0, 3) * rows, rows), rows)
-                act(pltpu.make_async_copy(piece, out.at[spot], sems.at[at]))
-
-    each(lambda copy: copy.start())
-    each(lambda copy: copy.wait())
-
-
-def place_rows(index, pieces):
-    rows, width = pieces[0].shape
+NORM_COLUMNS = 512
+
+
+def norm_grad_kernel(
+    core, grad_projected, mixer_in, own_before, own_up, rest_before, rest_up, rows, centre, scale,
+    gains, partial, sums,
+):
+    one = product_back(grad_projected[...], mixer_in[...])
+    two = product_back(own_before[...], own_up[...]) + product_back(rest_before[...], rest_up[...])
+    unit = (rows[...].astype(jnp.float32) - centre[...]) * scale[...]
+    partial[...] = one * gains[0:1, :] + two * gains[1:2, :]
+    for at, value in enumerate((one * unit, one, two * unit, two)):
+        sums[at : at + 1, :] = jnp.sum(value, axis=0, keepdims=True)
+
+
+def norm_grad(core, grad_projected, mixer_in, own_before, rest_before, up, rows, centre, scale, gains):
+    tokens = rows.shape[0]
+    half = up.shape[1] // 2
+
+    def whole(value):
+        return pl.BlockSpec(value.shape, lambda i, core: (0, 0))
+
+    block = pl.BlockSpec((tokens, NORM_COLUMNS), lambda i, core: (0, i))
     return pl.pallas_call(
-        place_rows_kernel,
-        out_shape=jax.ShapeDtypeStruct((4 * rows, width), pieces[0].dtype),
-        in_specs=[pl.BlockSpec(memory_space=pltpu.SMEM)] + [pl.BlockSpec(memory_space=HBM)] * 7,
-        out_specs=pl.BlockSpec(memory_space=pltpu.VMEM),
-        scratch_shapes=[pltpu.SemaphoreType.DMA((7,))],
-        compiler_params=params(12),
-        name="place_rows",
-    )(index, *pieces)
+        norm_grad_kernel,
+        out_shape=[
+            jax.ShapeDtypeStruct((tokens, D), jnp.float32),
+            jax.ShapeDtypeStruct((4, D), jnp.float32),
+        ],
+        grid_spec=pltpu.PrefetchScalarGridSpec(
+            num_scalar_prefetch=1,
+            grid=(D // NORM_COLUMNS,),
+            in_specs=[
+                whole(grad_projected),
+                pl.BlockSpec((NORM_COLUMNS, mixer_in.shape[1]), lambda i, core: (i, 0)),
+                whole(own_before),
+                pl.BlockSpec((NORM_COLUMNS, half), lambda i, core: (i, core[0])),
+                whole(rest_before),
+                pl.BlockSpec((NORM_COLUMNS, half), lambda i, core: (i, 1 - core[0])),
+                block,
+                whole(centre),
+                whole(scale),
+                pl.BlockSpec((2, NORM_COLUMNS), lambda i, core: (0, i)),
+            ],
+            out_specs=[block, pl.BlockSpec((4, NORM_COLUMNS), lambda i, core: (0, i))],
+        ),
+        compiler_params=params(60),
+        name="norm_grad",
+    )(core, grad_projected, mixer_in, own_before, up, rest_before, up, rows, centre, scale, gains)
 
 
 ADAM_ROWS = 1024
@@ -819,7 +888,7 @@
             pltpu.VMEM((FRONT + steps * ADAM_ROWS, LANES), jnp.float32),
             pltpu.SemaphoreType.DMA((4,)),
         ],
-        compiler_params=params(40),
+        compiler_params=params(60),
         name="adam",
     )(table, scalars, rates, *pieces, small, *state)
 
@@ -827,59 +896,69 @@
 FF_BLOCK = 256
 
 
-def hidden_kernel(normed, up, up_bias, hidden, slope):
+def hidden_kernel(normed, up, up_bias, *refs):
+    hidden, slope = refs[-2:]
     before = matmul(normed[...], up[...]) + up_bias[...]
     half = 0.5 + 0.5 * lax.erf(before * math.sqrt(0.5))
     hidden[...] = (before * half).astype(jnp.bfloat16)
     slope[...] = half + before * jnp.exp(-0.5 * before * before) * (1.0 / math.sqrt(2.0 * math.pi))
 
 
-def hidden_layer(normed, up, up_bias):
+def hidden_layer(half, normed, up, up_bias, before):
     rows, units = normed.shape[0], up.shape[1]
-    block = pl.BlockSpec((rows, FF_BLOCK), lambda i: (0, i))
+    steps = units // FF_BLOCK // 2
+    block = pl.BlockSpec((rows, FF_BLOCK), lambda i: (0, i + half * steps))
     return pl.pallas_call(
         hidden_kernel,
-        grid=(units // FF_BLOCK,),
+        grid=(steps,),
         out_shape=[
             jax.ShapeDtypeStruct((rows, units), jnp.bfloat16),
             jax.ShapeDtypeStruct((rows, units), jnp.float32),
         ],
         in_specs=[
             pl.BlockSpec(memory_space=pltpu.VMEM),
-            pl.BlockSpec((D, FF_BLOCK), lambda i: (0, i)),
-            pl.BlockSpec((1, FF_BLOCK), lambda i: (0, i)),
-        ],
+            pl.BlockSpec((D, FF_BLOCK), lambda i: (0, i + half * steps)),
+            pl.BlockSpec((1, FF_BLOCK), lambda i: (0, i + half * steps)),
+        ]
+        + [pl.BlockSpec(memory_space=HBM)] * len(before),
         out_specs=[block, block],
-        compiler_params=params(40),
+        input_output_aliases={3 + at: at for at in range(len(before))},
+        compiler_params=params(60),
         name="hidden_layer",
-    )(normed, up, up_bias)
-
-
-def hidden_back_kernel(grads, down, slope, grad_before, grad_bias):
+    )(normed, up, up_bias, *before)
+
+
+def hidden_back_kernel(half, grads, down, slope, grad_before, grad_bias):
     rounded = (slope[...] * product_back(grads[...], down[...])).astype(jnp.bfloat16)
     grad_before[...] = rounded
     grad_bias[...] = jnp.sum(rounded.astype(jnp.float32), axis=0, keepdims=True)
 
 
-def hidden_back(grads, down, slope):
+def hidden_back(half, grads, down, slope):
     rows, units = slope.shape
-    block = pl.BlockSpec((rows, FF_BLOCK), lambda i: (0, i))
+    steps = units // FF_BLOCK // 2
     return pl.pallas_call(
         hidden_back_kernel,
-        grid=(units // FF_BLOCK,),
         out_shape=[
-            jax.ShapeDtypeStruct((rows, units), jnp.bfloat16),
-            jax.ShapeDtypeStruct((1, units), jnp.float32),
+            jax.ShapeDtypeStruct((rows, units // 2), jnp.bfloat16),
+            jax.ShapeDtypeStruct((1, units // 2), jnp.float32),
         ],
-        in_specs=[
-            pl.BlockSpec(memory_space=pltpu.VMEM),
-            pl.BlockSpec((FF_BLOCK, D), lambda i: (i, 0)),
-            block,
-        ],
-        out_specs=[block, pl.BlockSpec((1, FF_BLOCK), lambda i: (0, i))],
-        compiler_params=params(40),
+        grid_spec=pltpu.PrefetchScalarGridSpec(
+            num_scalar_prefetch=1,
+            grid=(steps,),
+            in_specs=[
+                pl.BlockSpec((rows, D), lambda i, half: (0, 0)),
+                pl.BlockSpec((FF_BLOCK, D), lambda i, half: (half[0] * steps + i, 0)),
+                pl.BlockSpec((rows, FF_BLOCK), lambda i, half: (0, half[0] * steps + i)),
+            ],
+            out_specs=[
+                pl.BlockSpec((rows, FF_BLOCK), lambda i, half: (0, i)),
+                pl.BlockSpec((1, FF_BLOCK), lambda i, half: (0, i)),
+            ],
+        ),
+        compiler_params=params(60),
         name="hidden_back",
-    )(grads, down, slope)
+    )(half, grads, down, slope)
 
 
 QUERY_BLOCK = 256
@@ -946,7 +1025,7 @@
         ],
         in_specs=[whole] * 6,
         out_specs=[whole] * 3,
-        compiler_params=params(48),
+        compiler_params=params(60),
         name="attend",
     )(projected, bias, *tables, begins)
 
@@ -996,7 +1075,7 @@
         in_specs=[whole] * 7,
         out_specs=whole,
         scratch_shapes=[pltpu.VMEM((rows, HD), jnp.float32)] * 2,
-        compiler_params=params(48),
+        compiler_params=params(60),
         name="attend_back",
     )(turned, logs, *tables, begins, grad_context)
 
@@ -1023,37 +1102,29 @@
     return lax.ppermute(value, "dp", [(i, i ^ 2) for i in range(4)])
 
 
+def along_line(value, bit):
+    return lax.ppermute(value, "tensor", [(i, i ^ bit) for i in range(4)])
+
+
 def across(value):
     return lax.ppermute(value, "chip", [(0, 1), (1, 0)])
 
 
-def spread_rows(value):
-    ups, downs = [value], [value]
-    for hop in range(3):
-        ups.append(lax.ppermute(ups[-1], "tensor", [(i, i + 1) for i in range(hop, 3)]))
-        downs.append(lax.ppermute(downs[-1], "tensor", [(i + 1, i) for i in range(3 - hop)]))
-    return [ups[3], ups[2], ups[1], value, downs[1], downs[2], downs[3]]
-
-
-def sum_rows(partial, here):
+def line_block(partial, index):
     rows = partial.shape[0] // 4
-
-    def block(index):
-        return lax.dynamic_slice_in_dim(partial, jnp.clip(index, 0, 3) * rows, rows, 0)
-
-    up = down = None
-    for hop in range(1, 4):
-        up_value, down_value = block(here + 4 - hop), block(here - 4 + hop)
-        if up is not None:
-            up_value = up_value + up.astype(jnp.float32)
-            down_value = down_value + down.astype(jnp.float32)
-        up = lax.ppermute(
-            up_value.astype(jnp.bfloat16), "tensor", [(i, i + 1) for i in range(hop)]
-        )
-        down = lax.ppermute(
-            down_value.astype(jnp.bfloat16), "tensor", [(i, i - 1) for i in range(4 - hop, 4)]
-        )
-    return block(here) + (up.astype(jnp.float32) + down.astype(jnp.float32))
+    return lax.dynamic_slice_in_dim(partial, jnp.clip(index, 0, 3) * rows, rows, 0)
+
+
+def line_hop(partial, here, hop, came):
+    up, down = line_block(partial, here + 4 - hop), line_block(partial, here - 4 + hop)
+    if came is not None:
+        up = up + came[0].astype(jnp.float32)
+        down = down + came[1].astype(jnp.float32)
+    ups, downs = [(i, i + 1) for i in range(hop)], [(i, i - 1) for i in range(4 - hop, 4)]
+    return (
+        lax.ppermute(up.astype(jnp.bfloat16), "tensor", ups),
+        lax.ppermute(down.astype(jnp.bfloat16), "tensor", downs),
+    )
 
 
 def on_device_fast(
@@ -1085,48 +1156,82 @@
         jnp.where(buckets[None, :] == slots[:, None], slots[None, :], 0), axis=1
     )
     hop, other = partner_of % 4, partner_of // 4
-    grad_tables = [
-        jnp.concatenate([core[None], hop % 2, (hop // 2) * 2 + other]).astype(jnp.int32),
-        jnp.concatenate([core[None], hop // 2, (hop % 2) * 2 + other]).astype(jnp.int32),
-    ]
-
-    row_pieces = spread_rows(residual[0])
-    grad_pieces = spread_rows(cotangent[0])
-    packed = pack(buckets[:1], master.reshape(FLAT, LANES))
-    weights = []
-    for part, own in enumerate(packed):
-        from_x, from_y = along_x(own), along_y(own)
-        diagonal = along_x(from_y) if part % 2 == 0 else along_y(from_x)
-        mine = [own, from_x, from_y, diagonal]
-        weights = unpack(part, buckets, mine + [across(value) for value in mine], weights)
-    mixer_in, mixer_out, expand_weight, shrink_weight, biases = weights
-    flat_bias = biases[:8].reshape(-1).astype(jnp.float32)
-    mixer_bias = flat_bias[: 3 * local_width]
-    expand_bias = flat_bias[3 * local_width : 3 * local_width + D]
-    small_params = flat_bias[3 * local_width + D : 3 * local_width + 7 * D].reshape(6, D)
-
-    index = here[None].astype(jnp.int32)
-    full_rows = place_rows(index, row_pieces)
-    other_rows = across(full_rows)
-    grad_rows = place_rows(index, grad_pieces)
-    half_width = D // 2
-    other_grads = across(lax.dynamic_slice_in_dim(grad_rows, (1 - core) * half_width, half_width, 1))
-
+    grad_table = [core[None]]
+    for first, second in ((hop % 2, hop // 2), (hop // 2, hop % 2)):
+        grad_table.append(first * (1 + second))
+        grad_table.append(other + 2 * second * (1 - first))
+    grad_table = jnp.concatenate(grad_table).astype(jnp.int32)
+
+    full_rows = lax.all_gather(residual[0], "tensor", axis=0, tiled=True)
+    grad_rows = lax.all_gather(cotangent[0], "tensor", axis=0, tiled=True)
     own_rows = residual[0].astype(jnp.float32)
     own_unit, own_scale = norm_stats(own_rows)
 
-    def norms(rows):
-        unit, _ = norm_stats(rows.astype(jnp.float32))
+    def moments(rows):
+        float_rows = rows.astype(jnp.float32)
+        centre = jnp.mean(float_rows, axis=-1, keepdims=True)
+        spread = jnp.mean((float_rows - centre) * (float_rows - centre), axis=-1, keepdims=True)
+        return centre, lax.rsqrt(spread + norm_epsilon)
+
+    def norms(rows, centre, scale, small_params):
+        unit = (rows.astype(jnp.float32) - centre) * scale
         return (
             (unit * small_params[0] + small_params[1]).astype(jnp.bfloat16),
             (unit * small_params[2] + small_params[3]).astype(jnp.bfloat16),
         )
 
-    full_one, full_two = norms(full_rows)
-    other_one, other_two = norms(other_rows)
-
-    order = jnp.arange(lengths.shape[1], dtype=jnp.int32)
-    seq_ends = jnp.sum(jnp.where(order[None, :] <= order[:, None], lengths[0][None, :], 0), axis=1)
+    def order(*values):
+        return lax.optimization_barrier(values)
+
+    def both(values, move):
+        return [move(value) for value in values]
+
+    packed = pack(buckets[:1], master.reshape(FLAT, LANES))
+    one, two = packed[:2], packed[2:]
+    one_x, one_y, one_own = order(both(one, along_x), both(one, along_y), both(one, across))
+
+    far = [along_x(one_y[0]), along_y(one_x[1])]
+    near = both([*one_x, *one_y], across)
+    far, near, two = order(far, near, two)
+
+    two_x, two_y, far_other = both(two, along_x), both(two, along_y), both(far, across)
+    two_own = both(two, across)
+    weights = []
+    for part in range(2):
+        sources = [one[part], one_x[part], one_y[part], far[part]]
+        sources += [one_own[part], near[part], near[2 + part], far_other[part]]
+        weights = unpack(part, buckets, sources, weights)
+    flat_bias = weights[4][:8].reshape(-1).astype(jnp.float32)
+    mixer_bias = flat_bias[: 3 * local_width]
+    expand_bias = flat_bias[3 * local_width : 3 * local_width + D]
+    small_params = flat_bias[3 * local_width + D : 3 * local_width + 7 * D].reshape(6, D)
+    centre, scale = moments(full_rows)
+    full_one, full_two = norms(full_rows, centre, scale, small_params)
+    other_rows = across(full_rows)
+    two_x, two_y, two_own, weights, full_one, full_two, other_rows = order(
+        two_x, two_y, two_own, weights, full_one, full_two, other_rows
+    )
+
+    far = [along_x(two_y[0]), along_y(two_x[1])]
+    near = both([*two_x, *two_y], across)
+    hidden_half = hidden_layer(0, full_two, weights[2], expand_bias[None], ())
+    other_one, other_two = norms(other_rows, *moments(other_rows), small_params)
+    far, near, hidden_half, weights, other_one, other_two = order(
+        far, near, hidden_half, weights, other_one, other_two
+    )
+
+    far_other = both(far, across)
+    for part in range(2):
+        sources = [two[part], two_x[part], two_y[part], far[part]]
+        sources += [two_own[part], near[part], near[2 + part], far_other[part]]
+        weights = unpack(2 + part, buckets, sources, weights)
+    mixer_in, mixer_out, expand_weight, shrink_weight = weights[:4]
+
+    half_width = D // 2
+    other_grads = across(lax.dynamic_slice_in_dim(grad_rows, (1 - core) * half_width, half_width, 1))
+
+    rank = jnp.arange(lengths.shape[1], dtype=jnp.int32)
+    seq_ends = jnp.sum(jnp.where(rank[None, :] <= rank[:, None], lengths[0][None, :], 0), axis=1)
     token_index = jnp.arange(group_rows, dtype=jnp.int32)
     passed = (token_index[:, None] >= seq_ends[None, :]).astype(jnp.int32)
     begins = jnp.sum(passed * lengths[0][None, :], axis=1)
@@ -1135,70 +1240,96 @@
 
     projected = matmul(full_one, mixer_in)
     context, turned, logs = attend(projected, mixer_bias[None], tables, begins)
-    hidden, slope = hidden_layer(full_two, expand_weight, expand_bias[None])
+    hidden, slope = hidden_layer(1, full_two, expand_weight, expand_bias[None], hidden_half)
     other_context, other_hidden = across(context), across(hidden)
-    branches = sum_rows(matmul(context, mixer_out) + matmul(hidden, shrink_weight), here)
+    branches = matmul(context, mixer_out) + matmul(hidden, shrink_weight)
+    branches, turned = order(branches, turned)
+    branches = lax.psum_scatter(branches, "tensor", scatter_dimension=0, tiled=True)
     output = own_rows + branches + small_params[4] + small_params[5]
-
-    grad_before, grad_expand_bias = hidden_back(grad_rows, shrink_weight, slope)
-    other_before = across(
-        lax.dynamic_slice_in_dim(grad_before, (1 - core) * half_width, half_width, 1)
-    )
     grad_context = product_back(grad_rows, mixer_out).astype(jnp.bfloat16)
     grad_projected = attend_back(turned, logs, tables, begins, grad_context)
     half_in = 3 * local_width // 2
-    other_projected = across(
-        lax.dynamic_slice_in_dim(grad_projected, (1 - core) * half_in, half_in, 1)
+    leaves = lax.dynamic_slice_in_dim(grad_projected, (1 - core) * half_in, half_in, 1)
+    leaves, slope = order(leaves, slope)
+    other_projected = across(leaves)
+    cores = core[None].astype(jnp.int32)
+    rest_before, rest_bias = hidden_back(1 - cores, grad_rows, shrink_weight, slope)
+    other_before = across(rest_before)
+    own_before, own_bias = hidden_back(cores, grad_rows, shrink_weight, slope)
+    grad_expand_bias = jnp.where(
+        core == 0,
+        jnp.concatenate([own_bias[0], rest_bias[0]]),
+        jnp.concatenate([rest_bias[0], own_bias[0]]),
     )
 
     lefts = [
         full_one, other_one, context, other_context, full_two, other_two, hidden, other_hidden
     ]
-    rights = [grad_projected, other_projected, grad_rows, other_grads, grad_before, other_before]
-    pieces = []
-    for part, (first, second) in enumerate(((along_x, along_y), (along_y, along_x))):
-        sent, kept = weight_grads(part, grad_tables[part], lefts, rights)
-        came = first(sent)
-        passed_on = second((kept[2:] + came[2:].astype(jnp.float32)).astype(jnp.bfloat16))
-        total = kept[:2] + came[:2].astype(jnp.float32) + passed_on.astype(jnp.float32)
-        pieces.append((total[0], across(total[1])))
-    pieces = [pieces[0][0], pieces[1][0], pieces[0][1], pieces[1][1]]
-
-    partial_one = product_back(grad_projected, mixer_in)
-    partial_two = product_back(grad_before, expand_weight)
-    unit_rows, _ = norm_stats(full_rows.astype(jnp.float32))
-    norm_grads = jnp.stack(
-        [
-            jnp.sum(partial_one * unit_rows, axis=0),
-            jnp.sum(partial_one, axis=0),
-            jnp.sum(partial_two * unit_rows, axis=0),
-            jnp.sum(partial_two, axis=0),
-        ]
-    )
-    scaled = sum_rows(partial_one * small_params[0] + partial_two * small_params[2], here)
-    grad_own = cotangent[0].astype(jnp.float32)
-    input_grad = grad_own + own_scale * (
-        scaled
-        - jnp.mean(scaled, axis=-1, keepdims=True)
-        - own_unit * jnp.mean(scaled * own_unit, axis=-1, keepdims=True)
-    )
-    seen = jnp.stack(spread_rows(norm_grads))
-    ordered = lax.dynamic_slice_in_dim(seen, 3 - here, 4, 0)
-    norm_grads = ((ordered[0] + ordered[1]) + ordered[2]) + ordered[3]
+    rights = [grad_projected, other_projected, grad_rows, other_grads, own_before, other_before]
+    sums = weight_grads(grad_table, lefts, rights)
+    grad_projected, own_before, rest_before, sums = order(
+        grad_projected, own_before, rest_before, sums
+    )
+    near_a, far_a, kept_a, near_b, far_b, kept_b = sums
+    came_a, came_b = along_x(far_a), along_y(far_b)
+
+    partial, norm_grads = norm_grad(
+        cores,
+        grad_projected,
+        mixer_in,
+        own_before,
+        rest_before,
+        expand_weight,
+        full_rows,
+        centre,
+        scale,
+        jnp.stack([small_params[0], small_params[2]]),
+    )
     bias_grad = jnp.sum(grad_rows.astype(jnp.float32), axis=0)
+    small = (
+        jnp.sum(grad_projected.astype(jnp.float32), axis=0),
+        grad_expand_bias,
+        bias_grad,
+    )
+
+    came_a, came_b, partial, norm_grads, small, near_a, near_b = lax.optimization_barrier(
+        (came_a, came_b, partial, norm_grads, small, near_a, near_b)
+    )
+    near_a, near_b = along_x(near_a), along_y(near_b)
+    line = line_hop(partial, here, 1, None)
+    pass_a = (kept_a[2:] + came_a.astype(jnp.float32)).astype(jnp.bfloat16)
+    pass_b = (kept_b[2:] + came_b.astype(jnp.float32)).astype(jnp.bfloat16)
+    norm_grads = norm_grads + along_line(norm_grads, 1)
+    near_a, near_b, pass_a, pass_b, line, norm_grads = lax.optimization_barrier(
+        (near_a, near_b, pass_a, pass_b, line, norm_grads)
+    )
+    far_a, far_b = along_y(pass_a), along_x(pass_b)
+    line = line_hop(partial, here, 2, line)
+    norm_grads = norm_grads + along_line(norm_grads, 2)
     small = jnp.concatenate(
         [
-            jnp.sum(grad_projected.astype(jnp.float32), axis=0),
-            grad_expand_bias[0],
+            small[0],
+            small[1],
             norm_grads.reshape(-1),
-            bias_grad,
-            bias_grad,
+            small[2],
+            small[2],
             jnp.zeros((8 * D - 3 * local_width - 7 * D,), jnp.float32),
         ]
     ).reshape(LANES, LANES)
-    for move in (across, along_x, along_y):
-        small = small + move(small)
-
+
+    small = small + across(small)
+    total_a = kept_a[:2] + near_a.astype(jnp.float32)
+    total_b = kept_b[:2] + near_b.astype(jnp.float32)
+
+    far_a, far_b, line, small, total_a, total_b = lax.optimization_barrier(
+        (far_a, far_b, line, small, total_a, total_b)
+    )
+    total_a = total_a + far_a.astype(jnp.float32)
+    total_b = total_b + far_b.astype(jnp.float32)
+    pieces = [total_a[0], total_b[0], across(total_a[1]), across(total_b[1])]
+    small = small + along_x(small)
+    small = small + along_y(small)
+    line = line_hop(partial, here, 3, line)
     step_value = step_count[0].astype(jnp.float32)
     scalars = jnp.stack(
         [
@@ -1211,6 +1342,16 @@
     state = [v.reshape(FLAT, LANES) for v in (master, moment_one, moment_two, average)]
     table = jnp.stack([buckets[0], core.astype(jnp.int32)])
     results = adam(table, scalars, rates, pieces, small, state)
+    line, results = order(line, results)
+    scaled = line_block(partial, here) + (
+        line[0].astype(jnp.float32) + line[1].astype(jnp.float32)
+    )
+    grad_own = cotangent[0].astype(jnp.float32)
+    input_grad = grad_own + own_scale * (
+        scaled
+        - jnp.mean(scaled, axis=-1, keepdims=True)
+        - own_unit * jnp.mean(scaled * own_unit, axis=-1, keepdims=True)
+    )
     return (output[None], input_grad[None], *[v.reshape(master.shape) for v in results])
 
 

time: 720 us -> 579 us (0.80)
  waiting for transfers between devices: 290 us -> 184 us
  starting transfers between devices: 84.6 us -> 43.9 us
  Pallas kernels: 175 us -> 208 us
  local copies, waits for them, and re-layouts: 45.4 us -> 21.7 us
  matrix products: 50.6 us -> 38 us
  between operations: 4.79 us -> 16.8 us
    ppermute x30 -> x8, waiting for transfers between devices: 136 us -> 27.6 us  [the longest x3 27.6 us: line_hop(): lax.ppermute(up.astype(jnp.bfloat16), 'tensor', ups)]
    ppermute x30 -> x8, starting transfers between devices: 61.9 us -> 16 us  [the longest x3 12.2 us: line_hop(): lax.ppermute(up.astype(jnp.bfloat16), 'tensor', ups)]
    all_gather x0 -> x2, waiting for transfers between devices: none -> 32.9 us  [the longest x1 32.9 us: on_device_fast(): full_rows = lax.all_gather(residual[0], 'tensor', axis=0, tiled=True)]
    unnamed x210 -> x87, local copies, waits for them, and re-layouts: 34.6 us -> 4.78 us
    pallas_call x11, Pallas kernels: 117 us -> 143 us  [the longest x1 45.8 us: weight_grads(): pl.pallas_call(weight_grad_kernel, out_shape=[short, short, jax.ShapeDtyp...]
    ppermute x9 -> x10, waiting for transfers between devices: 65.9 us -> 40.1 us  [along_y(): return lax.ppermute(value, 'dp', [(i, i ^ 2) for i in range(4)])]
    dot_general x3 -> x1, matrix products: 30.7 us -> 5.52 us  [product_back(): lax.dot_general(left, right, (((1,), (1,)), ((), ())), preferred_element_...]
    ppermute x9 -> x10, waiting for transfers between devices: 88.3 us -> 73.7 us  [along_x(): return lax.ppermute(value, 'dp', [(i, i ^ 1) for i in range(4)])]
  transfers between devices with their start and end apart: 73 -> 56, of which waited for: 21 -> 17; matrix products, arithmetic and copies ran while one was open for 17% -> 19% of each run, Pallas kernels for 21% -> 36%
where the time goes in v2:
time: 579 us; the launch traced here: 573 us
  Pallas kernels  208 us (36%)
  waiting for transfers between devices  184 us (32%)
  other arithmetic  60.8 us (11%)
  starting transfers between devices  43.9 us (8%)
  matrix products  38 us (7%)
  local copies, waits for them, and re-layouts  21.7 us (4%)
  between operations  16.8 us (3%)
    ppermute x10, waiting for transfers between devices, along_x(): return lax.ppermute(value, 'dp', [(i, i ^ 1) for i in range(4)])  73.7 us
    pallas_call x1, Pallas kernels, weight_grads(): pl.pallas_call(weight_grad_kernel, out_shape=[short, short, jax.ShapeDtyp...  45.8 us
    ppermute x10, waiting for transfers between devices, along_y(): return lax.ppermute(value, 'dp', [(i, i ^ 2) for i in range(4)])  40.1 us
    all_gather x1, waiting for transfers between devices, on_device_fast(): full_rows = lax.all_gather(residual[0], 'tensor', axis=0, tiled=True)  32.9 us
    dot_general x3, matrix products, matmul(): return jnp.dot(left, right, preferred_element_type=jnp.float32)  32.4 us
    pallas_call x1, Pallas kernels, adam(): pl.pallas_call(adam_kernel, grid=(steps,), out_shape=[jax.ShapeDtypeStruc...  28.9 us
    ppermute x3, waiting for transfers between devices, line_hop(): lax.ppermute(up.astype(jnp.bfloat16), 'tensor', ups)  27.6 us
    pallas_call x4, Pallas kernels, unpack(): pl.pallas_call(functools.partial(unpack_kernel, part), out_shape=shapes i...  27.1 us
  transfers between devices with their start and end apart: 56, of which 17 were waited for; matrix products, arithmetic and copies ran while one was open for 19% of the time, Pallas kernels for 36%

profile of v2, /device:TPU:0, one launch (start us, length us, event | category | flops | bytes accessed | tf_op | source)
XLA Modules:
  0.0 573.1 jit_solution(9939347619606077328)
XLA Ops:
  9.6 6.5 %pack_params.1 = (bf16[3328,128]{1,0:T(8,128)(2,1)}, bf16[3072,128]{1,0:T(8,128)(2,1)}, bf16[3072,128]{1,0:T(8,128)(2,1)}, bf16[3072,128]{1,0:T(8,128)(2,1)}) custom-call(s32[1]{0:T(128)} %bitcast.130, f32[12304,128]{1,0:T(8,128)} %bitcast.108), custom_call_target="tpu_custom_call" | custom-call | tf_op jit(solution)/shard_map/pack_params/pallas_call | solution.py:416
  16.1 3.8 collective-permute-start.1
  20.0 2.0 collective-permute-start.2
  22.1 16.6 %collective-permute-done.1.refs_1_ = bf16[3072,128]{1,0:T(8,128)(2,1)} collective-permute-done((bf16[3072,128]{1,0:T(8,128)(2,1)}, bf16[3072,128]{1,0:T(8,128)(2,1)}, u32[]{:S(2)}, u32[]{:S(2)}) %collective-permute-start.1) | collective-permute-done | bytes 786464 | tf_op jit(solution)/shard_map/ppermute | solution.py:1098
  38.6 19.0 %collective-permute-done.3.refs_2_ = bf16[3072,128]{1,0:T(8,128)(2,1)} collective-permute-done((bf16[3072,128]{1,0:T(8,128)(2,1)}, bf16[3072,128]{1,0:T(8,128)(2,1)}, u32[]{:S(2)}, u32[]{:S(2)}) %collective-permute-start.3) | collective-permute-done | bytes 786464 | tf_op jit(solution)/shard_map/ppermute | solution.py:1102
  58.5 1.7 collective-permute-start.7
  60.2 32.9 %all-gather.5.cloned.1.call-done = bf16[1,1024,2048]{2,1,0:T(8,128)(2,1)} async-done(((bf16[1,256,2048]{2,1,0:T(8,128)(2,1)}), bf16[1,1024,2048]{2,1,0:T(8,128)(2,1)}) %all-gather.5.cloned.1.call-update) | async-done | bytes 4194320 | tf_op jit(solution)/shard_map/all_gather | solution.py:1165
  93.6 1.5 collective-permute-start.6
  95.7 8.5 %collective-permute-done.9.refs_5_ = bf16[3072,128]{1,0:T(8,128)(2,1)} collective-permute-done((bf16[3072,128]{1,0:T(8,128)(2,1)}, bf16[3072,128]{1,0:T(8,128)(2,1)}, u32[]{:S(2)}, u32[]{:S(2)}) %collective-permute-start.9) | collective-permute-done | bytes 786464 | tf_op jit(solution)/shard_map/ppermute | solution.py:1110
  104.1 10.4 %collective-permute-done.6.refs_3_ = bf16[3328,128]{1,0:T(8,128)(2,1)} collective-permute-done((bf16[3328,128]{1,0:T(8,128)(2,1)S(1)}, bf16[3328,128]{1,0:T(8,128)(2,1)}, u32[]{:S(2)}, u32[]{:S(2)}) %collective-permute-start.6) | collective-permute-done | bytes 852000 | tf_op jit(solution)/shard_map/ppermute | solution.py:1098
  116.5 1.6 collective-permute-start.12
  118.0 1.5 collective-permute-start.14
  120.1 7.1 %unpack_params.4 = (bf16[2048,1536]{1,0:T(8,128)(2,1)}, bf16[512,2048]{1,0:T(8,128)(2,1)}, bf16[2048,2048]{1,0:T(8,128)(2,1)}, bf16[2048,2048]{1,0:T(8,128)(2,1)...) custom-call(s32[8]{0:T(128)} %select_reduce_fusion.3.bucket_ref, bf16[3328,128]{1,0:T(8,128)(2,1)} %get-tuple-element.139.refs_0_, ...), custom_call_target="tpu_custom_call" | custom-call | tf_op jit(solution)/shard_map/unpack_params/pallas_call | solution.py:533
  128.6 6.7 %unpack_params.5 = (bf16[2048,1536]{1,0:T(8,128)(2,1)}, bf16[512,2048]{1,0:T(8,128)(2,1)}, bf16[2048,2048]{1,0:T(8,128)(2,1)}, bf16[2048,2048]{1,0:T(8,128)(2,1)}) custom-call(s32[8]{0:T(128)} %select_reduce_fusion.3.bucket_ref, ...), custom_call_target="tpu_custom_call", output_to_operand_aliasing={{0}: (10, {}), {1}: (11, {}), {2}: (12, {}), {3}: (13, {})} | custom-call | tf_op jit(solution)/shard_map/unpack_params/pallas_call | solution.py:533
  135.9 3.2 convert_reduce_fusion.1
  140.5 12.7 %collective-permute-done.13.refs_1_ = bf16[3072,128]{1,0:T(8,128)(2,1)} collective-permute-done((bf16[3072,128]{1,0:T(8,128)(2,1)}, bf16[3072,128]{1,0:T(8,128)(2,1)}, u32[]{:S(2)}, u32[]{:S(2)}) %collective-permute-start.13) | collective-permute-done | bytes 786464 | tf_op jit(solution)/shard_map/ppermute | solution.py:1098
  153.2 5.1 fusion.11
  158.3 1.6 collective-permute-start.22
  160.1 1.5 collective-permute-start.21
  161.6 2.8 convert_reduce_fusion
  165.0 3.4 fusion.16
  168.4 11.8 %collective-permute-done.21.refs_3_ = bf16[3072,128]{1,0:T(8,128)(2,1)} collective-permute-done((bf16[3072,128]{1,0:T(8,128)(2,1)}, bf16[3072,128]{1,0:T(8,128)(2,1)}, u32[]{:S(2)}, u32[]{:S(2)}) %collective-permute-start.21) | collective-permute-done | bytes 786464 | tf_op jit(solution)/shard_map/ppermute | solution.py:1098
  180.2 10.2 %hidden_layer.2 = (bf16[1024,2048]{1,0:T(8,128)(2,1)}, f32[1024,2048]{1,0:T(8,128)}) custom-call(bf16[1024,2048]{1,0:T(8,128)(2,1)} %get-tuple-element.172.normed.refs_4_, bf16[2048,2048]{1,0:T(8,128)(2,1)} %get-tuple-element.192.up.refs_11_, f32[1,2048]{1,0:T(1,128)} %bitcast.124), custom_call_target="tpu_custom_call" | custom-call | tf_op jit(solution)/shard_map/hidden_layer/pallas_call | solution.py:911
  190.4 6.3 %fusion.15 = (bf16[1024,2048]{1,0:T(8,128)(2,1)}, bf16[1024,2048]{1,0:T(8,128)(2,1)}) fusion(bf16[1024,2048]{1,0:T(8,128)(2,1)} %collective-permute-done.20, f32[1024]{0:T(1024)S(1)} %add_rsqrt_fusion, f32[1024]{0:T(1024)S(1)} %broadcast_multiply_fusion, f32[2048]{0:T(1024)S(1)} %get-tuple-element.299, f32[2048]{0:T(1024)S(1)} %get-tuple-element.300, ...), kind=kLoop, calls=%fused_computation.19 | loop fusion | flops 18874368 | bytes 12623872 | tf_op jit(solution)/shard_map/convert_element_type | solution.py:1180
  197.3 1.9 multiply_sine_fusion
  202.2 3.1 dynamic-slice_bitcast_fusion
  205.8 6.7 %unpack_params.6 = (bf16[2048,1536]{1,0:T(8,128)(2,1)}, bf16[512,2048]{1,0:T(8,128)(2,1)}, bf16[2048,2048]{1,0:T(8,128)(2,1)}, bf16[2048,2048]{1,0:T(8,128)(2,1)}) custom-call(s32[8]{0:T(128)} %select_reduce_fusion.3.bucket_ref, ...), custom_call_target="tpu_custom_call", output_to_operand_aliasing={{0}: (10, {}), {1}: (11, {}), {2}: (12, {}), {3}: (13, {})} | custom-call | tf_op jit(solution)/shard_map/unpack_params/pallas_call | solution.py:533
  213.4 6.7 %unpack_params.7 = (bf16[2048,1536]{1,0:T(8,128)(2,1)}, bf16[512,2048]{1,0:T(8,128)(2,1)}, bf16[2048,2048]{1,0:T(8,128)(2,1)}, bf16[2048,2048]{1,0:T(8,128)(2,1)}) custom-call(s32[8]{0:T(128)} %select_reduce_fusion.3.bucket_ref, ...), custom_call_target="tpu_custom_call", output_to_operand_aliasing={{0}: (10, {}), {1}: (11, {}), {2}: (12, {}), {3}: (13, {})} | custom-call | tf_op jit(solution)/shard_map/unpack_params/pallas_call | solution.py:533
  220.1 10.6 %hidden_layer.3 = (bf16[1024,2048]{1,0:T(8,128)(2,1)}, f32[1024,2048]{1,0:T(8,128)}) custom-call(bf16[1024,2048]{1,0:T(8,128)(2,1)} %get-tuple-element.172.normed.refs_4_, bf16[2048,2048]{1,0:T(8,128)(2,1)} %get-tuple-element.201.up.own_up.rest_up, f32[1,2048]{1,0:T(1,128)} %bitcast.125, ...), custom_call_target="tpu_custom_call", output_to_operand_aliasing={{0}: (3, {}), {1}: (4, {})} | custom-call | tf_op jit(solution)/shard_map/hidden_layer/pallas_call | solution.py:911
  230.8 12.0 %fusion.38.projected = f32[1024,1536]{1,0:T(8,128)} fusion(bf16[1024,2048]{1,0:T(8,128)(2,1)} %get-tuple-element.167.refs_0_, bf16[2048,1536]{1,0:T(8,128)(2,1)} %get-tuple-element.198.mixer_in), kind=kOutput, calls=%fused_computation.119 | convolution fusion | flops 6442450944 | bytes 16777216 | tf_op jit(solution)/shard_map/dot_general | solution.py:27
  242.8 11.1 %fusion.39 = f32[1024,2048]{1,0:T(8,128)} fusion(bf16[1024,2048]{1,0:T(8,128)(2,1)S(1)} %copy-done.5, bf16[2048,2048]{1,0:T(8,128)(2,1)S(1)} %copy-done), kind=kOutput, calls=%fused_computation.120 | convolution fusion | flops 8589934592 | bytes 20971520 | tf_op jit(solution)/shard_map/dot_general | solution.py:27
  253.9 18.1 %attend.1 = (bf16[1024,512]{1,0:T(8,128)(2,1)}, bf16[1024,1536]{1,0:T(8,128)(2,1)}, f32[4,1024,1]{2,1,0:T(8,128)}) custom-call(f32[1024,1536]{1,0:T(8,128)} %fusion.38.projected, f32[1,1536]{1,0:T(1,128)} %broadcast_in_dim.46.bias, f32[1024,128]{1,0:T(8,128)} %maximum_maximum_fusion.plain, f32[1024,128]{1,0:T(8,128)} %get-tuple-element.295.lower, ...), custom_call_target="tpu_custom_call" | custom-call | tf_op jit(solution)/shard_map/attend/pallas_call | solution.py:1019
  271.9 9.3 %convolution_add_fusion = f32[1024,2048]{1,0:T(8,128)} fusion(f32[1024,2048]{1,0:T(8,128)} %fusion.39, bf16[1024,512]{1,0:T(8,128)(2,1)} %get-tuple-element.199.refs_2_, bf16[512,2048]{1,0:T(8,128)(2,1)S(1)} %copy-done.3), kind=kOutput, calls=%fused_computation.24 | convolution fusion | flops 2149580800 | bytes 19922944 | tf_op jit(solution)/shard_map/dot_general | solution.py:27
  281.3 5.5 fusion.33.grad_context
  286.8 18.3 %attend_back.1.refs_8_.grad_projected = bf16[1024,1536]{1,0:T(8,128)(2,1)} custom-call(bf16[1024,1536]{1,0:T(8,128)(2,1)} %get-tuple-element.208.turned, f32[4,1024,1]{2,1,0:T(8,128)} %get-tuple-element.209.logs, f32[1024,128]{1,0:T(8,128)} %maximum_maximum_fusion.plain, f32[1024,128]{1,0:T(8,128)} %get-tuple-element.295.lower, ...), custom_call_target="tpu_custom_call" | custom-call | tf_op jit(solution)/shard_map/attend_back/pallas_call | solution.py:1072
  305.1 2.7 constant_dynamic-slice_fusion
  307.8 9.5 %hidden_back.3 = (bf16[1024,1024]{1,0:T(8,128)(2,1)}, f32[1,1024]{1,0:T(1,128)}) custom-call(s32[1]{0:T(128)S(6)} %sub.104.half, bf16[1024,2048]{1,0:T(8,128)(2,1)} %bitcast.103, bf16[2048,2048]{1,0:T(8,128)(2,1)} %get-tuple-element.205.down, f32[1024,2048]{1,0:T(8,128)} %get-tuple-element.211.slope), custom_call_target="tpu_custom_call" | custom-call | tf_op jit(solution)/shard_map/hidden_back/pallas_call | solution.py:940
  319.0 9.5 %hidden_back.2 = (bf16[1024,1024]{1,0:T(8,128)(2,1)}, f32[1,1024]{1,0:T(1,128)}) custom-call(s32[1]{0:T(128)} %bitcast.18.half.core, bf16[1024,2048]{1,0:T(8,128)(2,1)} %bitcast.104, bf16[2048,2048]{1,0:T(8,128)(2,1)} %get-tuple-element.205.down, f32[1024,2048]{1,0:T(8,128)} %get-tuple-element.211.slope), custom_call_target="tpu_custom_call" | custom-call | tf_op jit(solution)/shard_map/hidden_back/pallas_call | solution.py:940
  329.9 45.8 %weight_grads.1 = (bf16[2,3136,128]{2,1,0:T(8,128)(2,1)}, bf16[2,3136,128]{2,1,0:T(8,128)(2,1)}, f32[4,3136,128]{2,1,0:T(8,128)}, bf16[2,3136,128]{2,1,0:T(8,128...) custom-call(s32[33]{0:T(128)} %concatenate.24.table, bf16[1024,2048]{1,0:T(8,128)(2,1)} %get-tuple-element.167.refs_0_, ...), custom_call_target="tpu_custom_call" | custom-call | tf_op jit(solution)/shard_map/weight_grads/pallas_call | solution.py:701
  375.7 1.7 collective-permute-start.34
  380.5 2.9 convert_reduce_fusion.2
  383.5 24.0 %norm_grad.1 = (f32[1024,2048]{1,0:T(8,128)}, f32[4,2048]{1,0:T(4,128)}) custom-call(s32[1]{0:T(128)} %bitcast.18.half.core, bf16[1024,1536]{1,0:T(8,128)(2,1)} %attend_back.1.refs_8_.grad_projected, bf16[2048,1536]{1,0:T(8,128)(2,1)} %get-tuple-element.198.mixer_in, bf16[1024,1024]{1,0:T(8,128)(2,1)} %get-tuple-element.226.refs_12_.own_before, ...), custom_call_target="tpu_custom_call" | custom-call | tf_op jit(solution)/shard_map/norm_grad/pallas_call | solution.py:746
  408.0 5.4 collective-permute-done.34
  414.7 2.7 dynamic-slice_convert_fusion
  417.4 4.2 collective-permute-start.38
  423.3 2.8 add_convert_fusion
  426.1 2.0 add_convert_fusion.1
  428.2 15.7 %collective-permute-done.38 = bf16[256,2048]{1,0:T(8,128)(2,1)S(1)} collective-permute-done((bf16[256,2048]{1,0:T(8,128)(2,1)S(1)}, bf16[256,2048]{1,0:T(8,128)(2,1)S(1)}, u32[]{:S(2)}, u32[]{:S(2)}) %collective-permute-start.38) | collective-permute-done | bytes 1048608 | tf_op jit(solution)/shard_map/ppermute | solution.py:1125
  443.9 14.2 %collective-permute-done.36 = bf16[2,3136,128]{2,1,0:T(8,128)(2,1)S(1)} collective-permute-done((bf16[2,3136,128]{2,1,0:T(8,128)(2,1)}, bf16[2,3136,128]{2,1,0:T(8,128)(2,1)S(1)}, u32[]{:S(2)}, u32[]{:S(2)}) %collective-permute-start.36) | collective-permute-done | bytes 1605664 | tf_op jit(solution)/shard_map/ppermute | solution.py:1098
  458.6 2.0 add_convert_fusion.4
  460.6 4.8 collective-permute-start.43
  465.5 1.7 collective-permute-start.44
  469.2 2.6 convert_add_fusion.2
  472.7 11.8 %collective-permute-done.43 = bf16[256,2048]{1,0:T(8,128)(2,1)} collective-permute-done((bf16[256,2048]{1,0:T(8,128)(2,1)}, bf16[256,2048]{1,0:T(8,128)(2,1)}, u32[]{:S(2)}, u32[]{:S(2)}) %collective-permute-start.43) | collective-permute-done | bytes 1048608 | tf_op jit(solution)/shard_map/ppermute | solution.py:1125
  484.5 16.5 %collective-permute-done.41 = bf16[2,3136,128]{2,1,0:T(8,128)(2,1)S(1)} collective-permute-done((bf16[2,3136,128]{2,1,0:T(8,128)(2,1)S(1)}, bf16[2,3136,128]{2,1,0:T(8,128)(2,1)S(1)}, u32[]{:S(2)}, u32[]{:S(2)}) %collective-permute-start.41) | collective-permute-done | bytes 1605664 | tf_op jit(solution)/shard_map/ppermute | solution.py:1102
  502.1 1.7 convert_add_fusion
  506.2 1.9 slice_bitcast_fusion.1
  508.1 4.9 add_convert_fusion.2
  513.0 3.1 collective-permute-start.47
  522.1 2.4 collective-permute-done.51
  525.8 3.0 collective-permute-done.52
  529.4 28.9 %adam.1 = (f32[12304,128]{1,0:T(8,128)}, f32[12304,128]{1,0:T(8,128)}, f32[12304,128]{1,0:T(8,128)}, f32[12304,128]{1,0:T(8,128)}, f32[12304,128]{1,0:T(8,128)}) custom-call(s32[2]{0:T(128)} %pad_add_fusion.table, f32[4]{0:T(128)} %pad_maximum_fusion.1.scalar_ref, f32[8]{0:T(128)} %rate_ref.1, f32[3136,128]{1,0:T(8,128)} %get-tuple-element.291.refs_0_, ...), custom_call_target="tpu_custom_call" | custom-call | tf_op jit(solution)/shard_map/adam/pallas_call | solution.py:877
  558.3 3.0 fusion.36
  561.4 5.0 fusion.28
  (228 shorter events, 38.5 us)
Async XLA Ops:
  7.2 85.9 %all-gather.5.cloned.1.call-start = ((), (), s32[]{:S(2)}) async-start(), calls=%async_computation.2 | async-start | bytes 5242880 | tf_op jit(solution)/shard_map/all_gather | solution.py:1165
  7.9 194.3 %all-gather.7.cloned.1.call-start = ((), (), s32[]{:S(2)}) async-start(), calls=%async_computation.3 | async-start | bytes 5242880 | tf_op jit(solution)/shard_map/all_gather | solution.py:1166
  9.6 105.6 %copy-start.33 = (s32[1,5]{1,0:T(1,128)S(1)}, s32[1,5]{1,0:T(1,128)}, u32[]{:S(2)}) copy-start(s32[1,5]{1,0:T(1,128)} %param.14) | copy-start | bytes 64
  16.1 22.5 %collective-permute-start.1 = (bf16[3072,128]{1,0:T(8,128)(2,1)}, bf16[3072,128]{1,0:T(8,128)(2,1)}, u32[]{:S(2)}, u32[]{:S(2)}) collective-permute-start(bf16[3072,128]{1,0:T(8,128)(2,1)} %get-tuple-element.140.refs_0_), channel_id=1, source_target_pairs={{0,8},{8,0},{16,24},{24,16},{1,9},{9,1},{17,25},{25,17},{2,10},{10... | collective-permute-start | bytes 2359304 | tf_op jit(solution)/shard_map/ppermute | solution.py:1098
  19.9 37.7 %collective-permute-start = (bf16[3328,128]{1,0:T(8,128)(2,1)}, bf16[3328,128]{1,0:T(8,128)(2,1)S(1)}, u32[]{:S(2)}, u32[]{:S(2)}) collective-permute-start(bf16[3328,128]{1,0:T(8,128)(2,1)} %get-tuple-element.139.refs_0_), channel_id=1, source_target_pairs={{0,8},{8,0},{16,24},{24,16},{1,9},{9,1},{17,25},{25,17},{2,10},{10... | collective-permute-start | bytes 2555912 | tf_op jit(solution)/shard_map/ppermute | solution.py:1098
  20.0 37.6 %collective-permute-start.2 = (bf16[3328,128]{1,0:T(8,128)(2,1)}, bf16[3328,128]{1,0:T(8,128)(2,1)S(1)}, u32[]{:S(2)}, u32[]{:S(2)}) collective-permute-start(bf16[3328,128]{1,0:T(8,128)(2,1)} %get-tuple-element.139.refs_0_), channel_id=1, source_target_pairs={{0,16},{8,24},{16,0},{24,8},{1,17},{9,25},{17,1},{25,9},{2,18},{10... | collective-permute-start | bytes 2555912 | tf_op jit(solution)/shard_map/ppermute | solution.py:1102
  22.0 35.7 %collective-permute-start.4 = (bf16[3328,128]{1,0:T(8,128)(2,1)}, bf16[3328,128]{1,0:T(8,128)(2,1)S(1)}, u32[]{:S(2)}, u32[]{:S(2)}) collective-permute-start(bf16[3328,128]{1,0:T(8,128)(2,1)} %get-tuple-element.139.refs_0_), channel_id=1, source_target_pairs={{0,1},{1,0},{2,3},{3,2},{4,5},{5,4},{6,7},{7,6},{8,9},{9,8},{10,11... | collective-permute-start | bytes 2555912 | tf_op jit(solution)/shard_map/ppermute | solution.py:1110
  22.0 35.6 %collective-permute-start.3 = (bf16[3072,128]{1,0:T(8,128)(2,1)}, bf16[3072,128]{1,0:T(8,128)(2,1)}, u32[]{:S(2)}, u32[]{:S(2)}) collective-permute-start(bf16[3072,128]{1,0:T(8,128)(2,1)} %get-tuple-element.140.refs_0_), channel_id=1, source_target_pairs={{0,16},{8,24},{16,0},{24,8},{1,17},{9,25},{17,1},{25,9},{2,18},{10... | collective-permute-start | bytes 2359304 | tf_op jit(solution)/shard_map/ppermute | solution.py:1102
  38.6 19.0 %collective-permute-start.5 = (bf16[3072,128]{1,0:T(8,128)(2,1)}, bf16[3072,128]{1,0:T(8,128)(2,1)S(1)}, u32[]{:S(2)}, u32[]{:S(2)}) collective-permute-start(bf16[3072,128]{1,0:T(8,128)(2,1)} %get-tuple-element.140.refs_0_), channel_id=1, source_target_pairs={{0,1},{1,0},{2,3},{3,2},{4,5},{5,4},{6,7},{7,6},{8,9},{9,8},{10,11... | collective-permute-start | bytes 2359304 | tf_op jit(solution)/shard_map/ppermute | solution.py:1110
  57.6 62.4 %copy-start.12 = (bf16[3328,128]{1,0:T(8,128)(2,1)}, bf16[3328,128]{1,0:T(8,128)(2,1)S(1)}, u32[]{:S(2)}) copy-start(bf16[3328,128]{1,0:T(8,128)(2,1)S(1)} %collective-permute-done.refs_1_) | copy-start | bytes 2555908
  57.7 62.4 %copy-start.13 = (bf16[3328,128]{1,0:T(8,128)(2,1)}, bf16[3328,128]{1,0:T(8,128)(2,1)S(1)}, u32[]{:S(2)}) copy-start(bf16[3328,128]{1,0:T(8,128)(2,1)S(1)} %collective-permute-done.2.refs_2_) | copy-start | bytes 2555908
  58.5 61.6 %copy-start.14 = (bf16[3328,128]{1,0:T(8,128)(2,1)}, bf16[3328,128]{1,0:T(8,128)(2,1)S(1)}, u32[]{:S(2)}) copy-start(bf16[3328,128]{1,0:T(8,128)(2,1)S(1)} %collective-permute-done.4.refs_4_) | copy-start | bytes 2555908
  58.5 36.6 %collective-permute-start.11 = (bf16[3072,128]{1,0:T(8,128)(2,1)}, bf16[3072,128]{1,0:T(8,128)(2,1)}, u32[]{:S(2)}, u32[]{:S(2)}) collective-permute-start(bf16[3072,128]{1,0:T(8,128)(2,1)} %collective-permute-done.3.refs_2_), channel_id=1, source_target_pairs={{0,1},{1,0},{2,3},{3,2},{4,5},{5,4},{6,7},{7,6},{8,9},{9,8},{10,11... | collective-permute-start | bytes 2359304 | tf_op jit(solution)/shard_map/ppermute | solution.py:1110
  58.5 36.6 %collective-permute-start.7 = (bf16[3072,128]{1,0:T(8,128)(2,1)}, bf16[3072,128]{1,0:T(8,128)(2,1)}, u32[]{:S(2)}, u32[]{:S(2)}) collective-permute-start(bf16[3072,128]{1,0:T(8,128)(2,1)} %collective-permute-done.1.refs_1_), channel_id=1, source_target_pairs={{0,16},{8,24},{16,0},{24,8},{1,17},{9,25},{17,1},{25,9},{2,18},{10... | collective-permute-start | bytes 2359304 | tf_op jit(solution)/shard_map/ppermute | solution.py:1102
  93.1 65.3 %collective-permute-start.20 = (bf16[1024,2048]{1,0:T(8,128)(2,1)}, bf16[1024,2048]{1,0:T(8,128)(2,1)}, u32[]{:S(2)}, u32[]{:S(2)}) collective-permute-start(bf16[1024,2048]{1,0:T(8,128)(2,1)} %bitcast.106), channel_id=1, source_target_pairs={{0,1},{1,0},{2,3},{3,2},{4,5},{5,4},{6,7},{7,6},{8,9},{9,8},{10,11... | collective-permute-start | bytes 12582920 | tf_op jit(solution)/shard_map/ppermute | solution.py:1110
  93.1 11.1 %collective-permute-start.10 = (bf16[3328,128]{1,0:T(8,128)(2,1)S(1)}, bf16[3328,128]{1,0:T(8,128)(2,1)S(1)}, u32[]{:S(2)}, u32[]{:S(2)}) collective-permute-start(bf16[3328,128]{1,0:T(8,128)(2,1)S(1)} %collective-permute-done.2.refs_2_), channel_id=1, source_target_pairs={{0,1},{1,0},{2,3},{3,2},{4,5},{5,4},{6,7},{7,6},{8,9},{9,8},{10,11... | collective-permute-start | bytes 2555912 | tf_op jit(solution)/shard_map/ppermute | solution.py:1110
  93.6 21.0 %collective-permute-start.6 = (bf16[3328,128]{1,0:T(8,128)(2,1)S(1)}, bf16[3328,128]{1,0:T(8,128)(2,1)}, u32[]{:S(2)}, u32[]{:S(2)}) collective-permute-start(bf16[3328,128]{1,0:T(8,128)(2,1)S(1)} %collective-permute-done.2.refs_2_), channel_id=1, source_target_pairs={{0,8},{8,0},{16,24},{24,16},{1,9},{9,1},{17,25},{25,17},{2,10},{10... | collective-permute-start | bytes 2555912 | tf_op jit(solution)/shard_map/ppermute | solution.py:1098
  95.1 19.4 %collective-permute-start.8 = (bf16[3328,128]{1,0:T(8,128)(2,1)S(1)}, bf16[3328,128]{1,0:T(8,128)(2,1)}, u32[]{:S(2)}, u32[]{:S(2)}) collective-permute-start(bf16[3328,128]{1,0:T(8,128)(2,1)S(1)} %collective-permute-done.refs_1_), channel_id=1, source_target_pairs={{0,1},{1,0},{2,3},{3,2},{4,5},{5,4},{6,7},{7,6},{8,9},{9,8},{10,11... | collective-permute-start | bytes 2555912 | tf_op jit(solution)/shard_map/ppermute | solution.py:1110
  95.1 9.0 %collective-permute-start.9 = (bf16[3072,128]{1,0:T(8,128)(2,1)}, bf16[3072,128]{1,0:T(8,128)(2,1)}, u32[]{:S(2)}, u32[]{:S(2)}) collective-permute-start(bf16[3072,128]{1,0:T(8,128)(2,1)} %collective-permute-done.1.refs_1_), channel_id=1, source_target_pairs={{0,1},{1,0},{2,3},{3,2},{4,5},{5,4},{6,7},{7,6},{8,9},{9,8},{10,11... | collective-permute-start | bytes 2359304 | tf_op jit(solution)/shard_map/ppermute | solution.py:1110
  95.6 465.8 %reduce-scatter.2.cloned.1.call-start = ((), (), s32[]{:S(2)}) async-start(), calls=%async_computation.1 | async-start | bytes 10485760 | tf_op jit(solution)/shard_map/reduce_scatter | solution.py:1247
  114.5 5.0 collective-permute-start.19
  114.7 13.3 %collective-permute-start.18 = (bf16[3072,128]{1,0:T(8,128)(2,1)}, bf16[3072,128]{1,0:T(8,128)(2,1)}, u32[]{:S(2)}, u32[]{:S(2)}) collective-permute-start(bf16[3072,128]{1,0:T(8,128)(2,1)} %collective-permute-done.7.refs_3_), channel_id=1, source_target_pairs={{0,1},{1,0},{2,3},{3,2},{4,5},{5,4},{6,7},{7,6},{8,9},{9,8},{10,11... | collective-permute-start | bytes 2359304 | tf_op jit(solution)/shard_map/ppermute | solution.py:1110
  116.5 23.9 %collective-permute-start.12 = (bf16[3072,128]{1,0:T(8,128)(2,1)}, bf16[3072,128]{1,0:T(8,128)(2,1)}, u32[]{:S(2)}, u32[]{:S(2)}) collective-permute-start(bf16[3072,128]{1,0:T(8,128)(2,1)} %get-tuple-element.147.refs_0_), channel_id=1, source_target_pairs={{0,8},{8,0},{16,24},{24,16},{1,9},{9,1},{17,25},{25,17},{2,10},{10... | collective-permute-start | bytes 2359304 | tf_op jit(solution)/shard_map/ppermute | solution.py:1098
  118.0 40.2 %collective-permute-start.14 = (bf16[3072,128]{1,0:T(8,128)(2,1)}, bf16[3072,128]{1,0:T(8,128)(2,1)}, u32[]{:S(2)}, u32[]{:S(2)}) collective-permute-start(bf16[3072,128]{1,0:T(8,128)(2,1)} %get-tuple-element.147.refs_0_), channel_id=1, source_target_pairs={{0,16},{8,24},{16,0},{24,8},{1,17},{9,25},{17,1},{25,9},{2,18},{10... | collective-permute-start | bytes 2359304 | tf_op jit(solution)/shard_map/ppermute | solution.py:1102
  119.5 33.6 %collective-permute-start.13 = (bf16[3072,128]{1,0:T(8,128)(2,1)}, bf16[3072,128]{1,0:T(8,128)(2,1)}, u32[]{:S(2)}, u32[]{:S(2)}) collective-permute-start(bf16[3072,128]{1,0:T(8,128)(2,1)} %get-tuple-element.148.refs_0_), channel_id=1, source_target_pairs={{0,8},{8,0},{16,24},{24,16},{1,9},{9,1},{17,25},{25,17},{2,10},{10... | collective-permute-start | bytes 2359304 | tf_op jit(solution)/shard_map/ppermute | solution.py:1098
  128.0 30.3 %collective-permute-start.15 = (bf16[3072,128]{1,0:T(8,128)(2,1)}, bf16[3072,128]{1,0:T(8,128)(2,1)S(1)}, u32[]{:S(2)}, u32[]{:S(2)}) collective-permute-start(bf16[3072,128]{1,0:T(8,128)(2,1)} %get-tuple-element.148.refs_0_), channel_id=1, source_target_pairs={{0,16},{8,24},{16,0},{24,8},{1,17},{9,25},{17,1},{25,9},{2,18},{10... | collective-permute-start | bytes 2359304 | tf_op jit(solution)/shard_map/ppermute | solution.py:1102
  140.4 17.9 %collective-permute-start.16 = (bf16[3072,128]{1,0:T(8,128)(2,1)S(1)}, bf16[3072,128]{1,0:T(8,128)(2,1)S(1)}, u32[]{:S(2)}, u32[]{:S(2)}) collective-permute-start(bf16[3072,128]{1,0:T(8,128)(2,1)S(1)} %copy-done.17), channel_id=1, source_target_pairs={{0,1},{1,0},{2,3},{3,2},{4,5},{5,4},{6,7},{7,6},{8,9},{9,8},{10,11... | collective-permute-start | bytes 2359304 | tf_op jit(solution)/shard_map/ppermute | solution.py:1110
  153.2 5.1 collective-permute-start.17
  158.3 38.3 %collective-permute-start.22 = (bf16[3072,128]{1,0:T(8,128)(2,1)}, bf16[3072,128]{1,0:T(8,128)(2,1)S(1)}, u32[]{:S(2)}, u32[]{:S(2)}) collective-permute-start(bf16[3072,128]{1,0:T(8,128)(2,1)} %collective-permute-done.13.refs_1_), channel_id=1, source_target_pairs={{0,16},{8,24},{16,0},{24,8},{1,17},{9,25},{17,1},{25,9},{2,18},{10... | collective-permute-start | bytes 2359304 | tf_op jit(solution)/shard_map/ppermute | solution.py:1102
  159.9 36.7 %collective-permute-start.24 = (bf16[3072,128]{1,0:T(8,128)(2,1)}, bf16[3072,128]{1,0:T(8,128)(2,1)S(1)}, u32[]{:S(2)}, u32[]{:S(2)}) collective-permute-start(bf16[3072,128]{1,0:T(8,128)(2,1)} %collective-permute-done.13.refs_1_), channel_id=1, source_target_pairs={{0,1},{1,0},{2,3},{3,2},{4,5},{5,4},{6,7},{7,6},{8,9},{9,8},{10,11... | collective-permute-start | bytes 2359304 | tf_op jit(solution)/shard_map/ppermute | solution.py:1110
  160.1 20.1 %collective-permute-start.21 = (bf16[3072,128]{1,0:T(8,128)(2,1)}, bf16[3072,128]{1,0:T(8,128)(2,1)}, u32[]{:S(2)}, u32[]{:S(2)}) collective-permute-start(bf16[3072,128]{1,0:T(8,128)(2,1)} %collective-permute-done.14.refs_2_), channel_id=1, source_target_pairs={{0,8},{8,0},{16,24},{24,16},{1,9},{9,1},{17,25},{25,17},{2,10},{10... | collective-permute-start | bytes 2359304 | tf_op jit(solution)/shard_map/ppermute | solution.py:1098
  161.6 35.1 %collective-permute-start.25 = (bf16[3072,128]{1,0:T(8,128)(2,1)}, bf16[3072,128]{1,0:T(8,128)(2,1)}, u32[]{:S(2)}, u32[]{:S(2)}) collective-permute-start(bf16[3072,128]{1,0:T(8,128)(2,1)} %collective-permute-done.14.refs_2_), channel_id=1, source_target_pairs={{0,1},{1,0},{2,3},{3,2},{4,5},{5,4},{6,7},{7,6},{8,9},{9,8},{10,11... | collective-permute-start | bytes 2359304 | tf_op jit(solution)/shard_map/ppermute | solution.py:1110
  164.4 32.2 %collective-permute-start.23 = (bf16[3072,128]{1,0:T(8,128)(2,1)}, bf16[3072,128]{1,0:T(8,128)(2,1)}, u32[]{:S(2)}, u32[]{:S(2)}) collective-permute-start(bf16[3072,128]{1,0:T(8,128)(2,1)} %collective-permute-done.12.refs_1_), channel_id=1, source_target_pairs={{0,1},{1,0},{2,3},{3,2},{4,5},{5,4},{6,7},{7,6},{8,9},{9,8},{10,11... | collective-permute-start | bytes 2359304 | tf_op jit(solution)/shard_map/ppermute | solution.py:1110
  180.2 16.5 %collective-permute-start.26 = (bf16[3072,128]{1,0:T(8,128)(2,1)S(1)}, bf16[3072,128]{1,0:T(8,128)(2,1)S(1)}, u32[]{:S(2)}, u32[]{:S(2)}) collective-permute-start(bf16[3072,128]{1,0:T(8,128)(2,1)S(1)} %collective-permute-done.15.refs_2_), channel_id=1, source_target_pairs={{0,1},{1,0},{2,3},{3,2},{4,5},{5,4},{6,7},{7,6},{8,9},{9,8},{10,11... | collective-permute-start | bytes 2359304 | tf_op jit(solution)/shard_map/ppermute | solution.py:1110
  196.7 9.1 %collective-permute-start.28 = (bf16[3072,128]{1,0:T(8,128)(2,1)}, bf16[3072,128]{1,0:T(8,128)(2,1)}, u32[]{:S(2)}, u32[]{:S(2)}) collective-permute-start(bf16[3072,128]{1,0:T(8,128)(2,1)} %collective-permute-done.21.refs_3_), channel_id=1, source_target_pairs={{0,1},{1,0},{2,3},{3,2},{4,5},{5,4},{6,7},{7,6},{8,9},{9,8},{10,11... | collective-permute-start | bytes 2359304 | tf_op jit(solution)/shard_map/ppermute | solution.py:1110
  197.3 15.2 %collective-permute-start.27 = (bf16[3072,128]{1,0:T(8,128)(2,1)S(1)}, bf16[3072,128]{1,0:T(8,128)(2,1)S(1)}, u32[]{:S(2)}, u32[]{:S(2)}) collective-permute-start(bf16[3072,128]{1,0:T(8,128)(2,1)S(1)} %collective-permute-done.22.refs_3_), channel_id=1, source_target_pairs={{0,1},{1,0},{2,3},{3,2},{4,5},{5,4},{6,7},{7,6},{8,9},{9,8},{10,11... | collective-permute-start | bytes 2359304 | tf_op jit(solution)/shard_map/ppermute | solution.py:1110
  205.3 123.3 %collective-permute-start.32 = (bf16[1024,1024]{1,0:T(8,128)(2,1)}, bf16[1024,1024]{1,0:T(8,128)(2,1)}, u32[]{:S(2)}, u32[]{:S(2)}) collective-permute-start(bf16[1024,1024]{1,0:T(8,128)(2,1)} %dynamic-slice_bitcast_fusion), channel_id=1, source_target_pairs={{0,1},{1,0},{2,3},{3,2},{4,5},{5,4},{6,7},{7,6},{8,9},{9,8},{10,11... | collective-permute-start | bytes 6291464 | tf_op jit(solution)/shard_map/ppermute | solution.py:1110
  230.7 97.9 %collective-permute-start.30 = (bf16[1024,2048]{1,0:T(8,128)(2,1)}, bf16[1024,2048]{1,0:T(8,128)(2,1)}, u32[]{:S(2)}, u32[]{:S(2)}) collective-permute-start(bf16[1024,2048]{1,0:T(8,128)(2,1)} %get-tuple-element.204.refs_6_), channel_id=1, source_target_pairs={{0,1},{1,0},{2,3},{3,2},{4,5},{5,4},{6,7},{7,6},{8,9},{9,8},{10,11... | collective-permute-start | bytes 12582920 | tf_op jit(solution)/shard_map/ppermute | solution.py:1110
  317.3 11.3 %collective-permute-start.33 = (bf16[1024,1024]{1,0:T(8,128)(2,1)}, bf16[1024,1024]{1,0:T(8,128)(2,1)S(1)}, u32[]{:S(2)}, u32[]{:S(2)}) collective-permute-start(bf16[1024,1024]{1,0:T(8,128)(2,1)} %get-tuple-element.227.rest_before), channel_id=1, source_target_pairs={{0,1},{1,0},{2,3},{3,2},{4,5},{5,4},{6,7},{7,6},{8,9},{9,8},{10,11... | collective-permute-start | bytes 6291464 | tf_op jit(solution)/shard_map/ppermute | solution.py:1110
  317.7 10.9 %collective-permute-start.31 = (bf16[1024,768]{1,0:T(8,128)(2,1)}, bf16[1024,768]{1,0:T(8,128)(2,1)}, u32[]{:S(2)}, u32[]{:S(2)}) collective-permute-start(bf16[1024,768]{1,0:T(8,128)(2,1)} %constant_dynamic-slice_fusion), channel_id=1, source_target_pairs={{0,1},{1,0},{2,3},{3,2},{4,5},{5,4},{6,7},{7,6},{8,9},{9,8},{10,11... | collective-permute-start | bytes 4718600 | tf_op jit(solution)/shard_map/ppermute | solution.py:1110
  317.8 10.7 %collective-permute-start.29 = (bf16[1024,512]{1,0:T(8,128)(2,1)S(1)}, bf16[1024,512]{1,0:T(8,128)(2,1)}, u32[]{:S(2)}, u32[]{:S(2)}) collective-permute-start(bf16[1024,512]{1,0:T(8,128)(2,1)S(1)} %copy-done.6), channel_id=1, source_target_pairs={{0,1},{1,0},{2,3},{3,2},{4,5},{5,4},{6,7},{7,6},{8,9},{9,8},{10,11... | collective-permute-start | bytes 3145736 | tf_op jit(solution)/shard_map/ppermute | solution.py:1110
  375.7 37.7 %collective-permute-start.34 = (bf16[2,3136,128]{2,1,0:T(8,128)(2,1)}, bf16[2,3136,128]{2,1,0:T(8,128)(2,1)}, u32[]{:S(2)}, u32[]{:S(2)}) collective-permute-start(bf16[2,3136,128]{2,1,0:T(8,128)(2,1)} %get-tuple-element.223), channel_id=1, source_target_pairs={{0,8},{8,0},{16,24},{24,16},{1,9},{9,1},{17,25},{25,17},{2,10},{10... | collective-permute-start | bytes 4816904 | tf_op jit(solution)/shard_map/ppermute | solution.py:1098
  377.5 37.2 %collective-permute-start.35 = (bf16[2,3136,128]{2,1,0:T(8,128)(2,1)}, bf16[2,3136,128]{2,1,0:T(8,128)(2,1)}, u32[]{:S(2)}, u32[]{:S(2)}) collective-permute-start(bf16[2,3136,128]{2,1,0:T(8,128)(2,1)} %get-tuple-element.224), channel_id=1, source_target_pairs={{0,16},{8,24},{16,0},{24,8},{1,17},{9,25},{17,1},{25,9},{2,18},{10... | collective-permute-start | bytes 4816904 | tf_op jit(solution)/shard_map/ppermute | solution.py:1102
  414.7 13.5 %collective-permute-start.40 = (f32[4,2048]{1,0:T(4,128)}, f32[4,2048]{1,0:T(4,128)S(1)}, u32[]{:S(2)}, u32[]{:S(2)}) collective-permute-start(f32[4,2048]{1,0:T(4,128)} %get-tuple-element.241), channel_id=1, source_target_pairs={{0,2},{2,0},{4,6},{6,4},{1,3},{3,1},{5,7},{7,5},{8,10},{10,8},{12,... | collective-permute-start | bytes 98312 | tf_op jit(solution)/shard_map/ppermute | solution.py:1106
  414.7 43.9 %slice-start = ((s8[8388608]{0:T(1024)(128)(4,1)}), s8[4194304]{0:T(1024)(128)(4,1)S(1)}, s32[]{:S(2)}) async-start(s8[8388608]{0:T(1024)(128)(4,1)} %bitcast.110), calls=%async_computation.4 | async-start | bytes 8388608
  417.4 26.6 %collective-permute-start.38 = (bf16[256,2048]{1,0:T(8,128)(2,1)S(1)}, bf16[256,2048]{1,0:T(8,128)(2,1)S(1)}, u32[]{:S(2)}, u32[]{:S(2)}) collective-permute-start(bf16[256,2048]{1,0:T(8,128)(2,1)S(1)} %get-tuple-element.283), channel_id=1, source_target_pairs={{0,2},{1,3},{8,10},{9,11},{16,18},{17,19},{24,26},{25,27}} | collective-permute-start | bytes 3145736 | tf_op jit(solution)/shard_map/ppermute | solution.py:1125
  421.6 37.0 %slice-start.1 = ((s8[8388608]{0:T(1024)(128)(4,1)}), s8[4194304]{0:T(1024)(128)(4,1)S(1)}, s32[]{:S(2)}) async-start(s8[8388608]{0:T(1024)(128)(4,1)} %bitcast.110), calls=%async_computation.5 | async-start | bytes 8388608
  421.6 22.4 %collective-permute-start.39 = (bf16[256,2048]{1,0:T(8,128)(2,1)S(1)}, bf16[256,2048]{1,0:T(8,128)(2,1)S(1)}, u32[]{:S(2)}, u32[]{:S(2)}) collective-permute-start(bf16[256,2048]{1,0:T(8,128)(2,1)S(1)} %get-tuple-element.282), channel_id=1, source_target_pairs={{6,4},{7,5},{14,12},{15,13},{22,20},{23,21},{30,28},{31,29}} | collective-permute-start | bytes 3145736 | tf_op jit(solution)/shard_map/ppermute | solution.py:1126
  422.5 35.7 %collective-permute-start.36 = (bf16[2,3136,128]{2,1,0:T(8,128)(2,1)}, bf16[2,3136,128]{2,1,0:T(8,128)(2,1)S(1)}, u32[]{:S(2)}, u32[]{:S(2)}) collective-permute-start(bf16[2,3136,128]{2,1,0:T(8,128)(2,1)} %get-tuple-element.235), channel_id=1, source_target_pairs={{0,8},{8,0},{16,24},{24,16},{1,9},{9,1},{17,25},{25,17},{2,10},{10... | collective-permute-start | bytes 4816904 | tf_op jit(solution)/shard_map/ppermute | solution.py:1098
  423.0 35.5 %collective-permute-start.37 = (bf16[2,3136,128]{2,1,0:T(8,128)(2,1)}, bf16[2,3136,128]{2,1,0:T(8,128)(2,1)S(1)}, u32[]{:S(2)}, u32[]{:S(2)}) collective-permute-start(bf16[2,3136,128]{2,1,0:T(8,128)(2,1)} %get-tuple-element.236), channel_id=1, source_target_pairs={{0,16},{8,24},{16,0},{24,8},{1,17},{9,25},{17,1},{25,9},{2,18},{10... | collective-permute-start | bytes 4816904 | tf_op jit(solution)/shard_map/ppermute | solution.py:1102
  426.1 43.0 %slice-start.4 = ((s8[6422528]{0:T(1024)(128)(4,1)}), s8[4194304]{0:T(1024)(128)(4,1)S(1)}, s32[]{:S(2)}) async-start(s8[6422528]{0:T(1024)(128)(4,1)} %bitcast.114), calls=%async_computation.8 | async-start | bytes 8388608
  428.2 41.0 %slice-start.5 = ((s8[6422528]{0:T(1024)(128)(4,1)}), s8[2228224]{0:T(1024)(128)(4,1)S(1)}, s32[]{:S(2)}) async-start(s8[6422528]{0:T(1024)(128)(4,1)} %bitcast.114), calls=%async_computation.9 | async-start | bytes 4456448
  458.5 10.4 %collective-permute-start.45 = (f32[4,2048]{1,0:T(4,128)S(1)}, f32[4,2048]{1,0:T(4,128)S(1)}, u32[]{:S(2)}, u32[]{:S(2)}) collective-permute-start(f32[4,2048]{1,0:T(4,128)S(1)} %add.286), channel_id=1, source_target_pairs={{0,4},{2,6},{4,0},{6,2},{1,5},{3,7},{5,1},{7,3},{8,12},{10,14},{12... | collective-permute-start | bytes 98312 | tf_op jit(solution)/shard_map/ppermute | solution.py:1106
  460.6 23.9 %collective-permute-start.43 = (bf16[256,2048]{1,0:T(8,128)(2,1)}, bf16[256,2048]{1,0:T(8,128)(2,1)}, u32[]{:S(2)}, u32[]{:S(2)}) collective-permute-start(bf16[256,2048]{1,0:T(8,128)(2,1)} %get-tuple-element.281), channel_id=1, source_target_pairs={{0,2},{2,4},{1,3},{3,5},{8,10},{10,12},{9,11},{11,13},{16,18},{18,... | collective-permute-start | bytes 3145736 | tf_op jit(solution)/shard_map/ppermute | solution.py:1125
  465.5 19.0 %collective-permute-start.44 = (bf16[256,2048]{1,0:T(8,128)(2,1)}, bf16[256,2048]{1,0:T(8,128)(2,1)}, u32[]{:S(2)}, u32[]{:S(2)}) collective-permute-start(bf16[256,2048]{1,0:T(8,128)(2,1)} %get-tuple-element.280), channel_id=1, source_target_pairs={{4,2},{6,4},{5,3},{7,5},{12,10},{14,12},{13,11},{15,13},{20,18},{2... | collective-permute-start | bytes 3145736 | tf_op jit(solution)/shard_map/ppermute | solution.py:1126
  467.1 33.9 %collective-permute-start.41 = (bf16[2,3136,128]{2,1,0:T(8,128)(2,1)S(1)}, bf16[2,3136,128]{2,1,0:T(8,128)(2,1)S(1)}, u32[]{:S(2)}, u32[]{:S(2)}) collective-permute-start(bf16[2,3136,128]{2,1,0:T(8,128)(2,1)S(1)} %add_convert_fusion.1), channel_id=1, source_target_pairs={{0,16},{8,24},{16,0},{24,8},{1,17},{9,25},{17,1},{25,9},{2,18},{10... | collective-permute-start | bytes 4816904 | tf_op jit(solution)/shard_map/ppermute | solution.py:1102
  467.5 33.7 %collective-permute-start.42 = (bf16[2,3136,128]{2,1,0:T(8,128)(2,1)S(1)}, bf16[2,3136,128]{2,1,0:T(8,128)(2,1)}, u32[]{:S(2)}, u32[]{:S(2)}) collective-permute-start(bf16[2,3136,128]{2,1,0:T(8,128)(2,1)S(1)} %add_convert_fusion), channel_id=1, source_target_pairs={{0,8},{8,0},{16,24},{24,16},{1,9},{9,1},{17,25},{25,17},{2,10},{10... | collective-permute-start | bytes 4816904 | tf_op jit(solution)/shard_map/ppermute | solution.py:1098
  469.1 2.7 collective-permute-start.46
  505.3 24.2 %collective-permute-start.50 = (f32[3136,128]{1,0:T(8,128)S(1)}, f32[3136,128]{1,0:T(8,128)}, u32[]{:S(2)}, u32[]{:S(2)}) collective-permute-start(f32[3136,128]{1,0:T(8,128)S(1)} %get-tuple-element.288), channel_id=1, source_target_pairs={{0,1},{1,0},{2,3},{3,2},{4,5},{5,4},{6,7},{7,6},{8,9},{9,8},{10,11... | collective-permute-start | bytes 4816904 | tf_op jit(solution)/shard_map/ppermute | solution.py:1110
  508.1 21.3 %collective-permute-start.49 = (f32[3136,128]{1,0:T(8,128)}, f32[3136,128]{1,0:T(8,128)}, u32[]{:S(2)}, u32[]{:S(2)}) collective-permute-start(f32[3136,128]{1,0:T(8,128)} %get-tuple-element.290), channel_id=1, source_target_pairs={{0,1},{1,0},{2,3},{3,2},{4,5},{5,4},{6,7},{7,6},{8,9},{9,8},{10,11... | collective-permute-start | bytes 4816904 | tf_op jit(solution)/shard_map/ppermute | solution.py:1110
  513.0 45.3 %collective-permute-start.47 = (bf16[256,2048]{1,0:T(8,128)(2,1)}, bf16[256,2048]{1,0:T(8,128)(2,1)}, u32[]{:S(2)}, u32[]{:S(2)}) collective-permute-start(bf16[256,2048]{1,0:T(8,128)(2,1)} %get-tuple-element.279), channel_id=1, source_target_pairs={{0,2},{2,4},{4,6},{1,3},{3,5},{5,7},{8,10},{10,12},{12,14},{9,11},... | collective-permute-start | bytes 3145736 | tf_op jit(solution)/shard_map/ppermute | solution.py:1125
  516.2 42.1 %collective-permute-start.48 = (bf16[256,2048]{1,0:T(8,128)(2,1)}, bf16[256,2048]{1,0:T(8,128)(2,1)}, u32[]{:S(2)}, u32[]{:S(2)}) collective-permute-start(bf16[256,2048]{1,0:T(8,128)(2,1)} %get-tuple-element.278), channel_id=1, source_target_pairs={{2,0},{4,2},{6,4},{3,1},{5,3},{7,5},{10,8},{12,10},{14,12},{11,9},... | collective-permute-start | bytes 3145736 | tf_op jit(solution)/shard_map/ppermute | solution.py:1126
  520.1 4.3 collective-permute-start.51
  524.5 4.3 collective-permute-start.52
  (32 other events, 274.6 us)
Sparse Core Ops, SparseCore 0:
  9.6 83.4 all-gather.4
  95.7 78.3 all-gather.6
  281.4 142.8 reduce-scatter.1

commit v3 on v2

--- a/solution.py
+++ b/solution.py
@@ -350,12 +350,20 @@
 HBM = pltpu.HBM
 
 
+LIGHT = pl.CostEstimate(flops=1, bytes_accessed=1, transcendentals=0)
+
+
 def params(limit_mb, **more):
     return pltpu.CompilerParams(vmem_limit_bytes=limit_mb * 1024 * 1024, **more)
 
 
+def part_row(part):
+    rows = (16 // CHUNKS) * BROWS
+    return (0, rows + 16 * TROWS, 0, rows)[part]
+
+
 def pack_kernel(bucket_ref, flat_ref, *refs):
-    outs, padded, sem = refs[:CHUNKS], refs[CHUNKS], refs[CHUNKS + 1]
+    outs, padded, sem = refs[:2], refs[2], refs[3]
     bucket = bucket_ref[0]
     load = pltpu.make_async_copy(flat_ref, padded.at[pl.ds(FRONT, FLAT)], sem)
     load.start()
@@ -372,7 +380,9 @@
         def step(tile, carry):
             row = pl.multiple_of(tile * 16, 16)
             for panel in range(16):
-                outs[panel // wide][pl.ds((panel % wide) * BROWS + row, 16), :] = take(
+                part = panel // wide
+                at = part_row(part) + (panel % wide) * BROWS
+                outs[part // 2][pl.ds(at + row, 16), :] = take(
                     (row - bucket) * 16 + panel + FRONT, 16
                 )
             return carry
@@ -384,26 +394,28 @@
         def step(tile, carry):
             row = pl.multiple_of(tile * 16, 16)
             for panel in range(12):
-                outs[panel // narrow][pl.ds((panel % narrow) * QROWS + row, 16), :] = take(
+                part = panel // narrow
+                at = part_row(part) + (panel % narrow) * QROWS
+                outs[part // 2][pl.ds(at + row, 16), :] = take(
                     row * 12 + panel - 16 * bucket + FRONT, 12
                 )
             return carry
 
         lax.fori_loop(0, QROWS // 16, step, 0)
 
-    main = wide * BROWS
+    tails = wide * BROWS
 
     @pl.when(bucket >= 1)
     def _():
         for panel in range(16):
-            outs[0][pl.ds(main + panel * TROWS, TROWS), :] = take(
+            outs[0][pl.ds(tails + panel * TROWS, TROWS), :] = take(
                 (BROWS - bucket) * 16 + panel + FRONT, 16
             )
 
     @pl.when(bucket == 0)
     def _():
         for panel in range(16):
-            outs[0][pl.ds(main + panel * TROWS, TROWS), :] = take(
+            outs[0][pl.ds(tails + panel * TROWS, TROWS), :] = take(
                 QROWS * 12 + min(panel, 11) + FRONT, 12
             )
 
@@ -413,21 +425,21 @@
 
 
 def pack(bucket, flat):
+    rows = (32 // CHUNKS) * BROWS
     return pl.pallas_call(
         pack_kernel,
         out_shape=[
-            jax.ShapeDtypeStruct(
-                ((16 // CHUNKS) * BROWS + (0 if part else 16 * TROWS), LANES), jnp.bfloat16
-            )
-            for part in range(CHUNKS)
+            jax.ShapeDtypeStruct((rows + 16 * TROWS, LANES), jnp.bfloat16),
+            jax.ShapeDtypeStruct((rows, LANES), jnp.bfloat16),
         ],
         in_specs=[pl.BlockSpec(memory_space=pltpu.SMEM), pl.BlockSpec(memory_space=HBM)],
-        out_specs=[pl.BlockSpec(memory_space=pltpu.VMEM)] * CHUNKS,
+        out_specs=[pl.BlockSpec(memory_space=pltpu.VMEM)] * 2,
         scratch_shapes=[
             pltpu.VMEM((FRONT + FLAT + BACK, LANES), jnp.float32),
             pltpu.SemaphoreType.DMA,
         ],
-        compiler_params=params(60),
+        compiler_params=params(24),
+        cost_estimate=LIGHT,
         name="pack_params",
     )(bucket, flat)
 
@@ -477,7 +489,9 @@
     main = (16 // CHUNKS) * BROWS
     loads = [
         pltpu.make_async_copy(
-            sources[k].at[pl.ds(0, main)], staged.at[bucket_ref[k]], load_sems.at[k]
+            sources[k].at[pl.ds(0 if k % 4 == 3 else part_row(part), main)],
+            staged.at[bucket_ref[k]],
+            load_sems.at[k],
         )
         for k in range(8)
     ]
@@ -545,6 +559,7 @@
             pltpu.SemaphoreType.DMA((copies,)),
         ],
         compiler_params=params(60),
+        cost_estimate=LIGHT,
         name="unpack_params",
     )(buckets, *sources, *((before[5], *before[:4]) if part else ()))
     return [*results, *before[4:]] if part else results
@@ -559,86 +574,131 @@
 
 
 def weight_grad_kernel(table, *refs):
-    lefts, rights, outs = refs[:8], refs[8:14], refs[14:20]
-    wide32, wide16, tail32, tail16, sems, tail_sem = refs[20:]
+    lefts, projected, late, outs = refs[:8], refs[8:10], refs[10:14], refs[14:20]
+    wide32, wide16, tail32, tail16, held, sems, tail_sem, late_sem = refs[20:]
     step = pl.program_id(0)
+    core = table[0]
     main = (16 // CHUNKS) * BROWS
 
     def bucket_of(block):
         return jnp.where(block < 2 * IN_STEPS, block // 4, (block - 2) // 3)
 
-    def target(part, bucket):
-        kind, place = table[1 + 16 * part + bucket], table[9 + 16 * part + bucket]
+    def kind_of(part, bucket):
+        return table[1 + 16 * part + bucket], table[9 + 16 * part + bucket]
+
+    def targets(part, kind, place):
         return [
-            (kind == KEPT, False, outs[3 * part + 2].at[place]),
-            (kind == NEAR, True, outs[3 * part].at[jnp.minimum(place, 1)]),
-            (kind == FAR, True, outs[3 * part + 1].at[jnp.minimum(place, 1)]),
+            (kind == NEAR, True, outs[2 * part].at[jnp.minimum(place, 1)]),
+            (kind == FAR, True, outs[2 * part + 1].at[jnp.minimum(place, 1)]),
+            (jnp.logical_and(kind == KEPT, place >= 2), False, outs[4].at[part, jnp.clip(place - 2, 0, 1)]),
+            (jnp.logical_and(kind == KEPT, place < 2), False, outs[5].at[part, jnp.minimum(place, 1)]),
         ]
 
-    def copies(at, act):
+    def wait(at):
         slot = lax.rem(at, 2)
-        for half in range(2):
-            block = 2 * at + half
-            bucket = bucket_of(block)
-            inner = block < 2 * IN_STEPS
-            for panels, span, mine in ((3, QROWS, inner), (4, BROWS, jnp.logical_not(inner))):
-                offset = pl.multiple_of(
-                    (lax.rem(block, 4) if span == QROWS else lax.rem(block - 2, 3)) * GRAD_ROWS,
-                    GRAD_ROWS,
-                )
-                for part in range(2):
-                    for which, (is_it, short, place) in enumerate(target(part, bucket)):
-
-                        @pl.when(jnp.logical_and(mine, is_it))
-                        def _(
-                            panels=panels, span=span, offset=offset, part=part, short=short,
-                            place=place, half=half,
-                        ):
-                            stage = wide16 if short else wide32
-                            for panel in range(panels):
-                                act(
-                                    pltpu.make_async_copy(
-                                        stage.at[
-                                            slot, part, half, pl.ds(panel * GRAD_ROWS, GRAD_ROWS)
-                                        ],
-                                        place.at[pl.ds(panel * span + offset, GRAD_ROWS)],
-                                        sems.at[slot, part, half, panel],
-                                    )
-                                )
+        for panels, mine in ((3, at < IN_STEPS), (4, at >= IN_STEPS)):
+
+            @pl.when(mine)
+            def _(panels=panels):
+                rows = pl.ds(0, panels * GRAD_ROWS)
+                for half in range(2):
+                    bucket = bucket_of(2 * at + half)
+                    for part in range(2):
+                        kind, _ = kind_of(part, bucket)
+                        sem = sems.at[slot, part, half]
+
+                        @pl.when(kind == KEPT)
+                        def _(part=part, sem=sem):
+                            place = outs[5].at[part, 0, rows]
+                            pltpu.make_async_copy(place, place, sem).wait()
+
+                        @pl.when(kind != KEPT)
+                        def _(part=part, sem=sem):
+                            place = outs[2 * part].at[0, rows]
+                            pltpu.make_async_copy(place, place, sem).wait()
 
     @pl.when(step >= 2)
     def _():
-        copies(step - 2, lambda copy: copy.wait())
+        wait(step - 2)
+
+    late_copies = []
+    for at, source in enumerate(late):
+        width = held.shape[2]
+        if source.shape[1] > width:
+            source = source.at[:, pl.ds(pl.multiple_of(core * width, width), width)]
+        late_copies.append(pltpu.make_async_copy(source, held.at[at], late_sem.at[at]))
 
     @pl.when(step == 0)
     def _():
+        for copy in late_copies:
+            copy.start()
         tail32[...] = jnp.zeros_like(tail32)
         tail16[...] = jnp.zeros_like(tail16)
 
-    def multiply(pair, right, panels):
-        value = product_rows(lefts[2 * pair][...], rights[2 * right][...]) + product_rows(
-            lefts[2 * pair + 1][...], rights[2 * right + 1][...]
-        )
+    @pl.when(step == GRAD_EDGES[1])
+    def _():
+        for copy in late_copies[:2]:
+            copy.wait()
+
+    @pl.when(step == GRAD_EDGES[2])
+    def _():
+        for copy in late_copies[2:]:
+            copy.wait()
+
+    def multiply(pair, right, panels, span):
         slot = lax.rem(step, 2)
+        if right == 0:
+            own, other = projected[0][...], projected[1][...]
+        else:
+            own, other = held[2 * right - 2], held[2 * right - 1]
+        wide32[slot, :, pl.ds(0, 2 * panels * LANES)] = product_rows(
+            lefts[2 * pair][...], own
+        ) + product_rows(lefts[2 * pair + 1][...], other)
         for half in range(2):
             block = 2 * step + half
-            before = jnp.maximum(bucket_of(block) - 1, 0)
-            first = block == 4 if pair == 0 else lax.rem(block - 2, 3) == 0
+            bucket = bucket_of(block)
+            before = jnp.maximum(bucket - 1, 0)
+            if pair == 0:
+                first, offset = block == 4, lax.rem(block, 4)
+            else:
+                offset = lax.rem(block - 2, 3)
+                first = offset == 0
+            offset = pl.multiple_of(offset * GRAD_ROWS, GRAD_ROWS)
             for part in range(2):
-                for panel in range(panels):
-                    left = (part * panels + panel) * LANES
-                    tile = value[half * GRAD_ROWS : (half + 1) * GRAD_ROWS, left : left + LANES]
-                    rows = pl.ds(panel * GRAD_ROWS, GRAD_ROWS)
-                    wide32[slot, part, half, rows, :] = tile
-                    wide16[slot, part, half, rows, :] = tile.astype(jnp.bfloat16)
+                kind, place = kind_of(part, bucket)
+
+                @pl.when(kind != KEPT)
+                def _(half=half, part=part):
+                    for panel in range(panels):
+                        tile = wide32[
+                            slot, pl.ds(half * GRAD_ROWS, GRAD_ROWS), columns(part * panels + panel)
+                        ]
+                        rows = pl.ds(panel * GRAD_ROWS, GRAD_ROWS)
+                        wide16[slot, part, half, rows, :] = tile.astype(jnp.bfloat16)
+
+                for is_it, short, target in targets(part, kind, place):
+
+                    @pl.when(is_it)
+                    def _(half=half, part=part, short=short, target=target, offset=offset):
+                        for panel in range(panels):
+                            if short:
+                                rows = pl.ds(panel * GRAD_ROWS, GRAD_ROWS)
+                                source = wide16.at[slot, part, half, rows]
+                            else:
+                                rows = pl.ds(half * GRAD_ROWS, GRAD_ROWS)
+                                source = wide32.at[slot, rows, columns(part * panels + panel)]
+                            pltpu.make_async_copy(
+                                source,
+                                target.at[pl.ds(panel * span + offset, GRAD_ROWS)],
+                                sems.at[slot, part, half],
+                            ).start()
 
             @pl.when(first)
             def _(half=half, before=before):
                 for part in range(2):
                     for panel in range(panels):
-                        left = (part * panels + panel) * LANES
-                        tile = value[
-                            half * GRAD_ROWS : half * GRAD_ROWS + TROWS, left : left + LANES
+                        tile = wide32[
+                            slot, pl.ds(half * GRAD_ROWS, TROWS), columns(part * panels + panel)
                         ]
                         rows = pl.ds(panel * TROWS, TROWS)
                         tail32[part, before, rows, :] = tile
@@ -648,16 +708,14 @@
 
         @pl.when(jnp.logical_and(step >= GRAD_EDGES[pair], step < GRAD_EDGES[pair + 1]))
         def _(pair=pair, right=right):
-            multiply(pair, right, 3 if pair == 0 else 4)
-
-    copies(step, lambda copy: copy.start())
+            multiply(pair, right, *((3, QROWS) if pair == 0 else (4, BROWS)))
 
     @pl.when(step == GRAD_STEPS - 1)
     def _():
         def tails(act):
             for part in range(2):
                 for bucket in range(8):
-                    for is_it, short, place in target(part, bucket):
+                    for is_it, short, place in targets(part, *kind_of(part, bucket)):
 
                         @pl.when(is_it)
                         def _(part=part, bucket=bucket, short=short, place=place):
@@ -671,8 +729,8 @@
                             )
 
         tails(lambda copy: copy.start())
-        copies(step - 1, lambda copy: copy.wait())
-        copies(step, lambda copy: copy.wait())
+        wait(step - 1)
+        wait(step)
         tails(lambda copy: copy.wait())
 
 
@@ -689,33 +747,35 @@
         for first, last in zip(GRAD_EDGES, GRAD_EDGES[1:], strict=False)
         for _ in range(2)
     ]
-    right_specs = []
-    for own, other in zip(rights[::2], rights[1::2], strict=True):
-        if own.shape == other.shape:
-            right_specs.append(pl.BlockSpec(other.shape, lambda i, table: (0, 0)))
-        else:
-            right_specs.append(pl.BlockSpec(other.shape, lambda i, table: (0, table[0])))
-        right_specs.append(pl.BlockSpec(other.shape, lambda i, table: (0, 0)))
+    projected = rights[1].shape
+    right_specs = [
+        pl.BlockSpec(projected, lambda i, table: (0, table[0])),
+        pl.BlockSpec(projected, lambda i, table: (0, 0)),
+    ]
     rows = chunk_rows()
     short = jax.ShapeDtypeStruct((2, rows, LANES), jnp.bfloat16)
+    wide = jax.ShapeDtypeStruct((2, 2, rows, LANES), jnp.float32)
     return pl.pallas_call(
         weight_grad_kernel,
-        out_shape=[short, short, jax.ShapeDtypeStruct((4, rows, LANES), jnp.float32)] * 2,
+        out_shape=[short] * 4 + [wide] * 2,
         grid_spec=pltpu.PrefetchScalarGridSpec(
             num_scalar_prefetch=1,
             grid=(GRAD_STEPS,),
-            in_specs=left_specs + right_specs,
+            in_specs=left_specs + right_specs + [pl.BlockSpec(memory_space=HBM)] * 4,
             out_specs=[pl.BlockSpec(memory_space=HBM)] * 6,
             scratch_shapes=[
-                pltpu.VMEM((2, 2, 2, 4 * GRAD_ROWS, LANES), jnp.float32),
+                pltpu.VMEM((2, PAIR, 8 * LANES), jnp.float32),
                 pltpu.VMEM((2, 2, 2, 4 * GRAD_ROWS, LANES), jnp.bfloat16),
                 pltpu.VMEM((2, 8, 4 * TROWS, LANES), jnp.float32),
                 pltpu.VMEM((2, 8, 4 * TROWS, LANES), jnp.bfloat16),
-                pltpu.SemaphoreType.DMA((2, 2, 2, 4)),
+                pltpu.VMEM((4, tokens, 8 * LANES), jnp.bfloat16),
+                pltpu.SemaphoreType.DMA((2, 2, 2)),
                 pltpu.SemaphoreType.DMA((2, 8)),
+                pltpu.SemaphoreType.DMA((4,)),
             ],
         ),
         compiler_params=params(60),
+        cost_estimate=LIGHT,
         name="weight_grads",
     )(table, *lefts, *rights)
 
@@ -767,6 +827,7 @@
             out_specs=[block, pl.BlockSpec((4, NORM_COLUMNS), lambda i, core: (0, i))],
         ),
         compiler_params=params(60),
+        cost_estimate=LIGHT,
         name="norm_grad",
     )(core, grad_projected, mixer_in, own_before, up, rest_before, up, rows, centre, scale, gains)
 
@@ -775,58 +836,39 @@
 
 
 def adam_kernel(table, scalar_ref, rate_ref, *refs):
-    pieces, small = refs[:4], refs[4]
-    weights, first, second, moving = refs[5:9]
-    new_weights, new_first, new_second, new_moving, reduced = refs[9:14]
-    held, flat, sems = refs[14:]
+    stays, near, far, small = refs[:2], refs[2:6], refs[6:10], refs[10]
+    weights, first, second, moving = refs[11:15]
+    new_weights, new_first, new_second, new_moving, reduced = refs[15:20]
+    held32, held16, flat, sems = refs[20:]
     bucket, core = table[0], table[1]
     wide, narrow = 16 // CHUNKS, 12 // CHUNKS
     main = wide * BROWS
-
-    @pl.when(pl.program_id(0) == 0)
+    turn_at = pl.program_id(0)
+
+    def put(part, row, start, stride):
+        rows = pl.ds(row, 16)
+        value = held32[part, rows, :] + (
+            held16[0, part, rows, :].astype(jnp.float32) + held16[1, part, rows, :].astype(jnp.float32)
+        )
+        flat[pl.ds(start, 16, stride=stride), :] = value
+
+    @pl.when(turn_at == 0)
     def _():
         loads = []
-        for at, piece in enumerate(pieces):
-            half = core if at < 2 else 1 - core
-            loads.append(
-                pltpu.make_async_copy(piece, held.at[2 * half + at % 2], sems.at[at])
-            )
-            loads[-1].start()
+        for at in range(4):
+            place = 2 * (core if at < 2 else 1 - core) + at % 2
+            source = stays[at // 2].at[at % 2, at // 2]
+            loads.append(pltpu.make_async_copy(source, held32.at[place], sems.at[0, at]))
+            for which, came in enumerate((near, far)):
+                loads.append(
+                    pltpu.make_async_copy(
+                        came[at].at[at // 2], held16.at[which, place], sems.at[1 + which, at]
+                    )
+                )
+        for load in loads:
+            load.start()
         for load in loads:
             load.wait()
-
-        def put(part, row, start, stride):
-            flat[pl.ds(start, 16, stride=stride), :] = held[part, pl.ds(row, 16), :]
-
-        @pl.when(bucket >= 2)
-        def _():
-            def step(tile, carry):
-                row = pl.multiple_of(tile * 16, 16)
-                for panel in range(16):
-                    put(
-                        panel // wide,
-                        (panel % wide) * BROWS + row,
-                        (row - bucket) * 16 + panel + FRONT,
-                        16,
-                    )
-                return carry
-
-            lax.fori_loop(0, BROWS // 16, step, 0)
-
-        @pl.when(bucket < 2)
-        def _():
-            def step(tile, carry):
-                row = pl.multiple_of(tile * 16, 16)
-                for panel in range(12):
-                    put(
-                        panel // narrow,
-                        (panel % narrow) * QROWS + row,
-                        row * 12 + panel - 16 * bucket + FRONT,
-                        12,
-                    )
-                return carry
-
-            lax.fori_loop(0, QROWS // 16, step, 0)
 
         @pl.when(bucket >= 1)
         def _():
@@ -852,26 +894,77 @@
         def _():
             flat[pl.ds(FRONT + FLAT - LANES, LANES), :] = small[...]
 
-    start = pl.program_id(0) * ADAM_ROWS
+    @pl.when(bucket >= 2)
+    def _():
+        def reach(at):
+            return jnp.clip(at * (ADAM_ROWS // 256) + jnp.where(at > 0, 1, 0), 0, BROWS // 16)
+
+        def step(tile, carry):
+            row = pl.multiple_of(tile * 16, 16)
+            for panel in range(16):
+                put(
+                    panel // wide,
+                    (panel % wide) * BROWS + row,
+                    (row - bucket) * 16 + panel + FRONT,
+                    16,
+                )
+            return carry
+
+        lax.fori_loop(reach(turn_at), reach(turn_at + 1), step, 0)
+
+    @pl.when(bucket < 2)
+    def _():
+        def reach(at):
+            tiles = (at * ADAM_ROWS + 16) // 192 + 1
+            return jnp.clip(jnp.where(at > 0, tiles, 0), 0, QROWS // 16)
+
+        def step(tile, carry):
+            row = pl.multiple_of(tile * 16, 16)
+            for panel in range(12):
+                put(
+                    panel // narrow,
+                    (panel % narrow) * QROWS + row,
+                    row * 12 + panel - 16 * bucket + FRONT,
+                    12,
+                )
+            return carry
+
+        lax.fori_loop(reach(turn_at), reach(turn_at + 1), step, 0)
+
+    start = turn_at * ADAM_ROWS
     gradient = flat[pl.ds(pl.multiple_of(FRONT + start, 8), ADAM_ROWS), :]
-    row = bucket * FLAT + start + lax.broadcasted_iota(jnp.int32, (ADAM_ROWS, LANES), 0)
-    rate = jnp.full((ADAM_ROWS, LANES), rate_ref[0], jnp.float32)
-    for kind, bound in enumerate(bound_list(512, 2048)[1:]):
-        rate = jnp.where(row >= bound // LANES, rate_ref[kind + 1], rate)
     reduced[...] = gradient
-    bias_one, bias_two, decay, keep = (scalar_ref[at] for at in range(4))
+    scale_one, scale_two, decay, keep = (scalar_ref[at] for at in range(4))
     one = beta_one * first[...] + (1.0 - beta_one) * gradient
     two = beta_two * second[...] + (1.0 - beta_two) * gradient * gradient
-    old = weights[...]
-    ratio = one / bias_one / (jnp.sqrt(two / bias_two) + adam_epsilon)
-    fresh = old - rate * (ratio + decay * old)
-    new_weights[...] = fresh
     new_first[...] = one
     new_second[...] = two
-    new_moving[...] = keep * moving[...] + (1.0 - keep) * fresh
-
-
-def adam(table, scalars, rates, pieces, small, state):
+    old = weights[...]
+    change = (one * scale_one) / (jnp.sqrt(two * scale_two) + adam_epsilon) + decay * old
+
+    def write(rate):
+        fresh = old - rate * change
+        new_weights[...] = fresh
+        new_moving[...] = keep * moving[...] + (1.0 - keep) * fresh
+
+    first_row = bucket * FLAT + start
+    bounds = [bound // LANES for bound in bound_list(512, 2048)[1:]]
+    kinds = [sum(jnp.where(at >= bound, 1, 0) for bound in bounds) for at in (first_row, first_row + ADAM_ROWS - 1)]
+
+    @pl.when(kinds[0] == kinds[1])
+    def _():
+        write(rate_ref[kinds[0]])
+
+    @pl.when(kinds[0] != kinds[1])
+    def _():
+        row = first_row + lax.broadcasted_iota(jnp.int32, (ADAM_ROWS, LANES), 0)
+        rate = jnp.full((ADAM_ROWS, LANES), rate_ref[0], jnp.float32)
+        for kind, bound in enumerate(bounds):
+            rate = jnp.where(row >= bound, rate_ref[kind + 1], rate)
+        write(rate)
+
+
+def adam(table, scalars, rates, stays, near, far, small, state):
     steps = -(-FLAT // ADAM_ROWS)
     block = pl.BlockSpec((ADAM_ROWS, LANES), lambda i: (i, 0))
     return pl.pallas_call(
@@ -879,18 +972,55 @@
         grid=(steps,),
         out_shape=[jax.ShapeDtypeStruct((FLAT, LANES), jnp.float32)] * 5,
         in_specs=[pl.BlockSpec(memory_space=pltpu.SMEM)] * 3
-        + [pl.BlockSpec(memory_space=HBM)] * 4
+        + [pl.BlockSpec(memory_space=HBM)] * 10
         + [pl.BlockSpec(memory_space=pltpu.VMEM)]
         + [block] * 4,
         out_specs=[block] * 5,
         scratch_shapes=[
             pltpu.VMEM((4, chunk_rows(), LANES), jnp.float32),
+            pltpu.VMEM((2, 4, chunk_rows(), LANES), jnp.bfloat16),
             pltpu.VMEM((FRONT + steps * ADAM_ROWS, LANES), jnp.float32),
-            pltpu.SemaphoreType.DMA((4,)),
+            pltpu.SemaphoreType.DMA((3, 4)),
         ],
-        compiler_params=params(60),
+        compiler_params=params(48),
+        cost_estimate=LIGHT,
         name="adam",
-    )(table, scalars, rates, *pieces, small, *state)
+    )(table, scalars, rates, *stays, *near, *far, small, *state)
+
+
+def finish_kernel(index, partial, up, down, rows, grads, out):
+    scaled = partial[...] + (up[...].astype(jnp.float32) + down[...].astype(jnp.float32))
+    unit, scale = norm_stats(rows[...].astype(jnp.float32))
+    out[...] = grads[...].astype(jnp.float32) + scale * (
+        scaled
+        - jnp.mean(scaled, axis=-1, keepdims=True)
+        - unit * jnp.mean(scaled * unit, axis=-1, keepdims=True)
+    )
+
+
+def finish(index, partial, line, rows, grads):
+    count, width = rows.shape
+    steps = 4
+    block = pl.BlockSpec((count // steps, width), lambda i, index: (i, 0))
+    return pl.pallas_call(
+        finish_kernel,
+        out_shape=jax.ShapeDtypeStruct((count, width), jnp.float32),
+        grid_spec=pltpu.PrefetchScalarGridSpec(
+            num_scalar_prefetch=1,
+            grid=(steps,),
+            in_specs=[
+                pl.BlockSpec((count // steps, width), lambda i, index: (index[0] * steps + i, 0)),
+                block,
+                block,
+                block,
+                block,
+            ],
+            out_specs=block,
+        ),
+        compiler_params=params(24),
+        cost_estimate=LIGHT,
+        name="finish",
+    )(index, partial, *line, rows, grads)
 
 
 FF_BLOCK = 256
@@ -924,6 +1054,7 @@
         out_specs=[block, block],
         input_output_aliases={3 + at: at for at in range(len(before))},
         compiler_params=params(60),
+        cost_estimate=LIGHT,
         name="hidden_layer",
     )(normed, up, up_bias, *before)
 
@@ -957,8 +1088,69 @@
             ],
         ),
         compiler_params=params(60),
+        cost_estimate=LIGHT,
         name="hidden_back",
     )(half, grads, down, slope)
+
+
+def product_kernel(back, *refs):
+    total = None
+    for left, right in zip(refs[:-1:2], refs[1:-1:2], strict=True):
+        value = (product_back if back else matmul)(left[...], right[...])
+        total = value if total is None else total + value
+    refs[-1][...] = total.astype(refs[-1].dtype)
+
+
+def product(pairs, width, dtype, back=False):
+    rows = pairs[0][0].shape[0]
+    count = pairs[0][1].shape[0 if back else 1]
+    specs = []
+    for left, right in pairs:
+        specs.append(pl.BlockSpec(memory_space=pltpu.VMEM))
+        if back:
+            specs.append(pl.BlockSpec((width, right.shape[1]), lambda i: (i, 0)))
+        else:
+            specs.append(pl.BlockSpec((right.shape[0], width), lambda i: (0, i)))
+    return pl.pallas_call(
+        functools.partial(product_kernel, back),
+        grid=(count // width,),
+        out_shape=jax.ShapeDtypeStruct((rows, count), dtype),
+        in_specs=specs,
+        out_specs=pl.BlockSpec((rows, width), lambda i: (0, i)),
+        compiler_params=params(60),
+        cost_estimate=LIGHT,
+        name="product",
+    )(*[value for pair in pairs for value in pair])
+
+
+def norm_kernel(rows, gains, one, two, centre, scale):
+    values = rows[...].astype(jnp.float32)
+    middle = jnp.mean(values, axis=-1, keepdims=True)
+    values = values - middle
+    factor = lax.rsqrt(jnp.mean(values * values, axis=-1, keepdims=True) + norm_epsilon)
+    unit = values * factor
+    one[...] = (unit * gains[0:1, :] + gains[1:2, :]).astype(jnp.bfloat16)
+    two[...] = (unit * gains[2:3, :] + gains[3:4, :]).astype(jnp.bfloat16)
+    centre[...] = middle
+    scale[...] = factor
+
+
+def norms(rows, small_params):
+    count, width = rows.shape
+    height = 128
+    block = pl.BlockSpec((height, width), lambda i: (i, 0))
+    column = pl.BlockSpec((height, 1), lambda i: (i, 0))
+    return pl.pallas_call(
+        norm_kernel,
+        grid=(count // height,),
+        out_shape=[jax.ShapeDtypeStruct((count, width), jnp.bfloat16)] * 2
+        + [jax.ShapeDtypeStruct((count, 1), jnp.float32)] * 2,
+        in_specs=[block, pl.BlockSpec(memory_space=pltpu.VMEM)],
+        out_specs=[block, block, column, column],
+        compiler_params=params(60),
+        cost_estimate=LIGHT,
+        name="norms",
+    )(rows, small_params)
 
 
 QUERY_BLOCK = 256
@@ -974,10 +1166,10 @@
     )
 
 
-def block_scores(query, keys, begins, first):
+def block_scores(query, keys, begins, first, first_key):
     scores = product_back(query, keys) * (1.0 / math.sqrt(HD))
     row_index = first + lax.broadcasted_iota(jnp.int32, scores.shape, 0)
-    key_index = lax.broadcasted_iota(jnp.int32, scores.shape, 1)
+    key_index = first_key + lax.broadcasted_iota(jnp.int32, scores.shape, 1)
     allowed = (key_index <= row_index) & (key_index >= begins)
     return jnp.where(allowed, scores, masked_score)
 
@@ -1001,12 +1193,13 @@
         for first in range(0, rows, QUERY_BLOCK):
             last = first + QUERY_BLOCK
             mine = slice(first, last)
-            scores = block_scores(queries[mine], keys[:last], begins[mine, :], first)
+            seen = slice(max(0, first - rows // 2), last)
+            scores = block_scores(queries[mine], keys[seen], begins[mine, :], first, seen.start)
             top = jnp.max(scores, axis=-1, keepdims=True)
             raised = jnp.exp(scores - top)
             total = jnp.sum(raised, axis=-1, keepdims=True)
             rounded = (raised / total).astype(jnp.bfloat16)
-            context[mine, cols[0]] = matmul(rounded, values[:last]).astype(jnp.bfloat16)
+            context[mine, cols[0]] = matmul(rounded, values[seen]).astype(jnp.bfloat16)
             logs[head, mine, :] = top + jnp.log(total)
         return carry
 
@@ -1026,6 +1219,7 @@
         in_specs=[whole] * 6,
         out_specs=[whole] * 3,
         compiler_params=params(60),
+        cost_estimate=LIGHT,
         name="attend",
     )(projected, bias, *tables, begins)
 
@@ -1045,17 +1239,18 @@
             last = first + QUERY_BLOCK
             mine = slice(first, last)
             query = queries[mine]
-            scores = block_scores(query, keys[:last], begins[mine, :], first)
+            seen = slice(max(0, first - rows // 2), last)
+            scores = block_scores(query, keys[seen], begins[mine, :], first, seen.start)
             soft = jnp.exp(scores - logs[head, mine, :])
             grad_mine = grad_context[mine, cols[0]]
-            grad_soft = product_back(grad_mine, values[:last])
+            grad_soft = product_back(grad_mine, values[seen])
             delta = jnp.sum(soft * grad_soft, axis=-1, keepdims=True)
             grad_scores = (soft * (grad_soft - delta)).astype(jnp.bfloat16)
-            grad_query = matmul(grad_scores, keys[:last]) * score_scale
+            grad_query = matmul(grad_scores, keys[seen]) * score_scale
             tables = (plain[mine, :], lower[mine, :], upper[mine, :])
             grad_projected[mine, cols[0]] = turn(grad_query, tables, -1.0).astype(jnp.bfloat16)
-            key_sum[:last, :] += product_rows(grad_scores, query)
-            value_sum[:last, :] += product_rows(soft.astype(jnp.bfloat16), grad_mine)
+            key_sum[seen, :] += product_rows(grad_scores, query)
+            value_sum[seen, :] += product_rows(soft.astype(jnp.bfloat16), grad_mine)
         tables = (plain[...], lower[...], upper[...])
         grad_projected[:, cols[1]] = turn(key_sum[...] * score_scale, tables, -1.0).astype(
             jnp.bfloat16
@@ -1076,6 +1271,7 @@
         out_specs=whole,
         scratch_shapes=[pltpu.VMEM((rows, HD), jnp.float32)] * 2,
         compiler_params=params(60),
+        cost_estimate=LIGHT,
         name="attend_back",
     )(turned, logs, *tables, begins, grad_context)
 
@@ -1106,6 +1302,12 @@
     return lax.ppermute(value, "tensor", [(i, i ^ bit) for i in range(4)])
 
 
+def along(bit, value):
+    return lax.ppermute(
+        value, ("dp", "chip"), [(i, (i // 2 ^ bit) * 2 + (i % 2 ^ 1)) for i in range(8)]
+    )
+
+
 def across(value):
     return lax.ppermute(value, "chip", [(0, 1), (1, 0)])
 
@@ -1115,16 +1317,17 @@
     return lax.dynamic_slice_in_dim(partial, jnp.clip(index, 0, 3) * rows, rows, 0)
 
 
-def line_hop(partial, here, hop, came):
+def line_leaving(partial, here, hop, came):
     up, down = line_block(partial, here + 4 - hop), line_block(partial, here - 4 + hop)
     if came is not None:
         up = up + came[0].astype(jnp.float32)
         down = down + came[1].astype(jnp.float32)
+    return up.astype(jnp.bfloat16), down.astype(jnp.bfloat16)
+
+
+def line_hop(leaving, hop):
     ups, downs = [(i, i + 1) for i in range(hop)], [(i, i - 1) for i in range(4 - hop, 4)]
-    return (
-        lax.ppermute(up.astype(jnp.bfloat16), "tensor", ups),
-        lax.ppermute(down.astype(jnp.bfloat16), "tensor", downs),
-    )
+    return lax.ppermute(leaving[0], "tensor", ups), lax.ppermute(leaving[1], "tensor", downs)
 
 
 def on_device_fast(
@@ -1165,65 +1368,51 @@
     full_rows = lax.all_gather(residual[0], "tensor", axis=0, tiled=True)
     grad_rows = lax.all_gather(cotangent[0], "tensor", axis=0, tiled=True)
     own_rows = residual[0].astype(jnp.float32)
-    own_unit, own_scale = norm_stats(own_rows)
-
-    def moments(rows):
-        float_rows = rows.astype(jnp.float32)
-        centre = jnp.mean(float_rows, axis=-1, keepdims=True)
-        spread = jnp.mean((float_rows - centre) * (float_rows - centre), axis=-1, keepdims=True)
-        return centre, lax.rsqrt(spread + norm_epsilon)
-
-    def norms(rows, centre, scale, small_params):
-        unit = (rows.astype(jnp.float32) - centre) * scale
-        return (
-            (unit * small_params[0] + small_params[1]).astype(jnp.bfloat16),
-            (unit * small_params[2] + small_params[3]).astype(jnp.bfloat16),
-        )
 
     def order(*values):
         return lax.optimization_barrier(values)
 
-    def both(values, move):
-        return [move(value) for value in values]
-
-    packed = pack(buckets[:1], master.reshape(FLAT, LANES))
-    one, two = packed[:2], packed[2:]
-    one_x, one_y, one_own = order(both(one, along_x), both(one, along_y), both(one, across))
-
-    far = [along_x(one_y[0]), along_y(one_x[1])]
-    near = both([*one_x, *one_y], across)
-    far, near, two = order(far, near, two)
-
-    two_x, two_y, far_other = both(two, along_x), both(two, along_y), both(far, across)
-    two_own = both(two, across)
+    one, two = pack(buckets[:1], master.reshape(FLAT, LANES))
+    one_x, one_y, one_own = order(along_x(one), along_y(one), across(one))
+
+    def from_far(first, second, from_x, from_y):
+        rows = (16 // CHUNKS) * BROWS
+        start = part_row(second)
+        count = start if first == 0 else rows
+        return [along_x(from_y[:count]), along_y(from_x[start : start + rows])]
+
+    far = from_far(0, 1, one_x, one_y)
+    near_x, near_y, two_own = across(one_x), across(one_y), across(two)
+    far, near_x, near_y, two_own, two = order(far, near_x, near_y, two_own, two)
+
+    two_x, two_y = along_x(two), along_y(two)
+    far_other = [across(value) for value in far]
     weights = []
     for part in range(2):
-        sources = [one[part], one_x[part], one_y[part], far[part]]
-        sources += [one_own[part], near[part], near[2 + part], far_other[part]]
+        sources = [one, one_x, one_y, far[part], one_own, near_x, near_y, far_other[part]]
         weights = unpack(part, buckets, sources, weights)
+    weights, full_rows = order(weights, full_rows)
     flat_bias = weights[4][:8].reshape(-1).astype(jnp.float32)
     mixer_bias = flat_bias[: 3 * local_width]
     expand_bias = flat_bias[3 * local_width : 3 * local_width + D]
     small_params = flat_bias[3 * local_width + D : 3 * local_width + 7 * D].reshape(6, D)
-    centre, scale = moments(full_rows)
-    full_one, full_two = norms(full_rows, centre, scale, small_params)
+    full_one, full_two, centre, scale = norms(full_rows, small_params)
+    two_x, two_y, full_rows, full_one, full_two, weights = order(
+        two_x, two_y, full_rows, full_one, full_two, weights
+    )
     other_rows = across(full_rows)
-    two_x, two_y, two_own, weights, full_one, full_two, other_rows = order(
-        two_x, two_y, two_own, weights, full_one, full_two, other_rows
-    )
-
-    far = [along_x(two_y[0]), along_y(two_x[1])]
-    near = both([*two_x, *two_y], across)
+
+    far = from_far(2, 3, two_x, two_y)
+    near_x, near_y = across(two_x), across(two_y)
     hidden_half = hidden_layer(0, full_two, weights[2], expand_bias[None], ())
-    other_one, other_two = norms(other_rows, *moments(other_rows), small_params)
-    far, near, hidden_half, weights, other_one, other_two = order(
-        far, near, hidden_half, weights, other_one, other_two
-    )
-
-    far_other = both(far, across)
+    other_one, other_two, _, _ = norms(other_rows, small_params)
+    far, near_x, near_y, hidden_half, weights, other_one, other_two = order(
+        far, near_x, near_y, hidden_half, weights, other_one, other_two
+    )
+
+    far_other = [across(value) for value in far]
     for part in range(2):
-        sources = [two[part], two_x[part], two_y[part], far[part]]
-        sources += [two_own[part], near[part], near[2 + part], far_other[part]]
+        sources = [two, two_x, two_y, far[part], two_own, near_x, near_y, far_other[part]]
         weights = unpack(2 + part, buckets, sources, weights)
     mixer_in, mixer_out, expand_weight, shrink_weight = weights[:4]
 
@@ -1238,15 +1427,15 @@
     tables = rope_tables((token_index - begins).astype(jnp.float32))
     begins = begins[:, None]
 
-    projected = matmul(full_one, mixer_in)
+    projected = product([(full_one, mixer_in)], 256, jnp.float32)
     context, turned, logs = attend(projected, mixer_bias[None], tables, begins)
     hidden, slope = hidden_layer(1, full_two, expand_weight, expand_bias[None], hidden_half)
     other_context, other_hidden = across(context), across(hidden)
-    branches = matmul(context, mixer_out) + matmul(hidden, shrink_weight)
+    branches = product([(context, mixer_out), (hidden, shrink_weight)], 256, jnp.float32)
     branches, turned = order(branches, turned)
     branches = lax.psum_scatter(branches, "tensor", scatter_dimension=0, tiled=True)
     output = own_rows + branches + small_params[4] + small_params[5]
-    grad_context = product_back(grad_rows, mixer_out).astype(jnp.bfloat16)
+    grad_context = product([(grad_rows, mixer_out)], 256, jnp.bfloat16, back=True)
     grad_projected = attend_back(turned, logs, tables, begins, grad_context)
     half_in = 3 * local_width // 2
     leaves = lax.dynamic_slice_in_dim(grad_projected, (1 - core) * half_in, half_in, 1)
@@ -1270,8 +1459,8 @@
     grad_projected, own_before, rest_before, sums = order(
         grad_projected, own_before, rest_before, sums
     )
-    near_a, far_a, kept_a, near_b, far_b, kept_b = sums
-    came_a, came_b = along_x(far_a), along_y(far_b)
+    near_a, far_a, near_b, far_b, passed, stays = sums
+    came_a, came_b, other_stays = along_x(far_a), along_y(far_b), across(stays)
 
     partial, norm_grads = norm_grad(
         cores,
@@ -1292,20 +1481,17 @@
         bias_grad,
     )
 
-    came_a, came_b, partial, norm_grads, small, near_a, near_b = lax.optimization_barrier(
-        (came_a, came_b, partial, norm_grads, small, near_a, near_b)
+    norm_grads = norm_grads + along_line(norm_grads, 1)
+    leaving = line_leaving(partial, here, 1, None)
+    came_a, came_b, other_stays, partial, leaving, norm_grads, small, near_a, near_b = order(
+        came_a, came_b, other_stays, partial, leaving, norm_grads, small, near_a, near_b
     )
     near_a, near_b = along_x(near_a), along_y(near_b)
-    line = line_hop(partial, here, 1, None)
-    pass_a = (kept_a[2:] + came_a.astype(jnp.float32)).astype(jnp.bfloat16)
-    pass_b = (kept_b[2:] + came_b.astype(jnp.float32)).astype(jnp.bfloat16)
-    norm_grads = norm_grads + along_line(norm_grads, 1)
-    near_a, near_b, pass_a, pass_b, line, norm_grads = lax.optimization_barrier(
-        (near_a, near_b, pass_a, pass_b, line, norm_grads)
-    )
-    far_a, far_b = along_y(pass_a), along_x(pass_b)
-    line = line_hop(partial, here, 2, line)
+    line = line_hop(leaving, 1)
+    pass_a = (passed[0] + came_a.astype(jnp.float32)).astype(jnp.bfloat16)
+    pass_b = (passed[1] + came_b.astype(jnp.float32)).astype(jnp.bfloat16)
     norm_grads = norm_grads + along_line(norm_grads, 2)
+    leaving = line_leaving(partial, here, 2, line)
     small = jnp.concatenate(
         [
             small[0],
@@ -1316,42 +1502,35 @@
             jnp.zeros((8 * D - 3 * local_width - 7 * D,), jnp.float32),
         ]
     ).reshape(LANES, LANES)
-
+    near_a, near_b, pass_a, pass_b, leaving, small, output = order(
+        near_a, near_b, pass_a, pass_b, leaving, small, output
+    )
     small = small + across(small)
-    total_a = kept_a[:2] + near_a.astype(jnp.float32)
-    total_b = kept_b[:2] + near_b.astype(jnp.float32)
-
-    far_a, far_b, line, small, total_a, total_b = lax.optimization_barrier(
-        (far_a, far_b, line, small, total_a, total_b)
-    )
-    total_a = total_a + far_a.astype(jnp.float32)
-    total_b = total_b + far_b.astype(jnp.float32)
-    pieces = [total_a[0], total_b[0], across(total_a[1]), across(total_b[1])]
+    far_a, far_b = along_y(pass_a), along_x(pass_b)
+    line = line_hop(leaving, 2)
+    near = [near_a, near_b, across(near_a), across(near_b)]
+    leaving = line_leaving(partial, here, 3, line)
+
+    far_a, far_b, near, leaving, small = order(far_a, far_b, near, leaving, small)
     small = small + along_x(small)
     small = small + along_y(small)
-    line = line_hop(partial, here, 3, line)
+    far = [far_a, far_b, across(far_a), across(far_b)]
+    line = line_hop(leaving, 3)
+
     step_value = step_count[0].astype(jnp.float32)
     scalars = jnp.stack(
         [
-            1.0 - jnp.power(beta_one, step_value),
-            1.0 - jnp.power(beta_two, step_value),
+            1.0 / (1.0 - jnp.power(beta_one, step_value)),
+            1.0 / (1.0 - jnp.power(beta_two, step_value)),
             weight_decay[0],
             ema_decay[0],
         ]
     )
     state = [v.reshape(FLAT, LANES) for v in (master, moment_one, moment_two, average)]
     table = jnp.stack([buckets[0], core.astype(jnp.int32)])
-    results = adam(table, scalars, rates, pieces, small, state)
+    results = adam(table, scalars, rates, [stays, other_stays], near, far, small, state)
     line, results = order(line, results)
-    scaled = line_block(partial, here) + (
-        line[0].astype(jnp.float32) + line[1].astype(jnp.float32)
-    )
-    grad_own = cotangent[0].astype(jnp.float32)
-    input_grad = grad_own + own_scale * (
-        scaled
-        - jnp.mean(scaled, axis=-1, keepdims=True)
-        - own_unit * jnp.mean(scaled * own_unit, axis=-1, keepdims=True)
-    )
+    input_grad = finish(here[None].astype(jnp.int32), partial, line, residual[0], cotangent[0])
     return (output[None], input_grad[None], *[v.reshape(master.shape) for v in results])
 
 

time: 579 us -> 516 us (0.89)
  waiting for transfers between devices: 184 us -> 124 us
  Pallas kernels: 208 us -> 259 us
  matrix products: 38 us -> 0 us
  other arithmetic: 60.8 us -> 26.1 us
  starting transfers between devices: 43.9 us -> 57.1 us
  local copies, waits for them, and re-layouts: 21.7 us -> 28.9 us
    pallas_call x2 -> x8, Pallas kernels: 52.3 us -> 102 us  [the longest x1 41 us: weight_grads(): pl.pallas_call(weight_grad_kernel, out_shape=[short] * 4 + [wide] * 2, gr...]
    dot_general x4 -> x0, matrix products: 38 us -> none  [the longest x3 32.4 us: matmul(): return jnp.dot(left, right, preferred_element_type=jnp.float32)]
    all_gather x1, waiting for transfers between devices: 32.9 us -> 0.02 us  [on_device_fast(): full_rows = lax.all_gather(residual[0], 'tensor', axis=0, tiled=True)]
    ppermute x10 -> x8, waiting for transfers between devices: 73.7 us -> 48 us  [along_x(): return lax.ppermute(value, 'dp', [(i, i ^ 1) for i in range(4)])]
    reduce_sum x7 -> x0, other arithmetic: 14.3 us -> none  [the longest x2 6 us: moments(): centre = jnp.mean(float_rows, axis=-1, keepdims=True)]
    ppermute x6, starting transfers between devices: 16 us -> 27.7 us  [the longest x3 24 us: line_hop(): lax.ppermute(leaving[0], 'tensor', ups)]
    convert_element_type x6 -> x3, other arithmetic: 23.1 us -> 13 us  [the longest x2 6.86 us: line_leaving(): return (up.astype(jnp.bfloat16), down.astype(jnp.bfloat16))]
    ppermute x6, waiting for transfers between devices: 27.6 us -> 36.7 us  [the longest x3 36.7 us: line_hop(): lax.ppermute(leaving[0], 'tensor', ups)]
  transfers between devices with their start and end apart: 56 -> 49, of which waited for: 17 -> 18; matrix products, arithmetic and copies ran while one was open for 19% -> 8% of each run, Pallas kernels for 36% -> 50%
where the time goes in v3:
time: 516 us; the launch traced here: 512 us
  Pallas kernels  259 us (50%)
  waiting for transfers between devices  124 us (24%)
  starting transfers between devices  57.1 us (11%)
  local copies, waits for them, and re-layouts  28.9 us (6%)
  other arithmetic  26.1 us (5%)
  between operations  16.7 us (3%)
    ppermute x8, waiting for transfers between devices, along_x(): return lax.ppermute(value, 'dp', [(i, i ^ 1) for i in range(4)])  48 us
    pallas_call x1, Pallas kernels, weight_grads(): pl.pallas_call(weight_grad_kernel, out_shape=[short] * 4 + [wide] * 2, gr...  41 us
    ppermute x3, waiting for transfers between devices, line_hop(): lax.ppermute(leaving[0], 'tensor', ups)  36.7 us
    pallas_call x3, Pallas kernels, product(): pl.pallas_call(functools.partial(product_kernel, back), grid=(count // wi...  34.7 us
    ppermute x8, waiting for transfers between devices, along_y(): return lax.ppermute(value, 'dp', [(i, i ^ 2) for i in range(4)])  32.4 us
    pallas_call x1, Pallas kernels, adam(): pl.pallas_call(adam_kernel, grid=(steps,), out_shape=[jax.ShapeDtypeStruc...  30.4 us
    pallas_call x4, Pallas kernels, unpack(): pl.pallas_call(functools.partial(unpack_kernel, part), out_shape=shapes i...  27.3 us
    pallas_call x1, Pallas kernels, norm_grad(): pl.pallas_call(norm_grad_kernel, out_shape=[jax.ShapeDtypeStruct((tokens,...  24.1 us
  transfers between devices with their start and end apart: 49, of which 18 were waited for; matrix products, arithmetic and copies ran while one was open for 8% of the time, Pallas kernels for 50%

profile of v3, /device:TPU:0, one launch (start us, length us, event | category | flops | bytes accessed | tf_op | source)
XLA Modules:
  0.0 511.7 jit_solution(1732375826676148030)
XLA Ops:
  9.0 2.8 copy-done
  11.8 2.7 pack_params.1
  14.5 3.0 collective-permute-start
  17.5 1.5 collective-permute-start.1
  19.0 34.3 %collective-permute-done.refs_1_ = bf16[6400,128]{1,0:T(8,128)(2,1)S(1)} collective-permute-done((bf16[6400,128]{1,0:T(8,128)(2,1)S(1)}, bf16[6400,128]{1,0:T(8,128)(2,1)S(1)}, u32[]{:S(2)}, u32[]{:S(2)}) %collective-permute-start) | collective-permute-done | bytes 1638432 | tf_op jit(solution)/shard_map/ppermute | solution.py:1294
  53.3 1.5 collective-permute-done.1.refs_2_
  57.1 1.6 collective-permute-start.4
  58.7 4.3 collective-permute-done.7.refs_4_
  62.9 13.9 %collective-permute-done.4.refs_3_ = bf16[3072,128]{1,0:T(8,128)(2,1)S(1)} collective-permute-done((bf16[3072,128]{1,0:T(8,128)(2,1)S(1)}, bf16[3072,128]{1,0:T(8,128)(2,1)S(1)}, u32[]{:S(2)}, u32[]{:S(2)}) %collective-permute-start.4) | collective-permute-done | bytes 786464 | tf_op jit(solution)/shard_map/ppermute | solution.py:1298
  80.0 1.5 collective-permute-start.9
  82.2 2.1 collective-permute-done.11.refs_7_
  85.1 7.1 %unpack_params.4 = (bf16[2048,1536]{1,0:T(8,128)(2,1)}, bf16[512,2048]{1,0:T(8,128)(2,1)}, bf16[2048,2048]{1,0:T(8,128)(2,1)}, bf16[2048,2048]{1,0:T(8,128)(2,1)...) custom-call(s32[8]{0:T(128)} %copy-done.7, bf16[6400,128]{1,0:T(8,128)(2,1)} %copy-done.2, ...), custom_call_target="tpu_custom_call" | custom-call | flops 1 | bytes 1 | tf_op jit(solution)/shard_map/unpack_params/pallas_call | solution.py:547
  93.2 6.8 %unpack_params.5 = (bf16[2048,1536]{1,0:T(8,128)(2,1)}, bf16[512,2048]{1,0:T(8,128)(2,1)}, bf16[2048,2048]{1,0:T(8,128)(2,1)}, bf16[2048,2048]{1,0:T(8,128)(2,1)}) custom-call(s32[8]{0:T(128)} %copy-done.7, bf16[6400,128]{1,0:T(8,128)(2,1)} %copy-done.2, ...), custom_call_target="tpu_custom_call", output_to_operand_aliasing={{0}: (10, {}), {1}: (11, {}), {2}: (12, {}), {3}: (13, {})} | custom-call | flops 1 | bytes 1 | tf_op jit(solution)/shard_map/unpack_params/pallas_call | solution.py:547
  100.8 9.7 %norms.2 = (bf16[1024,2048]{1,0:T(8,128)(2,1)}, bf16[1024,2048]{1,0:T(8,128)(2,1)}, f32[1024,1]{1,0:T(8,128)}, f32[1024,1]{1,0:T(8,128)}) custom-call(bf16[1024,2048]{1,0:T(8,128)(2,1)} %bitcast.66, f32[6,2048]{1,0:T(8,128)} %reshape.86.gains), custom_call_target="tpu_custom_call" | custom-call | flops 1 | bytes 1 | tf_op jit(solution)/shard_map/norms/pallas_call | solution.py:1143
  110.4 3.9 collective-permute-done.8.refs_1_
  114.3 1.9 collective-permute-done.9.refs_2_
  116.7 2.1 slice.63
  118.8 2.1 slice.64
  121.3 1.5 collective-permute-start.13
  123.6 10.2 %hidden_layer.2 = (bf16[1024,2048]{1,0:T(8,128)(2,1)}, f32[1024,2048]{1,0:T(8,128)}) custom-call(bf16[1024,2048]{1,0:T(8,128)(2,1)} %get-tuple-element.177.normed.refs_4_, bf16[2048,2048]{1,0:T(8,128)(2,1)} %get-tuple-element.196.up.refs_11_, f32[1,2048]{1,0:T(1,128)} %bitcast.78), custom_call_target="tpu_custom_call" | custom-call | flops 1 | bytes 1 | tf_op jit(solution)/shard_map/hidden_layer/pallas_call | solution.py:1041
  133.9 9.3 %norms.3 = (bf16[1024,2048]{1,0:T(8,128)(2,1)}, bf16[1024,2048]{1,0:T(8,128)(2,1)}, f32[1024,1]{1,0:T(8,128)}, f32[1024,1]{1,0:T(8,128)}) custom-call(bf16[1024,2048]{1,0:T(8,128)(2,1)} %collective-permute-done.16.rows, f32[6,2048]{1,0:T(8,128)} %reshape.86.gains), custom_call_target="tpu_custom_call" | custom-call | flops 1 | bytes 1 | tf_op jit(solution)/shard_map/norms/pallas_call | solution.py:1143
  145.1 1.9 multiply_sine_fusion
  148.0 1.3 maximum_maximum_fusion.2
  150.0 6.7 %unpack_params.6 = (bf16[2048,1536]{1,0:T(8,128)(2,1)}, bf16[512,2048]{1,0:T(8,128)(2,1)}, bf16[2048,2048]{1,0:T(8,128)(2,1)}, bf16[2048,2048]{1,0:T(8,128)(2,1)}) custom-call(s32[8]{0:T(128)} %copy-done.7, bf16[6144,128]{1,0:T(8,128)(2,1)} %copy-done.3, ...), custom_call_target="tpu_custom_call", output_to_operand_aliasing={{0}: (10, {}), {1}: (11, {}), {2}: (12, {}), {3}: (13, {})} | custom-call | flops 1 | bytes 1 | tf_op jit(solution)/shard_map/unpack_params/pallas_call | solution.py:547
  156.7 6.7 %unpack_params.7 = (bf16[2048,1536]{1,0:T(8,128)(2,1)}, bf16[512,2048]{1,0:T(8,128)(2,1)}, bf16[2048,2048]{1,0:T(8,128)(2,1)}, bf16[2048,2048]{1,0:T(8,128)(2,1)}) custom-call(s32[8]{0:T(128)} %copy-done.7, bf16[6144,128]{1,0:T(8,128)(2,1)} %copy-done.3, ...), custom_call_target="tpu_custom_call", output_to_operand_aliasing={{0}: (10, {}), {1}: (11, {}), {2}: (12, {}), {3}: (13, {})} | custom-call | flops 1 | bytes 1 | tf_op jit(solution)/shard_map/unpack_params/pallas_call | solution.py:547
  163.4 11.9 %product.3.projected = f32[1024,1536]{1,0:T(8,128)} custom-call(bf16[1024,2048]{1,0:T(8,128)(2,1)} %get-tuple-element.174.refs_0_, bf16[2048,1536]{1,0:T(8,128)(2,1)} %get-tuple-element.202.refs_1_.mixer_in), custom_call_target="tpu_custom_call" | custom-call | flops 1 | bytes 1 | tf_op jit(solution)/shard_map/product/pallas_call | solution.py:1114
  175.3 10.5 %hidden_layer.3 = (bf16[1024,2048]{1,0:T(8,128)(2,1)}, f32[1024,2048]{1,0:T(8,128)}) custom-call(bf16[1024,2048]{1,0:T(8,128)(2,1)} %get-tuple-element.177.normed.refs_4_, bf16[2048,2048]{1,0:T(8,128)(2,1)} %get-tuple-element.205.up.own_up.rest_up, f32[1,2048]{1,0:T(1,128)} %bitcast.79, ...), custom_call_target="tpu_custom_call", output_to_operand_aliasing={{0}: (3, {}), {1}: (4, {})} | custom-call | flops 1 | bytes 1 | tf_op jit(solution)/shard_map/hidden_layer/pallas_call | solution.py:1041
  185.8 17.3 %attend.1 = (bf16[1024,512]{1,0:T(8,128)(2,1)}, bf16[1024,1536]{1,0:T(8,128)(2,1)}, f32[4,1024,1]{2,1,0:T(8,128)}) custom-call(f32[1024,1536]{1,0:T(8,128)} %product.3.projected, f32[1,1536]{1,0:T(1,128)} %broadcast_in_dim.75.bias, f32[1024,128]{1,0:T(8,128)} %maximum_maximum_fusion.plain, f32[1024,128]{1,0:T(8,128)} %get-tuple-element.296.lower, ...), custom_call_target="tpu_custom_call" | custom-call | flops 1 | bytes 1 | tf_op jit(solution)/shard_map/attend/pallas_call | solution.py:1212
  203.1 16.9 %product.4 = f32[1024,2048]{1,0:T(8,128)} custom-call(bf16[1024,512]{1,0:T(8,128)(2,1)} %get-tuple-element.203.refs_0_.refs_2_, bf16[512,2048]{1,0:T(8,128)(2,1)} %get-tuple-element.204.refs_1_, bf16[1024,2048]{1,0:T(8,128)(2,1)} %get-tuple-element.208.refs_2_.refs_6_, bf16[2048,2048]{1,0:T(8,128)(2,1)} %get-tuple-element.209.refs_3_.down), custom_call_target="tpu_custom_call" | custom-call | flops 1 | bytes 1 | tf_op jit(solution)/shard_map/product/pallas_call | solution.py:1114
  220.2 3.1 dynamic-slice_bitcast_fusion
  223.7 5.9 %product.5.grad_context = bf16[1024,512]{1,0:T(8,128)(2,1)} custom-call(bf16[1024,2048]{1,0:T(8,128)(2,1)} %bitcast.62, bf16[512,2048]{1,0:T(8,128)(2,1)} %get-tuple-element.204.refs_1_), custom_call_target="tpu_custom_call" | custom-call | flops 1 | bytes 1 | tf_op jit(solution)/shard_map/product/pallas_call | solution.py:1114
  229.7 17.9 %attend_back.1.refs_8_.grad_projected = bf16[1024,1536]{1,0:T(8,128)(2,1)} custom-call(bf16[1024,1536]{1,0:T(8,128)(2,1)} %get-tuple-element.211.turned, f32[4,1024,1]{2,1,0:T(8,128)} %get-tuple-element.212.logs, f32[1024,128]{1,0:T(8,128)} %maximum_maximum_fusion.plain, f32[1024,128]{1,0:T(8,128)} %get-tuple-element.296.lower, ...), custom_call_target="tpu_custom_call" | custom-call | flops 1 | bytes 1 | tf_op jit(solution)/shard_map/attend_back/pallas_call | solution.py:1267
  247.6 2.7 constant_dynamic-slice_fusion
  250.2 9.5 %hidden_back.3 = (bf16[1024,1024]{1,0:T(8,128)(2,1)}, f32[1,1024]{1,0:T(1,128)}) custom-call(s32[1]{0:T(128)S(6)} %sub.47.half, bf16[1024,2048]{1,0:T(8,128)(2,1)} %bitcast.63, bf16[2048,2048]{1,0:T(8,128)(2,1)} %get-tuple-element.209.refs_3_.down, f32[1024,2048]{1,0:T(8,128)} %get-tuple-element.214.slope), custom_call_target="tpu_custom_call" | custom-call | flops 1 | bytes 1 | tf_op jit(solution)/shard_map/hidden_back/pallas_call | solution.py:1071
  261.2 9.4 %hidden_back.2 = (bf16[1024,1024]{1,0:T(8,128)(2,1)}, f32[1,1024]{1,0:T(1,128)}) custom-call(s32[1]{0:T(128)} %bitcast.14.half.core, bf16[1024,2048]{1,0:T(8,128)(2,1)} %bitcast.64, bf16[2048,2048]{1,0:T(8,128)(2,1)} %get-tuple-element.209.refs_3_.down, f32[1024,2048]{1,0:T(8,128)} %get-tuple-element.214.slope), custom_call_target="tpu_custom_call" | custom-call | flops 1 | bytes 1 | tf_op jit(solution)/shard_map/hidden_back/pallas_call | solution.py:1071
  271.9 41.0 %weight_grads.1 = (bf16[2,3136,128]{2,1,0:T(8,128)(2,1)}, bf16[2,3136,128]{2,1,0:T(8,128)(2,1)}, bf16[2,3136,128]{2,1,0:T(8,128)(2,1)}, bf16[2,3136,128]{2,1,0:T...) custom-call(s32[33]{0:T(128)} %concatenate.24.table, ...), custom_call_target="tpu_custom_call" | custom-call | flops 1 | bytes 1 | tf_op jit(solution)/shard_map/weight_grads/pallas_call | solution.py:758
  313.5 1.3 collective-permute-start.24
  316.1 2.8 convert_reduce_fusion
  319.0 24.1 %norm_grad.1 = (f32[1024,2048]{1,0:T(8,128)}, f32[4,2048]{1,0:T(4,128)}) custom-call(s32[1]{0:T(128)} %bitcast.14.half.core, bf16[1024,1536]{1,0:T(8,128)(2,1)} %attend_back.1.refs_8_.grad_projected, bf16[2048,1536]{1,0:T(8,128)(2,1)} %get-tuple-element.202.refs_1_.mixer_in, bf16[1024,1024]{1,0:T(8,128)(2,1)} %get-tuple-element.230.refs_12_.own_before, ...), custom_call_target="tpu_custom_call" | custom-call | flops 1 | bytes 1 | tf_op jit(solution)/shard_map/norm_grad/pallas_call | solution.py:806
  343.1 1.5 collective-permute-start.27
  344.6 2.7 dynamic-slice_convert_fusion
  348.3 2.5 collective-permute-done.24
  351.8 2.6 collective-permute-start.32
  354.4 3.6 collective-permute-start.30
  360.4 6.1 %fusion = (bf16[2,3136,128]{2,1,0:T(8,128)(2,1)}, bf16[2,3136,128]{2,1,0:T(8,128)(2,1)}) fusion(bf16[2,3136,128]{2,1,0:T(8,128)(2,1)} %copy-done.22, f32[2,2,3136,128]{3,2,1,0:T(8,128)} %get-tuple-element.242, bf16[2,3136,128]{2,1,0:T(8,128)(2,1)} %copy-done.21), kind=kLoop, calls=%fused_computation.3 | loop fusion | flops 4816896 | bytes 12845056 | tf_op jit(solution)/shard_map/convert_element_type | solution.py:1492
  366.7 19.3 %collective-permute-done.30 = bf16[256,2048]{1,0:T(8,128)(2,1)S(1)} collective-permute-done((bf16[256,2048]{1,0:T(8,128)(2,1)S(1)}, bf16[256,2048]{1,0:T(8,128)(2,1)S(1)}, u32[]{:S(2)}, u32[]{:S(2)}) %collective-permute-start.30) | collective-permute-done | bytes 1048608 | tf_op jit(solution)/shard_map/ppermute | solution.py:1330
  386.0 2.0 add_convert_fusion.2
  388.0 3.4 add_add_fusion
  391.4 3.0 collective-permute-done.28.refs_2_
  395.1 2.5 collective-permute-start.37
  398.6 1.5 collective-permute-start.34
  400.6 17.3 %collective-permute-done.37 = bf16[256,2048]{1,0:T(8,128)(2,1)} collective-permute-done((bf16[256,2048]{1,0:T(8,128)(2,1)S(1)}, bf16[256,2048]{1,0:T(8,128)(2,1)}, u32[]{:S(2)}, u32[]{:S(2)}) %collective-permute-start.37) | collective-permute-done | bytes 1048608 | tf_op jit(solution)/shard_map/ppermute | solution.py:1330
  417.9 1.6 collective-permute-start.38
  419.6 4.8 add_convert_fusion
  424.4 11.0 %collective-permute-done.33.refs_6_ = bf16[2,3136,128]{2,1,0:T(8,128)(2,1)} collective-permute-done((bf16[2,3136,128]{2,1,0:T(8,128)(2,1)}, bf16[2,3136,128]{2,1,0:T(8,128)(2,1)}, u32[]{:S(2)}, u32[]{:S(2)}) %collective-permute-start.33) | collective-permute-done | bytes 1605664 | tf_op jit(solution)/shard_map/ppermute | solution.py:1298
  436.6 18.0 %collective-permute-start.40 = (bf16[256,2048]{1,0:T(8,128)(2,1)}, bf16[256,2048]{1,0:T(8,128)(2,1)S(1)}, u32[]{:S(2)}, u32[]{:S(2)}) collective-permute-start(bf16[256,2048]{1,0:T(8,128)(2,1)} %get-tuple-element.261), channel_id=1, source_target_pairs={{0,2},{2,4},{4,6},{1,3},{3,5},{5,7},{8,10},{10,12},{12,14},{9,11},... | collective-permute-start | bytes 3145736 | tf_op jit(solution)/shard_map/ppermute | solution.py:1330
  454.6 1.3 collective-permute-start.41
  458.0 1.8 collective-permute-start.44
  459.9 2.4 collective-permute-done.44
  462.3 1.7 collective-permute-start.45
  464.1 2.6 collective-permute-done.45
  468.4 1.6 copy-done.6
  470.0 30.4 %adam.1 = (f32[12304,128]{1,0:T(8,128)}, f32[12304,128]{1,0:T(8,128)}, f32[12304,128]{1,0:T(8,128)}, f32[12304,128]{1,0:T(8,128)}, f32[12304,128]{1,0:T(8,128)}) custom-call(s32[2]{0:T(128)S(1)} %pad_add_fusion.table, f32[4]{0:T(128)S(1)} %pad_maximum_fusion.1.scalar_ref, f32[8]{0:T(128)S(1)} %copy-done.9, f32[2,2,3136,128]{3,2,1,0:T(8,128)} %get-tuple-element.228.refs_0_, ...), custom_call_target="tpu_custom_call" | custom-call | flops 1 | bytes 1 | tf_op jit(solution)/shard_map/adam/pallas_call | solution.py:970
  500.5 4.5 finish.1
  (194 shorter events, 30.6 us)
Async XLA Ops:
  7.2 92.9 %all-gather.5.cloned.1.call-start = ((), (), s32[]{:S(2)}) async-start(), calls=%async_computation.2 | async-start | bytes 5242880 | tf_op jit(solution)/shard_map/all_gather | solution.py:1368
  7.9 212.3 %all-gather.7.cloned.1.call-start = ((), (), s32[]{:S(2)}) async-start(), calls=%async_computation.3 | async-start | bytes 5242880 | tf_op jit(solution)/shard_map/all_gather | solution.py:1369
  14.5 67.0 %copy-start.2 = (bf16[6400,128]{1,0:T(8,128)(2,1)}, bf16[6400,128]{1,0:T(8,128)(2,1)S(1)}, u32[]{:S(2)}) copy-start(bf16[6400,128]{1,0:T(8,128)(2,1)S(1)} %get-tuple-element.145.refs_0_) | copy-start | bytes 4915204
  14.5 67.0 %copy-start.3 = (bf16[6144,128]{1,0:T(8,128)(2,1)}, bf16[6144,128]{1,0:T(8,128)(2,1)S(1)}, u32[]{:S(2)}) copy-start(bf16[6144,128]{1,0:T(8,128)(2,1)S(1)} %get-tuple-element.149.refs_0_) | copy-start | bytes 4718596
  14.5 38.8 %collective-permute-start = (bf16[6400,128]{1,0:T(8,128)(2,1)S(1)}, bf16[6400,128]{1,0:T(8,128)(2,1)S(1)}, u32[]{:S(2)}, u32[]{:S(2)}) collective-permute-start(bf16[6400,128]{1,0:T(8,128)(2,1)S(1)} %get-tuple-element.145.refs_0_), channel_id=1, source_target_pairs={{0,8},{8,0},{16,24},{24,16},{1,9},{9,1},{17,25},{25,17},{2,10},{10... | collective-permute-start | bytes 4915208 | tf_op jit(solution)/shard_map/ppermute | solution.py:1294
  17.5 37.3 %collective-permute-start.1 = (bf16[6400,128]{1,0:T(8,128)(2,1)S(1)}, bf16[6400,128]{1,0:T(8,128)(2,1)S(1)}, u32[]{:S(2)}, u32[]{:S(2)}) collective-permute-start(bf16[6400,128]{1,0:T(8,128)(2,1)S(1)} %get-tuple-element.145.refs_0_), channel_id=1, source_target_pairs={{0,16},{8,24},{16,0},{24,8},{1,17},{9,25},{17,1},{25,9},{2,18},{10... | collective-permute-start | bytes 4915208 | tf_op jit(solution)/shard_map/ppermute | solution.py:1298
  19.0 35.7 %collective-permute-start.2 = (bf16[6400,128]{1,0:T(8,128)(2,1)S(1)}, bf16[6400,128]{1,0:T(8,128)(2,1)S(1)}, u32[]{:S(2)}, u32[]{:S(2)}) collective-permute-start(bf16[6400,128]{1,0:T(8,128)(2,1)S(1)} %get-tuple-element.145.refs_0_), channel_id=1, source_target_pairs={{0,1},{1,0},{2,3},{3,2},{4,5},{5,4},{6,7},{7,6},{8,9},{9,8},{10,11... | collective-permute-start | bytes 4915208 | tf_op jit(solution)/shard_map/ppermute | solution.py:1312
  53.3 25.2 %copy-start.12 = (bf16[6400,128]{1,0:T(8,128)(2,1)}, bf16[6400,128]{1,0:T(8,128)(2,1)S(1)}, u32[]{:S(2)}) copy-start(bf16[6400,128]{1,0:T(8,128)(2,1)S(1)} %collective-permute-done.refs_1_) | copy-start | bytes 4915204
  54.8 23.2 %copy-start.11 = (bf16[6400,128]{1,0:T(8,128)(2,1)}, bf16[6400,128]{1,0:T(8,128)(2,1)S(1)}, u32[]{:S(2)}) copy-start(bf16[6400,128]{1,0:T(8,128)(2,1)S(1)} %collective-permute-done.1.refs_2_) | copy-start | bytes 4915204
  54.8 23.2 %collective-permute-start.5 = (bf16[6400,128]{1,0:T(8,128)(2,1)S(1)}, bf16[6400,128]{1,0:T(8,128)(2,1)S(1)}, u32[]{:S(2)}, u32[]{:S(2)}) collective-permute-start(bf16[6400,128]{1,0:T(8,128)(2,1)S(1)} %collective-permute-done.refs_1_), channel_id=1, source_target_pairs={{0,1},{1,0},{2,3},{3,2},{4,5},{5,4},{6,7},{7,6},{8,9},{9,8},{10,11... | collective-permute-start | bytes 4915208 | tf_op jit(solution)/shard_map/ppermute | solution.py:1312
  54.9 23.1 %collective-permute-start.6 = (bf16[6400,128]{1,0:T(8,128)(2,1)S(1)}, bf16[6400,128]{1,0:T(8,128)(2,1)S(1)}, u32[]{:S(2)}, u32[]{:S(2)}) collective-permute-start(bf16[6400,128]{1,0:T(8,128)(2,1)S(1)} %collective-permute-done.1.refs_2_), channel_id=1, source_target_pairs={{0,1},{1,0},{2,3},{3,2},{4,5},{5,4},{6,7},{7,6},{8,9},{9,8},{10,11... | collective-permute-start | bytes 4915208 | tf_op jit(solution)/shard_map/ppermute | solution.py:1312
  56.5 6.5 %collective-permute-start.7 = (bf16[6144,128]{1,0:T(8,128)(2,1)S(1)}, bf16[6144,128]{1,0:T(8,128)(2,1)S(1)}, u32[]{:S(2)}, u32[]{:S(2)}) collective-permute-start(bf16[6144,128]{1,0:T(8,128)(2,1)S(1)} %get-tuple-element.149.refs_0_), channel_id=1, source_target_pairs={{0,1},{1,0},{2,3},{3,2},{4,5},{5,4},{6,7},{7,6},{8,9},{9,8},{10,11... | collective-permute-start | bytes 4718600 | tf_op jit(solution)/shard_map/ppermute | solution.py:1312
  56.5 21.4 %collective-permute-start.3 = (bf16[3328,128]{1,0:T(8,128)(2,1)S(1)}, bf16[3328,128]{1,0:T(8,128)(2,1)S(1)}, u32[]{:S(2)}, u32[]{:S(2)}) collective-permute-start(bf16[3328,128]{1,0:T(8,128)(2,1)S(1)} %slice.59), channel_id=1, source_target_pairs={{0,8},{8,0},{16,24},{24,16},{1,9},{9,1},{17,25},{25,17},{2,10},{10... | collective-permute-start | bytes 2555912 | tf_op jit(solution)/shard_map/ppermute | solution.py:1294
  57.1 19.7 %collective-permute-start.4 = (bf16[3072,128]{1,0:T(8,128)(2,1)S(1)}, bf16[3072,128]{1,0:T(8,128)(2,1)S(1)}, u32[]{:S(2)}, u32[]{:S(2)}) collective-permute-start(bf16[3072,128]{1,0:T(8,128)(2,1)S(1)} %slice.60), channel_id=1, source_target_pairs={{0,16},{8,24},{16,0},{24,8},{1,17},{9,25},{17,1},{25,9},{2,18},{10... | collective-permute-start | bytes 2359304 | tf_op jit(solution)/shard_map/ppermute | solution.py:1298
  62.9 15.6 %copy-start.16 = (bf16[6144,128]{1,0:T(8,128)(2,1)}, bf16[6144,128]{1,0:T(8,128)(2,1)S(1)}, u32[]{:S(2)}) copy-start(bf16[6144,128]{1,0:T(8,128)(2,1)S(1)} %collective-permute-done.7.refs_4_) | copy-start | bytes 4718596
  78.0 36.3 %collective-permute-start.8 = (bf16[6144,128]{1,0:T(8,128)(2,1)S(1)}, bf16[6144,128]{1,0:T(8,128)(2,1)}, u32[]{:S(2)}, u32[]{:S(2)}) collective-permute-start(bf16[6144,128]{1,0:T(8,128)(2,1)S(1)} %get-tuple-element.149.refs_0_), channel_id=1, source_target_pairs={{0,8},{8,0},{16,24},{24,16},{1,9},{9,1},{17,25},{25,17},{2,10},{10... | collective-permute-start | bytes 4718600 | tf_op jit(solution)/shard_map/ppermute | solution.py:1294
  80.0 36.2 %collective-permute-start.9 = (bf16[6144,128]{1,0:T(8,128)(2,1)S(1)}, bf16[6144,128]{1,0:T(8,128)(2,1)}, u32[]{:S(2)}, u32[]{:S(2)}) collective-permute-start(bf16[6144,128]{1,0:T(8,128)(2,1)S(1)} %get-tuple-element.149.refs_0_), channel_id=1, source_target_pairs={{0,16},{8,24},{16,0},{24,8},{1,17},{9,25},{17,1},{25,9},{2,18},{10... | collective-permute-start | bytes 4718600 | tf_op jit(solution)/shard_map/ppermute | solution.py:1298
  81.5 306.5 %reduce-scatter.2.cloned.1.call-start = ((), (), s32[]{:S(2)}) async-start(), calls=%async_computation.1 | async-start | bytes 10485760 | tf_op jit(solution)/shard_map/reduce_scatter | solution.py:1436
  81.6 2.7 collective-permute-start.11
  81.7 10.6 %collective-permute-start.10 = (bf16[3072,128]{1,0:T(8,128)(2,1)}, bf16[3072,128]{1,0:T(8,128)(2,1)S(1)}, u32[]{:S(2)}, u32[]{:S(2)}) collective-permute-start(bf16[3072,128]{1,0:T(8,128)(2,1)} %copy-done.28), channel_id=1, source_target_pairs={{0,1},{1,0},{2,3},{3,2},{4,5},{5,4},{6,7},{7,6},{8,9},{9,8},{10,11... | collective-permute-start | bytes 2359304 | tf_op jit(solution)/shard_map/ppermute | solution.py:1312
  110.4 12.3 %copy-start.34 = (s32[1,5]{1,0:T(1,128)S(1)}, s32[1,5]{1,0:T(1,128)}, u32[]{:S(2)}) copy-start(s32[1,5]{1,0:T(1,128)} %param.14) | copy-start | bytes 64
  116.2 17.6 %collective-permute-start.16 = (bf16[1024,2048]{1,0:T(8,128)(2,1)}, bf16[1024,2048]{1,0:T(8,128)(2,1)}, u32[]{:S(2)}, u32[]{:S(2)}) collective-permute-start(bf16[1024,2048]{1,0:T(8,128)(2,1)} %bitcast.67), channel_id=1, source_target_pairs={{0,1},{1,0},{2,3},{3,2},{4,5},{5,4},{6,7},{7,6},{8,9},{9,8},{10,11... | collective-permute-start | bytes 12582920 | tf_op jit(solution)/shard_map/ppermute | solution.py:1312
  116.2 27.0 %collective-permute-start.14 = (bf16[6144,128]{1,0:T(8,128)(2,1)}, bf16[6144,128]{1,0:T(8,128)(2,1)S(1)}, u32[]{:S(2)}, u32[]{:S(2)}) collective-permute-start(bf16[6144,128]{1,0:T(8,128)(2,1)} %collective-permute-done.8.refs_1_), channel_id=1, source_target_pairs={{0,1},{1,0},{2,3},{3,2},{4,5},{5,4},{6,7},{7,6},{8,9},{9,8},{10,11... | collective-permute-start | bytes 4718600 | tf_op jit(solution)/shard_map/ppermute | solution.py:1312
  116.7 26.5 %collective-permute-start.15 = (bf16[6144,128]{1,0:T(8,128)(2,1)}, bf16[6144,128]{1,0:T(8,128)(2,1)S(1)}, u32[]{:S(2)}, u32[]{:S(2)}) collective-permute-start(bf16[6144,128]{1,0:T(8,128)(2,1)} %collective-permute-done.9.refs_2_), channel_id=1, source_target_pairs={{0,1},{1,0},{2,3},{3,2},{4,5},{5,4},{6,7},{7,6},{8,9},{9,8},{10,11... | collective-permute-start | bytes 4718600 | tf_op jit(solution)/shard_map/ppermute | solution.py:1312
  120.9 22.4 %collective-permute-start.12 = (bf16[3072,128]{1,0:T(8,128)(2,1)}, bf16[3072,128]{1,0:T(8,128)(2,1)}, u32[]{:S(2)}, u32[]{:S(2)}) collective-permute-start(bf16[3072,128]{1,0:T(8,128)(2,1)} %slice.63), channel_id=1, source_target_pairs={{0,8},{8,0},{16,24},{24,16},{1,9},{9,1},{17,25},{25,17},{2,10},{10... | collective-permute-start | bytes 2359304 | tf_op jit(solution)/shard_map/ppermute | solution.py:1294
  121.3 22.0 %collective-permute-start.13 = (bf16[3072,128]{1,0:T(8,128)(2,1)}, bf16[3072,128]{1,0:T(8,128)(2,1)}, u32[]{:S(2)}, u32[]{:S(2)}) collective-permute-start(bf16[3072,128]{1,0:T(8,128)(2,1)} %slice.64), channel_id=1, source_target_pairs={{0,16},{8,24},{16,0},{24,8},{1,17},{9,25},{17,1},{25,9},{2,18},{10... | collective-permute-start | bytes 2359304 | tf_op jit(solution)/shard_map/ppermute | solution.py:1298
  143.3 6.7 %collective-permute-start.18 = (bf16[3072,128]{1,0:T(8,128)(2,1)}, bf16[3072,128]{1,0:T(8,128)(2,1)}, u32[]{:S(2)}, u32[]{:S(2)}) collective-permute-start(bf16[3072,128]{1,0:T(8,128)(2,1)} %collective-permute-done.12.refs_3_), channel_id=1, source_target_pairs={{0,1},{1,0},{2,3},{3,2},{4,5},{5,4},{6,7},{7,6},{8,9},{9,8},{10,11... | collective-permute-start | bytes 2359304 | tf_op jit(solution)/shard_map/ppermute | solution.py:1312
  143.3 13.4 %collective-permute-start.17 = (bf16[3072,128]{1,0:T(8,128)(2,1)}, bf16[3072,128]{1,0:T(8,128)(2,1)}, u32[]{:S(2)}, u32[]{:S(2)}) collective-permute-start(bf16[3072,128]{1,0:T(8,128)(2,1)} %collective-permute-done.13.refs_3_), channel_id=1, source_target_pairs={{0,1},{1,0},{2,3},{3,2},{4,5},{5,4},{6,7},{7,6},{8,9},{9,8},{10,11... | collective-permute-start | bytes 2359304 | tf_op jit(solution)/shard_map/ppermute | solution.py:1312
  220.0 50.6 %collective-permute-start.20 = (bf16[1024,2048]{1,0:T(8,128)(2,1)}, bf16[1024,2048]{1,0:T(8,128)(2,1)}, u32[]{:S(2)}, u32[]{:S(2)}) collective-permute-start(bf16[1024,2048]{1,0:T(8,128)(2,1)} %get-tuple-element.208.refs_2_.refs_6_), channel_id=1, source_target_pairs={{0,1},{1,0},{2,3},{3,2},{4,5},{5,4},{6,7},{7,6},{8,9},{9,8},{10,11... | collective-permute-start | bytes 12582920 | tf_op jit(solution)/shard_map/ppermute | solution.py:1312
  223.3 47.3 %collective-permute-start.22 = (bf16[1024,1024]{1,0:T(8,128)(2,1)}, bf16[1024,1024]{1,0:T(8,128)(2,1)S(1)}, u32[]{:S(2)}, u32[]{:S(2)}) collective-permute-start(bf16[1024,1024]{1,0:T(8,128)(2,1)} %dynamic-slice_bitcast_fusion), channel_id=1, source_target_pairs={{0,1},{1,0},{2,3},{3,2},{4,5},{5,4},{6,7},{7,6},{8,9},{9,8},{10,11... | collective-permute-start | bytes 6291464 | tf_op jit(solution)/shard_map/ppermute | solution.py:1312
  250.2 10.1 %copy-start.8 = (s32[8]{0:T(128)S(1)}, s32[8]{0:T(128)}, u32[]{:S(2)}) copy-start(s32[8]{0:T(128)} %copy-done.7) | copy-start | bytes 100
  259.7 10.9 %collective-permute-start.23 = (bf16[1024,1024]{1,0:T(8,128)(2,1)}, bf16[1024,1024]{1,0:T(8,128)(2,1)}, u32[]{:S(2)}, u32[]{:S(2)}) collective-permute-start(bf16[1024,1024]{1,0:T(8,128)(2,1)} %get-tuple-element.231.rest_before), channel_id=1, source_target_pairs={{0,1},{1,0},{2,3},{3,2},{4,5},{5,4},{6,7},{7,6},{8,9},{9,8},{10,11... | collective-permute-start | bytes 6291464 | tf_op jit(solution)/shard_map/ppermute | solution.py:1312
  259.8 10.8 %collective-permute-start.21 = (bf16[1024,768]{1,0:T(8,128)(2,1)}, bf16[1024,768]{1,0:T(8,128)(2,1)}, u32[]{:S(2)}, u32[]{:S(2)}) collective-permute-start(bf16[1024,768]{1,0:T(8,128)(2,1)} %constant_dynamic-slice_fusion), channel_id=1, source_target_pairs={{0,1},{1,0},{2,3},{3,2},{4,5},{5,4},{6,7},{7,6},{8,9},{9,8},{10,11... | collective-permute-start | bytes 4718600 | tf_op jit(solution)/shard_map/ppermute | solution.py:1312
  260.2 10.3 %collective-permute-start.19 = (bf16[1024,512]{1,0:T(8,128)(2,1)S(1)}, bf16[1024,512]{1,0:T(8,128)(2,1)}, u32[]{:S(2)}, u32[]{:S(2)}) collective-permute-start(bf16[1024,512]{1,0:T(8,128)(2,1)S(1)} %copy-done.19), channel_id=1, source_target_pairs={{0,1},{1,0},{2,3},{3,2},{4,5},{5,4},{6,7},{7,6},{8,9},{9,8},{10,11... | collective-permute-start | bytes 3145736 | tf_op jit(solution)/shard_map/ppermute | solution.py:1312
  312.9 38.9 %collective-permute-start.26 = (f32[2,2,3136,128]{3,2,1,0:T(8,128)}, f32[2,2,3136,128]{3,2,1,0:T(8,128)}, u32[]{:S(2)}, u32[]{:S(2)}) collective-permute-start(f32[2,2,3136,128]{3,2,1,0:T(8,128)} %get-tuple-element.228.refs_0_), channel_id=1, source_target_pairs={{0,1},{1,0},{2,3},{3,2},{4,5},{5,4},{6,7},{7,6},{8,9},{9,8},{10,11... | collective-permute-start | bytes 19267592 | tf_op jit(solution)/shard_map/ppermute | solution.py:1312
  313.5 37.3 %collective-permute-start.24 = (bf16[2,3136,128]{2,1,0:T(8,128)(2,1)}, bf16[2,3136,128]{2,1,0:T(8,128)(2,1)S(1)}, u32[]{:S(2)}, u32[]{:S(2)}) collective-permute-start(bf16[2,3136,128]{2,1,0:T(8,128)(2,1)} %get-tuple-element.226), channel_id=1, source_target_pairs={{0,8},{8,0},{16,24},{24,16},{1,9},{9,1},{17,25},{25,17},{2,10},{10... | collective-permute-start | bytes 4816904 | tf_op jit(solution)/shard_map/ppermute | solution.py:1294
  314.8 37.0 %collective-permute-start.25 = (bf16[2,3136,128]{2,1,0:T(8,128)(2,1)}, bf16[2,3136,128]{2,1,0:T(8,128)(2,1)S(1)}, u32[]{:S(2)}, u32[]{:S(2)}) collective-permute-start(bf16[2,3136,128]{2,1,0:T(8,128)(2,1)} %get-tuple-element.227), channel_id=1, source_target_pairs={{0,16},{8,24},{16,0},{24,8},{1,17},{9,25},{17,1},{25,9},{2,18},{10... | collective-permute-start | bytes 4816904 | tf_op jit(solution)/shard_map/ppermute | solution.py:1298
  343.1 5.2 %collective-permute-start.27 = (f32[4,2048]{1,0:T(4,128)}, f32[4,2048]{1,0:T(4,128)S(1)}, u32[]{:S(2)}, u32[]{:S(2)}) collective-permute-start(f32[4,2048]{1,0:T(4,128)} %get-tuple-element.235), channel_id=1, source_target_pairs={{0,2},{2,0},{4,6},{6,4},{1,3},{3,1},{5,7},{7,5},{8,10},{10,8},{12,... | collective-permute-start | bytes 98312 | tf_op jit(solution)/shard_map/ppermute | solution.py:1302
  347.8 38.2 %slice-start = ((s8[8388608]{0:T(1024)(128)(4,1)}), s8[4194304]{0:T(1024)(128)(4,1)S(1)}, s32[]{:S(2)}) async-start(s8[8388608]{0:T(1024)(128)(4,1)} %bitcast.52), calls=%async_computation.4 | async-start | bytes 8388608
  351.8 34.2 %slice-start.1 = ((s8[8388608]{0:T(1024)(128)(4,1)}), s8[4194304]{0:T(1024)(128)(4,1)S(1)}, s32[]{:S(2)}) async-start(s8[8388608]{0:T(1024)(128)(4,1)} %bitcast.52), calls=%async_computation.5 | async-start | bytes 8388608
  351.8 14.7 %collective-permute-start.32 = (f32[4,2048]{1,0:T(4,128)S(1)}, f32[4,2048]{1,0:T(4,128)S(1)}, u32[]{:S(2)}, u32[]{:S(2)}) collective-permute-start(f32[4,2048]{1,0:T(4,128)S(1)} %add.179), channel_id=1, source_target_pairs={{0,4},{2,6},{4,0},{6,2},{1,5},{3,7},{5,1},{7,3},{8,12},{10,14},{12... | collective-permute-start | bytes 98312 | tf_op jit(solution)/shard_map/ppermute | solution.py:1302
  354.4 31.6 %collective-permute-start.30 = (bf16[256,2048]{1,0:T(8,128)(2,1)S(1)}, bf16[256,2048]{1,0:T(8,128)(2,1)S(1)}, u32[]{:S(2)}, u32[]{:S(2)}) collective-permute-start(bf16[256,2048]{1,0:T(8,128)(2,1)S(1)} %get-tuple-element.246), channel_id=1, source_target_pairs={{0,2},{1,3},{8,10},{9,11},{16,18},{17,19},{24,26},{25,27}} | collective-permute-start | bytes 3145736 | tf_op jit(solution)/shard_map/ppermute | solution.py:1330
  358.0 28.0 %collective-permute-start.31 = (bf16[256,2048]{1,0:T(8,128)(2,1)S(1)}, bf16[256,2048]{1,0:T(8,128)(2,1)S(1)}, u32[]{:S(2)}, u32[]{:S(2)}) collective-permute-start(bf16[256,2048]{1,0:T(8,128)(2,1)S(1)} %get-tuple-element.247), channel_id=1, source_target_pairs={{6,4},{7,5},{14,12},{15,13},{22,20},{23,21},{30,28},{31,29}} | collective-permute-start | bytes 3145736 | tf_op jit(solution)/shard_map/ppermute | solution.py:1330
  358.7 35.7 %collective-permute-start.28 = (bf16[2,3136,128]{2,1,0:T(8,128)(2,1)}, bf16[2,3136,128]{2,1,0:T(8,128)(2,1)S(1)}, u32[]{:S(2)}, u32[]{:S(2)}) collective-permute-start(bf16[2,3136,128]{2,1,0:T(8,128)(2,1)} %get-tuple-element.240), channel_id=1, source_target_pairs={{0,8},{8,0},{16,24},{24,16},{1,9},{9,1},{17,25},{25,17},{2,10},{10... | collective-permute-start | bytes 4816904 | tf_op jit(solution)/shard_map/ppermute | solution.py:1294
  359.6 35.5 %collective-permute-start.29 = (bf16[2,3136,128]{2,1,0:T(8,128)(2,1)}, bf16[2,3136,128]{2,1,0:T(8,128)(2,1)}, u32[]{:S(2)}, u32[]{:S(2)}) collective-permute-start(bf16[2,3136,128]{2,1,0:T(8,128)(2,1)} %get-tuple-element.241), channel_id=1, source_target_pairs={{0,16},{8,24},{16,0},{24,8},{1,17},{9,25},{17,1},{25,9},{2,18},{10... | collective-permute-start | bytes 4816904 | tf_op jit(solution)/shard_map/ppermute | solution.py:1298
  366.7 21.4 %copy-start.1 = (bf16[1,256,2048]{2,1,0:T(8,128)(2,1)S(1)}, bf16[1,256,2048]{2,1,0:T(8,128)(2,1)}, u32[]{:S(2)}) copy-start(bf16[1,256,2048]{2,1,0:T(8,128)(2,1)} %param.12) | copy-start | bytes 3145732
  394.5 29.9 %copy-start.5 = (bf16[2,3136,128]{2,1,0:T(8,128)(2,1)}, bf16[2,3136,128]{2,1,0:T(8,128)(2,1)S(1)}, u32[]{:S(2)}) copy-start(bf16[2,3136,128]{2,1,0:T(8,128)(2,1)S(1)} %collective-permute-done.28.refs_2_) | copy-start | bytes 4816900
  395.1 22.8 %collective-permute-start.37 = (bf16[256,2048]{1,0:T(8,128)(2,1)S(1)}, bf16[256,2048]{1,0:T(8,128)(2,1)}, u32[]{:S(2)}, u32[]{:S(2)}) collective-permute-start(bf16[256,2048]{1,0:T(8,128)(2,1)S(1)} %copy-done.25), channel_id=1, source_target_pairs={{0,2},{2,4},{1,3},{3,5},{8,10},{10,12},{9,11},{11,13},{16,18},{18,... | collective-permute-start | bytes 3145736 | tf_op jit(solution)/shard_map/ppermute | solution.py:1330
  397.6 2.5 collective-permute-start.39
  397.6 37.8 %collective-permute-start.33 = (bf16[2,3136,128]{2,1,0:T(8,128)(2,1)}, bf16[2,3136,128]{2,1,0:T(8,128)(2,1)}, u32[]{:S(2)}, u32[]{:S(2)}) collective-permute-start(bf16[2,3136,128]{2,1,0:T(8,128)(2,1)} %get-tuple-element.254), channel_id=1, source_target_pairs={{0,16},{8,24},{16,0},{24,8},{1,17},{9,25},{17,1},{25,9},{2,18},{10... | collective-permute-start | bytes 4816904 | tf_op jit(solution)/shard_map/ppermute | solution.py:1298
  398.6 37.5 %collective-permute-start.34 = (bf16[2,3136,128]{2,1,0:T(8,128)(2,1)}, bf16[2,3136,128]{2,1,0:T(8,128)(2,1)}, u32[]{:S(2)}, u32[]{:S(2)}) collective-permute-start(bf16[2,3136,128]{2,1,0:T(8,128)(2,1)} %get-tuple-element.255), channel_id=1, source_target_pairs={{0,8},{8,0},{16,24},{24,16},{1,9},{9,1},{17,25},{25,17},{2,10},{10... | collective-permute-start | bytes 4816904 | tf_op jit(solution)/shard_map/ppermute | solution.py:1294
  400.0 36.1 %collective-permute-start.35 = (bf16[2,3136,128]{2,1,0:T(8,128)(2,1)S(1)}, bf16[2,3136,128]{2,1,0:T(8,128)(2,1)}, u32[]{:S(2)}, u32[]{:S(2)}) collective-permute-start(bf16[2,3136,128]{2,1,0:T(8,128)(2,1)S(1)} %collective-permute-done.28.refs_2_), channel_id=1, source_target_pairs={{0,1},{1,0},{2,3},{3,2},{4,5},{5,4},{6,7},{7,6},{8,9},{9,8},{10,11... | collective-permute-start | bytes 4816904 | tf_op jit(solution)/shard_map/ppermute | solution.py:1312
  400.0 36.1 %collective-permute-start.36 = (bf16[2,3136,128]{2,1,0:T(8,128)(2,1)}, bf16[2,3136,128]{2,1,0:T(8,128)(2,1)}, u32[]{:S(2)}, u32[]{:S(2)}) collective-permute-start(bf16[2,3136,128]{2,1,0:T(8,128)(2,1)} %collective-permute-done.29.refs_3_), channel_id=1, source_target_pairs={{0,1},{1,0},{2,3},{3,2},{4,5},{5,4},{6,7},{7,6},{8,9},{9,8},{10,11... | collective-permute-start | bytes 4816904 | tf_op jit(solution)/shard_map/ppermute | solution.py:1312
  417.9 1.7 collective-permute-start.38
  419.5 48.9 %copy-start.9 = (f32[8]{0:T(128)S(1)}, f32[8]{0:T(128)}, u32[]{:S(2)}) copy-start(f32[8]{0:T(128)} %rate_ref.1) | copy-start | bytes 100
  436.1 30.5 %collective-permute-start.42 = (bf16[2,3136,128]{2,1,0:T(8,128)(2,1)}, bf16[2,3136,128]{2,1,0:T(8,128)(2,1)S(1)}, u32[]{:S(2)}, u32[]{:S(2)}) collective-permute-start(bf16[2,3136,128]{2,1,0:T(8,128)(2,1)} %collective-permute-done.33.refs_6_), channel_id=1, source_target_pairs={{0,1},{1,0},{2,3},{3,2},{4,5},{5,4},{6,7},{7,6},{8,9},{9,8},{10,11... | collective-permute-start | bytes 4816904 | tf_op jit(solution)/shard_map/ppermute | solution.py:1312
  436.1 30.6 %collective-permute-start.43 = (bf16[2,3136,128]{2,1,0:T(8,128)(2,1)}, bf16[2,3136,128]{2,1,0:T(8,128)(2,1)S(1)}, u32[]{:S(2)}, u32[]{:S(2)}) collective-permute-start(bf16[2,3136,128]{2,1,0:T(8,128)(2,1)} %collective-permute-done.34.refs_7_), channel_id=1, source_target_pairs={{0,1},{1,0},{2,3},{3,2},{4,5},{5,4},{6,7},{7,6},{8,9},{9,8},{10,11... | collective-permute-start | bytes 4816904 | tf_op jit(solution)/shard_map/ppermute | solution.py:1312
  436.6 63.8 %collective-permute-start.40 = (bf16[256,2048]{1,0:T(8,128)(2,1)}, bf16[256,2048]{1,0:T(8,128)(2,1)S(1)}, u32[]{:S(2)}, u32[]{:S(2)}) collective-permute-start(bf16[256,2048]{1,0:T(8,128)(2,1)} %get-tuple-element.261), channel_id=1, source_target_pairs={{0,2},{2,4},{4,6},{1,3},{3,5},{5,7},{8,10},{10,12},{12,14},{9,11},... | collective-permute-start | bytes 3145736 | tf_op jit(solution)/shard_map/ppermute | solution.py:1330
  454.6 45.8 %collective-permute-start.41 = (bf16[256,2048]{1,0:T(8,128)(2,1)}, bf16[256,2048]{1,0:T(8,128)(2,1)}, u32[]{:S(2)}, u32[]{:S(2)}) collective-permute-start(bf16[256,2048]{1,0:T(8,128)(2,1)} %get-tuple-element.262), channel_id=1, source_target_pairs={{2,0},{4,2},{6,4},{3,1},{5,3},{7,5},{10,8},{12,10},{14,12},{11,9},... | collective-permute-start | bytes 3145736 | tf_op jit(solution)/shard_map/ppermute | solution.py:1330
  458.0 4.3 collective-permute-start.44
  462.3 4.3 collective-permute-start.45
  468.4 32.0 %slice-start.2 = ((s8[8388608]{0:T(1024)(128)(4,1)}), s8[4194304]{0:T(1024)(128)(4,1)S(1)}, s32[]{:S(2)}) async-start(s8[8388608]{0:T(1024)(128)(4,1)} %bitcast.54), calls=%async_computation.6 | async-start | bytes 8388608
  470.0 30.5 %slice-start.3 = ((s8[8388608]{0:T(1024)(128)(4,1)}), s8[4194304]{0:T(1024)(128)(4,1)S(1)}, s32[]{:S(2)}) async-start(s8[8388608]{0:T(1024)(128)(4,1)} %bitcast.54), calls=%async_computation.7 | async-start | bytes 8388608
  470.0 30.5 %copy-start.4 = (bf16[1,256,2048]{2,1,0:T(8,128)(2,1)S(1)}, bf16[1,256,2048]{2,1,0:T(8,128)(2,1)}, u32[]{:S(2)}) copy-start(bf16[1,256,2048]{2,1,0:T(8,128)(2,1)} %param.13) | copy-start | bytes 3145732
  (24 other events, 85.7 us)
Sparse Core Ops, SparseCore 0:
  9.6 83.4 all-gather.4
  94.6 79.2 all-gather.6
  220.1 151.6 reduce-scatter.1

commit v4 on v3

--- a/solution.py
+++ b/solution.py
@@ -447,14 +447,14 @@
 PLACES = {
     0: (("in", 0, 1024, 0),),
     1: (("in", 1024, 1024, 0),),
-    2: (("out", 0, 512, 0), ("up", 0, 256, 512)),
+    2: (("mix", 0, 512, 0), ("up", 0, 256, 512)),
     3: (("up", 256, 768, 0),),
     4: (("up", 1024, 768, 0),),
-    5: (("up", 1792, 256, 0), ("down", 0, 512, 256)),
-    6: (("down", 512, 768, 0),),
-    7: (("down", 1280, 768, 0),),
+    5: (("up", 1792, 256, 0), ("mix", 512, 512, 256)),
+    6: (("mix", 1024, 768, 0),),
+    7: (("mix", 1792, 768, 0),),
 }
-NAMES = ("in", "out", "up", "down", "bias")
+NAMES = ("in", "mix", "up", "bias")
 
 
 def panels_of(bucket):
@@ -463,106 +463,99 @@
 
 MATRICES = {
     "in": (2048, 1536),
-    "out": (512, 2048),
+    "mix": (2560, 2048),
     "up": (2048, 2048),
-    "down": (2048, 2048),
     "bias": (TROWS, 2048),
 }
 
 
-def head_of(bucket):
-    if bucket == 8:
-        return ("bias", 0)
-    name, first, _, _ = PLACES[bucket][0]
-    return (name, first)
-
-
 def columns(panel):
     return pl.ds(panel * LANES, LANES)
 
 
-def unpack_kernel(part, bucket_ref, *refs):
-    sources = refs[:8]
+def unpack_kernel(parts, bucket_ref, *refs):
+    sources = refs[:16]
     staged, tails, load_sems, tail_sem, store_sems = refs[-5:]
-    matrices = refs[-11:-5] if part == 0 else refs[-9:-5]
+    matrices = refs[-10:-5] if parts[0] == 0 else refs[-8:-5]
     outs = dict(zip(NAMES[: len(matrices)], matrices, strict=False))
     main = (16 // CHUNKS) * BROWS
-    loads = [
-        pltpu.make_async_copy(
-            sources[k].at[pl.ds(0 if k % 4 == 3 else part_row(part), main)],
-            staged.at[bucket_ref[k]],
-            load_sems.at[k],
-        )
-        for k in range(8)
-    ]
-    if part == 0:
+    if parts[0] == 0:
         for k in range(8):
             pltpu.make_async_copy(
                 sources[k].at[pl.ds(main, 16 * TROWS)], tails.at[bucket_ref[k]], tail_sem
             ).start()
         take_tails = pltpu.make_async_copy(tails, tails, tail_sem)
     else:
-        take_tails = pltpu.make_async_copy(refs[8], tails, tail_sem)
+        take_tails = pltpu.make_async_copy(refs[16], tails, tail_sem)
         take_tails.start()
-    for load in loads:
-        load.start()
+    for at in range(2):
+        for k in range(8):
+            pltpu.make_async_copy(
+                sources[8 * at + k].at[pl.ds(0 if k % 4 == 3 else part_row(parts[at]), main)],
+                staged.at[at, bucket_ref[k]],
+                load_sems.at[at, bucket_ref[k]],
+            ).start()
     take_tails.wait()
-    for load in loads:
-        load.wait()
     stores = []
 
     def store(source, target):
         stores.append(pltpu.make_async_copy(source, target, store_sems.at[len(stores)]))
         stores[-1].start()
 
-    if part == 0:
-        store(tails, matrices[5])
+    if parts[0] == 0:
+        store(tails, matrices[4])
         for panel in range(16):
             store(
                 tails.at[7, pl.ds(panel * TROWS, TROWS)],
                 outs["bias"].at[pl.ds(0, TROWS), columns(panel)],
             )
-    for bucket in range(8):
-        span = QROWS if bucket < 2 else BROWS
-        wide = panels_of(bucket)
-        for panel in range(wide):
-            if bucket:
-                head = pl.ds(panel * span, TROWS)
-                tail = pl.ds((part * wide + panel) * TROWS, TROWS)
-                staged[bucket, head, :] = staged[bucket, head, :] + tails[bucket - 1, tail, :]
-            for name, first, rows, offset in PLACES[bucket]:
-                store(
-                    staged.at[bucket, pl.ds(panel * span + offset, rows)],
-                    outs[name].at[pl.ds(first, rows), columns(part * wide + panel)],
-                )
+    for at, part in enumerate(parts):
+        for bucket in range(8):
+            held = staged.at[at, bucket]
+            pltpu.make_async_copy(held, held, load_sems.at[at, bucket]).wait()
+            span = QROWS if bucket < 2 else BROWS
+            wide = panels_of(bucket)
+            for panel in range(wide):
+                if bucket:
+                    head = pl.ds(panel * span, TROWS)
+                    tail = pl.ds((part * wide + panel) * TROWS, TROWS)
+                    staged[at, bucket, head, :] = (
+                        staged[at, bucket, head, :] + tails[bucket - 1, tail, :]
+                    )
+                for name, first, rows, offset in PLACES[bucket]:
+                    store(
+                        staged.at[at, bucket, pl.ds(panel * span + offset, rows)],
+                        outs[name].at[pl.ds(first, rows), columns(part * wide + panel)],
+                    )
     for put in stores:
         put.wait()
 
 
-def unpack(part, buckets, sources, before):
-    copies = sum(len(PLACES[b]) * panels_of(b) for b in range(8)) + (0 if part else 17)
-    names = NAMES[:4] if part else NAMES
+def unpack(parts, buckets, sources, before):
+    first = parts[0] == 0
+    copies = 2 * sum(len(PLACES[b]) * panels_of(b) for b in range(8)) + (17 if first else 0)
+    names = NAMES if first else NAMES[:3]
     tails = jax.ShapeDtypeStruct((8, 16 * TROWS, LANES), jnp.bfloat16)
     shapes = [jax.ShapeDtypeStruct(MATRICES[name], jnp.bfloat16) for name in names]
     results = pl.pallas_call(
-        functools.partial(unpack_kernel, part),
-        out_shape=shapes if part else [*shapes, tails],
+        functools.partial(unpack_kernel, parts),
+        out_shape=[*shapes, tails] if first else shapes,
         in_specs=[pl.BlockSpec(memory_space=pltpu.SMEM)]
-        + [pl.BlockSpec(memory_space=HBM)] * (8 + (5 if part else 0)),
-        out_specs=[pl.BlockSpec(memory_space=HBM)] * (4 if part else 6),
-        input_output_aliases={10 + at: at for at in range(4)} if part else {},
+        + [pl.BlockSpec(memory_space=HBM)] * (16 + (0 if first else 4)),
+        out_specs=[pl.BlockSpec(memory_space=HBM)] * (5 if first else 3),
+        input_output_aliases={} if first else {18 + at: at for at in range(3)},
         scratch_shapes=[
-            pltpu.VMEM((8, (16 // CHUNKS) * BROWS, LANES), jnp.bfloat16),
+            pltpu.VMEM((2, 8, (16 // CHUNKS) * BROWS, LANES), jnp.bfloat16),
             pltpu.VMEM(tails.shape, tails.dtype),
-            pltpu.SemaphoreType.DMA((8,)),
+            pltpu.SemaphoreType.DMA((2, 8)),
             pltpu.SemaphoreType.DMA,
             pltpu.SemaphoreType.DMA((copies,)),
         ],
         compiler_params=params(60),
         cost_estimate=LIGHT,
         name="unpack_params",
-    )(buckets, *sources, *((before[5], *before[:4]) if part else ()))
-    return [*results, *before[4:]] if part else results
+    )(buckets, *sources, *(() if first else (before[4], *before[:3])))
+    return results if first else [*results, *before[3:]]
 
 
 GRAD_ROWS = 256
@@ -737,21 +730,18 @@
 def weight_grads(table, lefts, rights):
     tokens = lefts[0].shape[0]
 
-    def columns_at(first, count):
+    def columns_at(first, count, ahead):
         return pl.BlockSpec(
-            (tokens, PAIR), lambda i, table: (0, jnp.clip(i - first, 0, count - 1))
+            (tokens, PAIR), lambda i, table: (0, ahead + jnp.clip(i - first, 0, count - 1))
         )
 
     left_specs = [
-        columns_at(first, last - first)
-        for first, last in zip(GRAD_EDGES, GRAD_EDGES[1:], strict=False)
+        columns_at(first, last - first, ahead)
+        for first, last, ahead in zip(GRAD_EDGES, GRAD_EDGES[1:], (0, 0, 0, 1), strict=False)
         for _ in range(2)
     ]
-    projected = rights[1].shape
-    right_specs = [
-        pl.BlockSpec(projected, lambda i, table: (0, table[0])),
-        pl.BlockSpec(projected, lambda i, table: (0, 0)),
-    ]
+    half = (tokens, rights[0].shape[1] // 2)
+    right_specs = [pl.BlockSpec(half, lambda i, table: (0, table[0]))] * 2
     rows = chunk_rows()
     short = jax.ShapeDtypeStruct((2, rows, LANES), jnp.bfloat16)
     wide = jax.ShapeDtypeStruct((2, 2, rows, LANES), jnp.float32)
@@ -790,7 +780,7 @@
     one = product_back(grad_projected[...], mixer_in[...])
     two = product_back(own_before[...], own_up[...]) + product_back(rest_before[...], rest_up[...])
     unit = (rows[...].astype(jnp.float32) - centre[...]) * scale[...]
-    partial[...] = one * gains[0:1, :] + two * gains[1:2, :]
+    partial[...] = (one * gains[0:1, :] + two * gains[1:2, :]).astype(jnp.bfloat16)
     for at, value in enumerate((one * unit, one, two * unit, two)):
         sums[at : at + 1, :] = jnp.sum(value, axis=0, keepdims=True)
 
@@ -806,7 +796,7 @@
     return pl.pallas_call(
         norm_grad_kernel,
         out_shape=[
-            jax.ShapeDtypeStruct((tokens, D), jnp.float32),
+            jax.ShapeDtypeStruct((tokens, D), jnp.bfloat16),
             jax.ShapeDtypeStruct((4, D), jnp.float32),
         ],
         grid_spec=pltpu.PrefetchScalarGridSpec(
@@ -832,7 +822,7 @@
     )(core, grad_projected, mixer_in, own_before, up, rest_before, up, rows, centre, scale, gains)
 
 
-ADAM_ROWS = 1024
+ADAM_ROWS = 3080
 
 
 def adam_kernel(table, scalar_ref, rate_ref, *refs):
@@ -897,7 +887,8 @@
     @pl.when(bucket >= 2)
     def _():
         def reach(at):
-            return jnp.clip(at * (ADAM_ROWS // 256) + jnp.where(at > 0, 1, 0), 0, BROWS // 16)
+            tiles = (at * (ADAM_ROWS // 8) // 2 + 23) // 16
+            return jnp.clip(jnp.where(at > 0, tiles, 0), 0, BROWS // 16)
 
         def step(tile, carry):
             row = pl.multiple_of(tile * 16, 16)
@@ -972,24 +963,27 @@
         grid=(steps,),
         out_shape=[jax.ShapeDtypeStruct((FLAT, LANES), jnp.float32)] * 5,
         in_specs=[pl.BlockSpec(memory_space=pltpu.SMEM)] * 3
-        + [pl.BlockSpec(memory_space=HBM)] * 10
+        + [pl.BlockSpec(memory_space=HBM)] * 2
+        + [pl.BlockSpec(memory_space=pl.ANY)] * 8
         + [pl.BlockSpec(memory_space=pltpu.VMEM)]
         + [block] * 4,
         out_specs=[block] * 5,
         scratch_shapes=[
             pltpu.VMEM((4, chunk_rows(), LANES), jnp.float32),
             pltpu.VMEM((2, 4, chunk_rows(), LANES), jnp.bfloat16),
-            pltpu.VMEM((FRONT + steps * ADAM_ROWS, LANES), jnp.float32),
+            pltpu.VMEM((FRONT + max(steps * ADAM_ROWS, FLAT + BACK), LANES), jnp.float32),
             pltpu.SemaphoreType.DMA((3, 4)),
         ],
-        compiler_params=params(48),
+        compiler_params=params(60),
         cost_estimate=LIGHT,
         name="adam",
     )(table, scalars, rates, *stays, *near, *far, small, *state)
 
 
-def finish_kernel(index, partial, up, down, rows, grads, out):
-    scaled = partial[...] + (up[...].astype(jnp.float32) + down[...].astype(jnp.float32))
+def finish_kernel(terms, rows, grads, out):
+    scaled = terms[0].astype(jnp.float32)
+    for at in range(1, terms.shape[0]):
+        scaled = scaled + terms[at].astype(jnp.float32)
     unit, scale = norm_stats(rows[...].astype(jnp.float32))
     out[...] = grads[...].astype(jnp.float32) + scale * (
         scaled
@@ -998,29 +992,24 @@
     )
 
 
-def finish(index, partial, line, rows, grads):
+def finish(terms, rows, grads):
     count, width = rows.shape
-    steps = 4
-    block = pl.BlockSpec((count // steps, width), lambda i, index: (i, 0))
+    height = count // 4
+    block = pl.BlockSpec((height, width), lambda i: (i, 0))
     return pl.pallas_call(
         finish_kernel,
+        grid=(count // height,),
         out_shape=jax.ShapeDtypeStruct((count, width), jnp.float32),
-        grid_spec=pltpu.PrefetchScalarGridSpec(
-            num_scalar_prefetch=1,
-            grid=(steps,),
-            in_specs=[
-                pl.BlockSpec((count // steps, width), lambda i, index: (index[0] * steps + i, 0)),
-                block,
-                block,
-                block,
-                block,
-            ],
-            out_specs=block,
-        ),
-        compiler_params=params(24),
+        in_specs=[
+            pl.BlockSpec((terms.shape[0], height, width), lambda i: (0, i, 0)),
+            block,
+            block,
+        ],
+        out_specs=block,
+        compiler_params=params(60),
         cost_estimate=LIGHT,
         name="finish",
-    )(index, partial, *line, rows, grads)
+    )(terms, rows, grads)
 
 
 FF_BLOCK = 256
@@ -1034,7 +1023,7 @@
     slope[...] = half + before * jnp.exp(-0.5 * before * before) * (1.0 / math.sqrt(2.0 * math.pi))
 
 
-def hidden_layer(half, normed, up, up_bias, before):
+def hidden_layer(half, width, normed, up, up_bias, before):
     rows, units = normed.shape[0], up.shape[1]
     steps = units // FF_BLOCK // 2
     block = pl.BlockSpec((rows, FF_BLOCK), lambda i: (0, i + half * steps))
@@ -1042,7 +1031,7 @@
         hidden_kernel,
         grid=(steps,),
         out_shape=[
-            jax.ShapeDtypeStruct((rows, units), jnp.bfloat16),
+            jax.ShapeDtypeStruct((rows, width + units), jnp.bfloat16),
             jax.ShapeDtypeStruct((rows, units), jnp.float32),
         ],
         in_specs=[
@@ -1051,7 +1040,10 @@
             pl.BlockSpec((1, FF_BLOCK), lambda i: (0, i + half * steps)),
         ]
         + [pl.BlockSpec(memory_space=HBM)] * len(before),
-        out_specs=[block, block],
+        out_specs=[
+            pl.BlockSpec((rows, FF_BLOCK), lambda i: (0, i + half * steps + width // FF_BLOCK)),
+            block,
+        ],
         input_output_aliases={3 + at: at for at in range(len(before))},
         compiler_params=params(60),
         cost_estimate=LIGHT,
@@ -1065,8 +1057,9 @@
     grad_bias[...] = jnp.sum(rounded.astype(jnp.float32), axis=0, keepdims=True)
 
 
-def hidden_back(half, grads, down, slope):
+def hidden_back(half, grads, mix, slope):
     rows, units = slope.shape
+    first = (mix.shape[0] - units) // FF_BLOCK
     steps = units // FF_BLOCK // 2
     return pl.pallas_call(
         hidden_back_kernel,
@@ -1079,7 +1072,7 @@
             grid=(steps,),
             in_specs=[
                 pl.BlockSpec((rows, D), lambda i, half: (0, 0)),
-                pl.BlockSpec((FF_BLOCK, D), lambda i, half: (half[0] * steps + i, 0)),
+                pl.BlockSpec((FF_BLOCK, D), lambda i, half: (first + half[0] * steps + i, 0)),
                 pl.BlockSpec((rows, FF_BLOCK), lambda i, half: (0, half[0] * steps + i)),
             ],
             out_specs=[
@@ -1090,37 +1083,7 @@
         compiler_params=params(60),
         cost_estimate=LIGHT,
         name="hidden_back",
-    )(half, grads, down, slope)
-
-
-def product_kernel(back, *refs):
-    total = None
-    for left, right in zip(refs[:-1:2], refs[1:-1:2], strict=True):
-        value = (product_back if back else matmul)(left[...], right[...])
-        total = value if total is None else total + value
-    refs[-1][...] = total.astype(refs[-1].dtype)
-
-
-def product(pairs, width, dtype, back=False):
-    rows = pairs[0][0].shape[0]
-    count = pairs[0][1].shape[0 if back else 1]
-    specs = []
-    for left, right in pairs:
-        specs.append(pl.BlockSpec(memory_space=pltpu.VMEM))
-        if back:
-            specs.append(pl.BlockSpec((width, right.shape[1]), lambda i: (i, 0)))
-        else:
-            specs.append(pl.BlockSpec((right.shape[0], width), lambda i: (0, i)))
-    return pl.pallas_call(
-        functools.partial(product_kernel, back),
-        grid=(count // width,),
-        out_shape=jax.ShapeDtypeStruct((rows, count), dtype),
-        in_specs=specs,
-        out_specs=pl.BlockSpec((rows, width), lambda i: (0, i)),
-        compiler_params=params(60),
-        cost_estimate=LIGHT,
-        name="product",
-    )(*[value for pair in pairs for value in pair])
+    )(half, grads, mix, slope)
 
 
 def norm_kernel(rows, gains, one, two, centre, scale):
@@ -1174,22 +1137,30 @@
     return jnp.where(allowed, scores, masked_score)
 
 
-def head_columns(width, head):
-    return [pl.ds(pl.multiple_of(part * width + head * HD, HD), HD) for part in range(3)]
-
-
-def attend_kernel(projected, bias, plain, lower, upper, begins, context, turned, logs):
-    rows, width = context.shape
+HEAD_PAIR = 2 * HD
+
+
+def attend_kernel(
+    normed, queries_in, keys_in, values_in, bias, plain, lower, upper, begins, _, context, turned, logs
+):
+    rows = normed.shape[0]
+    width = bias.shape[1] // 3
+    first_column = pl.program_id(0) * HEAD_PAIR
+    tables = (plain[...], lower[...], upper[...])
+    for part, weights in enumerate((queries_in, keys_in, values_in)):
+        projected = matmul(normed[...], weights[...])
+        projected = projected + bias[
+            :, pl.ds(pl.multiple_of(part * width + first_column, HEAD_PAIR), HEAD_PAIR)
+        ]
+        for head in range(2):
+            value = projected[:, head * HD : (head + 1) * HD]
+            if part < 2:
+                value = turn(value, tables, 1.0)
+            turned[part, :, head * HD : (head + 1) * HD] = value.astype(jnp.bfloat16)
 
     def one_head(head, carry):
-        cols = head_columns(width, head)
-        tables = (plain[...], lower[...], upper[...])
-        raw = [projected[:, col] + bias[:, col] for col in cols]
-        queries = turn(raw[0], tables, 1.0).astype(jnp.bfloat16)
-        keys = turn(raw[1], tables, 1.0).astype(jnp.bfloat16)
-        values = raw[2].astype(jnp.bfloat16)
-        for col, value in zip(cols, (queries, keys, values), strict=True):
-            turned[:, col] = value
+        column = pl.ds(pl.multiple_of(head * HD, HD), HD)
+        queries, keys, values = (turned[part, :, column] for part in range(3))
         for first in range(0, rows, QUERY_BLOCK):
             last = first + QUERY_BLOCK
             mine = slice(first, last)
@@ -1199,29 +1170,42 @@
             raised = jnp.exp(scores - top)
             total = jnp.sum(raised, axis=-1, keepdims=True)
             rounded = (raised / total).astype(jnp.bfloat16)
-            context[mine, cols[0]] = matmul(rounded, values[seen]).astype(jnp.bfloat16)
+            context[mine, column] = matmul(rounded, values[seen]).astype(jnp.bfloat16)
             logs[head, mine, :] = top + jnp.log(total)
         return carry
 
-    lax.fori_loop(0, width // HD, one_head, 0)
-
-
-def attend(projected, bias, tables, begins):
-    rows, width = projected.shape[0], projected.shape[1] // 3
+    lax.fori_loop(0, 2, one_head, 0)
+
+
+def attend(normed, mixer_in, bias, tables, begins, mixed):
+    rows, width = normed.shape[0], mixer_in.shape[1] // 3
+    pairs = width // HEAD_PAIR
     whole = pl.BlockSpec(memory_space=pltpu.VMEM)
+
+    def weights(part):
+        return pl.BlockSpec((mixer_in.shape[0], HEAD_PAIR), lambda i: (0, part * pairs + i))
+
     return pl.pallas_call(
         attend_kernel,
+        grid=(pairs,),
         out_shape=[
-            jax.ShapeDtypeStruct((rows, width), jnp.bfloat16),
-            jax.ShapeDtypeStruct((rows, 3 * width), jnp.bfloat16),
+            jax.ShapeDtypeStruct(mixed.shape, mixed.dtype),
+            jax.ShapeDtypeStruct((3, rows, width), jnp.bfloat16),
             jax.ShapeDtypeStruct((width // HD, rows, 1), jnp.float32),
         ],
-        in_specs=[whole] * 6,
-        out_specs=[whole] * 3,
+        in_specs=[whole, weights(0), weights(1), weights(2)]
+        + [whole] * 5
+        + [pl.BlockSpec(memory_space=HBM)],
+        out_specs=[
+            pl.BlockSpec((rows, HEAD_PAIR), lambda i: (0, i)),
+            pl.BlockSpec((3, rows, HEAD_PAIR), lambda i: (0, 0, i)),
+            pl.BlockSpec((2, rows, 1), lambda i: (i, 0, 0)),
+        ],
+        input_output_aliases={9: 0},
         compiler_params=params(60),
         cost_estimate=LIGHT,
         name="attend",
-    )(projected, bias, *tables, begins)
+    )(normed, mixer_in, mixer_in, mixer_in, bias, *tables, begins, mixed)
 
 
 def attend_back_kernel(
@@ -1231,8 +1215,8 @@
     score_scale = 1.0 / math.sqrt(HD)
 
     def one_head(head, carry):
-        cols = head_columns(width, head)
-        queries, keys, values = (turned[:, col] for col in cols)
+        cols = [pl.ds(pl.multiple_of(part * width + head * HD, HD), HD) for part in range(3)]
+        queries, keys, values = (turned[part, :, cols[0]] for part in range(3))
         key_sum[...] = jnp.zeros_like(key_sum)
         value_sum[...] = jnp.zeros_like(value_sum)
         for first in range(0, rows, QUERY_BLOCK):
@@ -1270,7 +1254,7 @@
         in_specs=[whole] * 7,
         out_specs=whole,
         scratch_shapes=[pltpu.VMEM((rows, HD), jnp.float32)] * 2,
-        compiler_params=params(60),
+        compiler_params=params(36),
         cost_estimate=LIGHT,
         name="attend_back",
     )(turned, logs, *tables, begins, grad_context)
@@ -1312,22 +1296,10 @@
     return lax.ppermute(value, "chip", [(0, 1), (1, 0)])
 
 
-def line_block(partial, index):
-    rows = partial.shape[0] // 4
-    return lax.dynamic_slice_in_dim(partial, jnp.clip(index, 0, 3) * rows, rows, 0)
-
-
-def line_leaving(partial, here, hop, came):
-    up, down = line_block(partial, here + 4 - hop), line_block(partial, here - 4 + hop)
-    if came is not None:
-        up = up + came[0].astype(jnp.float32)
-        down = down + came[1].astype(jnp.float32)
-    return up.astype(jnp.bfloat16), down.astype(jnp.bfloat16)
-
-
-def line_hop(leaving, hop):
-    ups, downs = [(i, i + 1) for i in range(hop)], [(i, i - 1) for i in range(4 - hop, 4)]
-    return lax.ppermute(leaving[0], "tensor", ups), lax.ppermute(leaving[1], "tensor", downs)
+def line_blocks(partial):
+    count = lax.axis_size("tensor")
+    rows = partial.shape[0] // count
+    return lax.all_to_all(partial.reshape(count, rows, partial.shape[1]), "tensor", 0, 0)
 
 
 def on_device_fast(
@@ -1372,53 +1344,6 @@
     def order(*values):
         return lax.optimization_barrier(values)
 
-    one, two = pack(buckets[:1], master.reshape(FLAT, LANES))
-    one_x, one_y, one_own = order(along_x(one), along_y(one), across(one))
-
-    def from_far(first, second, from_x, from_y):
-        rows = (16 // CHUNKS) * BROWS
-        start = part_row(second)
-        count = start if first == 0 else rows
-        return [along_x(from_y[:count]), along_y(from_x[start : start + rows])]
-
-    far = from_far(0, 1, one_x, one_y)
-    near_x, near_y, two_own = across(one_x), across(one_y), across(two)
-    far, near_x, near_y, two_own, two = order(far, near_x, near_y, two_own, two)
-
-    two_x, two_y = along_x(two), along_y(two)
-    far_other = [across(value) for value in far]
-    weights = []
-    for part in range(2):
-        sources = [one, one_x, one_y, far[part], one_own, near_x, near_y, far_other[part]]
-        weights = unpack(part, buckets, sources, weights)
-    weights, full_rows = order(weights, full_rows)
-    flat_bias = weights[4][:8].reshape(-1).astype(jnp.float32)
-    mixer_bias = flat_bias[: 3 * local_width]
-    expand_bias = flat_bias[3 * local_width : 3 * local_width + D]
-    small_params = flat_bias[3 * local_width + D : 3 * local_width + 7 * D].reshape(6, D)
-    full_one, full_two, centre, scale = norms(full_rows, small_params)
-    two_x, two_y, full_rows, full_one, full_two, weights = order(
-        two_x, two_y, full_rows, full_one, full_two, weights
-    )
-    other_rows = across(full_rows)
-
-    far = from_far(2, 3, two_x, two_y)
-    near_x, near_y = across(two_x), across(two_y)
-    hidden_half = hidden_layer(0, full_two, weights[2], expand_bias[None], ())
-    other_one, other_two, _, _ = norms(other_rows, small_params)
-    far, near_x, near_y, hidden_half, weights, other_one, other_two = order(
-        far, near_x, near_y, hidden_half, weights, other_one, other_two
-    )
-
-    far_other = [across(value) for value in far]
-    for part in range(2):
-        sources = [two, two_x, two_y, far[part], two_own, near_x, near_y, far_other[part]]
-        weights = unpack(2 + part, buckets, sources, weights)
-    mixer_in, mixer_out, expand_weight, shrink_weight = weights[:4]
-
-    half_width = D // 2
-    other_grads = across(lax.dynamic_slice_in_dim(grad_rows, (1 - core) * half_width, half_width, 1))
-
     rank = jnp.arange(lengths.shape[1], dtype=jnp.int32)
     seq_ends = jnp.sum(jnp.where(rank[None, :] <= rank[:, None], lengths[0][None, :], 0), axis=1)
     token_index = jnp.arange(group_rows, dtype=jnp.int32)
@@ -1427,33 +1352,76 @@
     tables = rope_tables((token_index - begins).astype(jnp.float32))
     begins = begins[:, None]
 
-    projected = product([(full_one, mixer_in)], 256, jnp.float32)
-    context, turned, logs = attend(projected, mixer_bias[None], tables, begins)
-    hidden, slope = hidden_layer(1, full_two, expand_weight, expand_bias[None], hidden_half)
-    other_context, other_hidden = across(context), across(hidden)
-    branches = product([(context, mixer_out), (hidden, shrink_weight)], 256, jnp.float32)
-    branches, turned = order(branches, turned)
+    one, two = pack(buckets[:1], master.reshape(FLAT, LANES))
+    one_x, one_y, one_own = order(along_x(one), along_y(one), across(one))
+
+    def from_far(first, second, from_x, from_y):
+        rows = (16 // CHUNKS) * BROWS
+        start = part_row(second)
+        count = start if first == 0 else rows
+        return [along_x(from_y[:count]), along_y(from_x[start : start + rows])]
+
+    far = from_far(0, 1, one_x, one_y)
+    near_x, near_y, two_own = across(one_x), across(one_y), across(two)
+    far, near_x, near_y, two_own, two, tables, begins = order(
+        far, near_x, near_y, two_own, two, tables, begins
+    )
+
+    two_x, two_y = along_x(two), along_y(two)
+    far_other = [across(value) for value in far]
+    sources = []
+    for part in range(2):
+        sources += [one, one_x, one_y, far[part], one_own, near_x, near_y, far_other[part]]
+    weights = unpack((0, 1), buckets, sources, [])
+    weights, full_rows = order(weights, full_rows)
+    flat_bias = weights[3][:8].reshape(-1).astype(jnp.float32)
+    mixer_bias = flat_bias[: 3 * local_width]
+    expand_bias = flat_bias[3 * local_width : 3 * local_width + D]
+    small_params = flat_bias[3 * local_width + D : 3 * local_width + 7 * D].reshape(6, D)
+    full_one, full_two, centre, scale = norms(full_rows, small_params)
+    hidden_half = hidden_layer(0, local_width, full_two, weights[2], expand_bias[None], ())
+    two_x, two_y, full_rows, full_one, full_two, weights, hidden_half = order(
+        two_x, two_y, full_rows, full_one, full_two, weights, hidden_half
+    )
+    other_rows = across(full_rows)
+
+    far = from_far(2, 3, two_x, two_y)
+    near_x, near_y = across(two_x), across(two_y)
+    other_one, other_two, _, _ = norms(other_rows, small_params)
+    far, near_x, near_y, hidden_half, weights, other_one, other_two = order(
+        far, near_x, near_y, hidden_half, weights, other_one, other_two
+    )
+
+    far_other = [across(value) for value in far]
+    sources = []
+    for part in range(2):
+        sources += [two, two_x, two_y, far[part], two_own, near_x, near_y, far_other[part]]
+    weights = unpack((2, 3), buckets, sources, weights)
+    mixer_in, mix_weight, expand_weight = weights[:3]
+
+    mixed, slope = hidden_layer(1, local_width, full_two, expand_weight, expand_bias[None], hidden_half)
+    mixed, turned, logs = attend(full_one, mixer_in, mixer_bias[None], tables, begins, mixed)
+    other_mixed = across(mixed)
+    branches = matmul(mixed, mix_weight)
+    branches, turned, grad_rows = order(branches, turned, grad_rows)
     branches = lax.psum_scatter(branches, "tensor", scatter_dimension=0, tiled=True)
-    output = own_rows + branches + small_params[4] + small_params[5]
-    grad_context = product([(grad_rows, mixer_out)], 256, jnp.bfloat16, back=True)
+    other_grads = across(grad_rows)
+
+    grad_context = product_back(grad_rows, mix_weight[:local_width]).astype(jnp.bfloat16)
     grad_projected = attend_back(turned, logs, tables, begins, grad_context)
-    half_in = 3 * local_width // 2
-    leaves = lax.dynamic_slice_in_dim(grad_projected, (1 - core) * half_in, half_in, 1)
-    leaves, slope = order(leaves, slope)
-    other_projected = across(leaves)
+    grad_projected, slope = order(grad_projected, slope)
+    other_projected = across(grad_projected)
     cores = core[None].astype(jnp.int32)
-    rest_before, rest_bias = hidden_back(1 - cores, grad_rows, shrink_weight, slope)
+    rest_before, rest_bias = hidden_back(1 - cores, grad_rows, mix_weight, slope)
     other_before = across(rest_before)
-    own_before, own_bias = hidden_back(cores, grad_rows, shrink_weight, slope)
+    own_before, own_bias = hidden_back(cores, grad_rows, mix_weight, slope)
     grad_expand_bias = jnp.where(
         core == 0,
         jnp.concatenate([own_bias[0], rest_bias[0]]),
         jnp.concatenate([rest_bias[0], own_bias[0]]),
     )
 
-    lefts = [
-        full_one, other_one, context, other_context, full_two, other_two, hidden, other_hidden
-    ]
+    lefts = [full_one, other_one, mixed, other_mixed, full_two, other_two, mixed, other_mixed]
     rights = [grad_projected, other_projected, grad_rows, other_grads, own_before, other_before]
     sums = weight_grads(grad_table, lefts, rights)
     grad_projected, own_before, rest_before, sums = order(
@@ -1481,17 +1449,15 @@
         bias_grad,
     )
 
-    norm_grads = norm_grads + along_line(norm_grads, 1)
-    leaving = line_leaving(partial, here, 1, None)
-    came_a, came_b, other_stays, partial, leaving, norm_grads, small, near_a, near_b = order(
-        came_a, came_b, other_stays, partial, leaving, norm_grads, small, near_a, near_b
+    for bit in (1, 2):
+        norm_grads = norm_grads + along_line(norm_grads, bit)
+    came_a, came_b, other_stays, partial, norm_grads, small, near_a, near_b = order(
+        came_a, came_b, other_stays, partial, norm_grads, small, near_a, near_b
     )
     near_a, near_b = along_x(near_a), along_y(near_b)
-    line = line_hop(leaving, 1)
+    terms = line_blocks(partial)
     pass_a = (passed[0] + came_a.astype(jnp.float32)).astype(jnp.bfloat16)
     pass_b = (passed[1] + came_b.astype(jnp.float32)).astype(jnp.bfloat16)
-    norm_grads = norm_grads + along_line(norm_grads, 2)
-    leaving = line_leaving(partial, here, 2, line)
     small = jnp.concatenate(
         [
             small[0],
@@ -1502,20 +1468,15 @@
             jnp.zeros((8 * D - 3 * local_width - 7 * D,), jnp.float32),
         ]
     ).reshape(LANES, LANES)
-    near_a, near_b, pass_a, pass_b, leaving, small, output = order(
-        near_a, near_b, pass_a, pass_b, leaving, small, output
-    )
     small = small + across(small)
+    small = small + along_x(small)
+    near_a, near_b, pass_a, pass_b, small = order(near_a, near_b, pass_a, pass_b, small)
+    output = residual[0].astype(jnp.float32) + branches + small_params[4] + small_params[5]
     far_a, far_b = along_y(pass_a), along_x(pass_b)
-    line = line_hop(leaving, 2)
     near = [near_a, near_b, across(near_a), across(near_b)]
-    leaving = line_leaving(partial, here, 3, line)
-
-    far_a, far_b, near, leaving, small = order(far_a, far_b, near, leaving, small)
-    small = small + along_x(small)
+    far_a, far_b, near, small, output = order(far_a, far_b, near, small, output)
+    far = [far_a, far_b, across(far_a), across(far_b)]
     small = small + along_y(small)
-    far = [far_a, far_b, across(far_a), across(far_b)]
-    line = line_hop(leaving, 3)
 
     step_value = step_count[0].astype(jnp.float32)
     scalars = jnp.stack(
@@ -1529,8 +1490,8 @@
     state = [v.reshape(FLAT, LANES) for v in (master, moment_one, moment_two, average)]
     table = jnp.stack([buckets[0], core.astype(jnp.int32)])
     results = adam(table, scalars, rates, [stays, other_stays], near, far, small, state)
-    line, results = order(line, results)
-    input_grad = finish(here[None].astype(jnp.int32), partial, line, residual[0], cotangent[0])
+    terms, results = order(terms, results)
+    input_grad = finish(terms, residual[0], cotangent[0])
     return (output[None], input_grad[None], *[v.reshape(master.shape) for v in results])
 
 

time: 516 us -> 467 us (0.905)
  Pallas kernels: 259 us -> 214 us
  matrix products: 0 us -> 23.2 us
  starting transfers between devices: 57.1 us -> 34 us
  local copies, waits for them, and re-layouts: 28.9 us -> 13.3 us
  waiting for transfers between devices: 124 us -> 139 us
    ppermute x6 -> x0, waiting for transfers between devices: 36.7 us -> none  [the longest x3 36.7 us: line_hop(): lax.ppermute(leaving[0], 'tensor', ups)]
    pallas_call x9 -> x4, Pallas kernels: 83.8 us -> 48.9 us  [the longest x1 22 us: attend(): pl.pallas_call(attend_kernel, grid=(pairs,), out_shape=[jax.ShapeDtypeStr...]
    ppermute x6 -> x0, starting transfers between devices: 27.7 us -> none  [the longest x3 24 us: line_hop(): lax.ppermute(leaving[0], 'tensor', ups)]
    ppermute x8, waiting for transfers between devices: 48 us -> 73.4 us  [along_x(): return lax.ppermute(value, 'dp', [(i, i ^ 1) for i in range(4)])]
    dot_general x0 -> x2, matrix products: none -> 23.2 us  [the longest x1 17.7 us: matmul(): return jnp.dot(left, right, preferred_element_type=jnp.float32)]
    ppermute x8, waiting for transfers between devices: 32.4 us -> 46.2 us  [along_y(): return lax.ppermute(value, 'dp', [(i, i ^ 2) for i in range(4)])]
    ppermute x2, waiting for transfers between devices: 0.01 us -> 8.62 us  [along_line(): return lax.ppermute(value, 'tensor', [(i, i ^ bit) for i in range(4)])]
    convert_element_type x2 -> x0, other arithmetic: 6.86 us -> none  [line_leaving(): return (up.astype(jnp.bfloat16), down.astype(jnp.bfloat16))]
  transfers between devices with their start and end apart: 49 -> 43, of which waited for: 18 -> 18; matrix products, arithmetic and copies ran while one was open for 8% -> 11% of each run, Pallas kernels for 50% -> 45%
where the time goes in v4:
time: 467 us; the launch traced here: 461 us
  Pallas kernels  214 us (46%)
  waiting for transfers between devices  139 us (30%)
  starting transfers between devices  34 us (7%)
  matrix products  23.2 us (5%)
  other arithmetic  21.3 us (5%)
  between operations  16.6 us (4%)
  local copies, waits for them, and re-layouts  13.3 us (3%)
    ppermute x8, waiting for transfers between devices, along_x(): return lax.ppermute(value, 'dp', [(i, i ^ 1) for i in range(4)])  73.4 us
    ppermute x8, waiting for transfers between devices, along_y(): return lax.ppermute(value, 'dp', [(i, i ^ 2) for i in range(4)])  46.2 us
    pallas_call x1, Pallas kernels, weight_grads(): pl.pallas_call(weight_grad_kernel, out_shape=[short] * 4 + [wide] * 2, gr...  40.5 us
    pallas_call x1, Pallas kernels, adam(): pl.pallas_call(adam_kernel, grid=(steps,), out_shape=[jax.ShapeDtypeStruc...  26.5 us
    pallas_call x1, Pallas kernels, norm_grad(): pl.pallas_call(norm_grad_kernel, out_shape=[jax.ShapeDtypeStruct((tokens,...  23.7 us
    pallas_call x1, Pallas kernels, attend(): pl.pallas_call(attend_kernel, grid=(pairs,), out_shape=[jax.ShapeDtypeStr...  22 us
    pallas_call x2, Pallas kernels, unpack(): pl.pallas_call(functools.partial(unpack_kernel, parts), out_shape=[*shape...  21.4 us
    pallas_call x2, Pallas kernels, hidden_layer(): pl.pallas_call(hidden_kernel, grid=(steps,), out_shape=[jax.ShapeDtypeStr...  20.5 us
  transfers between devices with their start and end apart: 43, of which 18 were waited for; matrix products, arithmetic and copies ran while one was open for 11% of the time, Pallas kernels for 45%

profile of v4, /device:TPU:0, one launch (start us, length us, event | category | flops | bytes accessed | tf_op | source)
XLA Modules:
  0.0 460.8 jit_solution(15890443074524181079)
XLA Ops:
  7.2 0.7 all-gather.5.cloned.1.call-update
  8.1 0.8 select_reduce_fusion.4
  9.0 2.8 copy-done.2
  11.8 2.7 pack_params.1
  14.5 3.0 collective-permute-start
  17.5 1.5 collective-permute-start.1
  19.0 34.3 %collective-permute-done.refs_1_.refs_9_ = bf16[6400,128]{1,0:T(8,128)(2,1)S(1)} collective-permute-done((bf16[6400,128]{1,0:T(8,128)(2,1)S(1)}, bf16[6400,128]{1,0:T(8,128)(2,1)S(1)}, u32[]{:S(2)}, u32[]{:S(2)}) %collective-permute-start) | collective-permute-done | bytes 1638432 | tf_op jit(solution)/shard_map/ppermute | solution.py:1278
  53.3 1.5 collective-permute-done.1.refs_2_.refs_10_
  56.2 1.7 collective-permute-start.4
  58.1 1.9 multiply_sine_fusion
  60.1 1.7 maximum_maximum_fusion.2
  61.7 1.2 collective-permute-done.7.refs_4_.refs_12_
  62.9 12.9 %collective-permute-done.4.refs_11_ = bf16[3072,128]{1,0:T(8,128)(2,1)S(1)} collective-permute-done((bf16[3072,128]{1,0:T(8,128)(2,1)S(1)}, bf16[3072,128]{1,0:T(8,128)(2,1)S(1)}, u32[]{:S(2)}, u32[]{:S(2)}) %collective-permute-start.4) | collective-permute-done | bytes 786464 | tf_op jit(solution)/shard_map/ppermute | solution.py:1282
  75.8 1.3 collective-permute-done.3.refs_3_
  77.6 1.7 collective-permute-start.9
  79.8 3.0 collective-permute-done.11.refs_15_
  82.8 0.9 copy-done.26
  83.7 10.8 %unpack_params.2 = (bf16[2048,1536]{1,0:T(8,128)(2,1)}, bf16[2560,2048]{1,0:T(8,128)(2,1)}, bf16[2048,2048]{1,0:T(8,128)(2,1)}, bf16[16,2048]{1,0:T(8,128)(2,1)}, bf16[8,256,128]{2,1,0:T(8,128)(2,1)}) custom-call(s32[8]{0:T(128)} %copy-done.11, bf16[6400,128]{1,0:T(8,128)(2,1)} %copy-done.3, bf16[6400,128]{1,0:T(8,128)(2,1)} %copy-done.14, ...), custom_call_target="tpu_custom_call" | custom-call | flops 1 | bytes 1 | tf_op jit(solution)/shard_map/unpack_params/pallas_call | solution.py:540
  94.6 0.8 convert_bitcast_fusion
  96.0 9.1 %norms.2 = (bf16[1024,2048]{1,0:T(8,128)(2,1)}, bf16[1024,2048]{1,0:T(8,128)(2,1)}, f32[1024,1]{1,0:T(8,128)}, f32[1024,1]{1,0:T(8,128)}) custom-call(bf16[1024,2048]{1,0:T(8,128)(2,1)} %bitcast.64, f32[6,2048]{1,0:T(8,128)} %reshape.89.gains), custom_call_target="tpu_custom_call" | custom-call | flops 1 | bytes 1 | tf_op jit(solution)/shard_map/norms/pallas_call | solution.py:1106
  105.7 10.2 %hidden_layer.2 = (bf16[1024,2560]{1,0:T(8,128)(2,1)}, f32[1024,2048]{1,0:T(8,128)}) custom-call(bf16[1024,2048]{1,0:T(8,128)(2,1)} %get-tuple-element.183.normed.refs_4_, bf16[2048,2048]{1,0:T(8,128)(2,1)} %get-tuple-element.177.up.refs_19_, f32[1,2048]{1,0:T(1,128)} %bitcast.81), custom_call_target="tpu_custom_call" | custom-call | flops 1 | bytes 1 | tf_op jit(solution)/shard_map/hidden_layer/pallas_call | solution.py:1030
  117.1 2.1 slice.67
  119.2 0.9 slice.68
  120.1 0.9 collective-permute-start.12
  121.0 1.1 collective-permute-start.13
  122.1 1.8 collective-permute-done.16.rows
  123.9 9.4 %norms.3 = (bf16[1024,2048]{1,0:T(8,128)(2,1)}, bf16[1024,2048]{1,0:T(8,128)(2,1)}, f32[1024,1]{1,0:T(8,128)}, f32[1024,1]{1,0:T(8,128)}) custom-call(bf16[1024,2048]{1,0:T(8,128)(2,1)} %collective-permute-done.16.rows, f32[6,2048]{1,0:T(8,128)} %reshape.89.gains), custom_call_target="tpu_custom_call" | custom-call | flops 1 | bytes 1 | tf_op jit(solution)/shard_map/norms/pallas_call | solution.py:1106
  133.2 7.0 %collective-permute-done.12.refs_3_ = bf16[3072,128]{1,0:T(8,128)(2,1)} collective-permute-done((bf16[3072,128]{1,0:T(8,128)(2,1)}, bf16[3072,128]{1,0:T(8,128)(2,1)}, u32[]{:S(2)}, u32[]{:S(2)}) %collective-permute-start.12) | collective-permute-done | bytes 786464 | tf_op jit(solution)/shard_map/ppermute | solution.py:1278
  141.4 1.0 copy.30.begins
  143.4 1.1 collective-permute-done.18.refs_15_
  144.5 0.9 copy-done.28
  145.5 10.6 %unpack_params.3 = (bf16[2048,1536]{1,0:T(8,128)(2,1)}, bf16[2560,2048]{1,0:T(8,128)(2,1)}, bf16[2048,2048]{1,0:T(8,128)(2,1)}) custom-call(s32[8]{0:T(128)} %copy-done.11, bf16[6144,128]{1,0:T(8,128)(2,1)} %copy-done.4, bf16[6144,128]{1,0:T(8,128)(2,1)} %copy-done.15, ...), custom_call_target="tpu_custom_call", output_to_operand_aliasing={{0}: (18, {}), {1}: (19, {}), {2}: (20, {})} | custom-call | flops 1 | bytes 1 | tf_op jit(solution)/shard_map/unpack_params/pallas_call | solution.py:540
  156.1 10.2 %hidden_layer.3 = (bf16[1024,2560]{1,0:T(8,128)(2,1)}, f32[1024,2048]{1,0:T(8,128)}) custom-call(bf16[1024,2048]{1,0:T(8,128)(2,1)} %get-tuple-element.183.normed.refs_4_, bf16[2048,2048]{1,0:T(8,128)(2,1)} %get-tuple-element.184.up.own_up.rest_up, f32[1,2048]{1,0:T(1,128)} %bitcast.82, ...), custom_call_target="tpu_custom_call", output_to_operand_aliasing={{0}: (3, {}), {1}: (4, {})} | custom-call | flops 1 | bytes 1 | tf_op jit(solution)/shard_map/hidden_layer/pallas_call | solution.py:1030
  166.3 22.0 %attend.1 = (bf16[1024,2560]{1,0:T(8,128)(2,1)}, bf16[3,1024,512]{2,1,0:T(8,128)(2,1)}, f32[4,1024,1]{2,1,0:T(8,128)}) custom-call(bf16[1024,2048]{1,0:T(8,128)(2,1)} %get-tuple-element.157.normed.refs_0_, bf16[2048,1536]{1,0:T(8,128)(2,1)} %get-tuple-element.178.queries_in.keys_in.values_in.mixer_in, ...), custom_call_target="tpu_custom_call", output_to_operand_aliasing={{0}: (9, {})} | custom-call | flops 1 | bytes 1 | tf_op jit(solution)/shard_map/attend/pallas_call | solution.py:1188
  188.3 17.7 %fusion.9 = f32[1024,2048]{1,0:T(8,128)} fusion(bf16[1024,2560]{1,0:T(8,128)(2,1)} %get-tuple-element.188.refs_2_.refs_6_, bf16[2560,2048]{1,0:T(8,128)(2,1)} %get-tuple-element.189.down), kind=kOutput, calls=%fused_computation.55 | convolution fusion | flops 10737418240 | bytes 24117248 | tf_op jit(solution)/shard_map/dot_general | solution.py:27
  206.7 5.5 %fusion.4.grad_context = bf16[1024,512]{1,0:T(8,128)(2,1)S(1)} fusion(bf16[1024,2048]{1,0:T(8,128)(2,1)} %bitcast.59, bf16[2560,2048]{1,0:T(8,128)(2,1)} %get-tuple-element.189.down), kind=kOutput, calls=%fused_computation.9 | convolution fusion | flops 2148007936 | bytes 7340032 | tf_op jit(solution)/shard_map/dot_general | solution.py:37
  212.3 12.8 %attend_back.1.refs_8_.grad_projected = bf16[1024,1536]{1,0:T(8,128)(2,1)S(1)} custom-call(bf16[3,1024,512]{2,1,0:T(8,128)(2,1)S(1)} %copy-done.9, f32[4,1024,1]{2,1,0:T(8,128)S(1)} %copy-done.10, f32[1024,128]{1,0:T(8,128)S(1)} %copy-done.8, f32[1024,128]{1,0:T(8,128)S(1)} %copy-done.7, f32[1024,128]{1,0:T(8,128)S(1)} %copy-done.6, ...), custom_call_target="tpu_custom_call" | custom-call | flops 1 | bytes 1 | tf_op jit(solution)/shard_map/attend_back/pallas_call | solution.py:1251
  225.4 10.4 %hidden_back.3 = (bf16[1024,1024]{1,0:T(8,128)(2,1)}, f32[1,1024]{1,0:T(1,128)}) custom-call(s32[1]{0:T(128)S(6)} %sub.30.half, bf16[1024,2048]{1,0:T(8,128)(2,1)} %bitcast.60, bf16[2560,2048]{1,0:T(8,128)(2,1)} %get-tuple-element.189.down, f32[1024,2048]{1,0:T(8,128)} %get-tuple-element.196.slope), custom_call_target="tpu_custom_call" | custom-call | flops 1 | bytes 1 | tf_op jit(solution)/shard_map/hidden_back/pallas_call | solution.py:1064
  236.6 9.4 %hidden_back.2 = (bf16[1024,1024]{1,0:T(8,128)(2,1)}, f32[1,1024]{1,0:T(1,128)}) custom-call(s32[1]{0:T(128)} %bitcast.14.half.core, bf16[1024,2048]{1,0:T(8,128)(2,1)} %bitcast.61, bf16[2560,2048]{1,0:T(8,128)(2,1)} %get-tuple-element.189.down, f32[1024,2048]{1,0:T(8,128)} %get-tuple-element.196.slope), custom_call_target="tpu_custom_call" | custom-call | flops 1 | bytes 1 | tf_op jit(solution)/shard_map/hidden_back/pallas_call | solution.py:1064
  246.1 40.5 %weight_grads.1 = (bf16[2,3136,128]{2,1,0:T(8,128)(2,1)}, bf16[2,3136,128]{2,1,0:T(8,128)(2,1)}, bf16[2,3136,128]{2,1,0:T(8,128)(2,1)}, bf16[2,3136,128]{2,1,0:T...) custom-call(s32[33]{0:T(128)} %concatenate.24.table, ...), custom_call_target="tpu_custom_call" | custom-call | flops 1 | bytes 1 | tf_op jit(solution)/shard_map/weight_grads/pallas_call | solution.py:748
  287.1 1.6 collective-permute-start.23
  289.7 2.8 convert_reduce_fusion
  292.6 23.7 %norm_grad.1 = (bf16[1024,2048]{1,0:T(8,128)(2,1)}, f32[4,2048]{1,0:T(4,128)}) custom-call(s32[1]{0:T(128)} %bitcast.14.half.core, bf16[1024,1536]{1,0:T(8,128)(2,1)} %copy-done, bf16[2048,1536]{1,0:T(8,128)(2,1)} %get-tuple-element.178.queries_in.keys_in.values_in.mixer_in, bf16[1024,1024]{1,0:T(8,128)(2,1)} %get-tuple-element.211.refs_12_.own_before, ...), custom_call_target="tpu_custom_call" | custom-call | flops 1 | bytes 1 | tf_op jit(solution)/shard_map/norm_grad/pallas_call | solution.py:796
  316.3 1.8 collective-permute-start.26
  318.1 4.3 collective-permute-done.26
  322.4 0.8 add.110
  323.2 1.7 collective-permute-start.27
  325.3 4.3 collective-permute-done.27
  329.7 5.1 %all-to-all-start = ((bf16[4,256,2048]{2,1,0:T(8,128)(2,1)}), bf16[4,256,2048]{2,1,0:T(8,128)(2,1)}, u32[]{:S(2)}, u32[]{:S(2)}) async-start(bf16[4,256,2048]{2,1,0:T(8,128)(2,1)} %bitcast.71), calls=%async_computation.1 | async-start | bytes 8388608 | tf_op jit(solution)/shard_map/all_to_all | solution.py:1302
  335.0 1.6 collective-permute-start.28
  336.5 1.3 collective-permute-start.29
  337.9 0.8 collective-permute-start.31
  338.7 5.7 %fusion = (bf16[2,3136,128]{2,1,0:T(8,128)(2,1)S(1)}, bf16[2,3136,128]{2,1,0:T(8,128)(2,1)}) fusion(bf16[2,3136,128]{2,1,0:T(8,128)(2,1)} %collective-permute-done.24, f32[2,2,3136,128]{3,2,1,0:T(8,128)} %get-tuple-element.223, bf16[2,3136,128]{2,1,0:T(8,128)(2,1)} %collective-permute-done.23), kind=kLoop, calls=%fused_computation.3 | loop fusion | flops 4816896 | bytes 12845056 | tf_op jit(solution)/shard_map/convert_element_type | solution.py:1460
  344.3 29.8 %collective-permute-done.31 = f32[128,128]{1,0:T(8,128)S(1)} collective-permute-done((f32[128,128]{1,0:T(8,128)S(1)}, f32[128,128]{1,0:T(8,128)S(1)}, u32[]{:S(2)}, u32[]{:S(2)}) %collective-permute-start.31) | collective-permute-done | bytes 65568 | tf_op jit(solution)/shard_map/ppermute | solution.py:1278
  374.1 1.6 collective-permute-start.32
  375.7 1.3 collective-permute-start.33
  377.5 2.2 reduce-scatter.2.cloned.1.call-done
  379.7 3.3 add_add_fusion
  383.1 28.2 %collective-permute-done.32.refs_6_ = bf16[2,3136,128]{2,1,0:T(8,128)(2,1)} collective-permute-done((bf16[2,3136,128]{2,1,0:T(8,128)(2,1)}, bf16[2,3136,128]{2,1,0:T(8,128)(2,1)}, u32[]{:S(2)}, u32[]{:S(2)}) %collective-permute-start.32) | collective-permute-done | bytes 1605664 | tf_op jit(solution)/shard_map/ppermute | solution.py:1282
  411.3 1.0 collective-permute-done.33.refs_7_
  416.7 3.0 collective-permute-done.38
  420.4 1.1 copy-done.22
  422.1 26.5 %adam.1 = (f32[12304,128]{1,0:T(8,128)}, f32[12304,128]{1,0:T(8,128)}, f32[12304,128]{1,0:T(8,128)}, f32[12304,128]{1,0:T(8,128)}, f32[12304,128]{1,0:T(8,128)}) custom-call(s32[2]{0:T(128)} %pad_add_fusion.table, f32[4]{0:T(128)} %pad_maximum_fusion.1.scalar_ref, f32[8]{0:T(128)} %rate_ref.1, f32[2,2,3136,128]{3,2,1,0:T(8,128)} %get-tuple-element.209.refs_0_, ...), custom_call_target="tpu_custom_call" | custom-call | flops 1 | bytes 1 | tf_op jit(solution)/shard_map/adam/pallas_call | solution.py:961
  448.6 5.5 %finish.1 = f32[256,2048]{1,0:T(8,128)} custom-call(bf16[4,256,2048]{2,1,0:T(8,128)(2,1)} %all-to-all-done.terms, bf16[256,2048]{1,0:T(8,128)(2,1)} %bitcast.67, bf16[256,2048]{1,0:T(8,128)(2,1)} %bitcast.72), custom_call_target="tpu_custom_call" | custom-call | flops 1 | bytes 1 | tf_op jit(solution)/shard_map/finish/pallas_call | solution.py:999
  (157 shorter events, 15.6 us)
Async XLA Ops:
  7.2 87.4 %all-gather.5.cloned.1.call-start = ((), (), s32[]{:S(2)}) async-start(), calls=%async_computation.3 | async-start | bytes 5242880 | tf_op jit(solution)/shard_map/all_gather | solution.py:1340
  7.9 47.5 %copy-start.31 = (s32[1,5]{1,0:T(1,128)S(1)}, s32[1,5]{1,0:T(1,128)}, u32[]{:S(2)}) copy-start(s32[1,5]{1,0:T(1,128)} %param.14) | copy-start | bytes 64
  7.9 198.1 %all-gather.7.cloned.1.call-start = ((), (), s32[]{:S(2)}) async-start(), calls=%async_computation.4 | async-start | bytes 5242880 | tf_op jit(solution)/shard_map/all_gather | solution.py:1341
  9.0 46.7 %copy-start.11 = (s32[8]{0:T(128)}, s32[8]{0:T(128)S(1)}, u32[]{:S(2)}) copy-start(s32[8]{0:T(128)S(1)} %select_reduce_fusion.3.bucket_ref) | copy-start | bytes 100
  14.5 47.2 %copy-start.3 = (bf16[6400,128]{1,0:T(8,128)(2,1)}, bf16[6400,128]{1,0:T(8,128)(2,1)S(1)}, u32[]{:S(2)}) copy-start(bf16[6400,128]{1,0:T(8,128)(2,1)S(1)} %get-tuple-element.132.refs_0_.refs_8_) | copy-start | bytes 4915204
  14.5 63.1 %copy-start.4 = (bf16[6144,128]{1,0:T(8,128)(2,1)}, bf16[6144,128]{1,0:T(8,128)(2,1)S(1)}, u32[]{:S(2)}) copy-start(bf16[6144,128]{1,0:T(8,128)(2,1)S(1)} %get-tuple-element.136.refs_0_.refs_8_) | copy-start | bytes 4718596
  14.5 38.8 %collective-permute-start = (bf16[6400,128]{1,0:T(8,128)(2,1)S(1)}, bf16[6400,128]{1,0:T(8,128)(2,1)S(1)}, u32[]{:S(2)}, u32[]{:S(2)}) collective-permute-start(bf16[6400,128]{1,0:T(8,128)(2,1)S(1)} %get-tuple-element.132.refs_0_.refs_8_), channel_id=1, source_target_pairs={{0,8},{8,0},{16,24},{24,16},{1,9},{9,1},{17,25},{25,17},{2,10},{10... | collective-permute-start | bytes 4915208 | tf_op jit(solution)/shard_map/ppermute | solution.py:1278
  17.5 37.3 %collective-permute-start.1 = (bf16[6400,128]{1,0:T(8,128)(2,1)S(1)}, bf16[6400,128]{1,0:T(8,128)(2,1)S(1)}, u32[]{:S(2)}, u32[]{:S(2)}) collective-permute-start(bf16[6400,128]{1,0:T(8,128)(2,1)S(1)} %get-tuple-element.132.refs_0_.refs_8_), channel_id=1, source_target_pairs={{0,16},{8,24},{16,0},{24,8},{1,17},{9,25},{17,1},{25,9},{2,18},{10... | collective-permute-start | bytes 4915208 | tf_op jit(solution)/shard_map/ppermute | solution.py:1282
  19.0 35.7 %collective-permute-start.2 = (bf16[6400,128]{1,0:T(8,128)(2,1)S(1)}, bf16[6400,128]{1,0:T(8,128)(2,1)S(1)}, u32[]{:S(2)}, u32[]{:S(2)}) collective-permute-start(bf16[6400,128]{1,0:T(8,128)(2,1)S(1)} %get-tuple-element.132.refs_0_.refs_8_), channel_id=1, source_target_pairs={{0,1},{1,0},{2,3},{3,2},{4,5},{5,4},{6,7},{7,6},{8,9},{9,8},{10,11... | collective-permute-start | bytes 4915208 | tf_op jit(solution)/shard_map/ppermute | solution.py:1296
  53.3 8.4 %copy-start.14 = (bf16[6400,128]{1,0:T(8,128)(2,1)}, bf16[6400,128]{1,0:T(8,128)(2,1)S(1)}, u32[]{:S(2)}) copy-start(bf16[6400,128]{1,0:T(8,128)(2,1)S(1)} %collective-permute-done.refs_1_.refs_9_) | copy-start | bytes 4915204
  54.8 6.9 %copy-start.13 = (bf16[6400,128]{1,0:T(8,128)(2,1)}, bf16[6400,128]{1,0:T(8,128)(2,1)S(1)}, u32[]{:S(2)}) copy-start(bf16[6400,128]{1,0:T(8,128)(2,1)S(1)} %collective-permute-done.1.refs_2_.refs_10_) | copy-start | bytes 4915204
  54.8 6.9 %copy-start.17 = (bf16[6400,128]{1,0:T(8,128)(2,1)}, bf16[6400,128]{1,0:T(8,128)(2,1)S(1)}, u32[]{:S(2)}) copy-start(bf16[6400,128]{1,0:T(8,128)(2,1)S(1)} %collective-permute-done.2.refs_4_.refs_12_) | copy-start | bytes 4915204
  54.8 22.4 %collective-permute-start.5 = (bf16[6400,128]{1,0:T(8,128)(2,1)S(1)}, bf16[6400,128]{1,0:T(8,128)(2,1)S(1)}, u32[]{:S(2)}, u32[]{:S(2)}) collective-permute-start(bf16[6400,128]{1,0:T(8,128)(2,1)S(1)} %collective-permute-done.refs_1_.refs_9_), channel_id=1, source_target_pairs={{0,1},{1,0},{2,3},{3,2},{4,5},{5,4},{6,7},{7,6},{8,9},{9,8},{10,11... | collective-permute-start | bytes 4915208 | tf_op jit(solution)/shard_map/ppermute | solution.py:1296
  54.9 22.3 %collective-permute-start.6 = (bf16[6400,128]{1,0:T(8,128)(2,1)S(1)}, bf16[6400,128]{1,0:T(8,128)(2,1)S(1)}, u32[]{:S(2)}, u32[]{:S(2)}) collective-permute-start(bf16[6400,128]{1,0:T(8,128)(2,1)S(1)} %collective-permute-done.1.refs_2_.refs_10_), channel_id=1, source_target_pairs={{0,1},{1,0},{2,3},{3,2},{4,5},{5,4},{6,7},{7,6},{8,9},{9,8},{10,11... | collective-permute-start | bytes 4915208 | tf_op jit(solution)/shard_map/ppermute | solution.py:1296
  55.4 7.6 %collective-permute-start.7 = (bf16[6144,128]{1,0:T(8,128)(2,1)S(1)}, bf16[6144,128]{1,0:T(8,128)(2,1)S(1)}, u32[]{:S(2)}, u32[]{:S(2)}) collective-permute-start(bf16[6144,128]{1,0:T(8,128)(2,1)S(1)} %get-tuple-element.136.refs_0_.refs_8_), channel_id=1, source_target_pairs={{0,1},{1,0},{2,3},{3,2},{4,5},{5,4},{6,7},{7,6},{8,9},{9,8},{10,11... | collective-permute-start | bytes 4718600 | tf_op jit(solution)/shard_map/ppermute | solution.py:1296
  55.8 21.4 %collective-permute-start.3 = (bf16[3328,128]{1,0:T(8,128)(2,1)S(1)}, bf16[3328,128]{1,0:T(8,128)(2,1)S(1)}, u32[]{:S(2)}, u32[]{:S(2)}) collective-permute-start(bf16[3328,128]{1,0:T(8,128)(2,1)S(1)} %slice.62), channel_id=1, source_target_pairs={{0,8},{8,0},{16,24},{24,16},{1,9},{9,1},{17,25},{25,17},{2,10},{10... | collective-permute-start | bytes 2555912 | tf_op jit(solution)/shard_map/ppermute | solution.py:1278
  56.2 19.6 %collective-permute-start.4 = (bf16[3072,128]{1,0:T(8,128)(2,1)S(1)}, bf16[3072,128]{1,0:T(8,128)(2,1)S(1)}, u32[]{:S(2)}, u32[]{:S(2)}) collective-permute-start(bf16[3072,128]{1,0:T(8,128)(2,1)S(1)} %slice.63), channel_id=1, source_target_pairs={{0,16},{8,24},{16,0},{24,8},{1,17},{9,25},{17,1},{25,9},{2,18},{10... | collective-permute-start | bytes 2359304 | tf_op jit(solution)/shard_map/ppermute | solution.py:1282
  62.9 16.9 %copy-start.20 = (bf16[6144,128]{1,0:T(8,128)(2,1)}, bf16[6144,128]{1,0:T(8,128)(2,1)S(1)}, u32[]{:S(2)}) copy-start(bf16[6144,128]{1,0:T(8,128)(2,1)S(1)} %collective-permute-done.7.refs_4_.refs_12_) | copy-start | bytes 4718596
  75.8 7.0 %copy-start.25 = (bf16[3072,128]{1,0:T(8,128)(2,1)}, bf16[3072,128]{1,0:T(8,128)(2,1)S(1)}, u32[]{:S(2)}) copy-start(bf16[3072,128]{1,0:T(8,128)(2,1)S(1)} %collective-permute-done.4.refs_11_) | copy-start | bytes 2359300
  77.2 38.8 %collective-permute-start.8 = (bf16[6144,128]{1,0:T(8,128)(2,1)S(1)}, bf16[6144,128]{1,0:T(8,128)(2,1)S(1)}, u32[]{:S(2)}, u32[]{:S(2)}) collective-permute-start(bf16[6144,128]{1,0:T(8,128)(2,1)S(1)} %get-tuple-element.136.refs_0_.refs_8_), channel_id=1, source_target_pairs={{0,8},{8,0},{16,24},{24,16},{1,9},{9,1},{17,25},{25,17},{2,10},{10... | collective-permute-start | bytes 4718600 | tf_op jit(solution)/shard_map/ppermute | solution.py:1278
  77.6 38.3 %collective-permute-start.9 = (bf16[6144,128]{1,0:T(8,128)(2,1)S(1)}, bf16[6144,128]{1,0:T(8,128)(2,1)}, u32[]{:S(2)}, u32[]{:S(2)}) collective-permute-start(bf16[6144,128]{1,0:T(8,128)(2,1)S(1)} %get-tuple-element.136.refs_0_.refs_8_), channel_id=1, source_target_pairs={{0,16},{8,24},{16,0},{24,8},{1,17},{9,25},{17,1},{25,9},{2,18},{10... | collective-permute-start | bytes 4718600 | tf_op jit(solution)/shard_map/ppermute | solution.py:1282
  79.3 4.4 collective-permute-start.10
  79.3 3.5 collective-permute-start.11
  115.9 17.3 %copy-start.15 = (bf16[6144,128]{1,0:T(8,128)(2,1)}, bf16[6144,128]{1,0:T(8,128)(2,1)S(1)}, u32[]{:S(2)}) copy-start(bf16[6144,128]{1,0:T(8,128)(2,1)S(1)} %collective-permute-done.8.refs_1_.refs_9_) | copy-start | bytes 4718596
  116.0 7.9 %collective-permute-start.16 = (bf16[1024,2048]{1,0:T(8,128)(2,1)}, bf16[1024,2048]{1,0:T(8,128)(2,1)}, u32[]{:S(2)}, u32[]{:S(2)}) collective-permute-start(bf16[1024,2048]{1,0:T(8,128)(2,1)} %bitcast.65), channel_id=1, source_target_pairs={{0,1},{1,0},{2,3},{3,2},{4,5},{5,4},{6,7},{7,6},{8,9},{9,8},{10,11... | collective-permute-start | bytes 12582920 | tf_op jit(solution)/shard_map/ppermute | solution.py:1296
  116.2 263.6 %reduce-scatter.2.cloned.1.call-start = ((), (), s32[]{:S(2)}) async-start(), calls=%async_computation.2 | async-start | bytes 10485760 | tf_op jit(solution)/shard_map/reduce_scatter | solution.py:1407
  116.5 24.3 %collective-permute-start.14 = (bf16[6144,128]{1,0:T(8,128)(2,1)S(1)}, bf16[6144,128]{1,0:T(8,128)(2,1)S(1)}, u32[]{:S(2)}, u32[]{:S(2)}) collective-permute-start(bf16[6144,128]{1,0:T(8,128)(2,1)S(1)} %collective-permute-done.8.refs_1_.refs_9_), channel_id=1, source_target_pairs={{0,1},{1,0},{2,3},{3,2},{4,5},{5,4},{6,7},{7,6},{8,9},{9,8},{10,11... | collective-permute-start | bytes 4718600 | tf_op jit(solution)/shard_map/ppermute | solution.py:1296
  117.0 23.9 %collective-permute-start.15 = (bf16[6144,128]{1,0:T(8,128)(2,1)}, bf16[6144,128]{1,0:T(8,128)(2,1)}, u32[]{:S(2)}, u32[]{:S(2)}) collective-permute-start(bf16[6144,128]{1,0:T(8,128)(2,1)} %collective-permute-done.9.refs_2_.refs_10_), channel_id=1, source_target_pairs={{0,1},{1,0},{2,3},{3,2},{4,5},{5,4},{6,7},{7,6},{8,9},{9,8},{10,11... | collective-permute-start | bytes 4718600 | tf_op jit(solution)/shard_map/ppermute | solution.py:1296
  120.1 20.1 %collective-permute-start.12 = (bf16[3072,128]{1,0:T(8,128)(2,1)}, bf16[3072,128]{1,0:T(8,128)(2,1)}, u32[]{:S(2)}, u32[]{:S(2)}) collective-permute-start(bf16[3072,128]{1,0:T(8,128)(2,1)} %slice.67), channel_id=1, source_target_pairs={{0,8},{8,0},{16,24},{24,16},{1,9},{9,1},{17,25},{25,17},{2,10},{10... | collective-permute-start | bytes 2359304 | tf_op jit(solution)/shard_map/ppermute | solution.py:1278
  121.0 19.8 %collective-permute-start.13 = (bf16[3072,128]{1,0:T(8,128)(2,1)}, bf16[3072,128]{1,0:T(8,128)(2,1)}, u32[]{:S(2)}, u32[]{:S(2)}) collective-permute-start(bf16[3072,128]{1,0:T(8,128)(2,1)} %slice.68), channel_id=1, source_target_pairs={{0,16},{8,24},{16,0},{24,8},{1,17},{9,25},{17,1},{25,9},{2,18},{10... | collective-permute-start | bytes 2359304 | tf_op jit(solution)/shard_map/ppermute | solution.py:1282
  140.8 2.6 collective-permute-start.17
  140.9 3.6 collective-permute-start.18
  206.0 6.2 %copy-start.5 = (s32[1024,1]{1,0:T(8,128)S(1)}, s32[1024,1]{1,0:T(8,128)}, u32[]{:S(2)}) copy-start(s32[1024,1]{1,0:T(8,128)} %copy.30.begins) | copy-start | bytes 12292
  206.0 6.2 %copy-start.6 = (f32[1024,128]{1,0:T(8,128)S(1)}, f32[1024,128]{1,0:T(8,128)}, u32[]{:S(2)}) copy-start(f32[1024,128]{1,0:T(8,128)} %get-tuple-element.181.upper) | copy-start | bytes 1572868
  206.0 6.2 %copy-start.7 = (f32[1024,128]{1,0:T(8,128)S(1)}, f32[1024,128]{1,0:T(8,128)}, u32[]{:S(2)}) copy-start(f32[1024,128]{1,0:T(8,128)} %get-tuple-element.180.lower) | copy-start | bytes 1572868
  206.1 6.2 %copy-start.8 = (f32[1024,128]{1,0:T(8,128)S(1)}, f32[1024,128]{1,0:T(8,128)}, u32[]{:S(2)}) copy-start(f32[1024,128]{1,0:T(8,128)} %get-tuple-element.179.plain) | copy-start | bytes 1572868
  206.1 6.2 %copy-start.9 = (bf16[3,1024,512]{2,1,0:T(8,128)(2,1)S(1)}, bf16[3,1024,512]{2,1,0:T(8,128)(2,1)}, u32[]{:S(2)}) copy-start(bf16[3,1024,512]{2,1,0:T(8,128)(2,1)} %get-tuple-element.191.turned) | copy-start | bytes 9437188
  206.1 40.0 %collective-permute-start.19 = (bf16[1024,2560]{1,0:T(8,128)(2,1)}, bf16[1024,2560]{1,0:T(8,128)(2,1)}, u32[]{:S(2)}, u32[]{:S(2)}) collective-permute-start(bf16[1024,2560]{1,0:T(8,128)(2,1)} %get-tuple-element.188.refs_2_.refs_6_), channel_id=1, source_target_pairs={{0,1},{1,0},{2,3},{3,2},{4,5},{5,4},{6,7},{7,6},{8,9},{9,8},{10,11... | collective-permute-start | bytes 15728648 | tf_op jit(solution)/shard_map/ppermute | solution.py:1296
  206.3 39.7 %collective-permute-start.21 = (bf16[1024,2048]{1,0:T(8,128)(2,1)}, bf16[1024,2048]{1,0:T(8,128)(2,1)}, u32[]{:S(2)}, u32[]{:S(2)}) collective-permute-start(bf16[1024,2048]{1,0:T(8,128)(2,1)} %bitcast.58), channel_id=1, source_target_pairs={{0,1},{1,0},{2,3},{3,2},{4,5},{5,4},{6,7},{7,6},{8,9},{9,8},{10,11... | collective-permute-start | bytes 12582920 | tf_op jit(solution)/shard_map/ppermute | solution.py:1296
  225.1 10.6 %copy-start = (bf16[1024,1536]{1,0:T(8,128)(2,1)}, bf16[1024,1536]{1,0:T(8,128)(2,1)S(1)}, u32[]{:S(2)}) copy-start(bf16[1024,1536]{1,0:T(8,128)(2,1)S(1)} %attend_back.1.refs_8_.grad_projected) | copy-start | bytes 9437188
  225.1 20.9 %collective-permute-start.20 = (bf16[1024,1536]{1,0:T(8,128)(2,1)S(1)}, bf16[1024,1536]{1,0:T(8,128)(2,1)}, u32[]{:S(2)}, u32[]{:S(2)}) collective-permute-start(bf16[1024,1536]{1,0:T(8,128)(2,1)S(1)} %attend_back.1.refs_8_.grad_projected), channel_id=1, source_target_pairs={{0,1},{1,0},{2,3},{3,2},{4,5},{5,4},{6,7},{7,6},{8,9},{9,8},{10,11... | collective-permute-start | bytes 9437192 | tf_op jit(solution)/shard_map/ppermute | solution.py:1296
  225.4 10.5 %copy-start.12 = (s32[8]{0:T(128)S(1)}, s32[8]{0:T(128)}, u32[]{:S(2)}) copy-start(s32[8]{0:T(128)} %copy-done.11) | copy-start | bytes 100
  235.7 10.3 %collective-permute-start.22 = (bf16[1024,1024]{1,0:T(8,128)(2,1)}, bf16[1024,1024]{1,0:T(8,128)(2,1)}, u32[]{:S(2)}, u32[]{:S(2)}) collective-permute-start(bf16[1024,1024]{1,0:T(8,128)(2,1)} %get-tuple-element.212.rest_before), channel_id=1, source_target_pairs={{0,1},{1,0},{2,3},{3,2},{4,5},{5,4},{6,7},{7,6},{8,9},{9,8},{10,11... | collective-permute-start | bytes 6291464 | tf_op jit(solution)/shard_map/ppermute | solution.py:1296
  286.5 43.1 %collective-permute-start.25 = (f32[2,2,3136,128]{3,2,1,0:T(8,128)}, f32[2,2,3136,128]{3,2,1,0:T(8,128)}, u32[]{:S(2)}, u32[]{:S(2)}) collective-permute-start(f32[2,2,3136,128]{3,2,1,0:T(8,128)} %get-tuple-element.209.refs_0_), channel_id=1, source_target_pairs={{0,1},{1,0},{2,3},{3,2},{4,5},{5,4},{6,7},{7,6},{8,9},{9,8},{10,11... | collective-permute-start | bytes 19267592 | tf_op jit(solution)/shard_map/ppermute | solution.py:1296
  287.1 42.6 %collective-permute-start.23 = (bf16[2,3136,128]{2,1,0:T(8,128)(2,1)}, bf16[2,3136,128]{2,1,0:T(8,128)(2,1)}, u32[]{:S(2)}, u32[]{:S(2)}) collective-permute-start(bf16[2,3136,128]{2,1,0:T(8,128)(2,1)} %get-tuple-element.207), channel_id=1, source_target_pairs={{0,8},{8,0},{16,24},{24,16},{1,9},{9,1},{17,25},{25,17},{2,10},{10... | collective-permute-start | bytes 4816904 | tf_op jit(solution)/shard_map/ppermute | solution.py:1278
  288.7 41.0 %collective-permute-start.24 = (bf16[2,3136,128]{2,1,0:T(8,128)(2,1)}, bf16[2,3136,128]{2,1,0:T(8,128)(2,1)}, u32[]{:S(2)}, u32[]{:S(2)}) collective-permute-start(bf16[2,3136,128]{2,1,0:T(8,128)(2,1)} %get-tuple-element.208), channel_id=1, source_target_pairs={{0,16},{8,24},{16,0},{24,8},{1,17},{9,25},{17,1},{25,9},{2,18},{10... | collective-permute-start | bytes 4816904 | tf_op jit(solution)/shard_map/ppermute | solution.py:1282
  292.6 25.5 %copy-start.29 = (f32[1,1024]{1,0:T(1,128)S(1)}, f32[1,1024]{1,0:T(1,128)}, u32[]{:S(2)}) copy-start(f32[1,1024]{1,0:T(1,128)} %get-tuple-element.218) | copy-start | bytes 12292
  292.6 25.5 %copy-start.30 = (f32[1,1024]{1,0:T(1,128)S(1)}, f32[1,1024]{1,0:T(1,128)}, u32[]{:S(2)}) copy-start(f32[1,1024]{1,0:T(1,128)} %get-tuple-element.217) | copy-start | bytes 12292
  292.6 32.3 %copy-start.1 = (bf16[1024,1536]{1,0:T(8,128)(2,1)S(1)}, bf16[1024,1536]{1,0:T(8,128)(2,1)}, u32[]{:S(2)}) copy-start(bf16[1024,1536]{1,0:T(8,128)(2,1)} %copy-done) | copy-start | bytes 9437188
  316.3 6.1 %collective-permute-start.26 = (f32[4,2048]{1,0:T(4,128)}, f32[4,2048]{1,0:T(4,128)S(1)}, u32[]{:S(2)}, u32[]{:S(2)}) collective-permute-start(f32[4,2048]{1,0:T(4,128)} %get-tuple-element.216), channel_id=1, source_target_pairs={{0,2},{2,0},{4,6},{6,4},{1,3},{3,1},{5,7},{7,5},{8,10},{10,8},{12,... | collective-permute-start | bytes 98312 | tf_op jit(solution)/shard_map/ppermute | solution.py:1286
  323.2 6.5 %collective-permute-start.27 = (f32[4,2048]{1,0:T(4,128)S(1)}, f32[4,2048]{1,0:T(4,128)S(1)}, u32[]{:S(2)}, u32[]{:S(2)}) collective-permute-start(f32[4,2048]{1,0:T(4,128)S(1)} %add.110), channel_id=1, source_target_pairs={{0,4},{2,6},{4,0},{6,2},{1,5},{3,7},{5,1},{7,3},{8,12},{10,14},{12... | collective-permute-start | bytes 98312 | tf_op jit(solution)/shard_map/ppermute | solution.py:1286
  329.7 118.9 %all-to-all-start = ((bf16[4,256,2048]{2,1,0:T(8,128)(2,1)}), bf16[4,256,2048]{2,1,0:T(8,128)(2,1)}, u32[]{:S(2)}, u32[]{:S(2)}) async-start(bf16[4,256,2048]{2,1,0:T(8,128)(2,1)} %bitcast.71), calls=%async_computation.1 | async-start | bytes 8388608 | tf_op jit(solution)/shard_map/all_to_all | solution.py:1302
  334.9 3.0 collective-permute-start.30
  335.0 39.1 %collective-permute-start.28 = (bf16[2,3136,128]{2,1,0:T(8,128)(2,1)}, bf16[2,3136,128]{2,1,0:T(8,128)(2,1)}, u32[]{:S(2)}, u32[]{:S(2)}) collective-permute-start(bf16[2,3136,128]{2,1,0:T(8,128)(2,1)} %get-tuple-element.221), channel_id=1, source_target_pairs={{0,8},{8,0},{16,24},{24,16},{1,9},{9,1},{17,25},{25,17},{2,10},{10... | collective-permute-start | bytes 4816904 | tf_op jit(solution)/shard_map/ppermute | solution.py:1278
  336.5 37.6 %collective-permute-start.29 = (bf16[2,3136,128]{2,1,0:T(8,128)(2,1)}, bf16[2,3136,128]{2,1,0:T(8,128)(2,1)}, u32[]{:S(2)}, u32[]{:S(2)}) collective-permute-start(bf16[2,3136,128]{2,1,0:T(8,128)(2,1)} %get-tuple-element.222), channel_id=1, source_target_pairs={{0,16},{8,24},{16,0},{24,8},{1,17},{9,25},{17,1},{25,9},{2,18},{10... | collective-permute-start | bytes 4816904 | tf_op jit(solution)/shard_map/ppermute | solution.py:1282
  337.9 41.9 %copy-start.16 = (bf16[1,256,2048]{2,1,0:T(8,128)(2,1)S(1)}, bf16[1,256,2048]{2,1,0:T(8,128)(2,1)}, u32[]{:S(2)}) copy-start(bf16[1,256,2048]{2,1,0:T(8,128)(2,1)} %param.12) | copy-start | bytes 3145732
  337.9 36.2 %collective-permute-start.31 = (f32[128,128]{1,0:T(8,128)S(1)}, f32[128,128]{1,0:T(8,128)S(1)}, u32[]{:S(2)}, u32[]{:S(2)}) collective-permute-start(f32[128,128]{1,0:T(8,128)S(1)} %bitcast_add_fusion.2), channel_id=1, source_target_pairs={{0,8},{8,0},{16,24},{24,16},{1,9},{9,1},{17,25},{25,17},{2,10},{10... | collective-permute-start | bytes 196616 | tf_op jit(solution)/shard_map/ppermute | solution.py:1278
  374.1 37.1 %collective-permute-start.32 = (bf16[2,3136,128]{2,1,0:T(8,128)(2,1)}, bf16[2,3136,128]{2,1,0:T(8,128)(2,1)}, u32[]{:S(2)}, u32[]{:S(2)}) collective-permute-start(bf16[2,3136,128]{2,1,0:T(8,128)(2,1)} %get-tuple-element.230), channel_id=1, source_target_pairs={{0,16},{8,24},{16,0},{24,8},{1,17},{9,25},{17,1},{25,9},{2,18},{10... | collective-permute-start | bytes 4816904 | tf_op jit(solution)/shard_map/ppermute | solution.py:1282
  375.7 36.6 %collective-permute-start.33 = (bf16[2,3136,128]{2,1,0:T(8,128)(2,1)S(1)}, bf16[2,3136,128]{2,1,0:T(8,128)(2,1)}, u32[]{:S(2)}, u32[]{:S(2)}) collective-permute-start(bf16[2,3136,128]{2,1,0:T(8,128)(2,1)S(1)} %get-tuple-element.231), channel_id=1, source_target_pairs={{0,8},{8,0},{16,24},{24,16},{1,9},{9,1},{17,25},{25,17},{2,10},{10... | collective-permute-start | bytes 4816904 | tf_op jit(solution)/shard_map/ppermute | solution.py:1278
  377.0 35.3 %collective-permute-start.34 = (bf16[2,3136,128]{2,1,0:T(8,128)(2,1)}, bf16[2,3136,128]{2,1,0:T(8,128)(2,1)}, u32[]{:S(2)}, u32[]{:S(2)}) collective-permute-start(bf16[2,3136,128]{2,1,0:T(8,128)(2,1)} %collective-permute-done.28.refs_2_), channel_id=1, source_target_pairs={{0,1},{1,0},{2,3},{3,2},{4,5},{5,4},{6,7},{7,6},{8,9},{9,8},{10,11... | collective-permute-start | bytes 4816904 | tf_op jit(solution)/shard_map/ppermute | solution.py:1296
  377.0 35.3 %collective-permute-start.35 = (bf16[2,3136,128]{2,1,0:T(8,128)(2,1)}, bf16[2,3136,128]{2,1,0:T(8,128)(2,1)}, u32[]{:S(2)}, u32[]{:S(2)}) collective-permute-start(bf16[2,3136,128]{2,1,0:T(8,128)(2,1)} %collective-permute-done.29.refs_3_), channel_id=1, source_target_pairs={{0,1},{1,0},{2,3},{3,2},{4,5},{5,4},{6,7},{7,6},{8,9},{9,8},{10,11... | collective-permute-start | bytes 4816904 | tf_op jit(solution)/shard_map/ppermute | solution.py:1296
  412.3 8.1 %collective-permute-start.36 = (bf16[2,3136,128]{2,1,0:T(8,128)(2,1)}, bf16[2,3136,128]{2,1,0:T(8,128)(2,1)S(1)}, u32[]{:S(2)}, u32[]{:S(2)}) collective-permute-start(bf16[2,3136,128]{2,1,0:T(8,128)(2,1)} %collective-permute-done.32.refs_6_), channel_id=1, source_target_pairs={{0,1},{1,0},{2,3},{3,2},{4,5},{5,4},{6,7},{7,6},{8,9},{9,8},{10,11... | collective-permute-start | bytes 4816904 | tf_op jit(solution)/shard_map/ppermute | solution.py:1296
  412.3 8.1 %collective-permute-start.37 = (bf16[2,3136,128]{2,1,0:T(8,128)(2,1)}, bf16[2,3136,128]{2,1,0:T(8,128)(2,1)S(1)}, u32[]{:S(2)}, u32[]{:S(2)}) collective-permute-start(bf16[2,3136,128]{2,1,0:T(8,128)(2,1)} %collective-permute-done.33.refs_7_), channel_id=1, source_target_pairs={{0,1},{1,0},{2,3},{3,2},{4,5},{5,4},{6,7},{7,6},{8,9},{9,8},{10,11... | collective-permute-start | bytes 4816904 | tf_op jit(solution)/shard_map/ppermute | solution.py:1296
  415.5 4.3 collective-permute-start.38
  (11 other events, 28.4 us)
Sparse Core Ops, SparseCore 0:
  9.6 83.4 all-gather.4
  116.3 81.0 all-gather.6
  206.1 173.5 reduce-scatter.1

commit v5 on v4

--- a/solution.py
+++ b/solution.py
@@ -420,6 +420,33 @@
             )
 
 
+def cut_kernel(starts, *refs):
+    count = len(starts)
+    copies = [
+        pltpu.make_async_copy(
+            refs[at].at[pl.ds(start, refs[count + at].shape[0])], refs[count + at], refs[-1].at[at]
+        )
+        for at, start in enumerate(starts)
+    ]
+    for copy in copies:
+        copy.start()
+    for copy in copies:
+        copy.wait()
+
+
+def cut(values, starts, counts):
+    return pl.pallas_call(
+        functools.partial(cut_kernel, starts),
+        out_shape=[jax.ShapeDtypeStruct((count, LANES), jnp.bfloat16) for count in counts],
+        in_specs=[pl.BlockSpec(memory_space=pl.ANY)] * len(values),
+        out_specs=[pl.BlockSpec(memory_space=pltpu.VMEM)] * len(values),
+        scratch_shapes=[pltpu.SemaphoreType.DMA((len(values),))],
+        compiler_params=params(60),
+        cost_estimate=LIGHT,
+        name="cut",
+    )(*values)
+
+
 def chunk_rows():
     return (16 // CHUNKS) * (BROWS + TROWS)
 
@@ -473,20 +500,17 @@
     return pl.ds(panel * LANES, LANES)
 
 
-def unpack_kernel(parts, bucket_ref, *refs):
-    sources = refs[:16]
-    staged, tails, load_sems, tail_sem, store_sems = refs[-5:]
-    matrices = refs[-10:-5] if parts[0] == 0 else refs[-8:-5]
-    outs = dict(zip(NAMES[: len(matrices)], matrices, strict=False))
+def place_parts(parts, bucket_ref, sources, tails_from, outs, tails_out, scratch):
+    staged, tails, load_sems, tail_sem, store_sems = scratch
     main = (16 // CHUNKS) * BROWS
-    if parts[0] == 0:
+    if tails_from is None:
         for k in range(8):
             pltpu.make_async_copy(
                 sources[k].at[pl.ds(main, 16 * TROWS)], tails.at[bucket_ref[k]], tail_sem
             ).start()
         take_tails = pltpu.make_async_copy(tails, tails, tail_sem)
     else:
-        take_tails = pltpu.make_async_copy(refs[16], tails, tail_sem)
+        take_tails = pltpu.make_async_copy(tails_from, tails, tail_sem)
         take_tails.start()
     for at in range(2):
         for k in range(8):
@@ -502,8 +526,8 @@
         stores.append(pltpu.make_async_copy(source, target, store_sems.at[len(stores)]))
         stores[-1].start()
 
-    if parts[0] == 0:
-        store(tails, matrices[4])
+    if tails_from is None:
+        store(tails, tails_out)
         for panel in range(16):
             store(
                 tails.at[7, pl.ds(panel * TROWS, TROWS)],
@@ -527,35 +551,122 @@
                         staged.at[at, bucket, pl.ds(panel * span + offset, rows)],
                         outs[name].at[pl.ds(first, rows), columns(part * wide + panel)],
                     )
-    for put in stores:
+    return stores
+
+
+def part_scratch(copies):
+    return [
+        pltpu.VMEM((2, 8, (16 // CHUNKS) * BROWS, LANES), jnp.bfloat16),
+        pltpu.VMEM((8, 16 * TROWS, LANES), jnp.bfloat16),
+        pltpu.SemaphoreType.DMA((2, 8)),
+        pltpu.SemaphoreType.DMA,
+        pltpu.SemaphoreType.DMA((copies,)),
+    ]
+
+
+def copies_of_parts():
+    return 2 * sum(len(PLACES[b]) * panels_of(b) for b in range(8))
+
+
+def unpack_kernel(bucket_ref, *refs):
+    outs = dict(zip(NAMES, refs[16:20], strict=True))
+    for put in place_parts((0, 1), bucket_ref, refs[:16], None, outs, refs[20], refs[21:]):
         put.wait()
 
 
-def unpack(parts, buckets, sources, before):
-    first = parts[0] == 0
-    copies = 2 * sum(len(PLACES[b]) * panels_of(b) for b in range(8)) + (17 if first else 0)
-    names = NAMES if first else NAMES[:3]
+def unpack(buckets, sources):
+    shapes = [jax.ShapeDtypeStruct(MATRICES[name], jnp.bfloat16) for name in NAMES]
     tails = jax.ShapeDtypeStruct((8, 16 * TROWS, LANES), jnp.bfloat16)
-    shapes = [jax.ShapeDtypeStruct(MATRICES[name], jnp.bfloat16) for name in names]
+    return pl.pallas_call(
+        unpack_kernel,
+        out_shape=[*shapes, tails],
+        in_specs=[pl.BlockSpec(memory_space=pltpu.SMEM)] + [pl.BlockSpec(memory_space=HBM)] * 16,
+        out_specs=[pl.BlockSpec(memory_space=HBM)] * 5,
+        scratch_shapes=part_scratch(copies_of_parts() + 17),
+        compiler_params=params(60),
+        cost_estimate=LIGHT,
+        name="unpack_params",
+    )(buckets, *sources)
+
+
+def unpack_hidden_kernel(width, bucket_ref, *refs):
+    sources, tails_from, normed_from, up_bias = refs[:16], refs[16], refs[17], refs[18]
+    outs = dict(zip(NAMES[:3], refs[24:27], strict=True))
+    hidden_to, slope_to = refs[27:29]
+    scratch, (normed, hidden, slope, normed_sem, out_sems) = refs[29:34], refs[34:]
+    staged = scratch[0]
+    load = pltpu.make_async_copy(normed_from, normed, normed_sem)
+    load.start()
+    stores = place_parts((2, 3), bucket_ref, sources, tails_from, outs, None, scratch)
+    load.wait()
+    rows_of_up = [
+        (bucket, rows, offset)
+        for bucket in range(8)
+        for name, _, rows, offset in PLACES[bucket]
+        if name == "up"
+    ]
+    half = up_bias.shape[1] // 2
+    puts = []
+    for block in range(half // FF_BLOCK):
+        slot = block % 2
+        if block >= 2:
+            for put in puts[2 * block - 4 : 2 * block - 2]:
+                put.wait()
+        panels = []
+        for panel in range(2 * block, 2 * block + 2):
+            at, inner = panel // (16 // CHUNKS), panel % (16 // CHUNKS)
+            pieces = [
+                staged[at, bucket, pl.ds(inner * BROWS + offset, rows), :]
+                for bucket, rows, offset in rows_of_up
+            ]
+            panels.append(jnp.concatenate(pieces, axis=0))
+        first = half + block * FF_BLOCK
+        gelu(
+            matmul(normed[...], jnp.concatenate(panels, axis=1))
+            + up_bias[:, first : first + FF_BLOCK],
+            hidden.at[slot],
+            slope.at[slot],
+        )
+        for which, (source, target, column) in enumerate(
+            ((hidden, hidden_to, width + first), (slope, slope_to, first))
+        ):
+            puts.append(
+                pltpu.make_async_copy(
+                    source.at[slot],
+                    target.at[:, pl.ds(column, FF_BLOCK)],
+                    out_sems.at[slot, which],
+                )
+            )
+            puts[-1].start()
+    for put in [*puts[-4:], *stores]:
+        put.wait()
+
+
+def unpack_hidden(width, buckets, sources, before, normed, up_bias, halves):
+    rows = normed.shape[0]
+    hidden, slope = halves
     results = pl.pallas_call(
-        functools.partial(unpack_kernel, parts),
-        out_shape=[*shapes, tails] if first else shapes,
+        functools.partial(unpack_hidden_kernel, width),
+        out_shape=[jax.ShapeDtypeStruct(v.shape, v.dtype) for v in (*before[:3], hidden, slope)],
         in_specs=[pl.BlockSpec(memory_space=pltpu.SMEM)]
-        + [pl.BlockSpec(memory_space=HBM)] * (16 + (0 if first else 4)),
-        out_specs=[pl.BlockSpec(memory_space=HBM)] * (5 if first else 3),
-        input_output_aliases={} if first else {18 + at: at for at in range(3)},
-        scratch_shapes=[
-            pltpu.VMEM((2, 8, (16 // CHUNKS) * BROWS, LANES), jnp.bfloat16),
-            pltpu.VMEM(tails.shape, tails.dtype),
-            pltpu.SemaphoreType.DMA((2, 8)),
+        + [pl.BlockSpec(memory_space=HBM)] * 18
+        + [pl.BlockSpec(memory_space=pltpu.VMEM)]
+        + [pl.BlockSpec(memory_space=HBM)] * 5,
+        out_specs=[pl.BlockSpec(memory_space=HBM)] * 5,
+        input_output_aliases={20 + at: at for at in range(5)},
+        scratch_shapes=part_scratch(copies_of_parts())
+        + [
+            pltpu.VMEM(normed.shape, normed.dtype),
+            pltpu.VMEM((2, rows, FF_BLOCK), jnp.bfloat16),
+            pltpu.VMEM((2, rows, FF_BLOCK), jnp.float32),
             pltpu.SemaphoreType.DMA,
-            pltpu.SemaphoreType.DMA((copies,)),
+            pltpu.SemaphoreType.DMA((2, 2)),
         ],
         compiler_params=params(60),
         cost_estimate=LIGHT,
-        name="unpack_params",
-    )(buckets, *sources, *(() if first else (before[4], *before[:3])))
-    return results if first else [*results, *before[3:]]
+        name="unpack_hidden",
+    )(buckets, *sources, before[4], normed, up_bias, *before[:3], hidden, slope)
+    return results[:3], results[3], results[4]
 
 
 GRAD_ROWS = 256
@@ -567,8 +678,8 @@
 
 
 def weight_grad_kernel(table, *refs):
-    lefts, projected, late, outs = refs[:8], refs[8:10], refs[10:14], refs[14:20]
-    wide32, wide16, tail32, tail16, held, sems, tail_sem, late_sem = refs[20:]
+    lefts, projected, late, outs = refs[:8], refs[8:10], refs[10:14], refs[14:22]
+    wide32, wide16, tail32, tail16, held, sems, tail_sem, late_sem = refs[22:]
     step = pl.program_id(0)
     core = table[0]
     main = (16 // CHUNKS) * BROWS
@@ -580,11 +691,13 @@
         return table[1 + 16 * part + bucket], table[9 + 16 * part + bucket]
 
     def targets(part, kind, place):
+        near = kind == NEAR
         return [
-            (kind == NEAR, True, outs[2 * part].at[jnp.minimum(place, 1)]),
-            (kind == FAR, True, outs[2 * part + 1].at[jnp.minimum(place, 1)]),
-            (jnp.logical_and(kind == KEPT, place >= 2), False, outs[4].at[part, jnp.clip(place - 2, 0, 1)]),
-            (jnp.logical_and(kind == KEPT, place < 2), False, outs[5].at[part, jnp.minimum(place, 1)]),
+            (jnp.logical_and(near, place == 0), True, outs[3 * part]),
+            (jnp.logical_and(near, place == 1), True, outs[3 * part + 1]),
+            (kind == FAR, True, outs[3 * part + 2].at[jnp.minimum(place, 1)]),
+            (jnp.logical_and(kind == KEPT, place >= 2), False, outs[6].at[part, jnp.clip(place - 2, 0, 1)]),
+            (jnp.logical_and(kind == KEPT, place < 2), False, outs[7].at[part, jnp.minimum(place, 1)]),
         ]
 
     def wait(at):
@@ -602,12 +715,12 @@
 
                         @pl.when(kind == KEPT)
                         def _(part=part, sem=sem):
-                            place = outs[5].at[part, 0, rows]
+                            place = outs[7].at[part, 0, rows]
                             pltpu.make_async_copy(place, place, sem).wait()
 
                         @pl.when(kind != KEPT)
                         def _(part=part, sem=sem):
-                            place = outs[2 * part].at[0, rows]
+                            place = outs[3 * part].at[rows]
                             pltpu.make_async_copy(place, place, sem).wait()
 
     @pl.when(step >= 2)
@@ -743,16 +856,17 @@
     half = (tokens, rights[0].shape[1] // 2)
     right_specs = [pl.BlockSpec(half, lambda i, table: (0, table[0]))] * 2
     rows = chunk_rows()
+    near = jax.ShapeDtypeStruct((rows, LANES), jnp.bfloat16)
     short = jax.ShapeDtypeStruct((2, rows, LANES), jnp.bfloat16)
     wide = jax.ShapeDtypeStruct((2, 2, rows, LANES), jnp.float32)
     return pl.pallas_call(
         weight_grad_kernel,
-        out_shape=[short] * 4 + [wide] * 2,
+        out_shape=[near, near, short] * 2 + [wide] * 2,
         grid_spec=pltpu.PrefetchScalarGridSpec(
             num_scalar_prefetch=1,
             grid=(GRAD_STEPS,),
             in_specs=left_specs + right_specs + [pl.BlockSpec(memory_space=HBM)] * 4,
-            out_specs=[pl.BlockSpec(memory_space=HBM)] * 6,
+            out_specs=[pl.BlockSpec(memory_space=HBM)] * 8,
             scratch_shapes=[
                 pltpu.VMEM((2, PAIR, 8 * LANES), jnp.float32),
                 pltpu.VMEM((2, 2, 2, 4 * GRAD_ROWS, LANES), jnp.bfloat16),
@@ -851,9 +965,7 @@
             loads.append(pltpu.make_async_copy(source, held32.at[place], sems.at[0, at]))
             for which, came in enumerate((near, far)):
                 loads.append(
-                    pltpu.make_async_copy(
-                        came[at].at[at // 2], held16.at[which, place], sems.at[1 + which, at]
-                    )
+                    pltpu.make_async_copy(came[at], held16.at[which, place], sems.at[1 + which, at])
                 )
         for load in loads:
             load.start()
@@ -1015,40 +1127,36 @@
 FF_BLOCK = 256
 
 
-def hidden_kernel(normed, up, up_bias, *refs):
-    hidden, slope = refs[-2:]
-    before = matmul(normed[...], up[...]) + up_bias[...]
+def gelu(before, hidden, slope):
     half = 0.5 + 0.5 * lax.erf(before * math.sqrt(0.5))
     hidden[...] = (before * half).astype(jnp.bfloat16)
     slope[...] = half + before * jnp.exp(-0.5 * before * before) * (1.0 / math.sqrt(2.0 * math.pi))
 
 
-def hidden_layer(half, width, normed, up, up_bias, before):
+def hidden_kernel(normed, up, up_bias, hidden, slope):
+    gelu(matmul(normed[...], up[...]) + up_bias[...], hidden, slope)
+
+
+def hidden_layer(width, normed, up, up_bias):
     rows, units = normed.shape[0], up.shape[1]
-    steps = units // FF_BLOCK // 2
-    block = pl.BlockSpec((rows, FF_BLOCK), lambda i: (0, i + half * steps))
+    block = pl.BlockSpec((rows, FF_BLOCK), lambda i: (0, i))
     return pl.pallas_call(
         hidden_kernel,
-        grid=(steps,),
+        grid=(units // FF_BLOCK // 2,),
         out_shape=[
             jax.ShapeDtypeStruct((rows, width + units), jnp.bfloat16),
             jax.ShapeDtypeStruct((rows, units), jnp.float32),
         ],
         in_specs=[
             pl.BlockSpec(memory_space=pltpu.VMEM),
-            pl.BlockSpec((D, FF_BLOCK), lambda i: (0, i + half * steps)),
-            pl.BlockSpec((1, FF_BLOCK), lambda i: (0, i + half * steps)),
-        ]
-        + [pl.BlockSpec(memory_space=HBM)] * len(before),
-        out_specs=[
-            pl.BlockSpec((rows, FF_BLOCK), lambda i: (0, i + half * steps + width // FF_BLOCK)),
-            block,
+            pl.BlockSpec((D, FF_BLOCK), lambda i: (0, i)),
+            pl.BlockSpec((1, FF_BLOCK), lambda i: (0, i)),
         ],
-        input_output_aliases={3 + at: at for at in range(len(before))},
+        out_specs=[pl.BlockSpec((rows, FF_BLOCK), lambda i: (0, i + width // FF_BLOCK)), block],
         compiler_params=params(60),
         cost_estimate=LIGHT,
         name="hidden_layer",
-    )(normed, up, up_bias, *before)
+    )(normed, up, up_bias)
 
 
 def hidden_back_kernel(half, grads, down, slope, grad_before, grad_bias):
@@ -1359,7 +1467,11 @@
         rows = (16 // CHUNKS) * BROWS
         start = part_row(second)
         count = start if first == 0 else rows
-        return [along_x(from_y[:count]), along_y(from_x[start : start + rows])]
+        if first == 0:
+            from_y, from_x = from_y[:count], from_x[start : start + rows]
+        else:
+            from_y, from_x = cut([from_y, from_x], (0, start), (count, rows))
+        return [along_x(from_y), along_y(from_x)]
 
     far = from_far(0, 1, one_x, one_y)
     near_x, near_y, two_own = across(one_x), across(one_y), across(two)
@@ -1372,14 +1484,14 @@
     sources = []
     for part in range(2):
         sources += [one, one_x, one_y, far[part], one_own, near_x, near_y, far_other[part]]
-    weights = unpack((0, 1), buckets, sources, [])
+    weights = unpack(buckets, sources)
     weights, full_rows = order(weights, full_rows)
     flat_bias = weights[3][:8].reshape(-1).astype(jnp.float32)
     mixer_bias = flat_bias[: 3 * local_width]
     expand_bias = flat_bias[3 * local_width : 3 * local_width + D]
     small_params = flat_bias[3 * local_width + D : 3 * local_width + 7 * D].reshape(6, D)
     full_one, full_two, centre, scale = norms(full_rows, small_params)
-    hidden_half = hidden_layer(0, local_width, full_two, weights[2], expand_bias[None], ())
+    hidden_half = hidden_layer(local_width, full_two, weights[2], expand_bias[None])
     two_x, two_y, full_rows, full_one, full_two, weights, hidden_half = order(
         two_x, two_y, full_rows, full_one, full_two, weights, hidden_half
     )
@@ -1396,10 +1508,10 @@
     sources = []
     for part in range(2):
         sources += [two, two_x, two_y, far[part], two_own, near_x, near_y, far_other[part]]
-    weights = unpack((2, 3), buckets, sources, weights)
-    mixer_in, mix_weight, expand_weight = weights[:3]
-
-    mixed, slope = hidden_layer(1, local_width, full_two, expand_weight, expand_bias[None], hidden_half)
+    (mixer_in, mix_weight, expand_weight), mixed, slope = unpack_hidden(
+        local_width, buckets, sources, weights, full_two, expand_bias[None], hidden_half
+    )
+
     mixed, turned, logs = attend(full_one, mixer_in, mixer_bias[None], tables, begins, mixed)
     other_mixed = across(mixed)
     branches = matmul(mixed, mix_weight)
@@ -1427,7 +1539,7 @@
     grad_projected, own_before, rest_before, sums = order(
         grad_projected, own_before, rest_before, sums
     )
-    near_a, far_a, near_b, far_b, passed, stays = sums
+    near_a, cross_a, far_a, near_b, cross_b, far_b, passed, stays = sums
     came_a, came_b, other_stays = along_x(far_a), along_y(far_b), across(stays)
 
     partial, norm_grads = norm_grad(
@@ -1449,15 +1561,17 @@
         bias_grad,
     )
 
-    for bit in (1, 2):
-        norm_grads = norm_grads + along_line(norm_grads, bit)
-    came_a, came_b, other_stays, partial, norm_grads, small, near_a, near_b = order(
-        came_a, came_b, other_stays, partial, norm_grads, small, near_a, near_b
-    )
-    near_a, near_b = along_x(near_a), along_y(near_b)
+    norm_grads, other_stays = order(norm_grads, other_stays)
+    one, two, three = (along_line(norm_grads, bit) for bit in (1, 2, 3))
+    norm_grads = (norm_grads + one) + (two + three)
+    near = [near_a, near_b, cross_a, cross_b]
+    came_a, came_b, other_stays, partial, norm_grads, small, near = order(
+        came_a, came_b, other_stays, partial, norm_grads, small, near
+    )
+    near = [along_x(near[0]), along_y(near[1]), along(1, near[2]), along(2, near[3])]
     terms = line_blocks(partial)
-    pass_a = (passed[0] + came_a.astype(jnp.float32)).astype(jnp.bfloat16)
-    pass_b = (passed[1] + came_b.astype(jnp.float32)).astype(jnp.bfloat16)
+    pass_a = [(passed[0, at] + came_a[at].astype(jnp.float32)).astype(jnp.bfloat16) for at in range(2)]
+    pass_b = [(passed[1, at] + came_b[at].astype(jnp.float32)).astype(jnp.bfloat16) for at in range(2)]
     small = jnp.concatenate(
         [
             small[0],
@@ -1470,13 +1584,11 @@
     ).reshape(LANES, LANES)
     small = small + across(small)
     small = small + along_x(small)
-    near_a, near_b, pass_a, pass_b, small = order(near_a, near_b, pass_a, pass_b, small)
     output = residual[0].astype(jnp.float32) + branches + small_params[4] + small_params[5]
-    far_a, far_b = along_y(pass_a), along_x(pass_b)
-    near = [near_a, near_b, across(near_a), across(near_b)]
-    far_a, far_b, near, small, output = order(far_a, far_b, near, small, output)
-    far = [far_a, far_b, across(far_a), across(far_b)]
+    near, pass_a, pass_b, small, output = order(near, pass_a, pass_b, small, output)
+    far = [along_y(pass_a[0]), along_x(pass_b[0]), along(2, pass_a[1]), along(1, pass_b[1])]
     small = small + along_y(small)
+    far, small = order(far, small)
 
     step_value = step_count[0].astype(jnp.float32)
     scalars = jnp.stack(

time: 467 us -> 471 us (level)
    reduce_scatter x1, waiting for transfers between devices: 2.21 us -> 10.2 us  [on_device_fast(): lax.psum_scatter(branches, 'tensor', scatter_dimension=0, tiled=True)]
  transfers between devices with their start and end apart: 43 -> 44, of which waited for: 18 -> 17; matrix products, arithmetic and copies ran while one was open for 11% -> 10% of each run, Pallas kernels for 45% -> 45%
where the time goes in v5:
time: 471 us; the launch traced here: 463 us
  Pallas kernels  215 us (46%)
  waiting for transfers between devices  141 us (30%)
  starting transfers between devices  36.1 us (8%)
  matrix products  22.8 us (5%)
  other arithmetic  20.9 us (4%)
  between operations  16.9 us (4%)
  local copies, waits for them, and re-layouts  10.4 us (2%)
    ppermute x8, waiting for transfers between devices, along_x(): return lax.ppermute(value, 'dp', [(i, i ^ 1) for i in range(4)])  71.3 us
    ppermute x8, waiting for transfers between devices, along_y(): return lax.ppermute(value, 'dp', [(i, i ^ 2) for i in range(4)])  45.1 us
    pallas_call x1, Pallas kernels, weight_grads(): pl.pallas_call(weight_grad_kernel, out_shape=[near, near, short] * 2 + [w...  40.9 us
    pallas_call x1, Pallas kernels, adam(): pl.pallas_call(adam_kernel, grid=(steps,), out_shape=[jax.ShapeDtypeStruc...  26.5 us
    pallas_call x1, Pallas kernels, norm_grad(): pl.pallas_call(norm_grad_kernel, out_shape=[jax.ShapeDtypeStruct((tokens,...  23.9 us
    pallas_call x1, Pallas kernels, attend(): pl.pallas_call(attend_kernel, grid=(pairs,), out_shape=[jax.ShapeDtypeStr...  22 us
    pallas_call x2, Pallas kernels, hidden_back(): pl.pallas_call(hidden_back_kernel, out_shape=[jax.ShapeDtypeStruct((rows,...  19.9 us
    pallas_call x1, Pallas kernels, unpack_hidden(): pl.pallas_call(functools.partial(unpack_hidden_kernel, width), out_shape=...  18.9 us
  transfers between devices with their start and end apart: 44, of which 17 were waited for; matrix products, arithmetic and copies ran while one was open for 10% of the time, Pallas kernels for 45%

profile of v5, /device:TPU:0, one launch (start us, length us, event | category | flops | bytes accessed | tf_op | source)
XLA Modules:
  0.0 463.3 jit_solution(17052481281320404303)
XLA Ops:
  7.2 0.7 all-gather.5.cloned.1.call-update
  8.1 0.8 select_reduce_fusion.4
  9.0 2.8 copy-done.2
  11.8 2.7 pack_params.1
  14.5 3.0 collective-permute-start
  17.5 0.9 collective-permute-start.1
  18.4 34.9 %collective-permute-done.refs_1_.refs_9_ = bf16[6400,128]{1,0:T(8,128)(2,1)S(1)} collective-permute-done((bf16[6400,128]{1,0:T(8,128)(2,1)S(1)}, bf16[6400,128]{1,0:T(8,128)(2,1)S(1)}, u32[]{:S(2)}, u32[]{:S(2)}) %collective-permute-start) | collective-permute-done | bytes 1638432 | tf_op jit(solution)/shard_map/ppermute | solution.py:1386
  53.3 1.5 collective-permute-done.1.refs_2_.refs_10_
  56.2 1.7 collective-permute-start.4
  58.1 1.9 multiply_sine_fusion
  60.1 1.6 maximum_maximum_fusion.2
  61.7 1.3 collective-permute-done.7.refs_4_.refs_12_
  62.9 12.9 %collective-permute-done.4.refs_11_ = bf16[3072,128]{1,0:T(8,128)(2,1)S(1)} collective-permute-done((bf16[3072,128]{1,0:T(8,128)(2,1)S(1)}, bf16[3072,128]{1,0:T(8,128)(2,1)S(1)}, u32[]{:S(2)}, u32[]{:S(2)}) %collective-permute-start.4) | collective-permute-done | bytes 786464 | tf_op jit(solution)/shard_map/ppermute | solution.py:1390
  75.8 1.3 collective-permute-done.3.refs_3_
  77.6 1.7 collective-permute-start.9
  79.8 3.0 collective-permute-done.11.refs_15_
  82.8 0.9 copy-done.29
  83.7 10.8 %unpack_params.1 = (bf16[2048,1536]{1,0:T(8,128)(2,1)}, bf16[2560,2048]{1,0:T(8,128)(2,1)}, bf16[2048,2048]{1,0:T(8,128)(2,1)}, bf16[16,2048]{1,0:T(8,128)(2,1)}, bf16[8,256,128]{2,1,0:T(8,128)(2,1)}) custom-call(s32[8]{0:T(128)} %copy-done.11, bf16[6400,128]{1,0:T(8,128)(2,1)} %copy-done.3, bf16[6400,128]{1,0:T(8,128)(2,1)} %copy-done.15, ...), custom_call_target="tpu_custom_call" | custom-call | flops 1 | bytes 1 | tf_op jit(solution)/shard_map/unpack_params/pallas_call | solution.py:580
  94.6 0.8 convert_bitcast_fusion
  96.0 9.1 %norms.2 = (bf16[1024,2048]{1,0:T(8,128)(2,1)}, bf16[1024,2048]{1,0:T(8,128)(2,1)}, f32[1024,1]{1,0:T(8,128)}, f32[1024,1]{1,0:T(8,128)}) custom-call(bf16[1024,2048]{1,0:T(8,128)(2,1)} %bitcast.76, f32[6,2048]{1,0:T(8,128)} %reshape.97.gains), custom_call_target="tpu_custom_call" | custom-call | flops 1 | bytes 1 | tf_op jit(solution)/shard_map/norms/pallas_call | solution.py:1214
  105.7 10.2 %hidden_layer.1 = (bf16[1024,2560]{1,0:T(8,128)(2,1)}, f32[1024,2048]{1,0:T(8,128)}) custom-call(bf16[1024,2048]{1,0:T(8,128)(2,1)} %get-tuple-element.189.normed.refs_17_.refs_4_, bf16[2048,2048]{1,0:T(8,128)(2,1)} %get-tuple-element.192.up.refs_21_, f32[1,2048]{1,0:T(1,128)} %bitcast.93), custom_call_target="tpu_custom_call" | custom-call | flops 1 | bytes 1 | tf_op jit(solution)/shard_map/hidden_layer/pallas_call | solution.py:1143
  117.2 2.5 cut.1
  119.8 1.6 collective-permute-start.12
  121.8 1.7 collective-permute-done.16.rows
  123.5 9.4 %norms.3 = (bf16[1024,2048]{1,0:T(8,128)(2,1)}, bf16[1024,2048]{1,0:T(8,128)(2,1)}, f32[1024,1]{1,0:T(8,128)}, f32[1024,1]{1,0:T(8,128)}) custom-call(bf16[1024,2048]{1,0:T(8,128)(2,1)} %collective-permute-done.16.rows, f32[6,2048]{1,0:T(8,128)} %reshape.97.gains), custom_call_target="tpu_custom_call" | custom-call | flops 1 | bytes 1 | tf_op jit(solution)/shard_map/norms/pallas_call | solution.py:1214
  132.9 7.1 %collective-permute-done.12.refs_3_ = bf16[3072,128]{1,0:T(8,128)(2,1)} collective-permute-done((bf16[3072,128]{1,0:T(8,128)(2,1)}, bf16[3072,128]{1,0:T(8,128)(2,1)}, u32[]{:S(2)}, u32[]{:S(2)}) %collective-permute-start.12) | collective-permute-done | bytes 786464 | tf_op jit(solution)/shard_map/ppermute | solution.py:1386
  140.0 1.2 collective-permute-done.13.refs_11_
  141.8 1.0 copy.30.begins
  143.7 1.1 collective-permute-done.18.refs_15_
  144.9 0.9 copy-done.31
  145.8 18.9 %unpack_hidden.1 = (bf16[2048,1536]{1,0:T(8,128)(2,1)}, bf16[2560,2048]{1,0:T(8,128)(2,1)}, bf16[2048,2048]{1,0:T(8,128)(2,1)}, bf16[1024,2560]{1,0:T(8,128)(2,1)}, f32[1024,2048]{1,0:T(8,128)}) custom-call(s32[8]{0:T(128)} %copy-done.11, ...), custom_call_target="tpu_custom_call", output_to_operand_aliasing={{0}: (20, {}), {1}: (21, {}), {2}: (22, {}), {3}: (23, {}),... | custom-call | flops 1 | bytes 1 | tf_op jit(solution)/shard_map/unpack_hidden/pallas_call | solution.py:648
  164.7 22.0 %attend.1 = (bf16[1024,2560]{1,0:T(8,128)(2,1)}, bf16[3,1024,512]{2,1,0:T(8,128)(2,1)}, f32[4,1024,1]{2,1,0:T(8,128)}) custom-call(bf16[1024,2048]{1,0:T(8,128)(2,1)} %get-tuple-element.169.normed.refs_0_, bf16[2048,1536]{1,0:T(8,128)(2,1)} %get-tuple-element.195.queries_in.keys_in.values_in.mixer_in, ...), custom_call_target="tpu_custom_call", output_to_operand_aliasing={{0}: (9, {})} | custom-call | flops 1 | bytes 1 | tf_op jit(solution)/shard_map/attend/pallas_call | solution.py:1296
  186.9 17.4 %fusion.11 = f32[1024,2048]{1,0:T(8,128)} fusion(bf16[1024,2560]{1,0:T(8,128)(2,1)} %get-tuple-element.201.refs_2_.refs_6_, bf16[2560,2048]{1,0:T(8,128)(2,1)} %get-tuple-element.202.down), kind=kOutput, calls=%fused_computation.60 | convolution fusion | flops 10737418240 | bytes 24117248 | tf_op jit(solution)/shard_map/dot_general | solution.py:27
  204.8 5.5 %fusion.6.grad_context = bf16[1024,512]{1,0:T(8,128)(2,1)S(1)} fusion(bf16[1024,2048]{1,0:T(8,128)(2,1)} %bitcast.71, bf16[2560,2048]{1,0:T(8,128)(2,1)} %get-tuple-element.202.down), kind=kOutput, calls=%fused_computation.13 | convolution fusion | flops 2148007936 | bytes 7340032 | tf_op jit(solution)/shard_map/dot_general | solution.py:37
  210.4 12.8 %attend_back.1.refs_8_.grad_projected = bf16[1024,1536]{1,0:T(8,128)(2,1)S(1)} custom-call(bf16[3,1024,512]{2,1,0:T(8,128)(2,1)S(1)} %copy-done.9, f32[4,1024,1]{2,1,0:T(8,128)S(1)} %copy-done.10, f32[1024,128]{1,0:T(8,128)S(1)} %copy-done.8, f32[1024,128]{1,0:T(8,128)S(1)} %copy-done.7, f32[1024,128]{1,0:T(8,128)S(1)} %copy-done.6, ...), custom_call_target="tpu_custom_call" | custom-call | flops 1 | bytes 1 | tf_op jit(solution)/shard_map/attend_back/pallas_call | solution.py:1359
  223.3 10.5 %hidden_back.3 = (bf16[1024,1024]{1,0:T(8,128)(2,1)}, f32[1,1024]{1,0:T(1,128)}) custom-call(s32[1]{0:T(128)S(6)} %sub.30.half, bf16[1024,2048]{1,0:T(8,128)(2,1)} %bitcast.72, bf16[2560,2048]{1,0:T(8,128)(2,1)} %get-tuple-element.202.down, f32[1024,2048]{1,0:T(8,128)} %get-tuple-element.209.slope), custom_call_target="tpu_custom_call" | custom-call | flops 1 | bytes 1 | tf_op jit(solution)/shard_map/hidden_back/pallas_call | solution.py:1172
  234.6 9.4 %hidden_back.2 = (bf16[1024,1024]{1,0:T(8,128)(2,1)}, f32[1,1024]{1,0:T(1,128)}) custom-call(s32[1]{0:T(128)} %bitcast.14.half.core, bf16[1024,2048]{1,0:T(8,128)(2,1)} %bitcast.73, bf16[2560,2048]{1,0:T(8,128)(2,1)} %get-tuple-element.202.down, f32[1024,2048]{1,0:T(8,128)} %get-tuple-element.209.slope), custom_call_target="tpu_custom_call" | custom-call | flops 1 | bytes 1 | tf_op jit(solution)/shard_map/hidden_back/pallas_call | solution.py:1172
  244.1 40.9 %weight_grads.1 = (bf16[3136,128]{1,0:T(8,128)(2,1)}, bf16[3136,128]{1,0:T(8,128)(2,1)}, bf16[2,3136,128]{2,1,0:T(8,128)(2,1)}, bf16[3136,128]{1,0:T(8,128)(2,1)...) custom-call(s32[33]{0:T(128)} %concatenate.24.table, ...), custom_call_target="tpu_custom_call" | custom-call | flops 1 | bytes 1 | tf_op jit(solution)/shard_map/weight_grads/pallas_call | solution.py:862
  285.6 0.7 collective-permute-start.23
  287.4 2.8 convert_reduce_fusion
  290.2 23.9 %norm_grad.1 = (bf16[1024,2048]{1,0:T(8,128)(2,1)}, f32[4,2048]{1,0:T(4,128)}) custom-call(s32[1]{0:T(128)} %bitcast.14.half.core, bf16[1024,1536]{1,0:T(8,128)(2,1)} %copy-done, bf16[2048,1536]{1,0:T(8,128)(2,1)} %get-tuple-element.195.queries_in.keys_in.values_in.mixer_in, bf16[1024,1024]{1,0:T(8,128)(2,1)} %get-tuple-element.225.refs_12_.own_before, ...), custom_call_target="tpu_custom_call" | custom-call | flops 1 | bytes 1 | tf_op jit(solution)/shard_map/norm_grad/pallas_call | solution.py:910
  314.2 2.7 collective-permute-start.27
  316.9 1.2 collective-permute-start.28
  318.9 2.0 collective-permute-done.27
  320.9 3.0 collective-permute-done.28
  323.9 1.2 collective-permute-done.26
  325.1 0.8 add_add_fusion.1
  325.9 4.9 %all-to-all-start = ((bf16[4,256,2048]{2,1,0:T(8,128)(2,1)}), bf16[4,256,2048]{2,1,0:T(8,128)(2,1)}, u32[]{:S(2)}, u32[]{:S(2)}) async-start(bf16[4,256,2048]{2,1,0:T(8,128)(2,1)} %bitcast.83), calls=%async_computation.1 | async-start | bytes 8388608 | tf_op jit(solution)/shard_map/all_to_all | solution.py:1410
  331.0 2.0 collective-permute-start.29
  333.0 2.2 collective-permute-start.30
  335.5 1.5 collective-permute-start.34
  337.0 5.2 %fusion.2 = (bf16[3136,128]{1,0:T(8,128)(2,1)S(1)}, bf16[3136,128]{1,0:T(8,128)(2,1)S(1)}, bf16[3136,128]{1,0:T(8,128)(2,1)}, bf16[3136,128]{1,0:T(8,128)(2,1)S(1)}) fusion(f32[2,2,3136,128]{3,2,1,0:T(8,128)} %get-tuple-element.245, bf16[2,3136,128]{2,1,0:T(8,128)(2,1)} %collective-permute-done.24, bf16[2,3136,128]{2,1,0:T(8,128)(2,1)} %collective-permute-done.23), kind=kLoop, calls=%fused_computation.6 | loop fusion | flops 4816896 | bytes 12845056 | tf_op jit(solution)/shard_map/convert_element_type | solution.py:1574
  342.3 28.0 %collective-permute-done.34 = f32[128,128]{1,0:T(8,128)S(1)} collective-permute-done((f32[128,128]{1,0:T(8,128)S(1)}, f32[128,128]{1,0:T(8,128)S(1)}, u32[]{:S(2)}, u32[]{:S(2)}) %collective-permute-start.34) | collective-permute-done | bytes 65568 | tf_op jit(solution)/shard_map/ppermute | solution.py:1386
  370.3 10.2 %reduce-scatter.2.cloned.1.call-done = f32[256,2048]{1,0:T(8,128)} async-done(((f32[1024,2048]{1,0:T(8,128)}), f32[256,2048]{1,0:T(8,128)}) %reduce-scatter.2.cloned.1.call-update) | async-done | bytes 2097168 | tf_op jit(solution)/shard_map/reduce_scatter | solution.py:1519
  380.5 3.4 add_add_fusion
  383.9 1.3 collective-permute-start.35
  385.2 1.5 collective-permute-start.36
  386.7 1.1 collective-permute-start.38
  390.4 1.2 collective-permute-start.39
  391.6 0.7 pad_maximum_fusion.1.scalar_ref
  392.3 29.6 %collective-permute-done.39 = f32[128,128]{1,0:T(8,128)S(1)} collective-permute-done((f32[128,128]{1,0:T(8,128)S(1)}, f32[128,128]{1,0:T(8,128)S(1)}, u32[]{:S(2)}, u32[]{:S(2)}) %collective-permute-start.39) | collective-permute-done | bytes 65568 | tf_op jit(solution)/shard_map/ppermute | solution.py:1390
  422.5 0.9 copy-done.25
  424.3 26.5 %adam.1 = (f32[12304,128]{1,0:T(8,128)}, f32[12304,128]{1,0:T(8,128)}, f32[12304,128]{1,0:T(8,128)}, f32[12304,128]{1,0:T(8,128)}, f32[12304,128]{1,0:T(8,128)}) custom-call(s32[2]{0:T(128)} %pad_add_fusion.table, f32[4]{0:T(128)} %pad_maximum_fusion.1.scalar_ref, f32[8]{0:T(128)} %rate_ref.1, f32[2,2,3136,128]{3,2,1,0:T(8,128)} %get-tuple-element.231.refs_0_, ...), custom_call_target="tpu_custom_call" | custom-call | flops 1 | bytes 1 | tf_op jit(solution)/shard_map/adam/pallas_call | solution.py:1073
  450.8 5.5 %finish.1 = f32[256,2048]{1,0:T(8,128)} custom-call(bf16[4,256,2048]{2,1,0:T(8,128)(2,1)} %all-to-all-done.terms, bf16[256,2048]{1,0:T(8,128)(2,1)} %bitcast.79, bf16[256,2048]{1,0:T(8,128)(2,1)} %bitcast.84), custom_call_target="tpu_custom_call" | custom-call | flops 1 | bytes 1 | tf_op jit(solution)/shard_map/finish/pallas_call | solution.py:1111
  (166 shorter events, 14.3 us)
Async XLA Ops:
  7.2 48.3 %copy-start.36 = (s32[1,5]{1,0:T(1,128)S(1)}, s32[1,5]{1,0:T(1,128)}, u32[]{:S(2)}) copy-start(s32[1,5]{1,0:T(1,128)} %param.14) | copy-start | bytes 64
  7.2 87.4 %all-gather.5.cloned.1.call-start = ((), (), s32[]{:S(2)}) async-start(), calls=%async_computation.3 | async-start | bytes 5242880 | tf_op jit(solution)/shard_map/all_gather | solution.py:1448
  7.9 196.4 %all-gather.7.cloned.1.call-start = ((), (), s32[]{:S(2)}) async-start(), calls=%async_computation.4 | async-start | bytes 5242880 | tf_op jit(solution)/shard_map/all_gather | solution.py:1449
  9.0 46.8 %copy-start.11 = (s32[8]{0:T(128)}, s32[8]{0:T(128)S(1)}, u32[]{:S(2)}) copy-start(s32[8]{0:T(128)S(1)} %select_reduce_fusion.3.bucket_ref) | copy-start | bytes 100
  14.5 47.2 %copy-start.3 = (bf16[6400,128]{1,0:T(8,128)(2,1)}, bf16[6400,128]{1,0:T(8,128)(2,1)S(1)}, u32[]{:S(2)}) copy-start(bf16[6400,128]{1,0:T(8,128)(2,1)S(1)} %get-tuple-element.144.refs_0_.refs_8_) | copy-start | bytes 4915204
  14.5 63.1 %copy-start.4 = (bf16[6144,128]{1,0:T(8,128)(2,1)}, bf16[6144,128]{1,0:T(8,128)(2,1)S(1)}, u32[]{:S(2)}) copy-start(bf16[6144,128]{1,0:T(8,128)(2,1)S(1)} %get-tuple-element.148.refs_0_.refs_8_) | copy-start | bytes 4718596
  14.5 38.8 %collective-permute-start = (bf16[6400,128]{1,0:T(8,128)(2,1)S(1)}, bf16[6400,128]{1,0:T(8,128)(2,1)S(1)}, u32[]{:S(2)}, u32[]{:S(2)}) collective-permute-start(bf16[6400,128]{1,0:T(8,128)(2,1)S(1)} %get-tuple-element.144.refs_0_.refs_8_), channel_id=1, source_target_pairs={{0,8},{8,0},{16,24},{24,16},{1,9},{9,1},{17,25},{25,17},{2,10},{10... | collective-permute-start | bytes 4915208 | tf_op jit(solution)/shard_map/ppermute | solution.py:1386
  17.5 37.3 %collective-permute-start.1 = (bf16[6400,128]{1,0:T(8,128)(2,1)S(1)}, bf16[6400,128]{1,0:T(8,128)(2,1)S(1)}, u32[]{:S(2)}, u32[]{:S(2)}) collective-permute-start(bf16[6400,128]{1,0:T(8,128)(2,1)S(1)} %get-tuple-element.144.refs_0_.refs_8_), channel_id=1, source_target_pairs={{0,16},{8,24},{16,0},{24,8},{1,17},{9,25},{17,1},{25,9},{2,18},{10... | collective-permute-start | bytes 4915208 | tf_op jit(solution)/shard_map/ppermute | solution.py:1390
  18.4 36.4 %collective-permute-start.2 = (bf16[6400,128]{1,0:T(8,128)(2,1)S(1)}, bf16[6400,128]{1,0:T(8,128)(2,1)S(1)}, u32[]{:S(2)}, u32[]{:S(2)}) collective-permute-start(bf16[6400,128]{1,0:T(8,128)(2,1)S(1)} %get-tuple-element.144.refs_0_.refs_8_), channel_id=1, source_target_pairs={{0,1},{1,0},{2,3},{3,2},{4,5},{5,4},{6,7},{7,6},{8,9},{9,8},{10,11... | collective-permute-start | bytes 4915208 | tf_op jit(solution)/shard_map/ppermute | solution.py:1404
  53.3 8.3 %copy-start.15 = (bf16[6400,128]{1,0:T(8,128)(2,1)}, bf16[6400,128]{1,0:T(8,128)(2,1)S(1)}, u32[]{:S(2)}) copy-start(bf16[6400,128]{1,0:T(8,128)(2,1)S(1)} %collective-permute-done.refs_1_.refs_9_) | copy-start | bytes 4915204
  54.8 6.9 %copy-start.14 = (bf16[6400,128]{1,0:T(8,128)(2,1)}, bf16[6400,128]{1,0:T(8,128)(2,1)S(1)}, u32[]{:S(2)}) copy-start(bf16[6400,128]{1,0:T(8,128)(2,1)S(1)} %collective-permute-done.1.refs_2_.refs_10_) | copy-start | bytes 4915204
  54.8 6.9 %copy-start.17 = (bf16[6400,128]{1,0:T(8,128)(2,1)}, bf16[6400,128]{1,0:T(8,128)(2,1)S(1)}, u32[]{:S(2)}) copy-start(bf16[6400,128]{1,0:T(8,128)(2,1)S(1)} %collective-permute-done.2.refs_4_.refs_12_) | copy-start | bytes 4915204
  54.8 22.4 %collective-permute-start.5 = (bf16[6400,128]{1,0:T(8,128)(2,1)S(1)}, bf16[6400,128]{1,0:T(8,128)(2,1)S(1)}, u32[]{:S(2)}, u32[]{:S(2)}) collective-permute-start(bf16[6400,128]{1,0:T(8,128)(2,1)S(1)} %collective-permute-done.refs_1_.refs_9_), channel_id=1, source_target_pairs={{0,1},{1,0},{2,3},{3,2},{4,5},{5,4},{6,7},{7,6},{8,9},{9,8},{10,11... | collective-permute-start | bytes 4915208 | tf_op jit(solution)/shard_map/ppermute | solution.py:1404
  54.9 22.3 %collective-permute-start.6 = (bf16[6400,128]{1,0:T(8,128)(2,1)S(1)}, bf16[6400,128]{1,0:T(8,128)(2,1)S(1)}, u32[]{:S(2)}, u32[]{:S(2)}) collective-permute-start(bf16[6400,128]{1,0:T(8,128)(2,1)S(1)} %collective-permute-done.1.refs_2_.refs_10_), channel_id=1, source_target_pairs={{0,1},{1,0},{2,3},{3,2},{4,5},{5,4},{6,7},{7,6},{8,9},{9,8},{10,11... | collective-permute-start | bytes 4915208 | tf_op jit(solution)/shard_map/ppermute | solution.py:1404
  55.4 7.6 %collective-permute-start.7 = (bf16[6144,128]{1,0:T(8,128)(2,1)S(1)}, bf16[6144,128]{1,0:T(8,128)(2,1)S(1)}, u32[]{:S(2)}, u32[]{:S(2)}) collective-permute-start(bf16[6144,128]{1,0:T(8,128)(2,1)S(1)} %get-tuple-element.148.refs_0_.refs_8_), channel_id=1, source_target_pairs={{0,1},{1,0},{2,3},{3,2},{4,5},{5,4},{6,7},{7,6},{8,9},{9,8},{10,11... | collective-permute-start | bytes 4718600 | tf_op jit(solution)/shard_map/ppermute | solution.py:1404
  55.8 21.4 %collective-permute-start.3 = (bf16[3328,128]{1,0:T(8,128)(2,1)S(1)}, bf16[3328,128]{1,0:T(8,128)(2,1)S(1)}, u32[]{:S(2)}, u32[]{:S(2)}) collective-permute-start(bf16[3328,128]{1,0:T(8,128)(2,1)S(1)} %slice.74), channel_id=1, source_target_pairs={{0,8},{8,0},{16,24},{24,16},{1,9},{9,1},{17,25},{25,17},{2,10},{10... | collective-permute-start | bytes 2555912 | tf_op jit(solution)/shard_map/ppermute | solution.py:1386
  56.2 19.6 %collective-permute-start.4 = (bf16[3072,128]{1,0:T(8,128)(2,1)S(1)}, bf16[3072,128]{1,0:T(8,128)(2,1)S(1)}, u32[]{:S(2)}, u32[]{:S(2)}) collective-permute-start(bf16[3072,128]{1,0:T(8,128)(2,1)S(1)} %slice.75), channel_id=1, source_target_pairs={{0,16},{8,24},{16,0},{24,8},{1,17},{9,25},{17,1},{25,9},{2,18},{10... | collective-permute-start | bytes 2359304 | tf_op jit(solution)/shard_map/ppermute | solution.py:1390
  62.9 16.9 %copy-start.20 = (bf16[6144,128]{1,0:T(8,128)(2,1)}, bf16[6144,128]{1,0:T(8,128)(2,1)S(1)}, u32[]{:S(2)}) copy-start(bf16[6144,128]{1,0:T(8,128)(2,1)S(1)} %collective-permute-done.7.refs_4_.refs_12_) | copy-start | bytes 4718596
  75.8 7.0 %copy-start.28 = (bf16[3072,128]{1,0:T(8,128)(2,1)}, bf16[3072,128]{1,0:T(8,128)(2,1)S(1)}, u32[]{:S(2)}) copy-start(bf16[3072,128]{1,0:T(8,128)(2,1)S(1)} %collective-permute-done.4.refs_11_) | copy-start | bytes 2359300
  77.2 38.7 %collective-permute-start.8 = (bf16[6144,128]{1,0:T(8,128)(2,1)S(1)}, bf16[6144,128]{1,0:T(8,128)(2,1)S(1)}, u32[]{:S(2)}, u32[]{:S(2)}) collective-permute-start(bf16[6144,128]{1,0:T(8,128)(2,1)S(1)} %get-tuple-element.148.refs_0_.refs_8_), channel_id=1, source_target_pairs={{0,8},{8,0},{16,24},{24,16},{1,9},{9,1},{17,25},{25,17},{2,10},{10... | collective-permute-start | bytes 4718600 | tf_op jit(solution)/shard_map/ppermute | solution.py:1386
  77.6 38.3 %collective-permute-start.9 = (bf16[6144,128]{1,0:T(8,128)(2,1)S(1)}, bf16[6144,128]{1,0:T(8,128)(2,1)}, u32[]{:S(2)}, u32[]{:S(2)}) collective-permute-start(bf16[6144,128]{1,0:T(8,128)(2,1)S(1)} %get-tuple-element.148.refs_0_.refs_8_), channel_id=1, source_target_pairs={{0,16},{8,24},{16,0},{24,8},{1,17},{9,25},{17,1},{25,9},{2,18},{10... | collective-permute-start | bytes 4718600 | tf_op jit(solution)/shard_map/ppermute | solution.py:1390
  79.3 4.4 collective-permute-start.10
  79.3 3.5 collective-permute-start.11
  115.9 7.6 %collective-permute-start.16 = (bf16[1024,2048]{1,0:T(8,128)(2,1)}, bf16[1024,2048]{1,0:T(8,128)(2,1)}, u32[]{:S(2)}, u32[]{:S(2)}) collective-permute-start(bf16[1024,2048]{1,0:T(8,128)(2,1)} %bitcast.77), channel_id=1, source_target_pairs={{0,1},{1,0},{2,3},{3,2},{4,5},{5,4},{6,7},{7,6},{8,9},{9,8},{10,11... | collective-permute-start | bytes 12582920 | tf_op jit(solution)/shard_map/ppermute | solution.py:1404
  116.1 264.3 %reduce-scatter.2.cloned.1.call-start = ((), (), s32[]{:S(2)}) async-start(), calls=%async_computation.2 | async-start | bytes 10485760 | tf_op jit(solution)/shard_map/reduce_scatter | solution.py:1519
  116.7 24.5 %collective-permute-start.14 = (bf16[6144,128]{1,0:T(8,128)(2,1)S(1)}, bf16[6144,128]{1,0:T(8,128)(2,1)S(1)}, u32[]{:S(2)}, u32[]{:S(2)}) collective-permute-start(bf16[6144,128]{1,0:T(8,128)(2,1)S(1)} %collective-permute-done.8.refs_1_.refs_9_), channel_id=1, source_target_pairs={{0,1},{1,0},{2,3},{3,2},{4,5},{5,4},{6,7},{7,6},{8,9},{9,8},{10,11... | collective-permute-start | bytes 4718600 | tf_op jit(solution)/shard_map/ppermute | solution.py:1404
  117.1 24.1 %collective-permute-start.15 = (bf16[6144,128]{1,0:T(8,128)(2,1)}, bf16[6144,128]{1,0:T(8,128)(2,1)}, u32[]{:S(2)}, u32[]{:S(2)}) collective-permute-start(bf16[6144,128]{1,0:T(8,128)(2,1)} %collective-permute-done.9.refs_0_.refs_2_.refs_10_), channel_id=1, source_target_pairs={{0,1},{1,0},{2,3},{3,2},{4,5},{5,4},{6,7},{7,6},{8,9},{9,8},{10,11... | collective-permute-start | bytes 4718600 | tf_op jit(solution)/shard_map/ppermute | solution.py:1404
  119.8 20.2 %collective-permute-start.12 = (bf16[3072,128]{1,0:T(8,128)(2,1)}, bf16[3072,128]{1,0:T(8,128)(2,1)}, u32[]{:S(2)}, u32[]{:S(2)}) collective-permute-start(bf16[3072,128]{1,0:T(8,128)(2,1)} %get-tuple-element.172), channel_id=1, source_target_pairs={{0,8},{8,0},{16,24},{24,16},{1,9},{9,1},{17,25},{25,17},{2,10},{10... | collective-permute-start | bytes 2359304 | tf_op jit(solution)/shard_map/ppermute | solution.py:1386
  121.3 19.8 %collective-permute-start.13 = (bf16[3072,128]{1,0:T(8,128)(2,1)}, bf16[3072,128]{1,0:T(8,128)(2,1)}, u32[]{:S(2)}, u32[]{:S(2)}) collective-permute-start(bf16[3072,128]{1,0:T(8,128)(2,1)} %get-tuple-element.173), channel_id=1, source_target_pairs={{0,16},{8,24},{16,0},{24,8},{1,17},{9,25},{17,1},{25,9},{2,18},{10... | collective-permute-start | bytes 2359304 | tf_op jit(solution)/shard_map/ppermute | solution.py:1390
  141.2 2.6 collective-permute-start.17
  141.3 3.6 collective-permute-start.18
  186.7 57.3 %collective-permute-start.19 = (bf16[1024,2560]{1,0:T(8,128)(2,1)}, bf16[1024,2560]{1,0:T(8,128)(2,1)}, u32[]{:S(2)}, u32[]{:S(2)}) collective-permute-start(bf16[1024,2560]{1,0:T(8,128)(2,1)} %get-tuple-element.201.refs_2_.refs_6_), channel_id=1, source_target_pairs={{0,1},{1,0},{2,3},{3,2},{4,5},{5,4},{6,7},{7,6},{8,9},{9,8},{10,11... | collective-permute-start | bytes 15728648 | tf_op jit(solution)/shard_map/ppermute | solution.py:1404
  204.3 6.0 %copy-start.5 = (s32[1024,1]{1,0:T(8,128)S(1)}, s32[1024,1]{1,0:T(8,128)}, u32[]{:S(2)}) copy-start(s32[1024,1]{1,0:T(8,128)} %copy.30.begins) | copy-start | bytes 12292
  204.3 6.0 %copy-start.6 = (f32[1024,128]{1,0:T(8,128)S(1)}, f32[1024,128]{1,0:T(8,128)}, u32[]{:S(2)}) copy-start(f32[1024,128]{1,0:T(8,128)} %get-tuple-element.198.upper) | copy-start | bytes 1572868
  204.3 6.0 %copy-start.7 = (f32[1024,128]{1,0:T(8,128)S(1)}, f32[1024,128]{1,0:T(8,128)}, u32[]{:S(2)}) copy-start(f32[1024,128]{1,0:T(8,128)} %get-tuple-element.197.lower) | copy-start | bytes 1572868
  204.3 6.0 %copy-start.8 = (f32[1024,128]{1,0:T(8,128)S(1)}, f32[1024,128]{1,0:T(8,128)}, u32[]{:S(2)}) copy-start(f32[1024,128]{1,0:T(8,128)} %get-tuple-element.196.plain) | copy-start | bytes 1572868
  204.4 39.7 %collective-permute-start.21 = (bf16[1024,2048]{1,0:T(8,128)(2,1)}, bf16[1024,2048]{1,0:T(8,128)(2,1)}, u32[]{:S(2)}, u32[]{:S(2)}) collective-permute-start(bf16[1024,2048]{1,0:T(8,128)(2,1)} %bitcast.70), channel_id=1, source_target_pairs={{0,1},{1,0},{2,3},{3,2},{4,5},{5,4},{6,7},{7,6},{8,9},{9,8},{10,11... | collective-permute-start | bytes 12582920 | tf_op jit(solution)/shard_map/ppermute | solution.py:1404
  223.2 10.6 %copy-start = (bf16[1024,1536]{1,0:T(8,128)(2,1)}, bf16[1024,1536]{1,0:T(8,128)(2,1)S(1)}, u32[]{:S(2)}) copy-start(bf16[1024,1536]{1,0:T(8,128)(2,1)S(1)} %attend_back.1.refs_8_.grad_projected) | copy-start | bytes 9437188
  223.2 20.8 %collective-permute-start.20 = (bf16[1024,1536]{1,0:T(8,128)(2,1)S(1)}, bf16[1024,1536]{1,0:T(8,128)(2,1)}, u32[]{:S(2)}, u32[]{:S(2)}) collective-permute-start(bf16[1024,1536]{1,0:T(8,128)(2,1)S(1)} %attend_back.1.refs_8_.grad_projected), channel_id=1, source_target_pairs={{0,1},{1,0},{2,3},{3,2},{4,5},{5,4},{6,7},{7,6},{8,9},{9,8},{10,11... | collective-permute-start | bytes 9437192 | tf_op jit(solution)/shard_map/ppermute | solution.py:1404
  223.3 10.6 %copy-start.12 = (s32[8]{0:T(128)S(1)}, s32[8]{0:T(128)}, u32[]{:S(2)}) copy-start(s32[8]{0:T(128)} %copy-done.11) | copy-start | bytes 100
  233.8 10.2 %collective-permute-start.22 = (bf16[1024,1024]{1,0:T(8,128)(2,1)}, bf16[1024,1024]{1,0:T(8,128)(2,1)}, u32[]{:S(2)}, u32[]{:S(2)}) collective-permute-start(bf16[1024,1024]{1,0:T(8,128)(2,1)} %get-tuple-element.227.rest_before), channel_id=1, source_target_pairs={{0,1},{1,0},{2,3},{3,2},{4,5},{5,4},{6,7},{7,6},{8,9},{9,8},{10,11... | collective-permute-start | bytes 6291464 | tf_op jit(solution)/shard_map/ppermute | solution.py:1404
  244.1 43.3 %copy-start.34 = (f32[1,1024]{1,0:T(1,128)S(1)}, f32[1,1024]{1,0:T(1,128)}, u32[]{:S(2)}) copy-start(f32[1,1024]{1,0:T(1,128)} %get-tuple-element.236) | copy-start | bytes 12292
  244.1 43.3 %copy-start.35 = (f32[1,1024]{1,0:T(1,128)S(1)}, f32[1,1024]{1,0:T(1,128)}, u32[]{:S(2)}) copy-start(f32[1,1024]{1,0:T(1,128)} %get-tuple-element.235) | copy-start | bytes 12292
  285.0 29.2 %collective-permute-start.25 = (f32[2,2,3136,128]{3,2,1,0:T(8,128)}, f32[2,2,3136,128]{3,2,1,0:T(8,128)}, u32[]{:S(2)}, u32[]{:S(2)}) collective-permute-start(f32[2,2,3136,128]{3,2,1,0:T(8,128)} %get-tuple-element.231.refs_0_), channel_id=1, source_target_pairs={{0,1},{1,0},{2,3},{3,2},{4,5},{5,4},{6,7},{7,6},{8,9},{9,8},{10,11... | collective-permute-start | bytes 19267592 | tf_op jit(solution)/shard_map/ppermute | solution.py:1404
  285.6 40.3 %collective-permute-start.23 = (bf16[2,3136,128]{2,1,0:T(8,128)(2,1)}, bf16[2,3136,128]{2,1,0:T(8,128)(2,1)}, u32[]{:S(2)}, u32[]{:S(2)}) collective-permute-start(bf16[2,3136,128]{2,1,0:T(8,128)(2,1)} %get-tuple-element.222), channel_id=1, source_target_pairs={{0,8},{8,0},{16,24},{24,16},{1,9},{9,1},{17,25},{25,17},{2,10},{10... | collective-permute-start | bytes 4816904 | tf_op jit(solution)/shard_map/ppermute | solution.py:1386
  286.3 39.6 %collective-permute-start.24 = (bf16[2,3136,128]{2,1,0:T(8,128)(2,1)}, bf16[2,3136,128]{2,1,0:T(8,128)(2,1)}, u32[]{:S(2)}, u32[]{:S(2)}) collective-permute-start(bf16[2,3136,128]{2,1,0:T(8,128)(2,1)} %get-tuple-element.223), channel_id=1, source_target_pairs={{0,16},{8,24},{16,0},{24,8},{1,17},{9,25},{17,1},{25,9},{2,18},{10... | collective-permute-start | bytes 4816904 | tf_op jit(solution)/shard_map/ppermute | solution.py:1390
  290.2 28.2 %copy-start.1 = (bf16[1024,1536]{1,0:T(8,128)(2,1)S(1)}, bf16[1024,1536]{1,0:T(8,128)(2,1)}, u32[]{:S(2)}) copy-start(bf16[1024,1536]{1,0:T(8,128)(2,1)} %copy-done) | copy-start | bytes 9437188
  314.2 6.7 %collective-permute-start.27 = (f32[4,2048]{1,0:T(4,128)}, f32[4,2048]{1,0:T(4,128)S(1)}, u32[]{:S(2)}, u32[]{:S(2)}) collective-permute-start(f32[4,2048]{1,0:T(4,128)} %get-tuple-element.234), channel_id=1, source_target_pairs={{0,4},{2,6},{4,0},{6,2},{1,5},{3,7},{5,1},{7,3},{8,12},{10,14},{12... | collective-permute-start | bytes 98312 | tf_op jit(solution)/shard_map/ppermute | solution.py:1394
  316.9 7.0 %collective-permute-start.28 = (f32[4,2048]{1,0:T(4,128)}, f32[4,2048]{1,0:T(4,128)S(1)}, u32[]{:S(2)}, u32[]{:S(2)}) collective-permute-start(f32[4,2048]{1,0:T(4,128)} %get-tuple-element.234), channel_id=1, source_target_pairs={{0,6},{2,4},{4,2},{6,0},{1,7},{3,5},{5,3},{7,1},{8,14},{10,12},{12... | collective-permute-start | bytes 98312 | tf_op jit(solution)/shard_map/ppermute | solution.py:1394
  318.1 7.0 %collective-permute-start.26 = (f32[4,2048]{1,0:T(4,128)}, f32[4,2048]{1,0:T(4,128)S(1)}, u32[]{:S(2)}, u32[]{:S(2)}) collective-permute-start(f32[4,2048]{1,0:T(4,128)} %get-tuple-element.234), channel_id=1, source_target_pairs={{0,2},{2,0},{4,6},{6,4},{1,3},{3,1},{5,7},{7,5},{8,10},{10,8},{12,... | collective-permute-start | bytes 98312 | tf_op jit(solution)/shard_map/ppermute | solution.py:1394
  325.9 124.9 %all-to-all-start = ((bf16[4,256,2048]{2,1,0:T(8,128)(2,1)}), bf16[4,256,2048]{2,1,0:T(8,128)(2,1)}, u32[]{:S(2)}, u32[]{:S(2)}) async-start(bf16[4,256,2048]{2,1,0:T(8,128)(2,1)} %bitcast.83), calls=%async_computation.1 | async-start | bytes 8388608 | tf_op jit(solution)/shard_map/all_to_all | solution.py:1410
  330.9 4.5 collective-permute-start.33
  331.0 52.9 %collective-permute-start.29 = (bf16[3136,128]{1,0:T(8,128)(2,1)}, bf16[3136,128]{1,0:T(8,128)(2,1)}, u32[]{:S(2)}, u32[]{:S(2)}) collective-permute-start(bf16[3136,128]{1,0:T(8,128)(2,1)} %get-tuple-element.241), channel_id=1, source_target_pairs={{0,8},{8,0},{16,24},{24,16},{1,9},{9,1},{17,25},{25,17},{2,10},{10... | collective-permute-start | bytes 2408456 | tf_op jit(solution)/shard_map/ppermute | solution.py:1386
  333.0 50.9 %collective-permute-start.30 = (bf16[3136,128]{1,0:T(8,128)(2,1)}, bf16[3136,128]{1,0:T(8,128)(2,1)}, u32[]{:S(2)}, u32[]{:S(2)}) collective-permute-start(bf16[3136,128]{1,0:T(8,128)(2,1)} %get-tuple-element.242), channel_id=1, source_target_pairs={{0,16},{8,24},{16,0},{24,8},{1,17},{9,25},{17,1},{25,9},{2,18},{10... | collective-permute-start | bytes 2408456 | tf_op jit(solution)/shard_map/ppermute | solution.py:1390
  335.2 48.7 %collective-permute-start.31 = (bf16[3136,128]{1,0:T(8,128)(2,1)}, bf16[3136,128]{1,0:T(8,128)(2,1)}, u32[]{:S(2)}, u32[]{:S(2)}) collective-permute-start(bf16[3136,128]{1,0:T(8,128)(2,1)} %get-tuple-element.243), channel_id=1, source_target_pairs={{0,9},{1,8},{8,1},{9,0},{16,25},{17,24},{24,17},{25,16},{2,11},{3,... | collective-permute-start | bytes 2408456 | tf_op jit(solution)/shard_map/ppermute | solution.py:1398
  335.2 48.7 %collective-permute-start.32 = (bf16[3136,128]{1,0:T(8,128)(2,1)}, bf16[3136,128]{1,0:T(8,128)(2,1)}, u32[]{:S(2)}, u32[]{:S(2)}) collective-permute-start(bf16[3136,128]{1,0:T(8,128)(2,1)} %get-tuple-element.244), channel_id=1, source_target_pairs={{0,17},{1,16},{8,25},{9,24},{16,1},{17,0},{24,9},{25,8},{2,19},{3,... | collective-permute-start | bytes 2408456 | tf_op jit(solution)/shard_map/ppermute | solution.py:1398
  335.5 34.8 %copy-start.33 = (f32[16384]{0:T(1024)S(1)}, f32[16384]{0:T(1024)}, u32[]{:S(2)}) copy-start(f32[16384]{0:T(1024)} %copy-done.32) | copy-start | bytes 196612
  335.5 45.0 %copy-start.16 = (bf16[1,256,2048]{2,1,0:T(8,128)(2,1)S(1)}, bf16[1,256,2048]{2,1,0:T(8,128)(2,1)}, u32[]{:S(2)}) copy-start(bf16[1,256,2048]{2,1,0:T(8,128)(2,1)} %param.12) | copy-start | bytes 3145732
  335.5 34.8 %collective-permute-start.34 = (f32[128,128]{1,0:T(8,128)S(1)}, f32[128,128]{1,0:T(8,128)S(1)}, u32[]{:S(2)}, u32[]{:S(2)}) collective-permute-start(f32[128,128]{1,0:T(8,128)S(1)} %bitcast_add_fusion), channel_id=1, source_target_pairs={{0,8},{8,0},{16,24},{24,16},{1,9},{9,1},{17,25},{25,17},{2,10},{10... | collective-permute-start | bytes 196616 | tf_op jit(solution)/shard_map/ppermute | solution.py:1386
  383.9 38.6 %collective-permute-start.35 = (bf16[3136,128]{1,0:T(8,128)(2,1)S(1)}, bf16[3136,128]{1,0:T(8,128)(2,1)S(1)}, u32[]{:S(2)}, u32[]{:S(2)}) collective-permute-start(bf16[3136,128]{1,0:T(8,128)(2,1)S(1)} %copy-done.23), channel_id=1, source_target_pairs={{0,16},{8,24},{16,0},{24,8},{1,17},{9,25},{17,1},{25,9},{2,18},{10... | collective-permute-start | bytes 2408456 | tf_op jit(solution)/shard_map/ppermute | solution.py:1390
  385.2 37.3 %collective-permute-start.36 = (bf16[3136,128]{1,0:T(8,128)(2,1)S(1)}, bf16[3136,128]{1,0:T(8,128)(2,1)S(1)}, u32[]{:S(2)}, u32[]{:S(2)}) collective-permute-start(bf16[3136,128]{1,0:T(8,128)(2,1)S(1)} %get-tuple-element.261), channel_id=1, source_target_pairs={{0,8},{8,0},{16,24},{24,16},{1,9},{9,1},{17,25},{25,17},{2,10},{10... | collective-permute-start | bytes 2408456 | tf_op jit(solution)/shard_map/ppermute | solution.py:1386
  386.7 35.8 %collective-permute-start.37 = (bf16[3136,128]{1,0:T(8,128)(2,1)S(1)}, bf16[3136,128]{1,0:T(8,128)(2,1)S(1)}, u32[]{:S(2)}, u32[]{:S(2)}) collective-permute-start(bf16[3136,128]{1,0:T(8,128)(2,1)S(1)} %get-tuple-element.262), channel_id=1, source_target_pairs={{0,17},{1,16},{8,25},{9,24},{16,1},{17,0},{24,9},{25,8},{2,19},{3,... | collective-permute-start | bytes 2408456 | tf_op jit(solution)/shard_map/ppermute | solution.py:1398
  386.7 35.8 %collective-permute-start.38 = (bf16[3136,128]{1,0:T(8,128)(2,1)S(1)}, bf16[3136,128]{1,0:T(8,128)(2,1)S(1)}, u32[]{:S(2)}, u32[]{:S(2)}) collective-permute-start(bf16[3136,128]{1,0:T(8,128)(2,1)S(1)} %get-tuple-element.263), channel_id=1, source_target_pairs={{0,9},{1,8},{8,1},{9,0},{16,25},{17,24},{24,17},{25,16},{2,11},{3,... | collective-permute-start | bytes 2408456 | tf_op jit(solution)/shard_map/ppermute | solution.py:1398
  390.4 31.5 %collective-permute-start.39 = (f32[128,128]{1,0:T(8,128)S(1)}, f32[128,128]{1,0:T(8,128)S(1)}, u32[]{:S(2)}, u32[]{:S(2)}) collective-permute-start(f32[128,128]{1,0:T(8,128)S(1)} %fusion.15), channel_id=1, source_target_pairs={{0,16},{8,24},{16,0},{24,8},{1,17},{9,25},{17,1},{25,9},{2,18},{10... | collective-permute-start | bytes 196616 | tf_op jit(solution)/shard_map/ppermute | solution.py:1390
  (17 other events, 45.7 us)
Sparse Core Ops, SparseCore 0:
  9.6 83.4 all-gather.4
  116.3 81.0 all-gather.6
  204.4 176.0 reduce-scatter.1

commit v6 on v5

--- a/solution.py
+++ b/solution.py
@@ -1584,11 +1584,12 @@
     ).reshape(LANES, LANES)
     small = small + across(small)
     small = small + along_x(small)
+    near, pass_a, pass_b, small = order(near, pass_a, pass_b, small)
     output = residual[0].astype(jnp.float32) + branches + small_params[4] + small_params[5]
-    near, pass_a, pass_b, small, output = order(near, pass_a, pass_b, small, output)
     far = [along_y(pass_a[0]), along_x(pass_b[0]), along(2, pass_a[1]), along(1, pass_b[1])]
+    output, small = order(output, small)
     small = small + along_y(small)
-    far, small = order(far, small)
+    far, output, small = order(far, output, small)
 
     step_value = step_count[0].astype(jnp.float32)
     scalars = jnp.stack(

time: 471 us -> 459 us (0.975)
  waiting for transfers between devices: 141 us -> 132 us
    ppermute x8, waiting for transfers between devices: 45.1 us -> 38.3 us  [along_y(): return lax.ppermute(value, 'dp', [(i, i ^ 2) for i in range(4)])]
    reduce_scatter x1, waiting for transfers between devices: 10.2 us -> 5.01 us  [on_device_fast(): lax.psum_scatter(branches, 'tensor', scatter_dimension=0, tiled=True)]
  transfers between devices with their start and end apart: 44 -> 44, of which waited for: 17 -> 18; matrix products, arithmetic and copies ran while one was open for 10% -> 10% of each run, Pallas kernels for 45% -> 46%
where the time goes in v6:
time: 459 us; the launch traced here: 453 us
  Pallas kernels  215 us (47%)
  waiting for transfers between devices  132 us (29%)
  starting transfers between devices  37.8 us (8%)
  matrix products  22.7 us (5%)
  other arithmetic  20.9 us (5%)
  between operations  16.9 us (4%)
  local copies, waits for them, and re-layouts  8.66 us (2%)
    ppermute x8, waiting for transfers between devices, along_x(): return lax.ppermute(value, 'dp', [(i, i ^ 1) for i in range(4)])  71.9 us
    pallas_call x1, Pallas kernels, weight_grads(): pl.pallas_call(weight_grad_kernel, out_shape=[near, near, short] * 2 + [w...  40.6 us
    ppermute x8, waiting for transfers between devices, along_y(): return lax.ppermute(value, 'dp', [(i, i ^ 2) for i in range(4)])  38.3 us
    pallas_call x1, Pallas kernels, adam(): pl.pallas_call(adam_kernel, grid=(steps,), out_shape=[jax.ShapeDtypeStruc...  26.8 us
    pallas_call x1, Pallas kernels, norm_grad(): pl.pallas_call(norm_grad_kernel, out_shape=[jax.ShapeDtypeStruct((tokens,...  23.9 us
    pallas_call x1, Pallas kernels, attend(): pl.pallas_call(attend_kernel, grid=(pairs,), out_shape=[jax.ShapeDtypeStr...  22.1 us
    pallas_call x2, Pallas kernels, hidden_back(): pl.pallas_call(hidden_back_kernel, out_shape=[jax.ShapeDtypeStruct((rows,...  19.8 us
    pallas_call x1, Pallas kernels, unpack_hidden(): pl.pallas_call(functools.partial(unpack_hidden_kernel, width), out_shape=...  18.8 us
  transfers between devices with their start and end apart: 44, of which 18 were waited for; matrix products, arithmetic and copies ran while one was open for 10% of the time, Pallas kernels for 46%

profile of v6, /device:TPU:0, one launch (start us, length us, event | category | flops | bytes accessed | tf_op | source)
XLA Modules:
  0.0 453.1 jit_solution(5515421957971172569)
XLA Ops:
  7.2 0.7 all-gather.5.cloned.1.call-update
  8.1 0.8 select_reduce_fusion.4
  9.0 2.8 copy-done.2
  11.8 2.1 pack_params.1
  13.9 3.6 collective-permute-start
  17.5 1.5 collective-permute-start.1
  19.0 34.3 %collective-permute-done.refs_1_.refs_9_ = bf16[6400,128]{1,0:T(8,128)(2,1)S(1)} collective-permute-done((bf16[6400,128]{1,0:T(8,128)(2,1)S(1)}, bf16[6400,128]{1,0:T(8,128)(2,1)S(1)}, u32[]{:S(2)}, u32[]{:S(2)}) %collective-permute-start) | collective-permute-done | bytes 1638432 | tf_op jit(solution)/shard_map/ppermute | solution.py:1386
  53.3 1.5 collective-permute-done.1.refs_2_.refs_10_
  56.2 1.7 collective-permute-start.4
  58.1 1.9 multiply_sine_fusion
  60.0 1.6 maximum_maximum_fusion.2
  61.7 1.3 collective-permute-done.7.refs_4_.refs_12_
  62.9 12.9 %collective-permute-done.4.refs_11_ = bf16[3072,128]{1,0:T(8,128)(2,1)S(1)} collective-permute-done((bf16[3072,128]{1,0:T(8,128)(2,1)S(1)}, bf16[3072,128]{1,0:T(8,128)(2,1)S(1)}, u32[]{:S(2)}, u32[]{:S(2)}) %collective-permute-start.4) | collective-permute-done | bytes 786464 | tf_op jit(solution)/shard_map/ppermute | solution.py:1390
  75.8 1.3 collective-permute-done.3.refs_3_
  77.6 1.7 collective-permute-start.9
  79.8 3.0 collective-permute-done.11.refs_15_
  82.8 0.9 copy-done.28
  83.7 10.8 %unpack_params.1 = (bf16[2048,1536]{1,0:T(8,128)(2,1)}, bf16[2560,2048]{1,0:T(8,128)(2,1)}, bf16[2048,2048]{1,0:T(8,128)(2,1)}, bf16[16,2048]{1,0:T(8,128)(2,1)}, bf16[8,256,128]{2,1,0:T(8,128)(2,1)}) custom-call(s32[8]{0:T(128)} %copy-done.11, bf16[6400,128]{1,0:T(8,128)(2,1)} %copy-done.3, bf16[6400,128]{1,0:T(8,128)(2,1)} %copy-done.15, ...), custom_call_target="tpu_custom_call" | custom-call | flops 1 | bytes 1 | tf_op jit(solution)/shard_map/unpack_params/pallas_call | solution.py:580
  94.6 0.8 convert_bitcast_fusion
  96.0 9.1 %norms.2 = (bf16[1024,2048]{1,0:T(8,128)(2,1)}, bf16[1024,2048]{1,0:T(8,128)(2,1)}, f32[1024,1]{1,0:T(8,128)}, f32[1024,1]{1,0:T(8,128)}) custom-call(bf16[1024,2048]{1,0:T(8,128)(2,1)} %bitcast.76, f32[6,2048]{1,0:T(8,128)} %reshape.97.gains), custom_call_target="tpu_custom_call" | custom-call | flops 1 | bytes 1 | tf_op jit(solution)/shard_map/norms/pallas_call | solution.py:1214
  105.7 10.2 %hidden_layer.1 = (bf16[1024,2560]{1,0:T(8,128)(2,1)}, f32[1024,2048]{1,0:T(8,128)}) custom-call(bf16[1024,2048]{1,0:T(8,128)(2,1)} %get-tuple-element.191.normed.refs_17_.refs_4_, bf16[2048,2048]{1,0:T(8,128)(2,1)} %get-tuple-element.194.up.refs_21_, f32[1,2048]{1,0:T(1,128)} %bitcast.93), custom_call_target="tpu_custom_call" | custom-call | flops 1 | bytes 1 | tf_op jit(solution)/shard_map/hidden_layer/pallas_call | solution.py:1143
  117.3 2.5 cut.1
  119.8 1.0 collective-permute-start.12
  120.8 1.1 collective-permute-start.13
  121.9 1.6 collective-permute-done.16.rows
  123.5 9.4 %norms.3 = (bf16[1024,2048]{1,0:T(8,128)(2,1)}, bf16[1024,2048]{1,0:T(8,128)(2,1)}, f32[1024,1]{1,0:T(8,128)}, f32[1024,1]{1,0:T(8,128)}) custom-call(bf16[1024,2048]{1,0:T(8,128)(2,1)} %collective-permute-done.16.rows, f32[6,2048]{1,0:T(8,128)} %reshape.97.gains), custom_call_target="tpu_custom_call" | custom-call | flops 1 | bytes 1 | tf_op jit(solution)/shard_map/norms/pallas_call | solution.py:1214
  132.9 7.1 %collective-permute-done.12.refs_3_ = bf16[3072,128]{1,0:T(8,128)(2,1)} collective-permute-done((bf16[3072,128]{1,0:T(8,128)(2,1)}, bf16[3072,128]{1,0:T(8,128)(2,1)}, u32[]{:S(2)}, u32[]{:S(2)}) %collective-permute-start.12) | collective-permute-done | bytes 786464 | tf_op jit(solution)/shard_map/ppermute | solution.py:1386
  141.2 1.0 copy.30.begins
  143.2 1.1 collective-permute-done.18.refs_15_
  144.3 0.9 copy-done.30
  145.3 18.8 %unpack_hidden.1 = (bf16[2048,1536]{1,0:T(8,128)(2,1)}, bf16[2560,2048]{1,0:T(8,128)(2,1)}, bf16[2048,2048]{1,0:T(8,128)(2,1)}, bf16[1024,2560]{1,0:T(8,128)(2,1)}, f32[1024,2048]{1,0:T(8,128)}) custom-call(s32[8]{0:T(128)} %copy-done.11, ...), custom_call_target="tpu_custom_call", output_to_operand_aliasing={{0}: (20, {}), {1}: (21, {}), {2}: (22, {}), {3}: (23, {}),... | custom-call | flops 1 | bytes 1 | tf_op jit(solution)/shard_map/unpack_hidden/pallas_call | solution.py:648
  164.1 22.1 %attend.1 = (bf16[1024,2560]{1,0:T(8,128)(2,1)}, bf16[3,1024,512]{2,1,0:T(8,128)(2,1)}, f32[4,1024,1]{2,1,0:T(8,128)}) custom-call(bf16[1024,2048]{1,0:T(8,128)(2,1)} %get-tuple-element.171.normed.refs_0_, bf16[2048,1536]{1,0:T(8,128)(2,1)} %get-tuple-element.197.queries_in.keys_in.values_in.mixer_in, ...), custom_call_target="tpu_custom_call", output_to_operand_aliasing={{0}: (9, {})} | custom-call | flops 1 | bytes 1 | tf_op jit(solution)/shard_map/attend/pallas_call | solution.py:1296
  186.4 17.3 %fusion.11 = f32[1024,2048]{1,0:T(8,128)} fusion(bf16[1024,2560]{1,0:T(8,128)(2,1)} %get-tuple-element.203.refs_2_.refs_6_, bf16[2560,2048]{1,0:T(8,128)(2,1)} %get-tuple-element.204.down), kind=kOutput, calls=%fused_computation.60 | convolution fusion | flops 10737418240 | bytes 24117248 | tf_op jit(solution)/shard_map/dot_general | solution.py:27
  204.2 5.4 %fusion.6.grad_context = bf16[1024,512]{1,0:T(8,128)(2,1)S(1)} fusion(bf16[1024,2048]{1,0:T(8,128)(2,1)} %bitcast.71, bf16[2560,2048]{1,0:T(8,128)(2,1)} %get-tuple-element.204.down), kind=kOutput, calls=%fused_computation.13 | convolution fusion | flops 2148007936 | bytes 7340032 | tf_op jit(solution)/shard_map/dot_general | solution.py:37
  209.6 12.8 %attend_back.1.refs_8_.grad_projected = bf16[1024,1536]{1,0:T(8,128)(2,1)S(1)} custom-call(bf16[3,1024,512]{2,1,0:T(8,128)(2,1)S(1)} %copy-done.9, f32[4,1024,1]{2,1,0:T(8,128)S(1)} %copy-done.10, f32[1024,128]{1,0:T(8,128)S(1)} %copy-done.8, f32[1024,128]{1,0:T(8,128)S(1)} %copy-done.7, f32[1024,128]{1,0:T(8,128)S(1)} %copy-done.6, ...), custom_call_target="tpu_custom_call" | custom-call | flops 1 | bytes 1 | tf_op jit(solution)/shard_map/attend_back/pallas_call | solution.py:1359
  222.7 10.4 %hidden_back.3 = (bf16[1024,1024]{1,0:T(8,128)(2,1)}, f32[1,1024]{1,0:T(1,128)}) custom-call(s32[1]{0:T(128)S(6)} %sub.30.half, bf16[1024,2048]{1,0:T(8,128)(2,1)} %bitcast.72, bf16[2560,2048]{1,0:T(8,128)(2,1)} %get-tuple-element.204.down, f32[1024,2048]{1,0:T(8,128)} %get-tuple-element.211.slope), custom_call_target="tpu_custom_call" | custom-call | flops 1 | bytes 1 | tf_op jit(solution)/shard_map/hidden_back/pallas_call | solution.py:1172
  234.1 9.4 %hidden_back.2 = (bf16[1024,1024]{1,0:T(8,128)(2,1)}, f32[1,1024]{1,0:T(1,128)}) custom-call(s32[1]{0:T(128)} %bitcast.14.half.core, bf16[1024,2048]{1,0:T(8,128)(2,1)} %bitcast.73, bf16[2560,2048]{1,0:T(8,128)(2,1)} %get-tuple-element.204.down, f32[1024,2048]{1,0:T(8,128)} %get-tuple-element.211.slope), custom_call_target="tpu_custom_call" | custom-call | flops 1 | bytes 1 | tf_op jit(solution)/shard_map/hidden_back/pallas_call | solution.py:1172
  243.5 40.6 %weight_grads.1 = (bf16[3136,128]{1,0:T(8,128)(2,1)}, bf16[3136,128]{1,0:T(8,128)(2,1)}, bf16[2,3136,128]{2,1,0:T(8,128)(2,1)}, bf16[3136,128]{1,0:T(8,128)(2,1)...) custom-call(s32[33]{0:T(128)} %concatenate.24.table, ...), custom_call_target="tpu_custom_call" | custom-call | flops 1 | bytes 1 | tf_op jit(solution)/shard_map/weight_grads/pallas_call | solution.py:862
  284.6 1.5 collective-permute-start.23
  286.1 0.8 collective-permute-start.24
  287.5 2.8 convert_reduce_fusion
  290.3 23.9 %norm_grad.1 = (bf16[1024,2048]{1,0:T(8,128)(2,1)}, f32[4,2048]{1,0:T(4,128)}) custom-call(s32[1]{0:T(128)} %bitcast.14.half.core, bf16[1024,1536]{1,0:T(8,128)(2,1)} %copy-done, bf16[2048,1536]{1,0:T(8,128)(2,1)} %get-tuple-element.197.queries_in.keys_in.values_in.mixer_in, bf16[1024,1024]{1,0:T(8,128)(2,1)} %get-tuple-element.227.refs_12_.own_before, ...), custom_call_target="tpu_custom_call" | custom-call | flops 1 | bytes 1 | tf_op jit(solution)/shard_map/norm_grad/pallas_call | solution.py:910
  314.2 2.9 collective-permute-start.27
  317.1 1.1 collective-permute-start.28
  319.1 1.9 collective-permute-done.27
  321.1 3.0 collective-permute-done.28
  324.3 0.8 add_add_fusion.1
  325.1 4.9 %all-to-all-start = ((bf16[4,256,2048]{2,1,0:T(8,128)(2,1)}), bf16[4,256,2048]{2,1,0:T(8,128)(2,1)}, u32[]{:S(2)}, u32[]{:S(2)}) async-start(bf16[4,256,2048]{2,1,0:T(8,128)(2,1)} %bitcast.83), calls=%async_computation.1 | async-start | bytes 8388608 | tf_op jit(solution)/shard_map/all_to_all | solution.py:1410
  332.2 0.9 collective-permute-start.29
  333.6 1.0 collective-permute-start.31
  334.6 1.5 collective-permute-start.32
  336.1 0.9 collective-permute-start.34
  337.0 5.2 %fusion.2 = (bf16[3136,128]{1,0:T(8,128)(2,1)S(1)}, bf16[3136,128]{1,0:T(8,128)(2,1)S(1)}, bf16[3136,128]{1,0:T(8,128)(2,1)}, bf16[3136,128]{1,0:T(8,128)(2,1)S(1)}) fusion(f32[2,2,3136,128]{3,2,1,0:T(8,128)} %get-tuple-element.247, bf16[2,3136,128]{2,1,0:T(8,128)(2,1)} %collective-permute-done.24, bf16[2,3136,128]{2,1,0:T(8,128)(2,1)} %collective-permute-done.23), kind=kLoop, calls=%fused_computation.6 | loop fusion | flops 4816896 | bytes 12845056 | tf_op jit(solution)/shard_map/convert_element_type | solution.py:1574
  342.2 29.2 %collective-permute-done.34 = f32[128,128]{1,0:T(8,128)S(1)} collective-permute-done((f32[128,128]{1,0:T(8,128)S(1)}, f32[128,128]{1,0:T(8,128)S(1)}, u32[]{:S(2)}, u32[]{:S(2)}) %collective-permute-start.34) | collective-permute-done | bytes 65568 | tf_op jit(solution)/shard_map/ppermute | solution.py:1386
  371.5 0.8 collective-permute-start.35
  373.3 2.1 collective-permute-start.38
  375.3 0.7 pad_add_fusion.table
  376.0 5.0 %reduce-scatter.2.cloned.1.call-done = f32[256,2048]{1,0:T(8,128)} async-done(((f32[1024,2048]{1,0:T(8,128)}), f32[256,2048]{1,0:T(8,128)}) %reduce-scatter.2.cloned.1.call-update) | async-done | bytes 2097168 | tf_op jit(solution)/shard_map/reduce_scatter | solution.py:1519
  381.0 3.3 add_add_fusion
  384.4 1.7 collective-permute-start.39
  386.7 23.3 %collective-permute-done.39 = f32[128,128]{1,0:T(8,128)S(1)} collective-permute-done((f32[128,128]{1,0:T(8,128)S(1)}, f32[128,128]{1,0:T(8,128)S(1)}, u32[]{:S(2)}, u32[]{:S(2)}) %collective-permute-start.39) | collective-permute-done | bytes 65568 | tf_op jit(solution)/shard_map/ppermute | solution.py:1390
  410.6 26.8 %adam.1 = (f32[12304,128]{1,0:T(8,128)}, f32[12304,128]{1,0:T(8,128)}, f32[12304,128]{1,0:T(8,128)}, f32[12304,128]{1,0:T(8,128)}, f32[12304,128]{1,0:T(8,128)}) custom-call(s32[2]{0:T(128)} %pad_add_fusion.table, f32[4]{0:T(128)} %pad_maximum_fusion.1.scalar_ref, f32[8]{0:T(128)} %rate_ref.1, f32[2,2,3136,128]{3,2,1,0:T(8,128)} %get-tuple-element.233.refs_0_, ...), custom_call_target="tpu_custom_call" | custom-call | flops 1 | bytes 1 | tf_op jit(solution)/shard_map/adam/pallas_call | solution.py:1073
  437.5 3.2 all-to-all-done.terms
  440.7 5.4 %finish.1 = f32[256,2048]{1,0:T(8,128)} custom-call(bf16[4,256,2048]{2,1,0:T(8,128)(2,1)} %all-to-all-done.terms, bf16[256,2048]{1,0:T(8,128)(2,1)} %bitcast.79, bf16[256,2048]{1,0:T(8,128)(2,1)} %bitcast.84), custom_call_target="tpu_custom_call" | custom-call | flops 1 | bytes 1 | tf_op jit(solution)/shard_map/finish/pallas_call | solution.py:1111
  (164 shorter events, 14.6 us)
Async XLA Ops:
  7.2 48.3 %copy-start.35 = (s32[1,5]{1,0:T(1,128)S(1)}, s32[1,5]{1,0:T(1,128)}, u32[]{:S(2)}) copy-start(s32[1,5]{1,0:T(1,128)} %param.14) | copy-start | bytes 64
  7.2 87.4 %all-gather.5.cloned.1.call-start = ((), (), s32[]{:S(2)}) async-start(), calls=%async_computation.3 | async-start | bytes 5242880 | tf_op jit(solution)/shard_map/all_gather | solution.py:1448
  7.9 195.8 %all-gather.7.cloned.1.call-start = ((), (), s32[]{:S(2)}) async-start(), calls=%async_computation.4 | async-start | bytes 5242880 | tf_op jit(solution)/shard_map/all_gather | solution.py:1449
  9.0 46.8 %copy-start.11 = (s32[8]{0:T(128)}, s32[8]{0:T(128)S(1)}, u32[]{:S(2)}) copy-start(s32[8]{0:T(128)S(1)} %select_reduce_fusion.3.bucket_ref) | copy-start | bytes 100
  13.9 47.7 %copy-start.3 = (bf16[6400,128]{1,0:T(8,128)(2,1)}, bf16[6400,128]{1,0:T(8,128)(2,1)S(1)}, u32[]{:S(2)}) copy-start(bf16[6400,128]{1,0:T(8,128)(2,1)S(1)} %get-tuple-element.146.refs_0_.refs_8_) | copy-start | bytes 4915204
  13.9 63.7 %copy-start.4 = (bf16[6144,128]{1,0:T(8,128)(2,1)}, bf16[6144,128]{1,0:T(8,128)(2,1)S(1)}, u32[]{:S(2)}) copy-start(bf16[6144,128]{1,0:T(8,128)(2,1)S(1)} %get-tuple-element.150.refs_0_.refs_8_) | copy-start | bytes 4718596
  13.9 39.4 %collective-permute-start = (bf16[6400,128]{1,0:T(8,128)(2,1)S(1)}, bf16[6400,128]{1,0:T(8,128)(2,1)S(1)}, u32[]{:S(2)}, u32[]{:S(2)}) collective-permute-start(bf16[6400,128]{1,0:T(8,128)(2,1)S(1)} %get-tuple-element.146.refs_0_.refs_8_), channel_id=1, source_target_pairs={{0,8},{8,0},{16,24},{24,16},{1,9},{9,1},{17,25},{25,17},{2,10},{10... | collective-permute-start | bytes 4915208 | tf_op jit(solution)/shard_map/ppermute | solution.py:1386
  17.5 37.3 %collective-permute-start.1 = (bf16[6400,128]{1,0:T(8,128)(2,1)S(1)}, bf16[6400,128]{1,0:T(8,128)(2,1)S(1)}, u32[]{:S(2)}, u32[]{:S(2)}) collective-permute-start(bf16[6400,128]{1,0:T(8,128)(2,1)S(1)} %get-tuple-element.146.refs_0_.refs_8_), channel_id=1, source_target_pairs={{0,16},{8,24},{16,0},{24,8},{1,17},{9,25},{17,1},{25,9},{2,18},{10... | collective-permute-start | bytes 4915208 | tf_op jit(solution)/shard_map/ppermute | solution.py:1390
  19.0 35.7 %collective-permute-start.2 = (bf16[6400,128]{1,0:T(8,128)(2,1)S(1)}, bf16[6400,128]{1,0:T(8,128)(2,1)S(1)}, u32[]{:S(2)}, u32[]{:S(2)}) collective-permute-start(bf16[6400,128]{1,0:T(8,128)(2,1)S(1)} %get-tuple-element.146.refs_0_.refs_8_), channel_id=1, source_target_pairs={{0,1},{1,0},{2,3},{3,2},{4,5},{5,4},{6,7},{7,6},{8,9},{9,8},{10,11... | collective-permute-start | bytes 4915208 | tf_op jit(solution)/shard_map/ppermute | solution.py:1404
  53.3 8.3 %copy-start.15 = (bf16[6400,128]{1,0:T(8,128)(2,1)}, bf16[6400,128]{1,0:T(8,128)(2,1)S(1)}, u32[]{:S(2)}) copy-start(bf16[6400,128]{1,0:T(8,128)(2,1)S(1)} %collective-permute-done.refs_1_.refs_9_) | copy-start | bytes 4915204
  54.8 6.9 %copy-start.14 = (bf16[6400,128]{1,0:T(8,128)(2,1)}, bf16[6400,128]{1,0:T(8,128)(2,1)S(1)}, u32[]{:S(2)}) copy-start(bf16[6400,128]{1,0:T(8,128)(2,1)S(1)} %collective-permute-done.1.refs_2_.refs_10_) | copy-start | bytes 4915204
  54.8 6.9 %copy-start.17 = (bf16[6400,128]{1,0:T(8,128)(2,1)}, bf16[6400,128]{1,0:T(8,128)(2,1)S(1)}, u32[]{:S(2)}) copy-start(bf16[6400,128]{1,0:T(8,128)(2,1)S(1)} %collective-permute-done.2.refs_4_.refs_12_) | copy-start | bytes 4915204
  54.8 22.4 %collective-permute-start.5 = (bf16[6400,128]{1,0:T(8,128)(2,1)S(1)}, bf16[6400,128]{1,0:T(8,128)(2,1)S(1)}, u32[]{:S(2)}, u32[]{:S(2)}) collective-permute-start(bf16[6400,128]{1,0:T(8,128)(2,1)S(1)} %collective-permute-done.refs_1_.refs_9_), channel_id=1, source_target_pairs={{0,1},{1,0},{2,3},{3,2},{4,5},{5,4},{6,7},{7,6},{8,9},{9,8},{10,11... | collective-permute-start | bytes 4915208 | tf_op jit(solution)/shard_map/ppermute | solution.py:1404
  54.9 22.3 %collective-permute-start.6 = (bf16[6400,128]{1,0:T(8,128)(2,1)S(1)}, bf16[6400,128]{1,0:T(8,128)(2,1)S(1)}, u32[]{:S(2)}, u32[]{:S(2)}) collective-permute-start(bf16[6400,128]{1,0:T(8,128)(2,1)S(1)} %collective-permute-done.1.refs_2_.refs_10_), channel_id=1, source_target_pairs={{0,1},{1,0},{2,3},{3,2},{4,5},{5,4},{6,7},{7,6},{8,9},{9,8},{10,11... | collective-permute-start | bytes 4915208 | tf_op jit(solution)/shard_map/ppermute | solution.py:1404
  55.4 7.6 %collective-permute-start.7 = (bf16[6144,128]{1,0:T(8,128)(2,1)S(1)}, bf16[6144,128]{1,0:T(8,128)(2,1)S(1)}, u32[]{:S(2)}, u32[]{:S(2)}) collective-permute-start(bf16[6144,128]{1,0:T(8,128)(2,1)S(1)} %get-tuple-element.150.refs_0_.refs_8_), channel_id=1, source_target_pairs={{0,1},{1,0},{2,3},{3,2},{4,5},{5,4},{6,7},{7,6},{8,9},{9,8},{10,11... | collective-permute-start | bytes 4718600 | tf_op jit(solution)/shard_map/ppermute | solution.py:1404
  55.8 21.4 %collective-permute-start.3 = (bf16[3328,128]{1,0:T(8,128)(2,1)S(1)}, bf16[3328,128]{1,0:T(8,128)(2,1)S(1)}, u32[]{:S(2)}, u32[]{:S(2)}) collective-permute-start(bf16[3328,128]{1,0:T(8,128)(2,1)S(1)} %slice.74), channel_id=1, source_target_pairs={{0,8},{8,0},{16,24},{24,16},{1,9},{9,1},{17,25},{25,17},{2,10},{10... | collective-permute-start | bytes 2555912 | tf_op jit(solution)/shard_map/ppermute | solution.py:1386
  56.2 19.6 %collective-permute-start.4 = (bf16[3072,128]{1,0:T(8,128)(2,1)S(1)}, bf16[3072,128]{1,0:T(8,128)(2,1)S(1)}, u32[]{:S(2)}, u32[]{:S(2)}) collective-permute-start(bf16[3072,128]{1,0:T(8,128)(2,1)S(1)} %slice.75), channel_id=1, source_target_pairs={{0,16},{8,24},{16,0},{24,8},{1,17},{9,25},{17,1},{25,9},{2,18},{10... | collective-permute-start | bytes 2359304 | tf_op jit(solution)/shard_map/ppermute | solution.py:1390
  62.9 16.9 %copy-start.20 = (bf16[6144,128]{1,0:T(8,128)(2,1)}, bf16[6144,128]{1,0:T(8,128)(2,1)S(1)}, u32[]{:S(2)}) copy-start(bf16[6144,128]{1,0:T(8,128)(2,1)S(1)} %collective-permute-done.7.refs_4_.refs_12_) | copy-start | bytes 4718596
  75.8 7.0 %copy-start.27 = (bf16[3072,128]{1,0:T(8,128)(2,1)}, bf16[3072,128]{1,0:T(8,128)(2,1)S(1)}, u32[]{:S(2)}) copy-start(bf16[3072,128]{1,0:T(8,128)(2,1)S(1)} %collective-permute-done.4.refs_11_) | copy-start | bytes 2359300
  77.1 5.7 %copy-start.22 = (bf16[3328,128]{1,0:T(8,128)(2,1)}, bf16[3328,128]{1,0:T(8,128)(2,1)S(1)}, u32[]{:S(2)}) copy-start(bf16[3328,128]{1,0:T(8,128)(2,1)S(1)} %collective-permute-done.3.refs_3_) | copy-start | bytes 2555908
  77.2 38.8 %collective-permute-start.8 = (bf16[6144,128]{1,0:T(8,128)(2,1)S(1)}, bf16[6144,128]{1,0:T(8,128)(2,1)S(1)}, u32[]{:S(2)}, u32[]{:S(2)}) collective-permute-start(bf16[6144,128]{1,0:T(8,128)(2,1)S(1)} %get-tuple-element.150.refs_0_.refs_8_), channel_id=1, source_target_pairs={{0,8},{8,0},{16,24},{24,16},{1,9},{9,1},{17,25},{25,17},{2,10},{10... | collective-permute-start | bytes 4718600 | tf_op jit(solution)/shard_map/ppermute | solution.py:1386
  77.6 38.4 %collective-permute-start.9 = (bf16[6144,128]{1,0:T(8,128)(2,1)S(1)}, bf16[6144,128]{1,0:T(8,128)(2,1)}, u32[]{:S(2)}, u32[]{:S(2)}) collective-permute-start(bf16[6144,128]{1,0:T(8,128)(2,1)S(1)} %get-tuple-element.150.refs_0_.refs_8_), channel_id=1, source_target_pairs={{0,16},{8,24},{16,0},{24,8},{1,17},{9,25},{17,1},{25,9},{2,18},{10... | collective-permute-start | bytes 4718600 | tf_op jit(solution)/shard_map/ppermute | solution.py:1390
  79.3 4.4 collective-permute-start.10
  79.3 3.5 collective-permute-start.11
  116.0 7.6 %collective-permute-start.16 = (bf16[1024,2048]{1,0:T(8,128)(2,1)}, bf16[1024,2048]{1,0:T(8,128)(2,1)}, u32[]{:S(2)}, u32[]{:S(2)}) collective-permute-start(bf16[1024,2048]{1,0:T(8,128)(2,1)} %bitcast.77), channel_id=1, source_target_pairs={{0,1},{1,0},{2,3},{3,2},{4,5},{5,4},{6,7},{7,6},{8,9},{9,8},{10,11... | collective-permute-start | bytes 12582920 | tf_op jit(solution)/shard_map/ppermute | solution.py:1404
  116.2 264.8 %reduce-scatter.2.cloned.1.call-start = ((), (), s32[]{:S(2)}) async-start(), calls=%async_computation.2 | async-start | bytes 10485760 | tf_op jit(solution)/shard_map/reduce_scatter | solution.py:1519
  116.7 23.9 %collective-permute-start.14 = (bf16[6144,128]{1,0:T(8,128)(2,1)S(1)}, bf16[6144,128]{1,0:T(8,128)(2,1)S(1)}, u32[]{:S(2)}, u32[]{:S(2)}) collective-permute-start(bf16[6144,128]{1,0:T(8,128)(2,1)S(1)} %collective-permute-done.8.refs_1_.refs_9_), channel_id=1, source_target_pairs={{0,1},{1,0},{2,3},{3,2},{4,5},{5,4},{6,7},{7,6},{8,9},{9,8},{10,11... | collective-permute-start | bytes 4718600 | tf_op jit(solution)/shard_map/ppermute | solution.py:1404
  117.1 23.5 %collective-permute-start.15 = (bf16[6144,128]{1,0:T(8,128)(2,1)}, bf16[6144,128]{1,0:T(8,128)(2,1)}, u32[]{:S(2)}, u32[]{:S(2)}) collective-permute-start(bf16[6144,128]{1,0:T(8,128)(2,1)} %collective-permute-done.9.refs_0_.refs_2_.refs_10_), channel_id=1, source_target_pairs={{0,1},{1,0},{2,3},{3,2},{4,5},{5,4},{6,7},{7,6},{8,9},{9,8},{10,11... | collective-permute-start | bytes 4718600 | tf_op jit(solution)/shard_map/ppermute | solution.py:1404
  119.8 20.2 %collective-permute-start.12 = (bf16[3072,128]{1,0:T(8,128)(2,1)}, bf16[3072,128]{1,0:T(8,128)(2,1)}, u32[]{:S(2)}, u32[]{:S(2)}) collective-permute-start(bf16[3072,128]{1,0:T(8,128)(2,1)} %get-tuple-element.174), channel_id=1, source_target_pairs={{0,8},{8,0},{16,24},{24,16},{1,9},{9,1},{17,25},{25,17},{2,10},{10... | collective-permute-start | bytes 2359304 | tf_op jit(solution)/shard_map/ppermute | solution.py:1386
  120.8 19.8 %collective-permute-start.13 = (bf16[3072,128]{1,0:T(8,128)(2,1)}, bf16[3072,128]{1,0:T(8,128)(2,1)}, u32[]{:S(2)}, u32[]{:S(2)}) collective-permute-start(bf16[3072,128]{1,0:T(8,128)(2,1)} %get-tuple-element.175), channel_id=1, source_target_pairs={{0,16},{8,24},{16,0},{24,8},{1,17},{9,25},{17,1},{25,9},{2,18},{10... | collective-permute-start | bytes 2359304 | tf_op jit(solution)/shard_map/ppermute | solution.py:1390
  140.6 2.6 collective-permute-start.17
  140.7 3.6 collective-permute-start.18
  186.2 57.3 %collective-permute-start.19 = (bf16[1024,2560]{1,0:T(8,128)(2,1)}, bf16[1024,2560]{1,0:T(8,128)(2,1)}, u32[]{:S(2)}, u32[]{:S(2)}) collective-permute-start(bf16[1024,2560]{1,0:T(8,128)(2,1)} %get-tuple-element.203.refs_2_.refs_6_), channel_id=1, source_target_pairs={{0,1},{1,0},{2,3},{3,2},{4,5},{5,4},{6,7},{7,6},{8,9},{9,8},{10,11... | collective-permute-start | bytes 15728648 | tf_op jit(solution)/shard_map/ppermute | solution.py:1404
  203.7 39.8 %collective-permute-start.21 = (bf16[1024,2048]{1,0:T(8,128)(2,1)}, bf16[1024,2048]{1,0:T(8,128)(2,1)}, u32[]{:S(2)}, u32[]{:S(2)}) collective-permute-start(bf16[1024,2048]{1,0:T(8,128)(2,1)} %bitcast.70), channel_id=1, source_target_pairs={{0,1},{1,0},{2,3},{3,2},{4,5},{5,4},{6,7},{7,6},{8,9},{9,8},{10,11... | collective-permute-start | bytes 12582920 | tf_op jit(solution)/shard_map/ppermute | solution.py:1404
  204.1 5.4 %copy-start.5 = (s32[1024,1]{1,0:T(8,128)S(1)}, s32[1024,1]{1,0:T(8,128)}, u32[]{:S(2)}) copy-start(s32[1024,1]{1,0:T(8,128)} %copy.30.begins) | copy-start | bytes 12292
  204.1 5.4 %copy-start.6 = (f32[1024,128]{1,0:T(8,128)S(1)}, f32[1024,128]{1,0:T(8,128)}, u32[]{:S(2)}) copy-start(f32[1024,128]{1,0:T(8,128)} %get-tuple-element.200.upper) | copy-start | bytes 1572868
  222.5 10.6 %copy-start = (bf16[1024,1536]{1,0:T(8,128)(2,1)}, bf16[1024,1536]{1,0:T(8,128)(2,1)S(1)}, u32[]{:S(2)}) copy-start(bf16[1024,1536]{1,0:T(8,128)(2,1)S(1)} %attend_back.1.refs_8_.grad_projected) | copy-start | bytes 9437188
  222.5 21.0 %collective-permute-start.20 = (bf16[1024,1536]{1,0:T(8,128)(2,1)S(1)}, bf16[1024,1536]{1,0:T(8,128)(2,1)}, u32[]{:S(2)}, u32[]{:S(2)}) collective-permute-start(bf16[1024,1536]{1,0:T(8,128)(2,1)S(1)} %attend_back.1.refs_8_.grad_projected), channel_id=1, source_target_pairs={{0,1},{1,0},{2,3},{3,2},{4,5},{5,4},{6,7},{7,6},{8,9},{9,8},{10,11... | collective-permute-start | bytes 9437192 | tf_op jit(solution)/shard_map/ppermute | solution.py:1404
  222.7 10.6 %copy-start.12 = (s32[8]{0:T(128)S(1)}, s32[8]{0:T(128)}, u32[]{:S(2)}) copy-start(s32[8]{0:T(128)} %copy-done.11) | copy-start | bytes 100
  233.1 10.3 %collective-permute-start.22 = (bf16[1024,1024]{1,0:T(8,128)(2,1)}, bf16[1024,1024]{1,0:T(8,128)(2,1)}, u32[]{:S(2)}, u32[]{:S(2)}) collective-permute-start(bf16[1024,1024]{1,0:T(8,128)(2,1)} %get-tuple-element.229.rest_before), channel_id=1, source_target_pairs={{0,1},{1,0},{2,3},{3,2},{4,5},{5,4},{6,7},{7,6},{8,9},{9,8},{10,11... | collective-permute-start | bytes 6291464 | tf_op jit(solution)/shard_map/ppermute | solution.py:1404
  243.5 44.0 %copy-start.33 = (f32[1,1024]{1,0:T(1,128)S(1)}, f32[1,1024]{1,0:T(1,128)}, u32[]{:S(2)}) copy-start(f32[1,1024]{1,0:T(1,128)} %get-tuple-element.238) | copy-start | bytes 12292
  243.5 44.0 %copy-start.34 = (f32[1,1024]{1,0:T(1,128)S(1)}, f32[1,1024]{1,0:T(1,128)}, u32[]{:S(2)}) copy-start(f32[1,1024]{1,0:T(1,128)} %get-tuple-element.237) | copy-start | bytes 12292
  284.1 30.1 %collective-permute-start.25 = (f32[2,2,3136,128]{3,2,1,0:T(8,128)}, f32[2,2,3136,128]{3,2,1,0:T(8,128)}, u32[]{:S(2)}, u32[]{:S(2)}) collective-permute-start(f32[2,2,3136,128]{3,2,1,0:T(8,128)} %get-tuple-element.233.refs_0_), channel_id=1, source_target_pairs={{0,1},{1,0},{2,3},{3,2},{4,5},{5,4},{6,7},{7,6},{8,9},{9,8},{10,11... | collective-permute-start | bytes 19267592 | tf_op jit(solution)/shard_map/ppermute | solution.py:1404
  284.6 40.5 %collective-permute-start.23 = (bf16[2,3136,128]{2,1,0:T(8,128)(2,1)}, bf16[2,3136,128]{2,1,0:T(8,128)(2,1)}, u32[]{:S(2)}, u32[]{:S(2)}) collective-permute-start(bf16[2,3136,128]{2,1,0:T(8,128)(2,1)} %get-tuple-element.224), channel_id=1, source_target_pairs={{0,8},{8,0},{16,24},{24,16},{1,9},{9,1},{17,25},{25,17},{2,10},{10... | collective-permute-start | bytes 4816904 | tf_op jit(solution)/shard_map/ppermute | solution.py:1386
  286.1 39.0 %collective-permute-start.24 = (bf16[2,3136,128]{2,1,0:T(8,128)(2,1)}, bf16[2,3136,128]{2,1,0:T(8,128)(2,1)}, u32[]{:S(2)}, u32[]{:S(2)}) collective-permute-start(bf16[2,3136,128]{2,1,0:T(8,128)(2,1)} %get-tuple-element.225), channel_id=1, source_target_pairs={{0,16},{8,24},{16,0},{24,8},{1,17},{9,25},{17,1},{25,9},{2,18},{10... | collective-permute-start | bytes 4816904 | tf_op jit(solution)/shard_map/ppermute | solution.py:1390
  290.3 28.3 %copy-start.1 = (bf16[1024,1536]{1,0:T(8,128)(2,1)S(1)}, bf16[1024,1536]{1,0:T(8,128)(2,1)}, u32[]{:S(2)}) copy-start(bf16[1024,1536]{1,0:T(8,128)(2,1)} %copy-done) | copy-start | bytes 9437188
  314.2 6.9 %collective-permute-start.27 = (f32[4,2048]{1,0:T(4,128)}, f32[4,2048]{1,0:T(4,128)S(1)}, u32[]{:S(2)}, u32[]{:S(2)}) collective-permute-start(f32[4,2048]{1,0:T(4,128)} %get-tuple-element.236), channel_id=1, source_target_pairs={{0,4},{2,6},{4,0},{6,2},{1,5},{3,7},{5,1},{7,3},{8,12},{10,14},{12... | collective-permute-start | bytes 98312 | tf_op jit(solution)/shard_map/ppermute | solution.py:1394
  317.1 7.0 %collective-permute-start.28 = (f32[4,2048]{1,0:T(4,128)}, f32[4,2048]{1,0:T(4,128)S(1)}, u32[]{:S(2)}, u32[]{:S(2)}) collective-permute-start(f32[4,2048]{1,0:T(4,128)} %get-tuple-element.236), channel_id=1, source_target_pairs={{0,6},{2,4},{4,2},{6,0},{1,7},{3,5},{5,3},{7,1},{8,14},{10,12},{12... | collective-permute-start | bytes 98312 | tf_op jit(solution)/shard_map/ppermute | solution.py:1394
  318.2 6.1 %collective-permute-start.26 = (f32[4,2048]{1,0:T(4,128)}, f32[4,2048]{1,0:T(4,128)S(1)}, u32[]{:S(2)}, u32[]{:S(2)}) collective-permute-start(f32[4,2048]{1,0:T(4,128)} %get-tuple-element.236), channel_id=1, source_target_pairs={{0,2},{2,0},{4,6},{6,4},{1,3},{3,1},{5,7},{7,5},{8,10},{10,8},{12,... | collective-permute-start | bytes 98312 | tf_op jit(solution)/shard_map/ppermute | solution.py:1394
  325.1 115.6 %all-to-all-start = ((bf16[4,256,2048]{2,1,0:T(8,128)(2,1)}), bf16[4,256,2048]{2,1,0:T(8,128)(2,1)}, u32[]{:S(2)}, u32[]{:S(2)}) async-start(bf16[4,256,2048]{2,1,0:T(8,128)(2,1)} %bitcast.83), calls=%async_computation.1 | async-start | bytes 8388608 | tf_op jit(solution)/shard_map/all_to_all | solution.py:1410
  330.1 6.0 %copy-start.31 = (f32[16384]{0:T(1024)}, f32[16384]{0:T(1024)S(1)}, u32[]{:S(2)}) copy-start(f32[16384]{0:T(1024)S(1)} %constant_dynamic-update-slice_fusion) | copy-start | bytes 196612
  330.1 5.9 %collective-permute-start.33 = (f32[128,128]{1,0:T(8,128)S(1)}, f32[128,128]{1,0:T(8,128)S(1)}, u32[]{:S(2)}, u32[]{:S(2)}) collective-permute-start(f32[128,128]{1,0:T(8,128)S(1)} %bitcast.90), channel_id=1, source_target_pairs={{0,1},{1,0},{2,3},{3,2},{4,5},{5,4},{6,7},{7,6},{8,9},{9,8},{10,11... | collective-permute-start | bytes 196616 | tf_op jit(solution)/shard_map/ppermute | solution.py:1404
  332.2 39.2 %collective-permute-start.29 = (bf16[3136,128]{1,0:T(8,128)(2,1)}, bf16[3136,128]{1,0:T(8,128)(2,1)S(1)}, u32[]{:S(2)}, u32[]{:S(2)}) collective-permute-start(bf16[3136,128]{1,0:T(8,128)(2,1)} %get-tuple-element.243), channel_id=1, source_target_pairs={{0,8},{8,0},{16,24},{24,16},{1,9},{9,1},{17,25},{25,17},{2,10},{10... | collective-permute-start | bytes 2408456 | tf_op jit(solution)/shard_map/ppermute | solution.py:1386
  333.1 38.3 %collective-permute-start.30 = (bf16[3136,128]{1,0:T(8,128)(2,1)}, bf16[3136,128]{1,0:T(8,128)(2,1)S(1)}, u32[]{:S(2)}, u32[]{:S(2)}) collective-permute-start(bf16[3136,128]{1,0:T(8,128)(2,1)} %get-tuple-element.244), channel_id=1, source_target_pairs={{0,16},{8,24},{16,0},{24,8},{1,17},{9,25},{17,1},{25,9},{2,18},{10... | collective-permute-start | bytes 2408456 | tf_op jit(solution)/shard_map/ppermute | solution.py:1390
  333.6 37.9 %collective-permute-start.31 = (bf16[3136,128]{1,0:T(8,128)(2,1)}, bf16[3136,128]{1,0:T(8,128)(2,1)S(1)}, u32[]{:S(2)}, u32[]{:S(2)}) collective-permute-start(bf16[3136,128]{1,0:T(8,128)(2,1)} %get-tuple-element.245), channel_id=1, source_target_pairs={{0,9},{1,8},{8,1},{9,0},{16,25},{17,24},{24,17},{25,16},{2,11},{3,... | collective-permute-start | bytes 2408456 | tf_op jit(solution)/shard_map/ppermute | solution.py:1398
  334.6 36.9 %collective-permute-start.32 = (bf16[3136,128]{1,0:T(8,128)(2,1)}, bf16[3136,128]{1,0:T(8,128)(2,1)S(1)}, u32[]{:S(2)}, u32[]{:S(2)}) collective-permute-start(bf16[3136,128]{1,0:T(8,128)(2,1)} %get-tuple-element.246), channel_id=1, source_target_pairs={{0,17},{1,16},{8,25},{9,24},{16,1},{17,0},{24,9},{25,8},{2,19},{3,... | collective-permute-start | bytes 2408456 | tf_op jit(solution)/shard_map/ppermute | solution.py:1398
  336.1 35.3 %copy-start.32 = (f32[16384]{0:T(1024)S(1)}, f32[16384]{0:T(1024)}, u32[]{:S(2)}) copy-start(f32[16384]{0:T(1024)} %copy-done.31) | copy-start | bytes 196612
  336.1 45.0 %copy-start.16 = (bf16[1,256,2048]{2,1,0:T(8,128)(2,1)S(1)}, bf16[1,256,2048]{2,1,0:T(8,128)(2,1)}, u32[]{:S(2)}) copy-start(bf16[1,256,2048]{2,1,0:T(8,128)(2,1)} %param.12) | copy-start | bytes 3145732
  336.1 35.3 %collective-permute-start.34 = (f32[128,128]{1,0:T(8,128)S(1)}, f32[128,128]{1,0:T(8,128)S(1)}, u32[]{:S(2)}, u32[]{:S(2)}) collective-permute-start(f32[128,128]{1,0:T(8,128)S(1)} %bitcast_add_fusion), channel_id=1, source_target_pairs={{0,8},{8,0},{16,24},{24,16},{1,9},{9,1},{17,25},{25,17},{2,10},{10... | collective-permute-start | bytes 196616 | tf_op jit(solution)/shard_map/ppermute | solution.py:1386
  371.5 39.1 %collective-permute-start.35 = (bf16[3136,128]{1,0:T(8,128)(2,1)}, bf16[3136,128]{1,0:T(8,128)(2,1)}, u32[]{:S(2)}, u32[]{:S(2)}) collective-permute-start(bf16[3136,128]{1,0:T(8,128)(2,1)} %get-tuple-element.254), channel_id=1, source_target_pairs={{0,16},{8,24},{16,0},{24,8},{1,17},{9,25},{17,1},{25,9},{2,18},{10... | collective-permute-start | bytes 2408456 | tf_op jit(solution)/shard_map/ppermute | solution.py:1390
  372.3 38.3 %collective-permute-start.36 = (bf16[3136,128]{1,0:T(8,128)(2,1)S(1)}, bf16[3136,128]{1,0:T(8,128)(2,1)}, u32[]{:S(2)}, u32[]{:S(2)}) collective-permute-start(bf16[3136,128]{1,0:T(8,128)(2,1)S(1)} %get-tuple-element.255), channel_id=1, source_target_pairs={{0,8},{8,0},{16,24},{24,16},{1,9},{9,1},{17,25},{25,17},{2,10},{10... | collective-permute-start | bytes 2408456 | tf_op jit(solution)/shard_map/ppermute | solution.py:1386
  372.8 37.8 %collective-permute-start.37 = (bf16[3136,128]{1,0:T(8,128)(2,1)S(1)}, bf16[3136,128]{1,0:T(8,128)(2,1)}, u32[]{:S(2)}, u32[]{:S(2)}) collective-permute-start(bf16[3136,128]{1,0:T(8,128)(2,1)S(1)} %get-tuple-element.256), channel_id=1, source_target_pairs={{0,17},{1,16},{8,25},{9,24},{16,1},{17,0},{24,9},{25,8},{2,19},{3,... | collective-permute-start | bytes 2408456 | tf_op jit(solution)/shard_map/ppermute | solution.py:1398
  373.3 37.4 %collective-permute-start.38 = (bf16[3136,128]{1,0:T(8,128)(2,1)S(1)}, bf16[3136,128]{1,0:T(8,128)(2,1)}, u32[]{:S(2)}, u32[]{:S(2)}) collective-permute-start(bf16[3136,128]{1,0:T(8,128)(2,1)S(1)} %get-tuple-element.257), channel_id=1, source_target_pairs={{0,9},{1,8},{8,1},{9,0},{16,25},{17,24},{24,17},{25,16},{2,11},{3,... | collective-permute-start | bytes 2408456 | tf_op jit(solution)/shard_map/ppermute | solution.py:1398
  384.4 25.6 %collective-permute-start.39 = (f32[128,128]{1,0:T(8,128)S(1)}, f32[128,128]{1,0:T(8,128)S(1)}, u32[]{:S(2)}, u32[]{:S(2)}) collective-permute-start(f32[128,128]{1,0:T(8,128)S(1)} %fusion.15), channel_id=1, source_target_pairs={{0,16},{8,24},{16,0},{24,8},{1,17},{9,25},{17,1},{25,9},{2,18},{10... | collective-permute-start | bytes 196616 | tf_op jit(solution)/shard_map/ppermute | solution.py:1390
  (16 other events, 52.3 us)
Sparse Core Ops, SparseCore 0:
  9.6 83.4 all-gather.4
  116.3 81.0 all-gather.6
  204.3 176.7 reduce-scatter.1

commit v7 on v6

--- a/solution.py
+++ b/solution.py
@@ -1106,7 +1106,7 @@
 
 def finish(terms, rows, grads):
     count, width = rows.shape
-    height = count // 4
+    height = count // 2
     block = pl.BlockSpec((height, width), lambda i: (i, 0))
     return pl.pallas_call(
         finish_kernel,
@@ -1310,7 +1310,7 @@
             pl.BlockSpec((2, rows, 1), lambda i: (i, 0, 0)),
         ],
         input_output_aliases={9: 0},
-        compiler_params=params(60),
+        compiler_params=params(40),
         cost_estimate=LIGHT,
         name="attend",
     )(normed, mixer_in, mixer_in, mixer_in, bias, *tables, begins, mixed)

time: 459 us -> 458 us (level)
  transfers between devices with their start and end apart: 44 -> 44, of which waited for: 18 -> 17; matrix products, arithmetic and copies ran while one was open for 10% -> 10% of each run, Pallas kernels for 46% -> 46%
where the time goes in v7:
time: 458 us; the launch traced here: 452 us
  Pallas kernels  212 us (46%)
  waiting for transfers between devices  135 us (29%)
  starting transfers between devices  35.4 us (8%)
  other arithmetic  20.6 us (4%)
  matrix products  20.4 us (4%)
  between operations  17 us (4%)
  local copies, waits for them, and re-layouts  11.6 us (3%)
    ppermute x8, waiting for transfers between devices, along_x(): return lax.ppermute(value, 'dp', [(i, i ^ 1) for i in range(4)])  71.8 us
    pallas_call x1, Pallas kernels, weight_grads(): pl.pallas_call(weight_grad_kernel, out_shape=[near, near, short] * 2 + [w...  41 us
    ppermute x8, waiting for transfers between devices, along_y(): return lax.ppermute(value, 'dp', [(i, i ^ 2) for i in range(4)])  38.3 us
    pallas_call x1, Pallas kernels, adam(): pl.pallas_call(adam_kernel, grid=(steps,), out_shape=[jax.ShapeDtypeStruc...  26.5 us
    pallas_call x1, Pallas kernels, norm_grad(): pl.pallas_call(norm_grad_kernel, out_shape=[jax.ShapeDtypeStruct((tokens,...  23.9 us
    pallas_call x2, Pallas kernels, hidden_back(): pl.pallas_call(hidden_back_kernel, out_shape=[jax.ShapeDtypeStruct((rows,...  19.8 us
    pallas_call x1, Pallas kernels, attend(): pl.pallas_call(attend_kernel, grid=(pairs,), out_shape=[jax.ShapeDtypeStr...  19.2 us
    pallas_call x1, Pallas kernels, unpack_hidden(): pl.pallas_call(functools.partial(unpack_hidden_kernel, width), out_shape=...  18.9 us
  transfers between devices with their start and end apart: 44, of which 17 were waited for; matrix products, arithmetic and copies ran while one was open for 10% of the time, Pallas kernels for 46%

profile of v7, /device:TPU:0, one launch (start us, length us, event | category | flops | bytes accessed | tf_op | source)
XLA Modules:
  0.0 451.6 jit_solution(17988488415435827566)
XLA Ops:
  7.2 0.7 all-gather.5.cloned.1.call-update
  8.1 0.8 select_reduce_fusion.4
  9.0 2.8 copy-done.2
  11.8 2.7 pack_params.1
  14.5 3.0 collective-permute-start
  17.5 0.9 collective-permute-start.1
  18.5 34.9 %collective-permute-done.refs_1_.refs_9_ = bf16[6400,128]{1,0:T(8,128)(2,1)S(1)} collective-permute-done((bf16[6400,128]{1,0:T(8,128)(2,1)S(1)}, bf16[6400,128]{1,0:T(8,128)(2,1)S(1)}, u32[]{:S(2)}, u32[]{:S(2)}) %collective-permute-start) | collective-permute-done | bytes 1638432 | tf_op jit(solution)/shard_map/ppermute | solution.py:1386
  53.3 1.5 collective-permute-done.1.refs_2_.refs_10_
  56.2 1.5 collective-permute-start.4
  57.9 1.9 multiply_sine_fusion
  59.9 1.5 maximum_maximum_fusion.2
  61.4 1.6 collective-permute-done.7.refs_4_.refs_12_
  62.9 12.9 %collective-permute-done.4.refs_11_ = bf16[3072,128]{1,0:T(8,128)(2,1)S(1)} collective-permute-done((bf16[3072,128]{1,0:T(8,128)(2,1)S(1)}, bf16[3072,128]{1,0:T(8,128)(2,1)S(1)}, u32[]{:S(2)}, u32[]{:S(2)}) %collective-permute-start.4) | collective-permute-done | bytes 786464 | tf_op jit(solution)/shard_map/ppermute | solution.py:1390
  75.8 1.3 collective-permute-done.3.refs_3_
  77.6 1.5 collective-permute-start.9
  79.7 3.0 collective-permute-done.11.refs_15_
  82.7 0.9 copy-done.35
  83.5 10.8 %unpack_params.1 = (bf16[2048,1536]{1,0:T(8,128)(2,1)}, bf16[2560,2048]{1,0:T(8,128)(2,1)}, bf16[2048,2048]{1,0:T(8,128)(2,1)}, bf16[16,2048]{1,0:T(8,128)(2,1)}, bf16[8,256,128]{2,1,0:T(8,128)(2,1)}) custom-call(s32[8]{0:T(128)} %copy-done.18, bf16[6400,128]{1,0:T(8,128)(2,1)} %copy-done.4, bf16[6400,128]{1,0:T(8,128)(2,1)} %copy-done.22, ...), custom_call_target="tpu_custom_call" | custom-call | flops 1 | bytes 1 | tf_op jit(solution)/shard_map/unpack_params/pallas_call | solution.py:580
  94.4 0.8 convert_bitcast_fusion
  95.8 9.1 %norms.2 = (bf16[1024,2048]{1,0:T(8,128)(2,1)}, bf16[1024,2048]{1,0:T(8,128)(2,1)}, f32[1024,1]{1,0:T(8,128)}, f32[1024,1]{1,0:T(8,128)}) custom-call(bf16[1024,2048]{1,0:T(8,128)(2,1)} %bitcast.76, f32[6,2048]{1,0:T(8,128)} %reshape.97.gains), custom_call_target="tpu_custom_call" | custom-call | flops 1 | bytes 1 | tf_op jit(solution)/shard_map/norms/pallas_call | solution.py:1214
  105.6 10.2 %hidden_layer.1 = (bf16[1024,2560]{1,0:T(8,128)(2,1)}, f32[1024,2048]{1,0:T(8,128)}) custom-call(bf16[1024,2048]{1,0:T(8,128)(2,1)} %get-tuple-element.191.normed.refs_17_.refs_4_, bf16[2048,2048]{1,0:T(8,128)(2,1)} %get-tuple-element.194.up.refs_21_, f32[1,2048]{1,0:T(1,128)} %bitcast.93), custom_call_target="tpu_custom_call" | custom-call | flops 1 | bytes 1 | tf_op jit(solution)/shard_map/hidden_layer/pallas_call | solution.py:1143
  117.1 2.5 cut.1
  119.6 1.7 collective-permute-start.12
  121.9 1.5 collective-permute-done.16.rows
  123.3 9.4 %norms.3 = (bf16[1024,2048]{1,0:T(8,128)(2,1)}, bf16[1024,2048]{1,0:T(8,128)(2,1)}, f32[1024,1]{1,0:T(8,128)}, f32[1024,1]{1,0:T(8,128)}) custom-call(bf16[1024,2048]{1,0:T(8,128)(2,1)} %collective-permute-done.16.rows, f32[6,2048]{1,0:T(8,128)} %reshape.97.gains), custom_call_target="tpu_custom_call" | custom-call | flops 1 | bytes 1 | tf_op jit(solution)/shard_map/norms/pallas_call | solution.py:1214
  132.7 7.1 %collective-permute-done.12.refs_3_ = bf16[3072,128]{1,0:T(8,128)(2,1)} collective-permute-done((bf16[3072,128]{1,0:T(8,128)(2,1)}, bf16[3072,128]{1,0:T(8,128)(2,1)}, u32[]{:S(2)}, u32[]{:S(2)}) %collective-permute-start.12) | collective-permute-done | bytes 786464 | tf_op jit(solution)/shard_map/ppermute | solution.py:1386
  139.8 1.4 collective-permute-done.13.refs_11_
  142.1 1.8 collective-permute-done.17.refs_7_
  143.9 1.1 collective-permute-done.18.refs_15_
  145.0 18.9 %unpack_hidden.1 = (bf16[2048,1536]{1,0:T(8,128)(2,1)}, bf16[2560,2048]{1,0:T(8,128)(2,1)}, bf16[2048,2048]{1,0:T(8,128)(2,1)}, bf16[1024,2560]{1,0:T(8,128)(2,1)}, f32[1024,2048]{1,0:T(8,128)}) custom-call(s32[8]{0:T(128)} %copy-done.18, ...), custom_call_target="tpu_custom_call", output_to_operand_aliasing={{0}: (20, {}), {1}: (21, {}), {2}: (22, {}), {3}: (23, {}),... | custom-call | flops 1 | bytes 1 | tf_op jit(solution)/shard_map/unpack_hidden/pallas_call | solution.py:648
  164.0 2.2 copy-done.3
  166.2 19.2 %attend.1 = (bf16[1024,2560]{1,0:T(8,128)(2,1)}, bf16[3,1024,512]{2,1,0:T(8,128)(2,1)S(1)}, f32[4,1024,1]{2,1,0:T(8,128)S(1)}) custom-call(bf16[1024,2048]{1,0:T(8,128)(2,1)S(1)} %copy-done.3, bf16[2048,1536]{1,0:T(8,128)(2,1)} %get-tuple-element.197.queries_in.keys_in.values_in.mixer_in, ...), custom_call_target="tpu_custom_call", output_to_operand_aliasing={{0}: (9, {})} | custom-call | flops 1 | bytes 1 | tf_op jit(solution)/shard_map/attend/pallas_call | solution.py:1296
  185.5 1.7 copy-done.14
  187.1 1.3 copy-done.16
  188.6 15.0 %fusion.11 = f32[1024,2048]{1,0:T(8,128)} fusion(bf16[1024,2560]{1,0:T(8,128)(2,1)} %get-tuple-element.203.refs_2_.refs_6_, bf16[2560,2048]{1,0:T(8,128)(2,1)S(1)} %copy-done.20), kind=kOutput, calls=%fused_computation.60 | convolution fusion | flops 10737418240 | bytes 24117248 | tf_op jit(solution)/shard_map/dot_general | solution.py:27
  204.0 5.4 %fusion.6.grad_context = bf16[1024,512]{1,0:T(8,128)(2,1)S(1)} fusion(bf16[1024,2048]{1,0:T(8,128)(2,1)} %bitcast.71, bf16[2560,2048]{1,0:T(8,128)(2,1)} %get-tuple-element.204.down), kind=kOutput, calls=%fused_computation.13 | convolution fusion | flops 2148007936 | bytes 7340032 | tf_op jit(solution)/shard_map/dot_general | solution.py:37
  209.5 12.9 %attend_back.1.refs_8_.grad_projected = bf16[1024,1536]{1,0:T(8,128)(2,1)S(1)} custom-call(bf16[3,1024,512]{2,1,0:T(8,128)(2,1)S(1)} %copy-done.15, f32[4,1024,1]{2,1,0:T(8,128)S(1)} %copy-done.17, f32[1024,128]{1,0:T(8,128)S(1)} %copy-done.13, f32[1024,128]{1,0:T(8,128)S(1)} %copy-done.11, f32[1024,128]{1,0:T(8,128)S(1)} %copy-done.9, ...), custom_call_target="tpu_custom_call" | custom-call | flops 1 | bytes 1 | tf_op jit(solution)/shard_map/attend_back/pallas_call | solution.py:1359
  222.5 10.4 %hidden_back.3 = (bf16[1024,1024]{1,0:T(8,128)(2,1)}, f32[1,1024]{1,0:T(1,128)}) custom-call(s32[1]{0:T(128)S(6)} %sub.30.half, bf16[1024,2048]{1,0:T(8,128)(2,1)} %bitcast.72, bf16[2560,2048]{1,0:T(8,128)(2,1)} %get-tuple-element.204.down, f32[1024,2048]{1,0:T(8,128)} %get-tuple-element.211.slope), custom_call_target="tpu_custom_call" | custom-call | flops 1 | bytes 1 | tf_op jit(solution)/shard_map/hidden_back/pallas_call | solution.py:1172
  233.9 9.4 %hidden_back.2 = (bf16[1024,1024]{1,0:T(8,128)(2,1)}, f32[1,1024]{1,0:T(1,128)}) custom-call(s32[1]{0:T(128)} %bitcast.14.half.core, bf16[1024,2048]{1,0:T(8,128)(2,1)} %bitcast.73, bf16[2560,2048]{1,0:T(8,128)(2,1)} %get-tuple-element.204.down, f32[1024,2048]{1,0:T(8,128)} %get-tuple-element.211.slope), custom_call_target="tpu_custom_call" | custom-call | flops 1 | bytes 1 | tf_op jit(solution)/shard_map/hidden_back/pallas_call | solution.py:1172
  243.3 41.0 %weight_grads.1 = (bf16[3136,128]{1,0:T(8,128)(2,1)}, bf16[3136,128]{1,0:T(8,128)(2,1)}, bf16[2,3136,128]{2,1,0:T(8,128)(2,1)}, bf16[3136,128]{1,0:T(8,128)(2,1)...) custom-call(s32[33]{0:T(128)} %concatenate.24.table, ...), custom_call_target="tpu_custom_call" | custom-call | flops 1 | bytes 1 | tf_op jit(solution)/shard_map/weight_grads/pallas_call | solution.py:862
  286.4 2.8 convert_reduce_fusion
  289.2 23.9 %norm_grad.1 = (bf16[1024,2048]{1,0:T(8,128)(2,1)}, f32[4,2048]{1,0:T(4,128)}) custom-call(s32[1]{0:T(128)} %bitcast.14.half.core, bf16[1024,1536]{1,0:T(8,128)(2,1)} %copy-done, bf16[2048,1536]{1,0:T(8,128)(2,1)} %get-tuple-element.197.queries_in.keys_in.values_in.mixer_in, bf16[1024,1024]{1,0:T(8,128)(2,1)} %get-tuple-element.227.refs_12_.own_before, ...), custom_call_target="tpu_custom_call" | custom-call | flops 1 | bytes 1 | tf_op jit(solution)/shard_map/norm_grad/pallas_call | solution.py:910
  313.2 2.8 collective-permute-start.27
  316.0 1.2 collective-permute-start.28
  318.0 2.6 collective-permute-done.27
  320.6 2.3 collective-permute-done.28
  322.9 0.8 add_add_fusion.1
  323.7 4.8 %all-to-all-start = ((bf16[4,256,2048]{2,1,0:T(8,128)(2,1)}), bf16[4,256,2048]{2,1,0:T(8,128)(2,1)}, u32[]{:S(2)}, u32[]{:S(2)}) async-start(bf16[4,256,2048]{2,1,0:T(8,128)(2,1)} %bitcast.83), calls=%async_computation.1 | async-start | bytes 8388608 | tf_op jit(solution)/shard_map/all_to_all | solution.py:1410
  330.8 1.5 collective-permute-start.29
  332.3 1.4 collective-permute-start.30
  333.7 0.9 collective-permute-start.32
  334.6 1.5 collective-permute-start.34
  336.2 5.2 %fusion.2 = (bf16[3136,128]{1,0:T(8,128)(2,1)S(1)}, bf16[3136,128]{1,0:T(8,128)(2,1)S(1)}, bf16[3136,128]{1,0:T(8,128)(2,1)}, bf16[3136,128]{1,0:T(8,128)(2,1)S(1)}) fusion(f32[2,2,3136,128]{3,2,1,0:T(8,128)} %get-tuple-element.247, bf16[2,3136,128]{2,1,0:T(8,128)(2,1)} %collective-permute-done.24, bf16[2,3136,128]{2,1,0:T(8,128)(2,1)} %collective-permute-done.23), kind=kLoop, calls=%fused_computation.6 | loop fusion | flops 4816896 | bytes 12845056 | tf_op jit(solution)/shard_map/convert_element_type | solution.py:1574
  341.4 28.5 %collective-permute-done.34 = f32[128,128]{1,0:T(8,128)S(1)} collective-permute-done((f32[128,128]{1,0:T(8,128)S(1)}, f32[128,128]{1,0:T(8,128)S(1)}, u32[]{:S(2)}, u32[]{:S(2)}) %collective-permute-start.34) | collective-permute-done | bytes 65568 | tf_op jit(solution)/shard_map/ppermute | solution.py:1386
  370.0 1.4 collective-permute-start.35
  371.4 1.6 collective-permute-start.36
  373.0 0.9 collective-permute-start.38
  374.5 6.0 %reduce-scatter.2.cloned.1.call-done = f32[256,2048]{1,0:T(8,128)} async-done(((f32[1024,2048]{1,0:T(8,128)}), f32[256,2048]{1,0:T(8,128)}) %reduce-scatter.2.cloned.1.call-update) | async-done | bytes 2097168 | tf_op jit(solution)/shard_map/reduce_scatter | solution.py:1519
  380.5 3.3 add_add_fusion
  383.9 1.5 collective-permute-start.39
  386.0 22.6 %collective-permute-done.39 = f32[128,128]{1,0:T(8,128)S(1)} collective-permute-done((f32[128,128]{1,0:T(8,128)S(1)}, f32[128,128]{1,0:T(8,128)S(1)}, u32[]{:S(2)}, u32[]{:S(2)}) %collective-permute-start.39) | collective-permute-done | bytes 65568 | tf_op jit(solution)/shard_map/ppermute | solution.py:1390
  409.2 26.5 %adam.1 = (f32[12304,128]{1,0:T(8,128)}, f32[12304,128]{1,0:T(8,128)}, f32[12304,128]{1,0:T(8,128)}, f32[12304,128]{1,0:T(8,128)}, f32[12304,128]{1,0:T(8,128)}) custom-call(s32[2]{0:T(128)} %pad_add_fusion.table, f32[4]{0:T(128)} %pad_maximum_fusion.1.scalar_ref, f32[8]{0:T(128)} %rate_ref.1, f32[2,2,3136,128]{3,2,1,0:T(8,128)} %get-tuple-element.233.refs_0_, ...), custom_call_target="tpu_custom_call" | custom-call | flops 1 | bytes 1 | tf_op jit(solution)/shard_map/adam/pallas_call | solution.py:1073
  435.8 4.2 all-to-all-done.terms
  440.0 4.6 %finish.1 = f32[256,2048]{1,0:T(8,128)} custom-call(bf16[4,256,2048]{2,1,0:T(8,128)(2,1)} %all-to-all-done.terms, bf16[256,2048]{1,0:T(8,128)(2,1)} %bitcast.79, bf16[256,2048]{1,0:T(8,128)(2,1)} %bitcast.84), custom_call_target="tpu_custom_call" | custom-call | flops 1 | bytes 1 | tf_op jit(solution)/shard_map/finish/pallas_call | solution.py:1111
  (174 shorter events, 13.4 us)
Async XLA Ops:
  7.2 48.3 %copy-start.40 = (s32[1,5]{1,0:T(1,128)S(1)}, s32[1,5]{1,0:T(1,128)}, u32[]{:S(2)}) copy-start(s32[1,5]{1,0:T(1,128)} %param.14) | copy-start | bytes 64
  7.2 87.2 %all-gather.5.cloned.1.call-start = ((), (), s32[]{:S(2)}) async-start(), calls=%async_computation.3 | async-start | bytes 5242880 | tf_op jit(solution)/shard_map/all_gather | solution.py:1448
  7.9 195.7 %all-gather.7.cloned.1.call-start = ((), (), s32[]{:S(2)}) async-start(), calls=%async_computation.4 | async-start | bytes 5242880 | tf_op jit(solution)/shard_map/all_gather | solution.py:1449
  9.0 46.8 %copy-start.18 = (s32[8]{0:T(128)}, s32[8]{0:T(128)S(1)}, u32[]{:S(2)}) copy-start(s32[8]{0:T(128)S(1)} %select_reduce_fusion.3.bucket_ref) | copy-start | bytes 100
  14.5 46.8 %copy-start.4 = (bf16[6400,128]{1,0:T(8,128)(2,1)}, bf16[6400,128]{1,0:T(8,128)(2,1)S(1)}, u32[]{:S(2)}) copy-start(bf16[6400,128]{1,0:T(8,128)(2,1)S(1)} %get-tuple-element.146.refs_0_.refs_8_) | copy-start | bytes 4915204
  14.5 63.1 %copy-start.5 = (bf16[6144,128]{1,0:T(8,128)(2,1)}, bf16[6144,128]{1,0:T(8,128)(2,1)S(1)}, u32[]{:S(2)}) copy-start(bf16[6144,128]{1,0:T(8,128)(2,1)S(1)} %get-tuple-element.150.refs_0_.refs_8_) | copy-start | bytes 4718596
  14.5 38.8 %collective-permute-start = (bf16[6400,128]{1,0:T(8,128)(2,1)S(1)}, bf16[6400,128]{1,0:T(8,128)(2,1)S(1)}, u32[]{:S(2)}, u32[]{:S(2)}) collective-permute-start(bf16[6400,128]{1,0:T(8,128)(2,1)S(1)} %get-tuple-element.146.refs_0_.refs_8_), channel_id=1, source_target_pairs={{0,8},{8,0},{16,24},{24,16},{1,9},{9,1},{17,25},{25,17},{2,10},{10... | collective-permute-start | bytes 4915208 | tf_op jit(solution)/shard_map/ppermute | solution.py:1386
  17.5 37.3 %collective-permute-start.1 = (bf16[6400,128]{1,0:T(8,128)(2,1)S(1)}, bf16[6400,128]{1,0:T(8,128)(2,1)S(1)}, u32[]{:S(2)}, u32[]{:S(2)}) collective-permute-start(bf16[6400,128]{1,0:T(8,128)(2,1)S(1)} %get-tuple-element.146.refs_0_.refs_8_), channel_id=1, source_target_pairs={{0,16},{8,24},{16,0},{24,8},{1,17},{9,25},{17,1},{25,9},{2,18},{10... | collective-permute-start | bytes 4915208 | tf_op jit(solution)/shard_map/ppermute | solution.py:1390
  18.5 36.3 %collective-permute-start.2 = (bf16[6400,128]{1,0:T(8,128)(2,1)S(1)}, bf16[6400,128]{1,0:T(8,128)(2,1)S(1)}, u32[]{:S(2)}, u32[]{:S(2)}) collective-permute-start(bf16[6400,128]{1,0:T(8,128)(2,1)S(1)} %get-tuple-element.146.refs_0_.refs_8_), channel_id=1, source_target_pairs={{0,1},{1,0},{2,3},{3,2},{4,5},{5,4},{6,7},{7,6},{8,9},{9,8},{10,11... | collective-permute-start | bytes 4915208 | tf_op jit(solution)/shard_map/ppermute | solution.py:1404
  53.3 8.0 %copy-start.22 = (bf16[6400,128]{1,0:T(8,128)(2,1)}, bf16[6400,128]{1,0:T(8,128)(2,1)S(1)}, u32[]{:S(2)}) copy-start(bf16[6400,128]{1,0:T(8,128)(2,1)S(1)} %collective-permute-done.refs_1_.refs_9_) | copy-start | bytes 4915204
  54.8 6.6 %copy-start.21 = (bf16[6400,128]{1,0:T(8,128)(2,1)}, bf16[6400,128]{1,0:T(8,128)(2,1)S(1)}, u32[]{:S(2)}) copy-start(bf16[6400,128]{1,0:T(8,128)(2,1)S(1)} %collective-permute-done.1.refs_2_.refs_10_) | copy-start | bytes 4915204
  54.8 22.4 %collective-permute-start.5 = (bf16[6400,128]{1,0:T(8,128)(2,1)S(1)}, bf16[6400,128]{1,0:T(8,128)(2,1)S(1)}, u32[]{:S(2)}, u32[]{:S(2)}) collective-permute-start(bf16[6400,128]{1,0:T(8,128)(2,1)S(1)} %collective-permute-done.refs_1_.refs_9_), channel_id=1, source_target_pairs={{0,1},{1,0},{2,3},{3,2},{4,5},{5,4},{6,7},{7,6},{8,9},{9,8},{10,11... | collective-permute-start | bytes 4915208 | tf_op jit(solution)/shard_map/ppermute | solution.py:1404
  54.9 22.3 %collective-permute-start.6 = (bf16[6400,128]{1,0:T(8,128)(2,1)S(1)}, bf16[6400,128]{1,0:T(8,128)(2,1)S(1)}, u32[]{:S(2)}, u32[]{:S(2)}) collective-permute-start(bf16[6400,128]{1,0:T(8,128)(2,1)S(1)} %collective-permute-done.1.refs_2_.refs_10_), channel_id=1, source_target_pairs={{0,1},{1,0},{2,3},{3,2},{4,5},{5,4},{6,7},{7,6},{8,9},{9,8},{10,11... | collective-permute-start | bytes 4915208 | tf_op jit(solution)/shard_map/ppermute | solution.py:1404
  55.4 7.6 %collective-permute-start.7 = (bf16[6144,128]{1,0:T(8,128)(2,1)S(1)}, bf16[6144,128]{1,0:T(8,128)(2,1)S(1)}, u32[]{:S(2)}, u32[]{:S(2)}) collective-permute-start(bf16[6144,128]{1,0:T(8,128)(2,1)S(1)} %get-tuple-element.150.refs_0_.refs_8_), channel_id=1, source_target_pairs={{0,1},{1,0},{2,3},{3,2},{4,5},{5,4},{6,7},{7,6},{8,9},{9,8},{10,11... | collective-permute-start | bytes 4718600 | tf_op jit(solution)/shard_map/ppermute | solution.py:1404
  55.8 21.4 %collective-permute-start.3 = (bf16[3328,128]{1,0:T(8,128)(2,1)S(1)}, bf16[3328,128]{1,0:T(8,128)(2,1)S(1)}, u32[]{:S(2)}, u32[]{:S(2)}) collective-permute-start(bf16[3328,128]{1,0:T(8,128)(2,1)S(1)} %slice.74), channel_id=1, source_target_pairs={{0,8},{8,0},{16,24},{24,16},{1,9},{9,1},{17,25},{25,17},{2,10},{10... | collective-permute-start | bytes 2555912 | tf_op jit(solution)/shard_map/ppermute | solution.py:1386
  56.2 19.6 %collective-permute-start.4 = (bf16[3072,128]{1,0:T(8,128)(2,1)S(1)}, bf16[3072,128]{1,0:T(8,128)(2,1)S(1)}, u32[]{:S(2)}, u32[]{:S(2)}) collective-permute-start(bf16[3072,128]{1,0:T(8,128)(2,1)S(1)} %slice.75), channel_id=1, source_target_pairs={{0,16},{8,24},{16,0},{24,8},{1,17},{9,25},{17,1},{25,9},{2,18},{10... | collective-permute-start | bytes 2359304 | tf_op jit(solution)/shard_map/ppermute | solution.py:1390
  61.4 102.6 %copy-start.8 = (f32[1024,128]{1,0:T(8,128)}, f32[1024,128]{1,0:T(8,128)S(1)}, u32[]{:S(2)}) copy-start(f32[1024,128]{1,0:T(8,128)S(1)} %get-tuple-element.200.upper) | copy-start | bytes 1572868
  62.9 16.7 %copy-start.27 = (bf16[6144,128]{1,0:T(8,128)(2,1)}, bf16[6144,128]{1,0:T(8,128)(2,1)S(1)}, u32[]{:S(2)}) copy-start(bf16[6144,128]{1,0:T(8,128)(2,1)S(1)} %collective-permute-done.7.refs_4_.refs_12_) | copy-start | bytes 4718596
  75.8 6.8 %copy-start.34 = (bf16[3072,128]{1,0:T(8,128)(2,1)}, bf16[3072,128]{1,0:T(8,128)(2,1)S(1)}, u32[]{:S(2)}) copy-start(bf16[3072,128]{1,0:T(8,128)(2,1)S(1)} %collective-permute-done.4.refs_11_) | copy-start | bytes 2359300
  77.2 38.6 %collective-permute-start.8 = (bf16[6144,128]{1,0:T(8,128)(2,1)S(1)}, bf16[6144,128]{1,0:T(8,128)(2,1)}, u32[]{:S(2)}, u32[]{:S(2)}) collective-permute-start(bf16[6144,128]{1,0:T(8,128)(2,1)S(1)} %get-tuple-element.150.refs_0_.refs_8_), channel_id=1, source_target_pairs={{0,8},{8,0},{16,24},{24,16},{1,9},{9,1},{17,25},{25,17},{2,10},{10... | collective-permute-start | bytes 4718600 | tf_op jit(solution)/shard_map/ppermute | solution.py:1386
  77.6 38.2 %collective-permute-start.9 = (bf16[6144,128]{1,0:T(8,128)(2,1)S(1)}, bf16[6144,128]{1,0:T(8,128)(2,1)}, u32[]{:S(2)}, u32[]{:S(2)}) collective-permute-start(bf16[6144,128]{1,0:T(8,128)(2,1)S(1)} %get-tuple-element.150.refs_0_.refs_8_), channel_id=1, source_target_pairs={{0,16},{8,24},{16,0},{24,8},{1,17},{9,25},{17,1},{25,9},{2,18},{10... | collective-permute-start | bytes 4718600 | tf_op jit(solution)/shard_map/ppermute | solution.py:1390
  79.1 4.4 collective-permute-start.10
  79.2 3.5 collective-permute-start.11
  115.8 7.6 %collective-permute-start.16 = (bf16[1024,2048]{1,0:T(8,128)(2,1)}, bf16[1024,2048]{1,0:T(8,128)(2,1)}, u32[]{:S(2)}, u32[]{:S(2)}) collective-permute-start(bf16[1024,2048]{1,0:T(8,128)(2,1)} %bitcast.77), channel_id=1, source_target_pairs={{0,1},{1,0},{2,3},{3,2},{4,5},{5,4},{6,7},{7,6},{8,9},{9,8},{10,11... | collective-permute-start | bytes 12582920 | tf_op jit(solution)/shard_map/ppermute | solution.py:1404
  116.0 264.5 %reduce-scatter.2.cloned.1.call-start = ((), (), s32[]{:S(2)}) async-start(), calls=%async_computation.2 | async-start | bytes 10485760 | tf_op jit(solution)/shard_map/reduce_scatter | solution.py:1519
  116.5 24.7 %collective-permute-start.14 = (bf16[6144,128]{1,0:T(8,128)(2,1)}, bf16[6144,128]{1,0:T(8,128)(2,1)S(1)}, u32[]{:S(2)}, u32[]{:S(2)}) collective-permute-start(bf16[6144,128]{1,0:T(8,128)(2,1)} %collective-permute-done.8.refs_1_.refs_9_), channel_id=1, source_target_pairs={{0,1},{1,0},{2,3},{3,2},{4,5},{5,4},{6,7},{7,6},{8,9},{9,8},{10,11... | collective-permute-start | bytes 4718600 | tf_op jit(solution)/shard_map/ppermute | solution.py:1404
  117.0 24.3 %collective-permute-start.15 = (bf16[6144,128]{1,0:T(8,128)(2,1)}, bf16[6144,128]{1,0:T(8,128)(2,1)}, u32[]{:S(2)}, u32[]{:S(2)}) collective-permute-start(bf16[6144,128]{1,0:T(8,128)(2,1)} %collective-permute-done.9.refs_0_.refs_2_.refs_10_), channel_id=1, source_target_pairs={{0,1},{1,0},{2,3},{3,2},{4,5},{5,4},{6,7},{7,6},{8,9},{9,8},{10,11... | collective-permute-start | bytes 4718600 | tf_op jit(solution)/shard_map/ppermute | solution.py:1404
  119.6 20.2 %collective-permute-start.12 = (bf16[3072,128]{1,0:T(8,128)(2,1)}, bf16[3072,128]{1,0:T(8,128)(2,1)}, u32[]{:S(2)}, u32[]{:S(2)}) collective-permute-start(bf16[3072,128]{1,0:T(8,128)(2,1)} %get-tuple-element.174), channel_id=1, source_target_pairs={{0,8},{8,0},{16,24},{24,16},{1,9},{9,1},{17,25},{25,17},{2,10},{10... | collective-permute-start | bytes 2359304 | tf_op jit(solution)/shard_map/ppermute | solution.py:1386
  121.4 19.8 %collective-permute-start.13 = (bf16[3072,128]{1,0:T(8,128)(2,1)}, bf16[3072,128]{1,0:T(8,128)(2,1)}, u32[]{:S(2)}, u32[]{:S(2)}) collective-permute-start(bf16[3072,128]{1,0:T(8,128)(2,1)} %get-tuple-element.175), channel_id=1, source_target_pairs={{0,16},{8,24},{16,0},{24,8},{1,17},{9,25},{17,1},{25,9},{2,18},{10... | collective-permute-start | bytes 2359304 | tf_op jit(solution)/shard_map/ppermute | solution.py:1390
  141.2 2.7 collective-permute-start.17
  141.3 3.7 collective-permute-start.18
  142.0 21.9 %copy-start.6 = (s32[1024,1]{1,0:T(8,128)}, s32[1024,1]{1,0:T(8,128)S(1)}, u32[]{:S(2)}) copy-start(s32[1024,1]{1,0:T(8,128)S(1)} %copy.30.begins) | copy-start | bytes 12292
  142.1 21.9 %copy-start.10 = (f32[1024,128]{1,0:T(8,128)S(1)}, f32[1024,128]{1,0:T(8,128)}, u32[]{:S(2)}) copy-start(f32[1024,128]{1,0:T(8,128)} %get-tuple-element.199.lower) | copy-start | bytes 1572868
  142.1 21.9 %copy-start.12 = (f32[1024,128]{1,0:T(8,128)S(1)}, f32[1024,128]{1,0:T(8,128)}, u32[]{:S(2)}) copy-start(f32[1024,128]{1,0:T(8,128)} %get-tuple-element.198.plain) | copy-start | bytes 1572868
  166.2 22.3 %copy-start.20 = (bf16[2560,2048]{1,0:T(8,128)(2,1)S(1)}, bf16[2560,2048]{1,0:T(8,128)(2,1)}, u32[]{:S(2)}) copy-start(bf16[2560,2048]{1,0:T(8,128)(2,1)} %get-tuple-element.204.down) | copy-start | bytes 31457284
  188.4 54.9 %collective-permute-start.19 = (bf16[1024,2560]{1,0:T(8,128)(2,1)}, bf16[1024,2560]{1,0:T(8,128)(2,1)}, u32[]{:S(2)}, u32[]{:S(2)}) collective-permute-start(bf16[1024,2560]{1,0:T(8,128)(2,1)} %get-tuple-element.203.refs_2_.refs_6_), channel_id=1, source_target_pairs={{0,1},{1,0},{2,3},{3,2},{4,5},{5,4},{6,7},{7,6},{8,9},{9,8},{10,11... | collective-permute-start | bytes 15728648 | tf_op jit(solution)/shard_map/ppermute | solution.py:1404
  203.6 39.7 %collective-permute-start.21 = (bf16[1024,2048]{1,0:T(8,128)(2,1)}, bf16[1024,2048]{1,0:T(8,128)(2,1)}, u32[]{:S(2)}, u32[]{:S(2)}) collective-permute-start(bf16[1024,2048]{1,0:T(8,128)(2,1)} %bitcast.70), channel_id=1, source_target_pairs={{0,1},{1,0},{2,3},{3,2},{4,5},{5,4},{6,7},{7,6},{8,9},{9,8},{10,11... | collective-permute-start | bytes 12582920 | tf_op jit(solution)/shard_map/ppermute | solution.py:1404
  222.3 10.6 %copy-start = (bf16[1024,1536]{1,0:T(8,128)(2,1)}, bf16[1024,1536]{1,0:T(8,128)(2,1)S(1)}, u32[]{:S(2)}) copy-start(bf16[1024,1536]{1,0:T(8,128)(2,1)S(1)} %attend_back.1.refs_8_.grad_projected) | copy-start | bytes 9437188
  222.3 20.9 %collective-permute-start.20 = (bf16[1024,1536]{1,0:T(8,128)(2,1)S(1)}, bf16[1024,1536]{1,0:T(8,128)(2,1)}, u32[]{:S(2)}, u32[]{:S(2)}) collective-permute-start(bf16[1024,1536]{1,0:T(8,128)(2,1)S(1)} %attend_back.1.refs_8_.grad_projected), channel_id=1, source_target_pairs={{0,1},{1,0},{2,3},{3,2},{4,5},{5,4},{6,7},{7,6},{8,9},{9,8},{10,11... | collective-permute-start | bytes 9437192 | tf_op jit(solution)/shard_map/ppermute | solution.py:1404
  222.5 10.5 %copy-start.19 = (s32[8]{0:T(128)S(1)}, s32[8]{0:T(128)}, u32[]{:S(2)}) copy-start(s32[8]{0:T(128)} %copy-done.18) | copy-start | bytes 100
  233.0 10.3 %collective-permute-start.22 = (bf16[1024,1024]{1,0:T(8,128)(2,1)}, bf16[1024,1024]{1,0:T(8,128)(2,1)}, u32[]{:S(2)}, u32[]{:S(2)}) collective-permute-start(bf16[1024,1024]{1,0:T(8,128)(2,1)} %get-tuple-element.229.rest_before), channel_id=1, source_target_pairs={{0,1},{1,0},{2,3},{3,2},{4,5},{5,4},{6,7},{7,6},{8,9},{9,8},{10,11... | collective-permute-start | bytes 6291464 | tf_op jit(solution)/shard_map/ppermute | solution.py:1404
  243.3 43.1 %copy-start.38 = (f32[1,1024]{1,0:T(1,128)S(1)}, f32[1,1024]{1,0:T(1,128)}, u32[]{:S(2)}) copy-start(f32[1,1024]{1,0:T(1,128)} %get-tuple-element.238) | copy-start | bytes 12292
  243.3 43.1 %copy-start.39 = (f32[1,1024]{1,0:T(1,128)S(1)}, f32[1,1024]{1,0:T(1,128)}, u32[]{:S(2)}) copy-start(f32[1,1024]{1,0:T(1,128)} %get-tuple-element.237) | copy-start | bytes 12292
  284.4 28.8 %collective-permute-start.25 = (f32[2,2,3136,128]{3,2,1,0:T(8,128)}, f32[2,2,3136,128]{3,2,1,0:T(8,128)}, u32[]{:S(2)}, u32[]{:S(2)}) collective-permute-start(f32[2,2,3136,128]{3,2,1,0:T(8,128)} %get-tuple-element.233.refs_0_), channel_id=1, source_target_pairs={{0,1},{1,0},{2,3},{3,2},{4,5},{5,4},{6,7},{7,6},{8,9},{9,8},{10,11... | collective-permute-start | bytes 19267592 | tf_op jit(solution)/shard_map/ppermute | solution.py:1404
  284.7 39.0 %collective-permute-start.23 = (bf16[2,3136,128]{2,1,0:T(8,128)(2,1)}, bf16[2,3136,128]{2,1,0:T(8,128)(2,1)}, u32[]{:S(2)}, u32[]{:S(2)}) collective-permute-start(bf16[2,3136,128]{2,1,0:T(8,128)(2,1)} %get-tuple-element.224), channel_id=1, source_target_pairs={{0,8},{8,0},{16,24},{24,16},{1,9},{9,1},{17,25},{25,17},{2,10},{10... | collective-permute-start | bytes 4816904 | tf_op jit(solution)/shard_map/ppermute | solution.py:1386
  285.1 38.6 %collective-permute-start.24 = (bf16[2,3136,128]{2,1,0:T(8,128)(2,1)}, bf16[2,3136,128]{2,1,0:T(8,128)(2,1)}, u32[]{:S(2)}, u32[]{:S(2)}) collective-permute-start(bf16[2,3136,128]{2,1,0:T(8,128)(2,1)} %get-tuple-element.225), channel_id=1, source_target_pairs={{0,16},{8,24},{16,0},{24,8},{1,17},{9,25},{17,1},{25,9},{2,18},{10... | collective-permute-start | bytes 4816904 | tf_op jit(solution)/shard_map/ppermute | solution.py:1390
  289.2 28.3 %copy-start.1 = (bf16[1024,1536]{1,0:T(8,128)(2,1)S(1)}, bf16[1024,1536]{1,0:T(8,128)(2,1)}, u32[]{:S(2)}) copy-start(bf16[1024,1536]{1,0:T(8,128)(2,1)} %copy-done) | copy-start | bytes 9437188
  313.2 7.4 %collective-permute-start.27 = (f32[4,2048]{1,0:T(4,128)}, f32[4,2048]{1,0:T(4,128)S(1)}, u32[]{:S(2)}, u32[]{:S(2)}) collective-permute-start(f32[4,2048]{1,0:T(4,128)} %get-tuple-element.236), channel_id=1, source_target_pairs={{0,4},{2,6},{4,0},{6,2},{1,5},{3,7},{5,1},{7,3},{8,12},{10,14},{12... | collective-permute-start | bytes 98312 | tf_op jit(solution)/shard_map/ppermute | solution.py:1394
  316.0 6.9 %collective-permute-start.28 = (f32[4,2048]{1,0:T(4,128)}, f32[4,2048]{1,0:T(4,128)S(1)}, u32[]{:S(2)}, u32[]{:S(2)}) collective-permute-start(f32[4,2048]{1,0:T(4,128)} %get-tuple-element.236), channel_id=1, source_target_pairs={{0,6},{2,4},{4,2},{6,0},{1,7},{3,5},{5,3},{7,1},{8,14},{10,12},{12... | collective-permute-start | bytes 98312 | tf_op jit(solution)/shard_map/ppermute | solution.py:1394
  317.1 5.7 %collective-permute-start.26 = (f32[4,2048]{1,0:T(4,128)}, f32[4,2048]{1,0:T(4,128)S(1)}, u32[]{:S(2)}, u32[]{:S(2)}) collective-permute-start(f32[4,2048]{1,0:T(4,128)} %get-tuple-element.236), channel_id=1, source_target_pairs={{0,2},{2,0},{4,6},{6,4},{1,3},{3,1},{5,7},{7,5},{8,10},{10,8},{12,... | collective-permute-start | bytes 98312 | tf_op jit(solution)/shard_map/ppermute | solution.py:1394
  323.7 116.3 %all-to-all-start = ((bf16[4,256,2048]{2,1,0:T(8,128)(2,1)}), bf16[4,256,2048]{2,1,0:T(8,128)(2,1)}, u32[]{:S(2)}, u32[]{:S(2)}) async-start(bf16[4,256,2048]{2,1,0:T(8,128)(2,1)} %bitcast.83), calls=%async_computation.1 | async-start | bytes 8388608 | tf_op jit(solution)/shard_map/all_to_all | solution.py:1410
  328.7 5.9 %collective-permute-start.33 = (f32[128,128]{1,0:T(8,128)S(1)}, f32[128,128]{1,0:T(8,128)S(1)}, u32[]{:S(2)}, u32[]{:S(2)}) collective-permute-start(f32[128,128]{1,0:T(8,128)S(1)} %bitcast.90), channel_id=1, source_target_pairs={{0,1},{1,0},{2,3},{3,2},{4,5},{5,4},{6,7},{7,6},{8,9},{9,8},{10,11... | collective-permute-start | bytes 196616 | tf_op jit(solution)/shard_map/ppermute | solution.py:1404
  330.8 39.2 %collective-permute-start.29 = (bf16[3136,128]{1,0:T(8,128)(2,1)}, bf16[3136,128]{1,0:T(8,128)(2,1)S(1)}, u32[]{:S(2)}, u32[]{:S(2)}) collective-permute-start(bf16[3136,128]{1,0:T(8,128)(2,1)} %get-tuple-element.243), channel_id=1, source_target_pairs={{0,8},{8,0},{16,24},{24,16},{1,9},{9,1},{17,25},{25,17},{2,10},{10... | collective-permute-start | bytes 2408456 | tf_op jit(solution)/shard_map/ppermute | solution.py:1386
  332.3 37.7 %collective-permute-start.30 = (bf16[3136,128]{1,0:T(8,128)(2,1)}, bf16[3136,128]{1,0:T(8,128)(2,1)S(1)}, u32[]{:S(2)}, u32[]{:S(2)}) collective-permute-start(bf16[3136,128]{1,0:T(8,128)(2,1)} %get-tuple-element.244), channel_id=1, source_target_pairs={{0,16},{8,24},{16,0},{24,8},{1,17},{9,25},{17,1},{25,9},{2,18},{10... | collective-permute-start | bytes 2408456 | tf_op jit(solution)/shard_map/ppermute | solution.py:1390
  333.7 36.3 %collective-permute-start.31 = (bf16[3136,128]{1,0:T(8,128)(2,1)}, bf16[3136,128]{1,0:T(8,128)(2,1)S(1)}, u32[]{:S(2)}, u32[]{:S(2)}) collective-permute-start(bf16[3136,128]{1,0:T(8,128)(2,1)} %get-tuple-element.245), channel_id=1, source_target_pairs={{0,9},{1,8},{8,1},{9,0},{16,25},{17,24},{24,17},{25,16},{2,11},{3,... | collective-permute-start | bytes 2408456 | tf_op jit(solution)/shard_map/ppermute | solution.py:1398
  333.7 36.3 %collective-permute-start.32 = (bf16[3136,128]{1,0:T(8,128)(2,1)}, bf16[3136,128]{1,0:T(8,128)(2,1)S(1)}, u32[]{:S(2)}, u32[]{:S(2)}) collective-permute-start(bf16[3136,128]{1,0:T(8,128)(2,1)} %get-tuple-element.246), channel_id=1, source_target_pairs={{0,17},{1,16},{8,25},{9,24},{16,1},{17,0},{24,9},{25,8},{2,19},{3,... | collective-permute-start | bytes 2408456 | tf_op jit(solution)/shard_map/ppermute | solution.py:1398
  334.6 35.3 %copy-start.37 = (f32[16384]{0:T(1024)S(1)}, f32[16384]{0:T(1024)}, u32[]{:S(2)}) copy-start(f32[16384]{0:T(1024)} %copy-done.36) | copy-start | bytes 196612
  334.6 45.9 %copy-start.23 = (bf16[1,256,2048]{2,1,0:T(8,128)(2,1)S(1)}, bf16[1,256,2048]{2,1,0:T(8,128)(2,1)}, u32[]{:S(2)}) copy-start(bf16[1,256,2048]{2,1,0:T(8,128)(2,1)} %param.12) | copy-start | bytes 3145732
  334.6 35.3 %collective-permute-start.34 = (f32[128,128]{1,0:T(8,128)S(1)}, f32[128,128]{1,0:T(8,128)S(1)}, u32[]{:S(2)}, u32[]{:S(2)}) collective-permute-start(f32[128,128]{1,0:T(8,128)S(1)} %bitcast_add_fusion), channel_id=1, source_target_pairs={{0,8},{8,0},{16,24},{24,16},{1,9},{9,1},{17,25},{25,17},{2,10},{10... | collective-permute-start | bytes 196616 | tf_op jit(solution)/shard_map/ppermute | solution.py:1386
  370.0 39.2 %collective-permute-start.35 = (bf16[3136,128]{1,0:T(8,128)(2,1)}, bf16[3136,128]{1,0:T(8,128)(2,1)}, u32[]{:S(2)}, u32[]{:S(2)}) collective-permute-start(bf16[3136,128]{1,0:T(8,128)(2,1)} %get-tuple-element.254), channel_id=1, source_target_pairs={{0,16},{8,24},{16,0},{24,8},{1,17},{9,25},{17,1},{25,9},{2,18},{10... | collective-permute-start | bytes 2408456 | tf_op jit(solution)/shard_map/ppermute | solution.py:1390
  371.4 37.8 %collective-permute-start.36 = (bf16[3136,128]{1,0:T(8,128)(2,1)S(1)}, bf16[3136,128]{1,0:T(8,128)(2,1)}, u32[]{:S(2)}, u32[]{:S(2)}) collective-permute-start(bf16[3136,128]{1,0:T(8,128)(2,1)S(1)} %get-tuple-element.255), channel_id=1, source_target_pairs={{0,8},{8,0},{16,24},{24,16},{1,9},{9,1},{17,25},{25,17},{2,10},{10... | collective-permute-start | bytes 2408456 | tf_op jit(solution)/shard_map/ppermute | solution.py:1386
  373.0 36.2 %collective-permute-start.37 = (bf16[3136,128]{1,0:T(8,128)(2,1)S(1)}, bf16[3136,128]{1,0:T(8,128)(2,1)}, u32[]{:S(2)}, u32[]{:S(2)}) collective-permute-start(bf16[3136,128]{1,0:T(8,128)(2,1)S(1)} %get-tuple-element.256), channel_id=1, source_target_pairs={{0,17},{1,16},{8,25},{9,24},{16,1},{17,0},{24,9},{25,8},{2,19},{3,... | collective-permute-start | bytes 2408456 | tf_op jit(solution)/shard_map/ppermute | solution.py:1398
  373.0 36.2 %collective-permute-start.38 = (bf16[3136,128]{1,0:T(8,128)(2,1)S(1)}, bf16[3136,128]{1,0:T(8,128)(2,1)}, u32[]{:S(2)}, u32[]{:S(2)}) collective-permute-start(bf16[3136,128]{1,0:T(8,128)(2,1)S(1)} %get-tuple-element.257), channel_id=1, source_target_pairs={{0,9},{1,8},{8,1},{9,0},{16,25},{17,24},{24,17},{25,16},{2,11},{3,... | collective-permute-start | bytes 2408456 | tf_op jit(solution)/shard_map/ppermute | solution.py:1398
  383.9 24.7 %collective-permute-start.39 = (f32[128,128]{1,0:T(8,128)S(1)}, f32[128,128]{1,0:T(8,128)S(1)}, u32[]{:S(2)}, u32[]{:S(2)}) collective-permute-start(f32[128,128]{1,0:T(8,128)S(1)} %fusion.15), channel_id=1, source_target_pairs={{0,16},{8,24},{16,0},{24,8},{1,17},{9,25},{17,1},{25,9},{2,18},{10... | collective-permute-start | bytes 196616 | tf_op jit(solution)/shard_map/ppermute | solution.py:1390
  (21 other events, 83.8 us)
Sparse Core Ops, SparseCore 0:
  9.6 83.4 all-gather.4
  116.1 81.2 all-gather.6
  204.1 176.3 reduce-scatter.1
